TPU v7x, 32 devices: a whole 2x2x4 slice. The times are simulated.
32 devices in a mesh: replica: 4 (over y, core), fsdp: 8 (over z, x).
Axes of the slice: x: 2, y: 2, z: 4, core: 2. Of those that a mesh axis runs over, the one named last changes fastest.
Arguments:
- local_weights: bfloat16 [4, 2048, 512], P('replica', 'fsdp'), may hold values from -0.125 to 0.125
- global_weights: bfloat16 [2048, 512], P('fsdp'), may hold values from -0.125 to 0.125
- momentum: float32 [2048, 512], P('fsdp', 'replica'), may hold values from -0.12 to 0.12
- activations: bfloat16 [4, 2048, 2048], P('replica', 'fsdp'), may hold values from -6 to 6
- kv_cotangent: bfloat16 [4, 2048, 512], P('replica', 'fsdp'), may hold values from -6 to 6
Outputs:
- kv_rows: bfloat16 [4, 2048, 512], P('replica', 'fsdp')
- input_grad: bfloat16 [4, 2048, 2048], P('replica', 'fsdp')
- weight_grad: bfloat16 [4, 2048, 512], P('replica', 'fsdp')
- new_global: bfloat16 [2048, 512], P('fsdp')
- new_momentum: float32 [2048, 512], P('fsdp', 'replica')
All inputs are finite; a program needn't handle non-finite values. Where the computation divides by a largest or mean magnitude, that divisor is 1e-20 or more.
Results may differ from a plain program's by a relative error of at most 0.0038.
Values may be sent and summed in bfloat16 or wider, within the bound.
No kernel may reach another device: no remote copies, remote signals or barrier semaphores. Data moves between devices by JAX's collectives and lax.ppermute only.
A program may use at most 64 MiB of HBM per device.

v0:
```python
import jax
import jax.numpy as jnp
from jax import lax
from jax.sharding import PartitionSpec as P

BLOCK = 64


outer_rate = 0.7
outer_momentum = 0.9
scale_epsilon = 1e-06


def per_device(local_weights, global_weights, momentum, activations, kv_cotangent):
    local_shard = local_weights[0]
    inputs_here = activations[0]
    cotangent = kv_cotangent[0]
    rows_here = local_shard.shape[0]
    kv_width = local_shard.shape[1]
    tok_rows = inputs_here.shape[0]
    token_weight = 1.0 / (tok_rows * lax.axis_size("fsdp"))
    columns = inputs_here
    kv_sum = jnp.dot(
        columns,
        lax.all_gather(local_shard, "fsdp", axis=0, tiled=True),
        preferred_element_type=jnp.float32,
    )
    grad_in = lax.dot_general(
        cotangent,
        lax.all_gather(local_shard, "fsdp", axis=0, tiled=True),
        (((1,), (1,)), ((), ())),
        preferred_element_type=jnp.float32,
    )
    columns = inputs_here
    grad_rows = lax.psum_scatter(
        lax.dot_general(
            columns, cotangent, (((0,), (0,)), ((), ())), preferred_element_type=jnp.float32
        )
        * token_weight,
        "fsdp",
        scatter_dimension=0,
        tiled=True,
    )
    replicas = lax.axis_size("replica")
    share_cols = kv_width // replicas
    block_count = kv_width // BLOCK
    my_replica = lax.axis_index("replica")
    drift = global_weights.astype(jnp.float32) - local_shard.astype(jnp.float32)
    drift_blocks = drift.reshape(rows_here, block_count, BLOCK)
    block_scale = (jnp.max(jnp.abs(drift_blocks), axis=2) + scale_epsilon).astype(jnp.bfloat16)
    quantized = (drift_blocks / block_scale.astype(jnp.float32)[..., None]).astype(jnp.bfloat16)
    unit_cols = min(BLOCK, share_cols)
    scale_units = jnp.repeat(block_scale, BLOCK // unit_cols, axis=1)
    units_share = share_cols // unit_cols
    quant_send = (
        quantized.reshape(rows_here, replicas, share_cols)
        .transpose(1, 0, 2)
        .reshape(replicas, rows_here * share_cols)
    )
    scale_send = (
        scale_units.reshape(rows_here, replicas, units_share)
        .transpose(1, 0, 2)
        .reshape(replicas, rows_here * units_share)
    )
    quant_got, scale_got = (
        lax.all_to_all(quant_send, "replica", split_axis=0, concat_axis=0, tiled=True),
        lax.all_to_all(scale_send, "replica", split_axis=0, concat_axis=0, tiled=True),
    )
    dequantized = (
        quant_got.reshape(replicas, rows_here, units_share, unit_cols).astype(jnp.float32)
        * scale_got.reshape(replicas, rows_here, units_share).astype(jnp.float32)[..., None]
    )
    mean_grad = jnp.sum(dequantized, axis=0).reshape(rows_here, share_cols) / replicas
    old_share = lax.dynamic_slice_in_dim(
        global_weights, my_replica * share_cols, share_cols, 1
    ).astype(jnp.float32)
    new_momentum = outer_momentum * momentum + mean_grad
    new_share = (old_share - outer_rate * (mean_grad + outer_momentum * new_momentum)).astype(
        jnp.bfloat16
    )
    new_global = lax.all_gather(new_share, "replica", axis=1, tiled=True)
    return (
        kv_sum.astype(jnp.bfloat16)[None],
        grad_in.astype(jnp.bfloat16)[None],
        grad_rows.astype(jnp.bfloat16)[None],
        new_global,
        new_momentum,
    )


def solution(mesh):
    placed = (
        P("replica", "fsdp", None),
        P("fsdp", None),
        P("fsdp", "replica"),
        P("replica", "fsdp", None),
        P("replica", "fsdp", None),
    )
    return jax.shard_map(
        per_device,
        mesh=mesh,
        in_specs=placed,
        out_specs=(
            P("replica", "fsdp", None),
            P("replica", "fsdp", None),
            P("replica", "fsdp", None),
            P("fsdp", None),
            P("fsdp", "replica"),
        ),
        check_vma=False,
    )
```

profile of v0, /device:TPU:0, one launch (start us, length us, event | category | flops | bytes accessed | tf_op | source)
XLA Modules:
  0.0 161.5 jit_solution(3088905626676366069)
XLA Ops:
  7.2 0.7 all-gather.3.cloned.1.call-update
  8.0 0.4 copy-done
  8.4 3.6 %convolution_multiply_fusion = f32[2048,512]{1,0:T(8,128)} fusion(bf16[1,256,2048]{2,1,0:T(8,128)(2,1)S(1)} %copy-done, bf16[1,256,512]{2,1,0:T(8,128)(2,1)} %param.9), kind=kOutput, calls=%fused_computation | convolution fusion | flops 537919488 | bytes 5505024 | tf_op jit(solution)/shard_map/dot_general | solution.py:36
  12.1 0.9 copy-done.2
  13.6 0.5 broadcast.21
  14.1 0.7 reduce.3
  14.9 0.6 reshape.62
  15.5 4.2 %all-to-all-start.1 = ((bf16[4,2,256]{2,1,0:T(2,128)(2,1)}), bf16[4,2,256]{2,1,0:T(2,128)(2,1)S(1)}, u32[]{:S(2)}, u32[]{:S(2)}) async-start(bf16[4,2,256]{2,1,0:T(2,128)(2,1)} %reshape.62), calls=%async_computation.2 | async-start | bytes 8192 | tf_op jit(solution)/shard_map/all_to_all | solution.py:67
  20.3 2.3 %reduce.4 = bf16[4,32768]{1,0:T(4,128)(2,1)S(1)} reduce(bf16[4,1,32768]{2,1,0:T(2,128)(2,1)S(1)} %all_to_all.16, bf16[]{:T(256)} %broadcast.21), dimensions={1}, to_apply=%all_to_all.16.reduce_sub_computation | reduce | bytes 524290 | tf_op jit(solution)/shard_map/all_to_all | solution.py:66
  22.6 1.0 reshape.64
  23.6 3.4 %all-to-all-start = ((bf16[4,2,16384]{2,1,0:T(2,128)(2,1)}), bf16[4,2,16384]{2,1,0:T(2,128)(2,1)S(1)}, u32[]{:S(2)}, u32[]{:S(2)}) async-start(bf16[4,2,16384]{2,1,0:T(2,128)(2,1)} %reshape.64), calls=%async_computation.1 | async-start | bytes 524288 | tf_op jit(solution)/shard_map/all_to_all | solution.py:66
  27.2 2.0 %copy.33 = f32[4,256,2]{2,1,0:T(8,128)S(1)} copy(f32[4,256,2]{0,2,1:T(2,128)S(1)} %bitcast.59) | data formatting | bytes 16384 | tf_op jit(solution)/shard_map/convert_element_type | solution.py:71
  29.1 1.2 mul.37
  30.4 0.9 mul.38
  31.3 1.7 %all-to-all-done = bf16[4,2,16384]{2,1,0:T(2,128)(2,1)S(1)} async-done(((bf16[4,2,16384]{2,1,0:T(2,128)(2,1)}), bf16[4,2,16384]{2,1,0:T(2,128)(2,1)S(1)}, u32[]{:S(2)}, u32[]{:S(2)}) %all-to-all-start) | async-done | bytes 262176 | tf_op jit(solution)/shard_map/all_to_all | solution.py:66
  33.3 0.6 multiply_reduce_fusion
  33.9 0.7 fusion.18
  34.6 5.8 %all_gather.8 = bf16[256,512]{1,0:T(8,128)(2,1)S(1)} all-gather(bf16[256,128]{1,0:T(8,128)(2,1)S(1)} %get-tuple-element.5), channel_id=1, replica_groups=mesh['replica'=4,'fsdp'=8] {'replica'}, dimensions={1}, use_global_device_ids=true | all-gather | bytes 327680 | tf_op jit(solution)/shard_map/all_gather | solution.py:81
  40.4 21.7 %all-gather.3.cloned.1.call-done = bf16[1,2048,512]{2,1,0:T(8,128)(2,1)} async-done(((bf16[1,256,512]{2,1,0:T(8,128)(2,1)}), bf16[1,2048,512]{2,1,0:T(8,128)(2,1)}) %all-gather.3.cloned.1.call-update) | async-done | bytes 2097168 | tf_op jit(solution)/shard_map/all_gather | solution.py:25
  62.2 3.5 %fusion = bf16[1,256,2048]{2,1,0:T(8,128)(2,1)} fusion(bf16[1,2048,512]{2,1,0:T(8,128)(2,1)} %all-gather.3.cloned.1.call-done, bf16[1,256,512]{2,1,0:T(8,128)(2,1)S(1)} %copy-done.3), kind=kOutput, calls=%fused_computation.2 | convolution fusion | flops 537395200 | bytes 3407872 | tf_op jit(solution)/shard_map/dot_general | solution.py:28
  65.6 1.4 fusion.7
  67.0 85.2 %reduce-scatter.2.cloned.1.call-done = f32[256,512]{1,0:T(8,128)} async-done(((f32[2048,512]{1,0:T(8,128)}), f32[256,512]{1,0:T(8,128)}) %reduce-scatter.2.cloned.1.call-update) | async-done | bytes 524304 | tf_op jit(solution)/shard_map/reduce_scatter | solution.py:35
  152.2 1.8 %convert_bitcast_fusion = bf16[1,256,512]{2,1,0:T(8,128)(2,1)} fusion(f32[256,512]{1,0:T(8,128)} %reduce-scatter.2.cloned.1.call-done), kind=kLoop, calls=%fused_computation.17 | loop fusion | flops 131072 | bytes 786432 | tf_op jit(solution)/shard_map/broadcast_in_dim | solution.py:85
  154.0 0.7 copy.38
  (30 shorter events, 1.7 us)
Async XLA Ops:
  7.2 1.2 copy-start
  7.2 55.0 %all-gather.3.cloned.1.call-start = ((), (), s32[]{:S(2)}) async-start(), calls=%async_computation.4 | async-start | bytes 2359296 | tf_op jit(solution)/shard_map/all_gather | solution.py:25
  7.9 144.3 %reduce-scatter.2.cloned.1.call-start = ((), (), s32[]{:S(2)}) async-start(), calls=%async_computation.3 | async-start | bytes 4718592 | tf_op jit(solution)/shard_map/reduce_scatter | solution.py:35
  12.0 0.9 copy-start.2
  12.0 1.1 copy-start.4
  15.5 8.1 %all-to-all-start.1 = ((bf16[4,2,256]{2,1,0:T(2,128)(2,1)}), bf16[4,2,256]{2,1,0:T(2,128)(2,1)S(1)}, u32[]{:S(2)}, u32[]{:S(2)}) async-start(bf16[4,2,256]{2,1,0:T(2,128)(2,1)} %reshape.62), calls=%async_computation.2 | async-start | bytes 8192 | tf_op jit(solution)/shard_map/all_to_all | solution.py:67
  23.6 9.4 %all-to-all-start = ((bf16[4,2,16384]{2,1,0:T(2,128)(2,1)}), bf16[4,2,16384]{2,1,0:T(2,128)(2,1)S(1)}, u32[]{:S(2)}, u32[]{:S(2)}) async-start(bf16[4,2,16384]{2,1,0:T(2,128)(2,1)} %reshape.64), calls=%async_computation.1 | async-start | bytes 524288 | tf_op jit(solution)/shard_map/all_to_all | solution.py:66
  30.4 3.5 %copy-start.5 = (f32[256,128]{1,0:T(8,128)S(1)}, f32[256,128]{1,0:T(8,128)}, u32[]{:S(2)}) copy-start(f32[256,128]{1,0:T(8,128)} %param.7) | copy-start | bytes 393220
  30.4 31.8 %copy-start.3 = (bf16[1,256,512]{2,1,0:T(8,128)(2,1)S(1)}, bf16[1,256,512]{2,1,0:T(8,128)(2,1)}, u32[]{:S(2)}) copy-start(bf16[1,256,512]{2,1,0:T(8,128)(2,1)} %param.9) | copy-start | bytes 786436
  62.2 3.5 %copy-start.1 = (bf16[1,2048,512]{2,1,0:T(8,128)(2,1)S(1)}, bf16[1,2048,512]{2,1,0:T(8,128)(2,1)}, u32[]{:S(2)}) copy-start(bf16[1,2048,512]{2,1,0:T(8,128)(2,1)} %all-gather.3.cloned.1.call-done) | copy-start | bytes 6291460
Sparse Core Ops, SparseCore 0:
  10.1 51.9 all-gather.2
  65.8 86.3 reduce-scatter.1
where the time goes:
time: 162 us
  waiting for transfers between devices  109 us (67%)
  between operations  14.2 us (9%)
  local copies, waits for them, and re-layouts  9.6 us (6%)
  matrix products  8.49 us (5%)
  starting transfers between devices  7.72 us (5%)
  other arithmetic  6.35 us (4%)
  blocking collectives  5.79 us (4%)
    reduce_scatter x1, waiting for transfers between devices, per_device(): lax.psum_scatter(lax.dot_general(columns, cotangent, (((0,), (0,)), ((),...  85.2 us
    all_gather x1, waiting for transfers between devices, per_device(): lax.all_gather(local_shard, 'fsdp', axis=0, tiled=True)  21.7 us
    all_gather x1, blocking collectives, per_device(): new_global = lax.all_gather(new_share, 'replica', axis=1, tiled=True)  5.79 us
    unnamed x20, local copies, waits for them, and re-layouts  4.35 us
    all_to_all x1, starting transfers between devices, per_device(): lax.all_to_all(scale_send, 'replica', split_axis=0, concat_axis=0, tiled=...  4.24 us
    dot_general x1, matrix products, per_device(): lax.dot_general(columns, cotangent, (((0,), (0,)), ((), ())), preferred_e...  3.63 us
    dot_general x1, matrix products, per_device(): lax.dot_general(cotangent, lax.all_gather(local_shard, 'fsdp', axis=0, ti...  3.45 us
    all_to_all x1, starting transfers between devices, per_device(): lax.all_to_all(quant_send, 'replica', split_axis=0, concat_axis=0, tiled=...  3.41 us
  transfers between devices with their start and end apart: 4, of which 3 were waited for; matrix products, arithmetic and copies ran while one was open for 13% of the time, Pallas kernels for 0%

commit v1 on v0

v1 whole, which is shorter than its diff:
```python
import functools

import jax
import jax.numpy as jnp
from jax import lax
from jax.experimental import pallas as pl
from jax.experimental.pallas import tpu as pltpu
from jax.sharding import PartitionSpec as P

BLOCK = 64

outer_rate = 0.7
outer_momentum = 0.9
scale_epsilon = 1e-06

F32 = jnp.float32
BF16 = jnp.bfloat16


def ring_order(size):
    return list(range(0, size, 2)) + list(range(1, size, 2))[::-1]


def ring_place(index, size):
    return jnp.where(index % 2 == 0, index // 2, size - 1 - index // 2)


def ring_index(place, size):
    place = (place + size) % size
    evens = (size + 1) // 2
    return jnp.where(place < evens, 2 * place, 2 * (size - 1 - place) + 1)


def vmem_call(kernel, out_shape, operands, flops, name):
    moved = sum(x.size * x.dtype.itemsize for x in operands)
    return pl.pallas_call(
        kernel,
        out_shape=out_shape,
        in_specs=[pl.BlockSpec(memory_space=pltpu.VMEM)] * len(operands),
        out_specs=jax.tree.map(lambda _: pl.BlockSpec(memory_space=pltpu.VMEM), out_shape),
        compiler_params=pltpu.CompilerParams(vmem_limit_bytes=32 * 2**20),
        cost_estimate=pl.CostEstimate(flops=flops, bytes_accessed=moved, transcendentals=0),
        name=name,
    )(*operands)


def outer_kernel(replicas, share_cols, *refs):
    local_refs = refs[:replicas]
    global_ref, momentum_ref, share_ref, new_momentum_ref = refs[replicas:]
    rows, window = global_ref.shape
    old = global_ref[...].astype(F32)
    lane = lax.broadcasted_iota(jnp.int32, (rows, window), 1) // BLOCK
    total = jnp.zeros((rows, window), F32)
    for local_ref in local_refs:
        drift = old - local_ref[...].astype(F32)
        size = jnp.abs(drift)
        scale = jnp.zeros((rows, window), F32)
        for block in range(window // BLOCK):
            top = jnp.max(jnp.where(lane == block, size, 0.0), axis=1, keepdims=True)
            top = (top + scale_epsilon).astype(BF16).astype(F32)
            scale = jnp.where(lane == block, top, scale)
        total = total + (drift / scale).astype(BF16).astype(F32) * scale
    mean_grad = total / replicas
    shares = window // share_cols
    mean_here, old_here = mean_grad[:, :share_cols], old[:, :share_cols]
    mine = lax.axis_index("replica") % shares
    for share in range(1, shares):
        columns = slice(share * share_cols, (share + 1) * share_cols)
        mean_here = jnp.where(mine == share, mean_grad[:, columns], mean_here)
        old_here = jnp.where(mine == share, old[:, columns], old_here)
    new_momentum = outer_momentum * momentum_ref[...] + mean_here
    new_momentum_ref[...] = new_momentum
    share_ref[...] = (old_here - outer_rate * (mean_here + outer_momentum * new_momentum)).astype(BF16)


def join_kernel(*refs):
    *share_refs, out_ref = refs
    me = lax.axis_index("replica")
    count = len(share_refs)
    width = out_ref.shape[1] // count
    pieces = [ref[...] for ref in share_refs]
    bit = 1
    while bit < count:
        odd = (me & bit) != 0
        pieces = [jnp.where(odd, pieces[at ^ bit], pieces[at]) for at in range(count)]
        bit *= 2
    for at in range(count):
        out_ref[:, at * width : (at + 1) * width] = pieces[at]


def outer_step(local_shard, global_weights, momentum):
    rows, kv_width = local_shard.shape
    replicas = lax.axis_size("replica")
    me = lax.axis_index("replica")
    share_cols = kv_width // replicas
    window = max(share_cols, BLOCK)

    def window_of(array, owner):
        return lax.dynamic_slice_in_dim(array, owner * share_cols // window * window, window, 1)

    def swap(array, bits):
        return lax.ppermute(array, "replica", [(at, at ^ bits) for at in range(replicas)])

    locals_here = [window_of(local_shard, me)]
    for bits in range(1, replicas):
        locals_here.append(swap(window_of(local_shard, me ^ bits), bits))
    new_share, new_momentum = vmem_call(
        functools.partial(outer_kernel, replicas, share_cols),
        (jax.ShapeDtypeStruct((rows, share_cols), BF16), jax.ShapeDtypeStruct((rows, share_cols), F32)),
        locals_here + [window_of(global_weights, me), momentum],
        20 * replicas * rows * window,
        "outer_update",
    )
    shares = [new_share] + [swap(new_share, bits) for bits in range(1, replicas)]
    new_global = vmem_call(
        join_kernel, jax.ShapeDtypeStruct((rows, kv_width), BF16), shares, rows * kv_width, "join_shares"
    )
    return new_global, new_momentum


def products_kernel(size, inputs_ref, cotangent_ref, *refs):
    *block_refs, rows_ref, grad_ref = refs
    depth = grad_ref.shape[1] // size
    place = ring_place(lax.axis_index("fsdp"), size)
    total = jnp.zeros(rows_ref.shape, F32)
    for step, block_ref in enumerate(block_refs):
        at = pl.multiple_of(ring_index(place + step, size) * depth, depth)
        block = block_ref[...]
        total = total + jnp.dot(inputs_ref[:, pl.ds(at, depth)], block, preferred_element_type=F32)
        grad_ref[:, pl.ds(at, depth)] = lax.dot_general(
            cotangent_ref[...], block, (((1,), (1,)), ((), ())), preferred_element_type=F32
        ).astype(BF16)
    rows_ref[...] = total.astype(BF16)


def products(inputs_here, cotangent, blocks):
    tokens, width = inputs_here.shape
    size = len(blocks)
    depth, kv_width = blocks[0].shape
    if depth % 128 == 0:
        return vmem_call(
            functools.partial(products_kernel, size),
            (jax.ShapeDtypeStruct((tokens, kv_width), BF16), jax.ShapeDtypeStruct((tokens, width), BF16)),
            [inputs_here, cotangent] + blocks,
            4 * tokens * width * kv_width,
            "projection_products",
        )
    place = ring_place(lax.axis_index("fsdp"), size)
    gathered = jnp.zeros((width, kv_width), BF16)
    for step, block in enumerate(blocks):
        gathered = lax.dynamic_update_slice_in_dim(gathered, block, ring_index(place + step, size) * depth, 0)
    rows = jnp.dot(inputs_here, gathered, preferred_element_type=F32).astype(BF16)
    grad = lax.dot_general(cotangent, gathered, (((1,), (1,)), ((), ())), preferred_element_type=F32)
    return rows, grad.astype(BF16)


def per_device(local_weights, global_weights, momentum, activations, kv_cotangent):
    local_shard = local_weights[0]
    inputs_here = activations[0]
    cotangent = kv_cotangent[0]
    depth = local_shard.shape[0]
    size = lax.axis_size("fsdp")
    token_weight = 1.0 / (inputs_here.shape[0] * size)
    order = ring_order(size)
    up = [(order[at], order[(at + 1) % size]) for at in range(size)]
    down = [(target, source) for source, target in up]
    place = ring_place(lax.axis_index("fsdp"), size)
    far = size // 2
    cut = depth // 2

    blocks = [None] * size
    blocks[0] = local_shard
    from_below = from_above = local_shard
    for step in range(1, far):
        from_below = lax.ppermute(from_below, "fsdp", up)
        from_above = lax.ppermute(from_above, "fsdp", down)
        blocks[size - step] = from_below
        blocks[step] = from_above
    blocks[far] = jnp.concatenate(
        [lax.ppermute(from_below[:cut], "fsdp", up), lax.ppermute(from_above[cut:], "fsdp", down)]
    )

    def terms(offset):
        columns = lax.dynamic_slice_in_dim(inputs_here, ring_index(place + offset, size) * depth, depth, 1)
        return (
            lax.dot_general(columns, cotangent, (((0,), (0,)), ((), ())), preferred_element_type=F32) * token_weight
        )

    farthest = terms(far).astype(BF16)
    sum_up = lax.ppermute(farthest[:cut], "fsdp", up)
    sum_down = lax.ppermute(farthest[cut:], "fsdp", down)
    sum_up = jnp.concatenate([sum_up, jnp.zeros_like(sum_up)])
    sum_down = jnp.concatenate([jnp.zeros_like(sum_down), sum_down])
    for step in range(far - 1, 0, -1):
        sum_up = lax.ppermute((terms(step) + sum_up.astype(F32)).astype(BF16), "fsdp", up)
        sum_down = lax.ppermute((terms(-step) + sum_down.astype(F32)).astype(BF16), "fsdp", down)
    grad_rows = (terms(0) + sum_up.astype(F32) + sum_down.astype(F32)).astype(BF16)

    new_global, new_momentum = outer_step(local_shard, global_weights, momentum)
    kv_rows, grad_in = products(inputs_here, cotangent, blocks)
    return kv_rows[None], grad_in[None], grad_rows[None], new_global, new_momentum


def solution(mesh):
    placed = (
        P("replica", "fsdp", None),
        P("fsdp", None),
        P("fsdp", "replica"),
        P("replica", "fsdp", None),
        P("replica", "fsdp", None),
    )
    return jax.shard_map(
        per_device,
        mesh=mesh,
        in_specs=placed,
        out_specs=(
            P("replica", "fsdp", None),
            P("replica", "fsdp", None),
            P("replica", "fsdp", None),
            P("fsdp", None),
            P("fsdp", "replica"),
        ),
        check_vma=False,
    )
```

time: 162 us -> 56.1 us (0.35)
  waiting for transfers between devices: 109 us -> 17.5 us
  starting transfers between devices: 7.72 us -> 22.2 us
  between operations: 14.2 us -> 1 us
  local copies, waits for them, and re-layouts: 9.6 us -> 0.78 us
  blocking collectives: 5.79 us -> 0 us
  Pallas kernels: 0 us -> 4.19 us
  matrix products: 8.49 us -> 5.58 us
  other arithmetic: 6.35 us -> 4.58 us
    reduce_scatter x1 -> x0, waiting for transfers between devices: 85.2 us -> none  [per_device(): lax.psum_scatter(lax.dot_general(columns, cotangent, (((0,), (0,)), ((),...]
    ppermute x0 -> x22, starting transfers between devices: none -> 22.2 us  [the longest x3 5.96 us: per_device(): from_above = lax.ppermute(from_above, 'fsdp', down)]
    all_gather x1 -> x0, waiting for transfers between devices: 21.7 us -> none  [per_device(): lax.all_gather(local_shard, 'fsdp', axis=0, tiled=True)]
    ppermute x0 -> x22, waiting for transfers between devices: none -> 17.5 us  [the longest x1 5.08 us: per_device(): lax.ppermute(from_above[cut:], 'fsdp', down)]
    all_to_all x2 -> x0, starting transfers between devices: 7.64 us -> none  [the longest x1 4.24 us: per_device(): lax.all_to_all(scale_send, 'replica', split_axis=0, concat_axis=0, tiled=...]
    all_gather x1 -> x0, blocking collectives: 5.79 us -> none  [per_device(): new_global = lax.all_gather(new_share, 'replica', axis=1, tiled=True)]
    pallas_call x0 -> x3, Pallas kernels: none -> 4.19 us  [vmem_call(): pl.pallas_call(kernel, out_shape=out_shape, in_specs=[pl.BlockSpec(memory...]
    unnamed x20 -> x14, local copies, waits for them, and re-layouts: 4.35 us -> 0.69 us
  transfers between devices with their start and end apart: 4 -> 22, of which waited for: 3 -> 6; matrix products, arithmetic and copies ran while one was open for 13% -> 17% of each run, Pallas kernels for 0% -> 7%
where the time goes in v1:
time: 56.1 us; the launch traced here: 55.9 us
  starting transfers between devices  22.2 us (40%)
  waiting for transfers between devices  17.5 us (31%)
  matrix products  5.58 us (10%)
  other arithmetic  4.58 us (8%)
  Pallas kernels  4.19 us (7%)
  between operations  1 us (2%)
  local copies, waits for them, and re-layouts  0.78 us (1%)
    ppermute x3, starting transfers between devices, per_device(): from_above = lax.ppermute(from_above, 'fsdp', down)  5.96 us
    dot_general x8, matrix products, terms(): lax.dot_general(columns, cotangent, (((0,), (0,)), ((), ())), preferred_e...  5.58 us
    ppermute x1, waiting for transfers between devices, per_device(): lax.ppermute(from_above[cut:], 'fsdp', down)  5.08 us
    pallas_call x3, Pallas kernels, vmem_call(): pl.pallas_call(kernel, out_shape=out_shape, in_specs=[pl.BlockSpec(memory...  4.19 us
    ppermute x3, waiting for transfers between devices, per_device(): from_above = lax.ppermute(from_above, 'fsdp', down)  3.83 us
    ppermute x3, starting transfers between devices, per_device(): lax.ppermute((terms(-step) + sum_down.astype(F32)).astype(BF16), 'fsdp',...  3.47 us
    ppermute x6, starting transfers between devices, swap(): lax.ppermute(array, 'replica', [(at, at ^ bits) for at in range(replicas)])  3.4 us
    ppermute x3, waiting for transfers between devices, per_device(): lax.ppermute((terms(-step) + sum_down.astype(F32)).astype(BF16), 'fsdp',...  3.38 us
  transfers between devices with their start and end apart: 22, of which 6 were waited for; matrix products, arithmetic and copies ran while one was open for 17% of the time, Pallas kernels for 7%

profile of v1, /device:TPU:0, one launch (start us, length us, event | category | flops | bytes accessed | tf_op | source)
XLA Modules:
  0.0 55.9 jit_solution(9489931432593142330)
XLA Ops:
  0.6 3.0 %collective-permute-start = (bf16[256,512]{1,0:T(8,128)(2,1)}, bf16[256,512]{1,0:T(8,128)(2,1)S(1)}, u32[]{:S(2)}, u32[]{:S(2)}) collective-permute-start(bf16[256,512]{1,0:T(8,128)(2,1)} %bitcast.57), channel_id=1, source_target_pairs={{2,0},{4,2},{6,4},{7,6},{5,7},{3,5},{1,3},{0,1},{10,8},{12,10},{14... | collective-permute-start | bytes 786440 | tf_op jit(solution)/shard_map/ppermute | solution.py:176
  3.8 1.3 %fusion = bf16[256,512]{1,0:T(8,128)(2,1)S(1)} fusion(bf16[1,256,2048]{2,1,0:T(8,128)(2,1)} %param.8, s32[]{:T(128)S(6)} %select_n.138, bf16[1,256,512]{2,1,0:T(8,128)(2,1)} %param.9), kind=kOutput, calls=%fused_computation.8 | convolution fusion | flops 67371008 | bytes 655364 | tf_op jit(solution)/shard_map/dot_general | solution.py:186
  5.2 1.9 %collective-permute-start.12 = (bf16[128,512]{1,0:T(8,128)(2,1)S(1)}, bf16[128,512]{1,0:T(8,128)(2,1)S(1)}, u32[]{:S(2)}, u32[]{:S(2)}) collective-permute-start(bf16[128,512]{1,0:T(8,128)(2,1)S(1)} %get-tuple-element.18), channel_id=1, source_target_pairs={{2,0},{4,2},{6,4},{7,6},{5,7},{3,5},{1,3},{0,1},{10,8},{12,10},{14... | collective-permute-start | bytes 393224 | tf_op jit(solution)/shard_map/ppermute | solution.py:191
  8.2 1.1 %convolution_multiply_fusion.2 = f32[256,512]{1,0:T(8,128)} fusion(bf16[1,256,2048]{2,1,0:T(8,128)(2,1)S(1)} %copy-done.2, s32[]{:T(128)S(6)} %select_n.141, bf16[1,256,512]{2,1,0:T(8,128)(2,1)S(1)} %copy-done.1), kind=kOutput, calls=%fused_computation.2 | convolution fusion | flops 67239936 | bytes 917508 | tf_op jit(solution)/shard_map/dot_general | solution.py:186
  9.3 1.1 %convolution_multiply_fusion.1 = f32[256,512]{1,0:T(8,128)} fusion(bf16[1,256,2048]{2,1,0:T(8,128)(2,1)S(1)} %copy-done.2, s32[]{:T(128)S(6)} %select_n.144, bf16[1,256,512]{2,1,0:T(8,128)(2,1)S(1)} %copy-done.1), kind=kOutput, calls=%fused_computation.1 | convolution fusion | flops 67239936 | bytes 917508 | tf_op jit(solution)/shard_map/dot_general | solution.py:186
  10.4 1.1 %convolution_multiply_fusion.6 = f32[256,512]{1,0:T(8,128)} fusion(bf16[1,256,2048]{2,1,0:T(8,128)(2,1)S(1)} %copy-done.2, s32[]{:T(128)S(6)} %select_n.129, bf16[1,256,512]{2,1,0:T(8,128)(2,1)S(1)} %copy-done.1), kind=kOutput, calls=%fused_computation.6 | convolution fusion | flops 67239936 | bytes 917508 | tf_op jit(solution)/shard_map/dot_general | solution.py:186
  11.4 1.6 %collective-permute-done.12 = bf16[128,512]{1,0:T(8,128)(2,1)S(1)} collective-permute-done((bf16[128,512]{1,0:T(8,128)(2,1)S(1)}, bf16[128,512]{1,0:T(8,128)(2,1)S(1)}, u32[]{:S(2)}, u32[]{:S(2)}) %collective-permute-start.12) | collective-permute-done | bytes 131104 | tf_op jit(solution)/shard_map/ppermute | solution.py:191
  13.3 1.7 %collective-permute-start.13 = (bf16[256,512]{1,0:T(8,128)(2,1)S(1)}, bf16[256,512]{1,0:T(8,128)(2,1)S(1)}, u32[]{:S(2)}, u32[]{:S(2)}) collective-permute-start(bf16[256,512]{1,0:T(8,128)(2,1)S(1)} %add_convert_fusion.3), channel_id=1, source_target_pairs={{2,0},{4,2},{6,4},{7,6},{5,7},{3,5},{1,3},{0,1},{10,8},{12,10},{14... | collective-permute-start | bytes 786440 | tf_op jit(solution)/shard_map/ppermute | solution.py:196
  16.0 1.7 %collective-permute-start.17 = (bf16[256,128]{1,0:T(8,128)(2,1)S(1)}, bf16[256,128]{1,0:T(8,128)(2,1)S(1)}, u32[]{:S(2)}, u32[]{:S(2)}) collective-permute-start(bf16[256,128]{1,0:T(8,128)(2,1)S(1)} %get-tuple-element.16), channel_id=1, source_target_pairs={{0,16},{8,24},{16,0},{24,8},{1,17},{9,25},{17,1},{25,9},{2,18},{10... | collective-permute-start | bytes 196616 | tf_op jit(solution)/shard_map/ppermute | solution.py:102
  17.8 1.5 %collective-permute-start.1 = (bf16[256,512]{1,0:T(8,128)(2,1)S(1)}, bf16[256,512]{1,0:T(8,128)(2,1)S(1)}, u32[]{:S(2)}, u32[]{:S(2)}) collective-permute-start(bf16[256,512]{1,0:T(8,128)(2,1)S(1)} %collective-permute-done.refs_1_), channel_id=1, source_target_pairs={{2,0},{4,2},{6,4},{7,6},{5,7},{3,5},{1,3},{0,1},{10,8},{12,10},{14... | collective-permute-start | bytes 786440 | tf_op jit(solution)/shard_map/ppermute | solution.py:176
  19.2 3.4 %collective-permute-done.13 = bf16[256,512]{1,0:T(8,128)(2,1)S(1)} collective-permute-done((bf16[256,512]{1,0:T(8,128)(2,1)S(1)}, bf16[256,512]{1,0:T(8,128)(2,1)S(1)}, u32[]{:S(2)}, u32[]{:S(2)}) %collective-permute-start.13) | collective-permute-done | bytes 262176 | tf_op jit(solution)/shard_map/ppermute | solution.py:196
  22.6 1.7 %collective-permute-start.4 = (bf16[256,512]{1,0:T(8,128)(2,1)S(1)}, bf16[256,512]{1,0:T(8,128)(2,1)S(1)}, u32[]{:S(2)}, u32[]{:S(2)}) collective-permute-start(bf16[256,512]{1,0:T(8,128)(2,1)S(1)} %collective-permute-done.3.refs_7_), channel_id=1, source_target_pairs={{0,2},{2,4},{4,6},{6,7},{7,5},{5,3},{3,1},{1,0},{8,10},{10,12},{12... | collective-permute-start | bytes 786440 | tf_op jit(solution)/shard_map/ppermute | solution.py:175
  26.2 1.8 %collective-permute-start.10 = (bf16[256,512]{1,0:T(8,128)(2,1)}, bf16[256,512]{1,0:T(8,128)(2,1)}, u32[]{:S(2)}, u32[]{:S(2)}) collective-permute-start(bf16[256,512]{1,0:T(8,128)(2,1)} %add_convert_fusion.5), channel_id=1, source_target_pairs={{0,2},{2,4},{4,6},{6,7},{7,5},{5,3},{3,1},{1,0},{8,10},{10,12},{12... | collective-permute-start | bytes 786440 | tf_op jit(solution)/shard_map/ppermute | solution.py:195
  28.1 2.3 %collective-permute-done.18.refs_3_ = bf16[256,128]{1,0:T(8,128)(2,1)S(1)} collective-permute-done((bf16[256,128]{1,0:T(8,128)(2,1)S(1)}, bf16[256,128]{1,0:T(8,128)(2,1)S(1)}, u32[]{:S(2)}, u32[]{:S(2)}) %collective-permute-start.18) | collective-permute-done | bytes 65568 | tf_op jit(solution)/shard_map/ppermute | solution.py:102
  30.4 1.1 %outer_update.1 = (bf16[256,128]{1,0:T(8,128)(2,1)S(1)}, f32[256,128]{1,0:T(8,128)}) custom-call(bf16[256,128]{1,0:T(8,128)(2,1)S(1)} %get-tuple-element.15.refs_0_, bf16[256,128]{1,0:T(8,128)(2,1)S(1)} %collective-permute-done.16.refs_1_, bf16[256,128]{1,0:T(8,128)(2,1)S(1)} %collective-permute-done.17.refs_2_, ...), custom_call_target="tpu_custom_call" | custom-call | flops 2621440 | bytes 458752 | tf_op jit(solution)/shard_map/outer_update/pallas_call | solution.py:36
  32.7 1.5 %collective-permute-start.2 = (bf16[256,512]{1,0:T(8,128)(2,1)S(1)}, bf16[256,512]{1,0:T(8,128)(2,1)S(1)}, u32[]{:S(2)}, u32[]{:S(2)}) collective-permute-start(bf16[256,512]{1,0:T(8,128)(2,1)S(1)} %collective-permute-done.1.refs_2_), channel_id=1, source_target_pairs={{2,0},{4,2},{6,4},{7,6},{5,7},{3,5},{1,3},{0,1},{10,8},{12,10},{14... | collective-permute-start | bytes 786440 | tf_op jit(solution)/shard_map/ppermute | solution.py:176
  34.8 1.2 %add_convert_fusion.1 = bf16[256,512]{1,0:T(8,128)(2,1)S(1)} fusion(f32[256,512]{1,0:T(8,128)} %convolution_multiply_fusion.2, bf16[256,512]{1,0:T(8,128)(2,1)} %collective-permute-done.14), kind=kLoop, calls=%fused_computation.10 | loop fusion | flops 393216 | bytes 1048576 | tf_op jit(solution)/shard_map/convert_element_type | solution.py:196
  36.2 1.0 %add_convert_fusion.4 = bf16[256,512]{1,0:T(8,128)(2,1)S(1)} fusion(f32[256,512]{1,0:T(8,128)S(1)} %copy-done.5, bf16[256,512]{1,0:T(8,128)(2,1)} %collective-permute-done.10), kind=kLoop, calls=%fused_computation.13 | loop fusion | flops 393216 | bytes 1048576 | tf_op jit(solution)/shard_map/convert_element_type | solution.py:195
  37.3 3.8 %collective-permute-done.2.refs_3_ = bf16[256,512]{1,0:T(8,128)(2,1)S(1)} collective-permute-done((bf16[256,512]{1,0:T(8,128)(2,1)S(1)}, bf16[256,512]{1,0:T(8,128)(2,1)S(1)}, u32[]{:S(2)}, u32[]{:S(2)}) %collective-permute-start.2) | collective-permute-done | bytes 262176 | tf_op jit(solution)/shard_map/ppermute | solution.py:176
  41.1 1.5 %collective-permute-start.15 = (bf16[256,512]{1,0:T(8,128)(2,1)S(1)}, bf16[256,512]{1,0:T(8,128)(2,1)S(1)}, u32[]{:S(2)}, u32[]{:S(2)}) collective-permute-start(bf16[256,512]{1,0:T(8,128)(2,1)S(1)} %add_convert_fusion.1), channel_id=1, source_target_pairs={{2,0},{4,2},{6,4},{7,6},{5,7},{3,5},{1,3},{0,1},{10,8},{12,10},{14... | collective-permute-start | bytes 786440 | tf_op jit(solution)/shard_map/ppermute | solution.py:196
  43.2 1.5 %collective-permute-start.7 = (bf16[128,512]{1,0:T(8,128)(2,1)S(1)}, bf16[128,512]{1,0:T(8,128)(2,1)S(1)}, u32[]{:S(2)}, u32[]{:S(2)}) collective-permute-start(bf16[128,512]{1,0:T(8,128)(2,1)S(1)} %slice.17), channel_id=1, source_target_pairs={{2,0},{4,2},{6,4},{7,6},{5,7},{3,5},{1,3},{0,1},{10,8},{12,10},{14... | collective-permute-start | bytes 393224 | tf_op jit(solution)/shard_map/ppermute | solution.py:180
  46.4 5.1 %collective-permute-done.7 = bf16[128,512]{1,0:T(8,128)(2,1)S(1)} collective-permute-done((bf16[128,512]{1,0:T(8,128)(2,1)S(1)}, bf16[128,512]{1,0:T(8,128)(2,1)S(1)}, u32[]{:S(2)}, u32[]{:S(2)}) %collective-permute-start.7) | collective-permute-done | bytes 131104 | tf_op jit(solution)/shard_map/ppermute | solution.py:180
  51.5 1.3 %collective-permute-done.6 = bf16[128,512]{1,0:T(8,128)(2,1)S(1)} collective-permute-done((bf16[128,512]{1,0:T(8,128)(2,1)S(1)}, bf16[128,512]{1,0:T(8,128)(2,1)S(1)}, u32[]{:S(2)}, u32[]{:S(2)}) %collective-permute-start.6) | collective-permute-done | bytes 131104 | tf_op jit(solution)/shard_map/ppermute | solution.py:180
  52.8 2.3 %projection_products.1 = (bf16[256,512]{1,0:T(8,128)(2,1)}, bf16[256,2048]{1,0:T(8,128)(2,1)}) custom-call(bf16[256,2048]{1,0:T(8,128)(2,1)S(1)} %bitcast.56, bf16[256,512]{1,0:T(8,128)(2,1)S(1)} %bitcast.55, bf16[256,512]{1,0:T(8,128)(2,1)S(1)} %bitcast.59, bf16[256,512]{1,0:T(8,128)(2,1)S(1)} %collective-permute-done.refs_1_, ...), custom_call_target="tpu_custom_call" | custom-call | flops 1073741824 | bytes 3407872 | tf_op jit(solution)/shard_map/projection_products/pallas_call | solution.py:36
  (56 shorter events, 9.4 us)
Async XLA Ops:
  0.6 27.4 %copy-start = (bf16[256,512]{1,0:T(8,128)(2,1)S(1)}, bf16[256,512]{1,0:T(8,128)(2,1)}, u32[]{:S(2)}) copy-start(bf16[256,512]{1,0:T(8,128)(2,1)} %param.6) | copy-start | bytes 786436
  0.6 15.4 %collective-permute-start = (bf16[256,512]{1,0:T(8,128)(2,1)}, bf16[256,512]{1,0:T(8,128)(2,1)S(1)}, u32[]{:S(2)}, u32[]{:S(2)}) collective-permute-start(bf16[256,512]{1,0:T(8,128)(2,1)} %bitcast.57), channel_id=1, source_target_pairs={{2,0},{4,2},{6,4},{7,6},{5,7},{3,5},{1,3},{0,1},{10,8},{12,10},{14... | collective-permute-start | bytes 786440 | tf_op jit(solution)/shard_map/ppermute | solution.py:176
  3.6 14.1 %collective-permute-start.3 = (bf16[256,512]{1,0:T(8,128)(2,1)}, bf16[256,512]{1,0:T(8,128)(2,1)S(1)}, u32[]{:S(2)}, u32[]{:S(2)}) collective-permute-start(bf16[256,512]{1,0:T(8,128)(2,1)} %bitcast.58), channel_id=1, source_target_pairs={{0,2},{2,4},{4,6},{6,7},{7,5},{5,3},{3,1},{1,0},{8,10},{10,12},{12... | collective-permute-start | bytes 786440 | tf_op jit(solution)/shard_map/ppermute | solution.py:175
  5.2 7.9 %collective-permute-start.12 = (bf16[128,512]{1,0:T(8,128)(2,1)S(1)}, bf16[128,512]{1,0:T(8,128)(2,1)S(1)}, u32[]{:S(2)}, u32[]{:S(2)}) collective-permute-start(bf16[128,512]{1,0:T(8,128)(2,1)S(1)} %get-tuple-element.18), channel_id=1, source_target_pairs={{2,0},{4,2},{6,4},{7,6},{5,7},{3,5},{1,3},{0,1},{10,8},{12,10},{14... | collective-permute-start | bytes 393224 | tf_op jit(solution)/shard_map/ppermute | solution.py:191
  7.1 7.9 %collective-permute-start.8 = (bf16[128,512]{1,0:T(8,128)(2,1)S(1)}, bf16[128,512]{1,0:T(8,128)(2,1)S(1)}, u32[]{:S(2)}, u32[]{:S(2)}) collective-permute-start(bf16[128,512]{1,0:T(8,128)(2,1)S(1)} %get-tuple-element.17), channel_id=1, source_target_pairs={{0,2},{2,4},{4,6},{6,7},{7,5},{5,3},{3,1},{1,0},{8,10},{10,12},{12... | collective-permute-start | bytes 393224 | tf_op jit(solution)/shard_map/ppermute | solution.py:190
  7.3 18.9 %collective-permute-start.16 = (bf16[256,128]{1,0:T(8,128)(2,1)S(1)}, bf16[256,128]{1,0:T(8,128)(2,1)S(1)}, u32[]{:S(2)}, u32[]{:S(2)}) collective-permute-start(bf16[256,128]{1,0:T(8,128)(2,1)S(1)} %get-tuple-element.14), channel_id=1, source_target_pairs={{0,8},{8,0},{16,24},{24,16},{1,9},{9,1},{17,25},{25,17},{2,10},{10... | collective-permute-start | bytes 196616 | tf_op jit(solution)/shard_map/ppermute | solution.py:102
  13.3 9.3 %collective-permute-start.13 = (bf16[256,512]{1,0:T(8,128)(2,1)S(1)}, bf16[256,512]{1,0:T(8,128)(2,1)S(1)}, u32[]{:S(2)}, u32[]{:S(2)}) collective-permute-start(bf16[256,512]{1,0:T(8,128)(2,1)S(1)} %add_convert_fusion.3), channel_id=1, source_target_pairs={{2,0},{4,2},{6,4},{7,6},{5,7},{3,5},{1,3},{0,1},{10,8},{12,10},{14... | collective-permute-start | bytes 786440 | tf_op jit(solution)/shard_map/ppermute | solution.py:196
  15.3 9.1 %copy-start.6 = (f32[256,512]{1,0:T(8,128)S(1)}, f32[256,512]{1,0:T(8,128)}, u32[]{:S(2)}) copy-start(f32[256,512]{1,0:T(8,128)} %convolution_multiply_fusion.1) | copy-start | bytes 1572868
  15.3 9.8 %collective-permute-start.9 = (bf16[256,512]{1,0:T(8,128)(2,1)S(1)}, bf16[256,512]{1,0:T(8,128)(2,1)S(1)}, u32[]{:S(2)}, u32[]{:S(2)}) collective-permute-start(bf16[256,512]{1,0:T(8,128)(2,1)S(1)} %add_convert_fusion.6), channel_id=1, source_target_pairs={{0,2},{2,4},{4,6},{6,7},{7,5},{5,3},{3,1},{1,0},{8,10},{10,12},{12... | collective-permute-start | bytes 786440 | tf_op jit(solution)/shard_map/ppermute | solution.py:195
  16.0 10.2 %collective-permute-start.17 = (bf16[256,128]{1,0:T(8,128)(2,1)S(1)}, bf16[256,128]{1,0:T(8,128)(2,1)S(1)}, u32[]{:S(2)}, u32[]{:S(2)}) collective-permute-start(bf16[256,128]{1,0:T(8,128)(2,1)S(1)} %get-tuple-element.16), channel_id=1, source_target_pairs={{0,16},{8,24},{16,0},{24,8},{1,17},{9,25},{17,1},{25,9},{2,18},{10... | collective-permute-start | bytes 196616 | tf_op jit(solution)/shard_map/ppermute | solution.py:102
  17.8 14.1 %collective-permute-start.1 = (bf16[256,512]{1,0:T(8,128)(2,1)S(1)}, bf16[256,512]{1,0:T(8,128)(2,1)S(1)}, u32[]{:S(2)}, u32[]{:S(2)}) collective-permute-start(bf16[256,512]{1,0:T(8,128)(2,1)S(1)} %collective-permute-done.refs_1_), channel_id=1, source_target_pairs={{2,0},{4,2},{6,4},{7,6},{5,7},{3,5},{1,3},{0,1},{10,8},{12,10},{14... | collective-permute-start | bytes 786440 | tf_op jit(solution)/shard_map/ppermute | solution.py:176
  22.6 10.1 %collective-permute-start.4 = (bf16[256,512]{1,0:T(8,128)(2,1)S(1)}, bf16[256,512]{1,0:T(8,128)(2,1)S(1)}, u32[]{:S(2)}, u32[]{:S(2)}) collective-permute-start(bf16[256,512]{1,0:T(8,128)(2,1)S(1)} %collective-permute-done.3.refs_7_), channel_id=1, source_target_pairs={{0,2},{2,4},{4,6},{6,7},{7,5},{5,3},{3,1},{1,0},{8,10},{10,12},{12... | collective-permute-start | bytes 786440 | tf_op jit(solution)/shard_map/ppermute | solution.py:175
  25.1 9.1 %collective-permute-start.14 = (bf16[256,512]{1,0:T(8,128)(2,1)}, bf16[256,512]{1,0:T(8,128)(2,1)}, u32[]{:S(2)}, u32[]{:S(2)}) collective-permute-start(bf16[256,512]{1,0:T(8,128)(2,1)} %add_convert_fusion.2), channel_id=1, source_target_pairs={{2,0},{4,2},{6,4},{7,6},{5,7},{3,5},{1,3},{0,1},{10,8},{12,10},{14... | collective-permute-start | bytes 786440 | tf_op jit(solution)/shard_map/ppermute | solution.py:196
  26.2 4.2 %collective-permute-start.18 = (bf16[256,128]{1,0:T(8,128)(2,1)S(1)}, bf16[256,128]{1,0:T(8,128)(2,1)S(1)}, u32[]{:S(2)}, u32[]{:S(2)}) collective-permute-start(bf16[256,128]{1,0:T(8,128)(2,1)S(1)} %get-tuple-element.13), channel_id=1, source_target_pairs={{0,24},{8,16},{16,8},{24,0},{1,25},{9,17},{17,9},{25,1},{2,26},{10... | collective-permute-start | bytes 196616 | tf_op jit(solution)/shard_map/ppermute | solution.py:102
  26.2 9.7 %collective-permute-start.10 = (bf16[256,512]{1,0:T(8,128)(2,1)}, bf16[256,512]{1,0:T(8,128)(2,1)}, u32[]{:S(2)}, u32[]{:S(2)}) collective-permute-start(bf16[256,512]{1,0:T(8,128)(2,1)} %add_convert_fusion.5), channel_id=1, source_target_pairs={{0,2},{2,4},{4,6},{6,7},{7,5},{5,3},{3,1},{1,0},{8,10},{10,12},{12... | collective-permute-start | bytes 786440 | tf_op jit(solution)/shard_map/ppermute | solution.py:195
  31.4 11.8 %collective-permute-start.19 = (bf16[256,128]{1,0:T(8,128)(2,1)S(1)}, bf16[256,128]{1,0:T(8,128)(2,1)S(1)}, u32[]{:S(2)}, u32[]{:S(2)}) collective-permute-start(bf16[256,128]{1,0:T(8,128)(2,1)S(1)} %get-tuple-element.11.refs_0_), channel_id=1, source_target_pairs={{0,8},{8,0},{16,24},{24,16},{1,9},{9,1},{17,25},{25,17},{2,10},{10... | collective-permute-start | bytes 196616 | tf_op jit(solution)/shard_map/ppermute | solution.py:102
  31.9 12.9 %collective-permute-start.20 = (bf16[256,128]{1,0:T(8,128)(2,1)S(1)}, bf16[256,128]{1,0:T(8,128)(2,1)S(1)}, u32[]{:S(2)}, u32[]{:S(2)}) collective-permute-start(bf16[256,128]{1,0:T(8,128)(2,1)S(1)} %get-tuple-element.11.refs_0_), channel_id=1, source_target_pairs={{0,16},{8,24},{16,0},{24,8},{1,17},{9,25},{17,1},{25,9},{2,18},{10... | collective-permute-start | bytes 196616 | tf_op jit(solution)/shard_map/ppermute | solution.py:102
  32.7 8.4 %collective-permute-start.2 = (bf16[256,512]{1,0:T(8,128)(2,1)S(1)}, bf16[256,512]{1,0:T(8,128)(2,1)S(1)}, u32[]{:S(2)}, u32[]{:S(2)}) collective-permute-start(bf16[256,512]{1,0:T(8,128)(2,1)S(1)} %collective-permute-done.1.refs_2_), channel_id=1, source_target_pairs={{2,0},{4,2},{6,4},{7,6},{5,7},{3,5},{1,3},{0,1},{10,8},{12,10},{14... | collective-permute-start | bytes 786440 | tf_op jit(solution)/shard_map/ppermute | solution.py:176
  34.2 8.4 %collective-permute-start.5 = (bf16[256,512]{1,0:T(8,128)(2,1)S(1)}, bf16[256,512]{1,0:T(8,128)(2,1)S(1)}, u32[]{:S(2)}, u32[]{:S(2)}) collective-permute-start(bf16[256,512]{1,0:T(8,128)(2,1)S(1)} %collective-permute-done.4.refs_6_), channel_id=1, source_target_pairs={{0,2},{2,4},{4,6},{6,7},{7,5},{5,3},{3,1},{1,0},{8,10},{10,12},{12... | collective-permute-start | bytes 786440 | tf_op jit(solution)/shard_map/ppermute | solution.py:175
  35.9 9.6 %collective-permute-start.21 = (bf16[256,128]{1,0:T(8,128)(2,1)S(1)}, bf16[256,128]{1,0:T(8,128)(2,1)S(1)}, u32[]{:S(2)}, u32[]{:S(2)}) collective-permute-start(bf16[256,128]{1,0:T(8,128)(2,1)S(1)} %get-tuple-element.11.refs_0_), channel_id=1, source_target_pairs={{0,24},{8,16},{16,8},{24,0},{1,25},{9,17},{17,9},{25,1},{2,26},{10... | collective-permute-start | bytes 196616 | tf_op jit(solution)/shard_map/ppermute | solution.py:102
  41.1 14.0 %collective-permute-start.15 = (bf16[256,512]{1,0:T(8,128)(2,1)S(1)}, bf16[256,512]{1,0:T(8,128)(2,1)S(1)}, u32[]{:S(2)}, u32[]{:S(2)}) collective-permute-start(bf16[256,512]{1,0:T(8,128)(2,1)S(1)} %add_convert_fusion.1), channel_id=1, source_target_pairs={{2,0},{4,2},{6,4},{7,6},{5,7},{3,5},{1,3},{0,1},{10,8},{12,10},{14... | collective-permute-start | bytes 786440 | tf_op jit(solution)/shard_map/ppermute | solution.py:196
  42.6 12.5 %collective-permute-start.11 = (bf16[256,512]{1,0:T(8,128)(2,1)S(1)}, bf16[256,512]{1,0:T(8,128)(2,1)S(1)}, u32[]{:S(2)}, u32[]{:S(2)}) collective-permute-start(bf16[256,512]{1,0:T(8,128)(2,1)S(1)} %add_convert_fusion.4), channel_id=1, source_target_pairs={{0,2},{2,4},{4,6},{6,7},{7,5},{5,3},{3,1},{1,0},{8,10},{10,12},{12... | collective-permute-start | bytes 786440 | tf_op jit(solution)/shard_map/ppermute | solution.py:195
  43.2 8.2 %collective-permute-start.7 = (bf16[128,512]{1,0:T(8,128)(2,1)S(1)}, bf16[128,512]{1,0:T(8,128)(2,1)S(1)}, u32[]{:S(2)}, u32[]{:S(2)}) collective-permute-start(bf16[128,512]{1,0:T(8,128)(2,1)S(1)} %slice.17), channel_id=1, source_target_pairs={{2,0},{4,2},{6,4},{7,6},{5,7},{3,5},{1,3},{0,1},{10,8},{12,10},{14... | collective-permute-start | bytes 393224 | tf_op jit(solution)/shard_map/ppermute | solution.py:180
  44.8 8.0 %collective-permute-start.6 = (bf16[128,512]{1,0:T(8,128)(2,1)S(1)}, bf16[128,512]{1,0:T(8,128)(2,1)S(1)}, u32[]{:S(2)}, u32[]{:S(2)}) collective-permute-start(bf16[128,512]{1,0:T(8,128)(2,1)S(1)} %slice.16), channel_id=1, source_target_pairs={{0,2},{2,4},{4,6},{6,7},{7,5},{5,3},{3,1},{1,0},{8,10},{10,12},{12... | collective-permute-start | bytes 393224 | tf_op jit(solution)/shard_map/ppermute | solution.py:180
  (5 other events, 15.8 us)

commit v2 on v1

v2 whole, which is shorter than its diff:
```python
import functools

import jax
import jax.numpy as jnp
from jax import lax
from jax.experimental import pallas as pl
from jax.experimental.pallas import tpu as pltpu
from jax.sharding import PartitionSpec as P

BLOCK = 64

outer_rate = 0.7
outer_momentum = 0.9
scale_epsilon = 1e-06

F32 = jnp.float32
BF16 = jnp.bfloat16
LANES = 128
ROWS_BYTES = 8 * 2**20


def ring_order(size):
    return list(range(0, size, 2)) + list(range(1, size, 2))[::-1]


def ring_place(index, size):
    return jnp.where((index & 1) == 0, index >> 1, size - 1 - (index >> 1))


def ring_index(place, size):
    place = lax.rem(place + size, size)
    evens = (size + 1) // 2
    return jnp.where(place < evens, 2 * place, 2 * (size - 1 - place) + 1)


def block_start(offset, size, depth):
    start = ring_index(ring_place(lax.axis_index("fsdp"), size) + offset, size) * depth
    return pl.multiple_of(start, depth)


def vmem_call(kernel, out_shape, operands, flops, name, after=(), moved=None):
    def body(*refs):
        kernel(*refs[: len(operands)], *refs[len(operands) + len(after) :])

    moved = moved or sum(x.size * x.dtype.itemsize for x in operands)
    whole = pl.BlockSpec(memory_space=pltpu.VMEM)
    return pl.pallas_call(
        body,
        out_shape=out_shape,
        in_specs=[whole] * len(operands) + [pl.BlockSpec(memory_space=pl.ANY)] * len(after),
        out_specs=jax.tree.map(lambda _: whole, out_shape),
        compiler_params=pltpu.CompilerParams(vmem_limit_bytes=32 * 2**20),
        cost_estimate=pl.CostEstimate(flops=flops, bytes_accessed=moved, transcendentals=0),
        name=name,
    )(*operands, *after)


def shape_of(rows, columns, dtype):
    return jax.ShapeDtypeStruct((rows, columns), dtype)


def outer_kernel(replicas, share_cols, *refs):
    local_refs = refs[:replicas]
    global_ref, momentum_ref, share_ref, new_momentum_ref = refs[replicas:]
    rows, window = global_ref.shape
    old = global_ref[...].astype(F32)
    lane = lax.broadcasted_iota(jnp.int32, (rows, window), 1) // BLOCK
    total = jnp.zeros((rows, window), F32)
    for local_ref in local_refs:
        drift = old - local_ref[...].astype(F32)
        size = jnp.abs(drift)
        scale = jnp.zeros((rows, window), F32)
        for block in range(window // BLOCK):
            top = jnp.max(jnp.where(lane == block, size, 0.0), axis=1, keepdims=True)
            top = (top + scale_epsilon).astype(BF16).astype(F32)
            scale = jnp.where(lane == block, top, scale)
        total = total + (drift / scale).astype(BF16).astype(F32) * scale
    mean_grad = total / replicas
    shares = window // share_cols
    mean_here, old_here = mean_grad[:, :share_cols], old[:, :share_cols]
    mine = lax.axis_index("replica") % shares
    for share in range(1, shares):
        columns = slice(share * share_cols, (share + 1) * share_cols)
        mean_here = jnp.where(mine == share, mean_grad[:, columns], mean_here)
        old_here = jnp.where(mine == share, old[:, columns], old_here)
    new_momentum = outer_momentum * momentum_ref[...] + mean_here
    new_momentum_ref[...] = new_momentum
    share_ref[...] = (old_here - outer_rate * (mean_here + outer_momentum * new_momentum)).astype(BF16)


def join_kernel(*refs):
    *share_refs, out_ref = refs
    me = lax.axis_index("replica")
    count = len(share_refs)
    width = out_ref.shape[1] // count
    if width % LANES == 0:
        for bits, share_ref in enumerate(share_refs):
            out_ref[:, pl.ds(pl.multiple_of((me ^ bits) * width, width), width)] = share_ref[...]
        return
    pieces = [ref[...] for ref in share_refs]
    bit = 1
    while bit < count:
        odd = (me & bit) != 0
        pieces = [jnp.where(odd, pieces[at ^ bit], pieces[at]) for at in range(count)]
        bit *= 2
    for at in range(count):
        out_ref[:, at * width : (at + 1) * width] = pieces[at]


def windows_kernel(width, array_ref, *out_refs):
    me = lax.axis_index("replica")
    for bits, out_ref in enumerate(out_refs, 1):
        out_ref[...] = array_ref[:, pl.ds(pl.multiple_of((me ^ bits) * width, width), width)]


def swap(array, bits):
    return lax.ppermute(array, "replica", [(at, at ^ bits) for at in range(lax.axis_size("replica"))])


def send_windows(local_shard, after):
    rows, kv_width = local_shard.shape
    replicas = lax.axis_size("replica")
    me = lax.axis_index("replica")
    share_cols = kv_width // replicas
    window = max(share_cols, BLOCK)

    def window_of(owner):
        return lax.dynamic_slice_in_dim(local_shard, owner * share_cols // window * window, window, 1)

    if window == share_cols and window % LANES == 0:
        leaving = vmem_call(
            functools.partial(windows_kernel, window),
            [shape_of(rows, window, BF16)] * (replicas - 1),
            [local_shard],
            rows * kv_width,
            "outer_windows",
            after,
        )
    else:
        leaving = [window_of(me ^ bits) for bits in range(1, replicas)]
    return [window_of(me)] + [swap(array, bits) for bits, array in enumerate(leaving, 1)]


def update_share(windows, global_weights, momentum, after):
    rows, share_cols = momentum.shape
    replicas = len(windows)
    window = windows[0].shape[1]
    start = lax.axis_index("replica") * share_cols // window * window
    new_share, new_momentum = vmem_call(
        functools.partial(outer_kernel, replicas, share_cols),
        (shape_of(rows, share_cols, BF16), shape_of(rows, share_cols, F32)),
        windows + [lax.dynamic_slice_in_dim(global_weights, start, window, 1), momentum],
        20 * replicas * rows * window,
        "outer_update",
        after,
    )
    return [new_share] + [swap(new_share, bits) for bits in range(1, replicas)], new_momentum


def rows_kernel(size, offsets, inputs_ref, *refs):
    *block_refs, total_ref = refs
    depth = inputs_ref.shape[1] // size
    total = jnp.zeros(total_ref.shape, F32)
    if len(block_refs) > len(offsets):
        total = block_refs.pop()[...]
    for offset, block_ref in zip(offsets, block_refs):
        columns = pl.ds(block_start(offset, size, depth), depth)
        total = total + jnp.dot(inputs_ref[:, columns], block_ref[...], preferred_element_type=F32)
    total_ref[...] = total


def grads_kernel(size, offsets, cotangent_ref, *refs):
    *block_refs, grad_ref = refs
    depth = grad_ref.shape[1] // size
    for offset, block_ref in zip(offsets, block_refs):
        grad_ref[:, pl.ds(block_start(offset, size, depth), depth)] = lax.dot_general(
            cotangent_ref[...], block_ref[...], (((1,), (1,)), ((), ())), preferred_element_type=F32
        ).astype(BF16)


def last_products_kernel(at_ref, inputs_ref, cotangent_ref, total_ref, upper_ref, lower_ref, _, rows_ref, grad_ref):
    cut = upper_ref.shape[0]
    upper, lower = upper_ref[...], lower_ref[...]
    rows_ref[...] = (
        total_ref[...]
        + jnp.dot(inputs_ref[:, :cut], upper, preferred_element_type=F32)
        + jnp.dot(inputs_ref[:, cut:], lower, preferred_element_type=F32)
    ).astype(BF16)
    for columns, half in ((slice(0, cut), upper), (slice(cut, 2 * cut), lower)):
        grad_ref[:, columns] = lax.dot_general(
            cotangent_ref[...], half, (((1,), (1,)), ((), ())), preferred_element_type=F32
        ).astype(BF16)


def add_rows(inputs_here, blocks, total, size, after):
    tokens, width = inputs_here.shape
    kv_width = blocks[max(blocks)].shape[1]
    operands = [inputs_here] + list(blocks.values()) + ([] if total is None else [total])
    return vmem_call(
        functools.partial(rows_kernel, size, list(blocks)),
        shape_of(tokens, kv_width, F32),
        operands,
        2 * tokens * width // size * len(blocks) * kv_width,
        "add_rows",
        after,
        ROWS_BYTES,
    )


def near_grads(cotangent, blocks, width, size, after):
    tokens, kv_width = cotangent.shape
    return vmem_call(
        functools.partial(grads_kernel, size, list(blocks)),
        shape_of(tokens, width, BF16),
        [cotangent] + list(blocks.values()),
        2 * tokens * width * kv_width,
        "near_grads",
        after,
    )


def last_products(inputs_here, cotangent, total, grad, upper, lower, size):
    tokens, width = inputs_here.shape
    kv_width = cotangent.shape[1]
    depth = width // size
    at = ring_index(ring_place(lax.axis_index("fsdp"), size) + size // 2, size)
    chosen = pl.BlockSpec((tokens, depth), lambda step, at_ref: (0, at_ref[0]))

    def fixed(array):
        return pl.BlockSpec(array.shape, lambda step, at_ref: (0, 0))

    return pl.pallas_call(
        last_products_kernel,
        out_shape=(shape_of(tokens, kv_width, BF16), shape_of(tokens, width, BF16)),
        grid_spec=pltpu.PrefetchScalarGridSpec(
            num_scalar_prefetch=1,
            grid=(1,),
            in_specs=[chosen, fixed(cotangent), fixed(total), fixed(upper), fixed(lower)]
            + [pl.BlockSpec(memory_space=pl.ANY)],
            out_specs=(fixed(total), chosen),
        ),
        input_output_aliases={6: 1},
        compiler_params=pltpu.CompilerParams(vmem_limit_bytes=32 * 2**20),
        cost_estimate=pl.CostEstimate(
            flops=4 * tokens * depth * kv_width, bytes_accessed=6 * tokens * kv_width, transcendentals=0
        ),
        name="last_products",
    )(at.reshape(1).astype(jnp.int32), inputs_here, cotangent, total, upper, lower, grad)


def all_products(inputs_here, cotangent, blocks, size):
    depth, kv_width = blocks[0].shape
    place = ring_place(lax.axis_index("fsdp"), size)
    gathered = jnp.zeros((depth * size, kv_width), BF16)
    for offset, block in blocks.items():
        gathered = lax.dynamic_update_slice_in_dim(gathered, block, ring_index(place + offset, size) * depth, 0)
    rows = jnp.dot(inputs_here, gathered, preferred_element_type=F32).astype(BF16)
    grad = lax.dot_general(cotangent, gathered, (((1,), (1,)), ((), ())), preferred_element_type=F32)
    return rows, grad.astype(BF16)


def terms_kernel(size, offsets, token_weight, inputs_ref, cotangent_ref, *out_refs):
    depth = inputs_ref.shape[1] // size
    at = 0
    for offset in offsets:
        columns = inputs_ref[:, pl.ds(block_start(offset, size, depth), depth)]
        terms = (
            lax.dot_general(columns, cotangent_ref[...], (((0,), (0,)), ((), ())), preferred_element_type=F32)
            * token_weight
        )
        filled = 0
        while filled < depth:
            count = out_refs[at].shape[0]
            out_refs[at][...] = terms[filled : filled + count].astype(out_refs[at].dtype)
            filled += count
            at += 1


def token_terms(inputs_here, cotangent, size, offsets, out_shape, token_weight, name):
    tokens, width = inputs_here.shape
    kv_width = cotangent.shape[1]
    depth = width // size
    if depth % LANES == 0:
        return vmem_call(
            functools.partial(terms_kernel, size, offsets, token_weight),
            out_shape,
            [inputs_here, cotangent],
            2 * tokens * depth * len(offsets) * kv_width,
            name,
        )
    place = ring_place(lax.axis_index("fsdp"), size)
    out = []
    for offset in offsets:
        columns = lax.dynamic_slice_in_dim(inputs_here, ring_index(place + offset, size) * depth, depth, 1)
        terms = (
            lax.dot_general(columns, cotangent, (((0,), (0,)), ((), ())), preferred_element_type=F32) * token_weight
        )
        filled = 0
        while filled < depth:
            like = out_shape[len(out)]
            out.append(terms[filled : filled + like.shape[0]].astype(like.dtype))
            filled += like.shape[0]
    return out


def add_kernel(up_terms_ref, down_terms_ref, up_ref, down_ref, up_out, down_out):
    depth = up_terms_ref.shape[0]
    count = up_ref.shape[0]
    up_out[:count] = (up_terms_ref[:count] + up_ref[...].astype(F32)).astype(BF16)
    down_out[depth - count :] = (down_terms_ref[depth - count :] + down_ref[...].astype(F32)).astype(BF16)
    if count < depth:
        up_out[count:] = up_terms_ref[count:].astype(BF16)
        down_out[: depth - count] = down_terms_ref[: depth - count].astype(BF16)


def end_kernel(terms_ref, up_ref, down_ref, out_ref):
    count = up_ref.shape[0]
    if count == terms_ref.shape[0]:
        out_ref[...] = (terms_ref[...] + up_ref[...].astype(F32) + down_ref[...].astype(F32)).astype(BF16)
    else:
        out_ref[:count] = (terms_ref[:count] + up_ref[...].astype(F32)).astype(BF16)
        out_ref[count:] = (terms_ref[count:] + down_ref[...].astype(F32)).astype(BF16)


def per_device(local_weights, global_weights, momentum, activations, kv_cotangent):
    local_shard = local_weights[0]
    inputs_here = activations[0]
    cotangent = kv_cotangent[0]
    depth, kv_width = local_shard.shape
    size = lax.axis_size("fsdp")
    token_weight = 1.0 / (inputs_here.shape[0] * size)
    order = ring_order(size)
    up = [(order[at], order[(at + 1) % size]) for at in range(size)]
    down = [(target, source) for source, target in up]
    far = size // 2
    cut = depth // 2
    whole, half = shape_of(depth, kv_width, F32), shape_of(cut, kv_width, BF16)

    blocks = {0: local_shard}
    from_below, from_above = lax.ppermute(local_shard, "fsdp", up), lax.ppermute(local_shard, "fsdp", down)
    farthest = token_terms(inputs_here, cotangent, size, [far], [half, half], token_weight, "farthest_terms")
    sum_up, sum_down = lax.ppermute(farthest[0], "fsdp", up), lax.ppermute(farthest[1], "fsdp", down)
    offsets = [sign * step for step in range(far - 1, 0, -1) for sign in (1, -1)] + [0]
    terms = token_terms(inputs_here, cotangent, size, offsets, [whole] * len(offsets), token_weight, "near_terms")
    terms = dict(zip(offsets, terms))
    wide = depth % (2 * LANES) == 0
    total = None
    sums = []
    for step in range(1, far):
        blocks[-step], blocks[step] = from_below, from_above
        near = far - step
        after = (from_below, from_above)
        if wide:
            news = {at: blocks[at] for at in ((0, -1, 1) if step == 1 else (-step, step))}
            total = add_rows(inputs_here, news, total, size, (shares[0],) if step == far - 1 else ())
            after = (total,)
        sums.append(
            vmem_call(
                add_kernel,
                [shape_of(depth, kv_width, BF16)] * 2,
                [terms[near], terms[-near], sum_up, sum_down],
                2 * depth * kv_width,
                "add_terms",
                after,
            )
        )
        if step < far - 1:
            from_below, from_above = lax.ppermute(from_below, "fsdp", up), lax.ppermute(from_above, "fsdp", down)
        else:
            from_below = lax.ppermute(from_below[:cut], "fsdp", up)
            from_above = lax.ppermute(from_above[cut:], "fsdp", down)
        sum_up, sum_down = lax.ppermute(sums[-1][0], "fsdp", up), lax.ppermute(sums[-1][1], "fsdp", down)
        if step == 1:
            windows = send_windows(local_shard, sums[-1])
        if step == min(2, far - 1):
            shares, new_momentum = update_share(windows, global_weights, momentum, sums[-1])
    grad_rows = vmem_call(
        end_kernel,
        shape_of(depth, kv_width, BF16),
        [terms[0], sum_up, sum_down],
        2 * depth * kv_width,
        "end_terms",
    )

    new_global = vmem_call(
        join_kernel, shape_of(depth, kv_width, BF16), shares, depth * kv_width, "join_shares", sums[-1]
    )

    if wide:
        grad = near_grads(cotangent, blocks, inputs_here.shape[1], size, sums[-1])
        kv_rows, grad_in = last_products(inputs_here, cotangent, total, grad, from_below, from_above, size)
    else:
        blocks[far] = jnp.concatenate([from_below, from_above])
        kv_rows, grad_in = all_products(inputs_here, cotangent, blocks, size)
    return kv_rows[None], grad_in[None], grad_rows[None], new_global, new_momentum


def solution(mesh):
    placed = (
        P("replica", "fsdp", None),
        P("fsdp", None),
        P("fsdp", "replica"),
        P("replica", "fsdp", None),
        P("replica", "fsdp", None),
    )
    return jax.shard_map(
        per_device,
        mesh=mesh,
        in_specs=placed,
        out_specs=(
            P("replica", "fsdp", None),
            P("replica", "fsdp", None),
            P("replica", "fsdp", None),
            P("fsdp", None),
            P("fsdp", "replica"),
        ),
        check_vma=False,
    )
```

time: 56.1 us -> 60.2 us (1.073)
  Pallas kernels: 4.19 us -> 12.9 us
  local copies, waits for them, and re-layouts: 0.78 us -> 7.14 us
  matrix products: 5.58 us -> 0 us
  other arithmetic: 4.58 us -> 0 us
  waiting for transfers between devices: 17.5 us -> 16.3 us
    pallas_call x3 -> x14, Pallas kernels: 4.19 us -> 12.9 us  [the longest x13 10.8 us: vmem_call(): pl.pallas_call(body, out_shape=out_shape, in_specs=[whole] * len(operands...]
    dot_general x8 -> x0, matrix products: 5.58 us -> none  [terms(): lax.dot_general(columns, cotangent, (((0,), (0,)), ((), ())), preferred_e...]
    unnamed x14 -> x44, local copies, waits for them, and re-layouts: 0.69 us -> 5.8 us
    convert_element_type x4 -> x0, other arithmetic: 3.75 us -> none  [the longest x2 1.95 us: per_device(): (terms(-step) + sum_down.astype(F32)).astype(BF16)]
    ppermute x22, waiting for transfers between devices: 17.5 us -> 16.3 us  [the longest x6 7.58 us: swap(): lax.ppermute(array, 'replica', [(at, at ^ bits) for at in range(lax.axis_...]
    slice x3 -> x2, local copies, waits for them, and re-layouts: 0.04 us -> 1.31 us  [the longest x1 0.66 us: per_device(): from_below = lax.ppermute(from_below[:cut], 'fsdp', up)]
    broadcast_in_dim x1 -> x0, other arithmetic: 0.81 us -> none  [per_device(): grad_rows[None]]
  transfers between devices with their start and end apart: 22 -> 22, of which waited for: 6 -> 8; matrix products, arithmetic and copies ran while one was open for 17% -> 2% of each run, Pallas kernels for 7% -> 17%
where the time goes in v2:
time: 60.2 us; the launch traced here: 59.8 us
  starting transfers between devices  22.7 us (38%)
  waiting for transfers between devices  16.3 us (27%)
  Pallas kernels  12.9 us (21%)
  local copies, waits for them, and re-layouts  7.14 us (12%)
  between operations  0.84 us (1%)
    pallas_call x13, Pallas kernels, vmem_call(): pl.pallas_call(body, out_shape=out_shape, in_specs=[whole] * len(operands...  10.8 us
    ppermute x6, waiting for transfers between devices, swap(): lax.ppermute(array, 'replica', [(at, at ^ bits) for at in range(lax.axis_...  7.58 us
    unnamed x44, local copies, waits for them, and re-layouts  5.8 us
    ppermute x6, starting transfers between devices, swap(): lax.ppermute(array, 'replica', [(at, at ^ bits) for at in range(lax.axis_...  4.99 us
    ppermute x3, starting transfers between devices, per_device(): lax.ppermute(sums[-1][0], 'fsdp', up)  4.83 us
    ppermute x2, starting transfers between devices, per_device(): lax.ppermute(from_below, 'fsdp', up)  4.25 us
    ppermute x1, starting transfers between devices, per_device(): lax.ppermute(local_shard, 'fsdp', up)  3.08 us
    pallas_call x1, Pallas kernels, last_products(): pl.pallas_call(last_products_kernel, out_shape=(shape_of(tokens, kv_width...  2.12 us
  transfers between devices with their start and end apart: 22, of which 8 were waited for; matrix products, arithmetic and copies ran while one was open for 2% of the time, Pallas kernels for 17%

profile of v2, /device:TPU:0, one launch (start us, length us, event | category | flops | bytes accessed | tf_op | source)
XLA Modules:
  0.0 59.8 jit_solution(9116460769682414591)
XLA Ops:
  0.6 3.1 %collective-permute-start = (bf16[256,512]{1,0:T(8,128)(2,1)}, bf16[256,512]{1,0:T(8,128)(2,1)S(1)}, u32[]{:S(2)}, u32[]{:S(2)}) collective-permute-start(bf16[256,512]{1,0:T(8,128)(2,1)} %bitcast.15), channel_id=1, source_target_pairs={{0,2},{2,4},{4,6},{6,7},{7,5},{5,3},{3,1},{1,0},{8,10},{10,12},{12... | collective-permute-start | bytes 786440 | tf_op jit(solution)/shard_map/ppermute | solution.py:340
  3.7 1.2 %copy-done.1 = bf16[1,256,2048]{2,1,0:T(8,128)(2,1)S(1)} copy-done((bf16[1,256,2048]{2,1,0:T(8,128)(2,1)S(1)}, bf16[1,256,2048]{2,1,0:T(8,128)(2,1)}, u32[]{:S(2)}) %copy-start.1) | copy-done | bytes 1048600
  6.2 2.1 %collective-permute-start.6 = (bf16[128,512]{1,0:T(8,128)(2,1)S(1)}, bf16[128,512]{1,0:T(8,128)(2,1)S(1)}, u32[]{:S(2)}, u32[]{:S(2)}) collective-permute-start(bf16[128,512]{1,0:T(8,128)(2,1)S(1)} %get-tuple-element.29), channel_id=1, source_target_pairs={{0,2},{2,4},{4,6},{6,7},{7,5},{5,3},{3,1},{1,0},{8,10},{10,12},{12... | collective-permute-start | bytes 393224 | tf_op jit(solution)/shard_map/ppermute | solution.py:342
  9.0 2.0 %collective-permute-done.refs_2_ = bf16[256,512]{1,0:T(8,128)(2,1)S(1)} collective-permute-done((bf16[256,512]{1,0:T(8,128)(2,1)}, bf16[256,512]{1,0:T(8,128)(2,1)S(1)}, u32[]{:S(2)}, u32[]{:S(2)}) %collective-permute-start) | collective-permute-done | bytes 262176 | tf_op jit(solution)/shard_map/ppermute | solution.py:340
  11.0 2.1 %collective-permute-start.1 = (bf16[256,512]{1,0:T(8,128)(2,1)S(1)}, bf16[256,512]{1,0:T(8,128)(2,1)S(1)}, u32[]{:S(2)}, u32[]{:S(2)}) collective-permute-start(bf16[256,512]{1,0:T(8,128)(2,1)S(1)} %collective-permute-done.refs_2_), channel_id=1, source_target_pairs={{0,2},{2,4},{4,6},{6,7},{7,5},{5,3},{3,1},{1,0},{8,10},{10,12},{12... | collective-permute-start | bytes 786440 | tf_op jit(solution)/shard_map/ppermute | solution.py:368
  13.8 1.9 %collective-permute-done.7.refs_3_ = bf16[128,512]{1,0:T(8,128)(2,1)S(1)} collective-permute-done((bf16[128,512]{1,0:T(8,128)(2,1)S(1)}, bf16[128,512]{1,0:T(8,128)(2,1)S(1)}, u32[]{:S(2)}, u32[]{:S(2)}) %collective-permute-start.7) | collective-permute-done | bytes 131104 | tf_op jit(solution)/shard_map/ppermute | solution.py:342
  15.8 1.6 %collective-permute-start.11 = (bf16[256,512]{1,0:T(8,128)(2,1)S(1)}, bf16[256,512]{1,0:T(8,128)(2,1)S(1)}, u32[]{:S(2)}, u32[]{:S(2)}) collective-permute-start(bf16[256,512]{1,0:T(8,128)(2,1)S(1)} %get-tuple-element.31.refs_1_), channel_id=1, source_target_pairs={{0,2},{2,4},{4,6},{6,7},{7,5},{5,3},{3,1},{1,0},{8,10},{10,12},{12... | collective-permute-start | bytes 786440 | tf_op jit(solution)/shard_map/ppermute | solution.py:372
  19.1 1.1 %collective-permute-done.1.refs_1_.refs_4_ = bf16[256,512]{1,0:T(8,128)(2,1)S(1)} collective-permute-done((bf16[256,512]{1,0:T(8,128)(2,1)S(1)}, bf16[256,512]{1,0:T(8,128)(2,1)S(1)}, u32[]{:S(2)}, u32[]{:S(2)}) %collective-permute-start.1) | collective-permute-done | bytes 262176 | tf_op jit(solution)/shard_map/ppermute | solution.py:368
  20.3 2.1 %collective-permute-start.2 = (bf16[256,512]{1,0:T(8,128)(2,1)S(1)}, bf16[256,512]{1,0:T(8,128)(2,1)S(1)}, u32[]{:S(2)}, u32[]{:S(2)}) collective-permute-start(bf16[256,512]{1,0:T(8,128)(2,1)S(1)} %collective-permute-done.1.refs_1_.refs_4_), channel_id=1, source_target_pairs={{0,2},{2,4},{4,6},{6,7},{7,5},{5,3},{3,1},{1,0},{8,10},{10,12},{12... | collective-permute-start | bytes 786440 | tf_op jit(solution)/shard_map/ppermute | solution.py:368
  23.1 1.9 %collective-permute-done.11.refs_2_ = bf16[256,512]{1,0:T(8,128)(2,1)S(1)} collective-permute-done((bf16[256,512]{1,0:T(8,128)(2,1)S(1)}, bf16[256,512]{1,0:T(8,128)(2,1)S(1)}, u32[]{:S(2)}, u32[]{:S(2)}) %collective-permute-start.11) | collective-permute-done | bytes 262176 | tf_op jit(solution)/shard_map/ppermute | solution.py:372
  25.0 1.8 %collective-permute-done.12.refs_3_ = bf16[256,512]{1,0:T(8,128)(2,1)S(1)} collective-permute-done((bf16[256,512]{1,0:T(8,128)(2,1)S(1)}, bf16[256,512]{1,0:T(8,128)(2,1)S(1)}, u32[]{:S(2)}, u32[]{:S(2)}) %collective-permute-start.12) | collective-permute-done | bytes 262176 | tf_op jit(solution)/shard_map/ppermute | solution.py:372
  27.6 1.6 %collective-permute-start.15 = (bf16[256,512]{1,0:T(8,128)(2,1)}, bf16[256,512]{1,0:T(8,128)(2,1)}, u32[]{:S(2)}, u32[]{:S(2)}) collective-permute-start(bf16[256,512]{1,0:T(8,128)(2,1)} %get-tuple-element.38.refs_6_), channel_id=1, source_target_pairs={{0,2},{2,4},{4,6},{6,7},{7,5},{5,3},{3,1},{1,0},{8,10},{10,12},{12... | collective-permute-start | bytes 786440 | tf_op jit(solution)/shard_map/ppermute | solution.py:372
  29.7 1.4 %collective-permute-done.8.refs_1_ = bf16[256,128]{1,0:T(8,128)(2,1)S(1)} collective-permute-done((bf16[256,128]{1,0:T(8,128)(2,1)}, bf16[256,128]{1,0:T(8,128)(2,1)S(1)}, u32[]{:S(2)}, u32[]{:S(2)}) %collective-permute-start.8) | collective-permute-done | bytes 65568 | tf_op jit(solution)/shard_map/ppermute | solution.py:117
  31.1 2.5 %collective-permute-start.9 = (bf16[256,128]{1,0:T(8,128)(2,1)S(1)}, bf16[256,128]{1,0:T(8,128)(2,1)S(1)}, u32[]{:S(2)}, u32[]{:S(2)}) collective-permute-start(bf16[256,128]{1,0:T(8,128)(2,1)S(1)} %get-tuple-element.34), channel_id=1, source_target_pairs={{0,16},{8,24},{16,0},{24,8},{1,17},{9,25},{17,1},{25,9},{2,18},{10... | collective-permute-start | bytes 196616 | tf_op jit(solution)/shard_map/ppermute | solution.py:117
  33.7 2.4 %collective-permute-done.9.refs_2_ = bf16[256,128]{1,0:T(8,128)(2,1)S(1)} collective-permute-done((bf16[256,128]{1,0:T(8,128)(2,1)S(1)}, bf16[256,128]{1,0:T(8,128)(2,1)S(1)}, u32[]{:S(2)}, u32[]{:S(2)}) %collective-permute-start.9) | collective-permute-done | bytes 65568 | tf_op jit(solution)/shard_map/ppermute | solution.py:117
  38.3 1.1 %add_terms.5 = (bf16[256,512]{1,0:T(8,128)(2,1)S(1)}, bf16[256,512]{1,0:T(8,128)(2,1)S(1)}) custom-call(f32[256,512]{1,0:T(8,128)S(1)} %copy-done.15, f32[256,512]{1,0:T(8,128)S(1)} %copy-done.17, bf16[256,512]{1,0:T(8,128)(2,1)} %collective-permute-done.15.refs_2_, bf16[256,512]{1,0:T(8,128)(2,1)} %collective-permute-done.16.refs_3_, ...), custom_call_target="tpu_custom_call" | custom-call | flops 262144 | bytes 1572864 | tf_op jit(solution)/shard_map/add_terms/pallas_call | solution.py:47
  39.5 1.6 %collective-permute-start.17 = (bf16[256,512]{1,0:T(8,128)(2,1)S(1)}, bf16[256,512]{1,0:T(8,128)(2,1)}, u32[]{:S(2)}, u32[]{:S(2)}) collective-permute-start(bf16[256,512]{1,0:T(8,128)(2,1)S(1)} %get-tuple-element.43.refs_8_.refs_4_), channel_id=1, source_target_pairs={{0,2},{2,4},{4,6},{6,7},{7,5},{5,3},{3,1},{1,0},{8,10},{10,12},{12... | collective-permute-start | bytes 786440 | tf_op jit(solution)/shard_map/ppermute | solution.py:372
  41.5 1.9 %collective-permute-start.20 = (bf16[256,128]{1,0:T(8,128)(2,1)S(1)}, bf16[256,128]{1,0:T(8,128)(2,1)S(1)}, u32[]{:S(2)}, u32[]{:S(2)}) collective-permute-start(bf16[256,128]{1,0:T(8,128)(2,1)S(1)} %get-tuple-element.40.refs_4_.refs_0_), channel_id=1, source_target_pairs={{0,16},{8,24},{16,0},{24,8},{1,17},{9,25},{17,1},{25,9},{2,18},{10... | collective-permute-start | bytes 196616 | tf_op jit(solution)/shard_map/ppermute | solution.py:117
  44.1 1.6 %collective-permute-start.13 = (bf16[128,512]{1,0:T(8,128)(2,1)}, bf16[128,512]{1,0:T(8,128)(2,1)}, u32[]{:S(2)}, u32[]{:S(2)}) collective-permute-start(bf16[128,512]{1,0:T(8,128)(2,1)} %slice.8), channel_id=1, source_target_pairs={{0,2},{2,4},{4,6},{6,7},{7,5},{5,3},{3,1},{1,0},{8,10},{10,12},{12... | collective-permute-start | bytes 393224 | tf_op jit(solution)/shard_map/ppermute | solution.py:370
  48.0 3.7 %collective-permute-done.21.refs_3_ = bf16[256,128]{1,0:T(8,128)(2,1)} collective-permute-done((bf16[256,128]{1,0:T(8,128)(2,1)S(1)}, bf16[256,128]{1,0:T(8,128)(2,1)}, u32[]{:S(2)}, u32[]{:S(2)}) %collective-permute-start.21) | collective-permute-done | bytes 65568 | tf_op jit(solution)/shard_map/ppermute | solution.py:117
  52.6 1.6 %join_shares.1 = bf16[256,512]{1,0:T(8,128)(2,1)} custom-call(bf16[256,128]{1,0:T(8,128)(2,1)S(1)} %get-tuple-element.40.refs_4_.refs_0_, bf16[256,128]{1,0:T(8,128)(2,1)S(1)} %collective-permute-done.19.refs_1_, bf16[256,128]{1,0:T(8,128)(2,1)S(1)} %copy-done.20, bf16[256,128]{1,0:T(8,128)(2,1)} %collective-permute-done.21.refs_3_, ...), custom_call_target="tpu_custom_call" | custom-call | flops 131072 | bytes 262144 | tf_op jit(solution)/shard_map/join_shares/pallas_call | solution.py:47
  54.2 1.7 %near_grads.1._ = bf16[256,2048]{1,0:T(8,128)(2,1)} custom-call(bf16[256,512]{1,0:T(8,128)(2,1)S(1)} %bitcast.22, bf16[256,512]{1,0:T(8,128)(2,1)S(1)} %bitcast.19, bf16[256,512]{1,0:T(8,128)(2,1)S(1)} %collective-permute-done.refs_2_, bf16[256,512]{1,0:T(8,128)(2,1)S(1)} %copy-done.7, bf16[256,512]{1,0:T(8,128)(2,1)S(1)} %copy-done.9, ...), custom_call_target="tpu_custom_call" | custom-call | flops 536870912 | bytes 2097152 | tf_op jit(solution)/shard_map/near_grads/pallas_call | solution.py:47
  55.9 2.1 %last_products.1 = (bf16[256,512]{1,0:T(8,128)(2,1)}, bf16[256,2048]{1,0:T(8,128)(2,1)}) custom-call(s32[1]{0:T(128)} %bitcast.at_ref, bf16[256,2048]{1,0:T(8,128)(2,1)S(1)} %bitcast.14, bf16[256,512]{1,0:T(8,128)(2,1)S(1)} %bitcast.23, f32[256,512]{1,0:T(8,128)S(1)} %add_rows.5.refs_4_.total_ref, ...), custom_call_target="tpu_custom_call", output_to_operand_aliasing={{1}: (6, {})} | custom-call | flops 134217728 | bytes 786432 | tf_op jit(solution)/shard_map/last_products/pallas_call | solution.py:232
  58.0 1.8 %end_terms.1 = bf16[256,512]{1,0:T(8,128)(2,1)} custom-call(f32[256,512]{1,0:T(8,128)S(1)} %copy-done.13, bf16[256,512]{1,0:T(8,128)(2,1)} %collective-permute-done.17.refs_1_, bf16[256,512]{1,0:T(8,128)(2,1)} %collective-permute-done.18.refs_2_), custom_call_target="tpu_custom_call" | custom-call | flops 262144 | bytes 1048576 | tf_op jit(solution)/shard_map/end_terms/pallas_call | solution.py:47
  (82 shorter events, 13.0 us)
Async XLA Ops:
  0.6 33.0 %copy-start = (bf16[256,512]{1,0:T(8,128)(2,1)S(1)}, bf16[256,512]{1,0:T(8,128)(2,1)}, u32[]{:S(2)}) copy-start(bf16[256,512]{1,0:T(8,128)(2,1)} %param.6) | copy-start | bytes 786436
  0.6 10.3 %collective-permute-start = (bf16[256,512]{1,0:T(8,128)(2,1)}, bf16[256,512]{1,0:T(8,128)(2,1)S(1)}, u32[]{:S(2)}, u32[]{:S(2)}) collective-permute-start(bf16[256,512]{1,0:T(8,128)(2,1)} %bitcast.15), channel_id=1, source_target_pairs={{0,2},{2,4},{4,6},{6,7},{7,5},{5,3},{3,1},{1,0},{8,10},{10,12},{12... | collective-permute-start | bytes 786440 | tf_op jit(solution)/shard_map/ppermute | solution.py:340
  3.7 9.4 %collective-permute-start.3 = (bf16[256,512]{1,0:T(8,128)(2,1)}, bf16[256,512]{1,0:T(8,128)(2,1)S(1)}, u32[]{:S(2)}, u32[]{:S(2)}) collective-permute-start(bf16[256,512]{1,0:T(8,128)(2,1)} %bitcast.16), channel_id=1, source_target_pairs={{2,0},{4,2},{6,4},{7,6},{5,7},{3,5},{1,3},{0,1},{10,8},{12,10},{14... | collective-permute-start | bytes 786440 | tf_op jit(solution)/shard_map/ppermute | solution.py:340
  6.2 7.7 %collective-permute-start.6 = (bf16[128,512]{1,0:T(8,128)(2,1)S(1)}, bf16[128,512]{1,0:T(8,128)(2,1)S(1)}, u32[]{:S(2)}, u32[]{:S(2)}) collective-permute-start(bf16[128,512]{1,0:T(8,128)(2,1)S(1)} %get-tuple-element.29), channel_id=1, source_target_pairs={{0,2},{2,4},{4,6},{6,7},{7,5},{5,3},{3,1},{1,0},{8,10},{10,12},{12... | collective-permute-start | bytes 393224 | tf_op jit(solution)/shard_map/ppermute | solution.py:342
  8.2 7.4 %collective-permute-start.7 = (bf16[128,512]{1,0:T(8,128)(2,1)S(1)}, bf16[128,512]{1,0:T(8,128)(2,1)S(1)}, u32[]{:S(2)}, u32[]{:S(2)}) collective-permute-start(bf16[128,512]{1,0:T(8,128)(2,1)S(1)} %get-tuple-element.30), channel_id=1, source_target_pairs={{2,0},{4,2},{6,4},{7,6},{5,7},{3,5},{1,3},{0,1},{10,8},{12,10},{14... | collective-permute-start | bytes 393224 | tf_op jit(solution)/shard_map/ppermute | solution.py:342
  11.0 9.3 %collective-permute-start.1 = (bf16[256,512]{1,0:T(8,128)(2,1)S(1)}, bf16[256,512]{1,0:T(8,128)(2,1)S(1)}, u32[]{:S(2)}, u32[]{:S(2)}) collective-permute-start(bf16[256,512]{1,0:T(8,128)(2,1)S(1)} %collective-permute-done.refs_2_), channel_id=1, source_target_pairs={{0,2},{2,4},{4,6},{6,7},{7,5},{5,3},{3,1},{1,0},{8,10},{10,12},{12... | collective-permute-start | bytes 786440 | tf_op jit(solution)/shard_map/ppermute | solution.py:368
  13.1 9.2 %collective-permute-start.4 = (bf16[256,512]{1,0:T(8,128)(2,1)S(1)}, bf16[256,512]{1,0:T(8,128)(2,1)S(1)}, u32[]{:S(2)}, u32[]{:S(2)}) collective-permute-start(bf16[256,512]{1,0:T(8,128)(2,1)S(1)} %collective-permute-done.3.refs_3_), channel_id=1, source_target_pairs={{2,0},{4,2},{6,4},{7,6},{5,7},{3,5},{1,3},{0,1},{10,8},{12,10},{14... | collective-permute-start | bytes 786440 | tf_op jit(solution)/shard_map/ppermute | solution.py:368
  15.7 6.7 %copy-start.2 = (bf16[1,256,2048]{2,1,0:T(8,128)(2,1)S(1)}, bf16[1,256,2048]{2,1,0:T(8,128)(2,1)}, u32[]{:S(2)}) copy-start(bf16[1,256,2048]{2,1,0:T(8,128)(2,1)} %param.8) | copy-start | bytes 3145732
  15.8 9.2 %collective-permute-start.11 = (bf16[256,512]{1,0:T(8,128)(2,1)S(1)}, bf16[256,512]{1,0:T(8,128)(2,1)S(1)}, u32[]{:S(2)}, u32[]{:S(2)}) collective-permute-start(bf16[256,512]{1,0:T(8,128)(2,1)S(1)} %get-tuple-element.31.refs_1_), channel_id=1, source_target_pairs={{0,2},{2,4},{4,6},{6,7},{7,5},{5,3},{3,1},{1,0},{8,10},{10,12},{12... | collective-permute-start | bytes 786440 | tf_op jit(solution)/shard_map/ppermute | solution.py:372
  17.4 9.4 %collective-permute-start.12 = (bf16[256,512]{1,0:T(8,128)(2,1)S(1)}, bf16[256,512]{1,0:T(8,128)(2,1)S(1)}, u32[]{:S(2)}, u32[]{:S(2)}) collective-permute-start(bf16[256,512]{1,0:T(8,128)(2,1)S(1)} %get-tuple-element.32.refs_2_), channel_id=1, source_target_pairs={{2,0},{4,2},{6,4},{7,6},{5,7},{3,5},{1,3},{0,1},{10,8},{12,10},{14... | collective-permute-start | bytes 786440 | tf_op jit(solution)/shard_map/ppermute | solution.py:372
  19.1 10.5 %collective-permute-start.10 = (bf16[256,128]{1,0:T(8,128)(2,1)}, bf16[256,128]{1,0:T(8,128)(2,1)S(1)}, u32[]{:S(2)}, u32[]{:S(2)}) collective-permute-start(bf16[256,128]{1,0:T(8,128)(2,1)} %get-tuple-element.35), channel_id=1, source_target_pairs={{0,24},{8,16},{16,8},{24,0},{1,25},{9,17},{17,9},{25,1},{2,26},{10... | collective-permute-start | bytes 196616 | tf_op jit(solution)/shard_map/ppermute | solution.py:117
  20.3 16.9 %collective-permute-start.2 = (bf16[256,512]{1,0:T(8,128)(2,1)S(1)}, bf16[256,512]{1,0:T(8,128)(2,1)S(1)}, u32[]{:S(2)}, u32[]{:S(2)}) collective-permute-start(bf16[256,512]{1,0:T(8,128)(2,1)S(1)} %collective-permute-done.1.refs_1_.refs_4_), channel_id=1, source_target_pairs={{0,2},{2,4},{4,6},{6,7},{7,5},{5,3},{3,1},{1,0},{8,10},{10,12},{12... | collective-permute-start | bytes 786440 | tf_op jit(solution)/shard_map/ppermute | solution.py:368
  22.4 14.8 %collective-permute-start.5 = (bf16[256,512]{1,0:T(8,128)(2,1)S(1)}, bf16[256,512]{1,0:T(8,128)(2,1)S(1)}, u32[]{:S(2)}, u32[]{:S(2)}) collective-permute-start(bf16[256,512]{1,0:T(8,128)(2,1)S(1)} %collective-permute-done.4.refs_2_.refs_5_), channel_id=1, source_target_pairs={{2,0},{4,2},{6,4},{7,6},{5,7},{3,5},{1,3},{0,1},{10,8},{12,10},{14... | collective-permute-start | bytes 786440 | tf_op jit(solution)/shard_map/ppermute | solution.py:368
  27.6 9.9 %collective-permute-start.15 = (bf16[256,512]{1,0:T(8,128)(2,1)}, bf16[256,512]{1,0:T(8,128)(2,1)}, u32[]{:S(2)}, u32[]{:S(2)}) collective-permute-start(bf16[256,512]{1,0:T(8,128)(2,1)} %get-tuple-element.38.refs_6_), channel_id=1, source_target_pairs={{0,2},{2,4},{4,6},{6,7},{7,5},{5,3},{3,1},{1,0},{8,10},{10,12},{12... | collective-permute-start | bytes 786440 | tf_op jit(solution)/shard_map/ppermute | solution.py:372
  29.2 8.3 %collective-permute-start.16 = (bf16[256,512]{1,0:T(8,128)(2,1)}, bf16[256,512]{1,0:T(8,128)(2,1)}, u32[]{:S(2)}, u32[]{:S(2)}) collective-permute-start(bf16[256,512]{1,0:T(8,128)(2,1)} %get-tuple-element.39.refs_7_), channel_id=1, source_target_pairs={{2,0},{4,2},{6,4},{7,6},{5,7},{3,5},{1,3},{0,1},{10,8},{12,10},{14... | collective-permute-start | bytes 786440 | tf_op jit(solution)/shard_map/ppermute | solution.py:372
  29.6 1.5 %collective-permute-start.8 = (bf16[256,128]{1,0:T(8,128)(2,1)}, bf16[256,128]{1,0:T(8,128)(2,1)S(1)}, u32[]{:S(2)}, u32[]{:S(2)}) collective-permute-start(bf16[256,128]{1,0:T(8,128)(2,1)} %copy-done.21), channel_id=1, source_target_pairs={{0,8},{8,0},{16,24},{24,16},{1,9},{9,1},{17,25},{25,17},{2,10},{10... | collective-permute-start | bytes 196616 | tf_op jit(solution)/shard_map/ppermute | solution.py:117
  31.1 4.9 %collective-permute-start.9 = (bf16[256,128]{1,0:T(8,128)(2,1)S(1)}, bf16[256,128]{1,0:T(8,128)(2,1)S(1)}, u32[]{:S(2)}, u32[]{:S(2)}) collective-permute-start(bf16[256,128]{1,0:T(8,128)(2,1)S(1)} %get-tuple-element.34), channel_id=1, source_target_pairs={{0,16},{8,24},{16,0},{24,8},{1,17},{9,25},{17,1},{25,9},{2,18},{10... | collective-permute-start | bytes 196616 | tf_op jit(solution)/shard_map/ppermute | solution.py:117
  39.5 18.5 %collective-permute-start.17 = (bf16[256,512]{1,0:T(8,128)(2,1)S(1)}, bf16[256,512]{1,0:T(8,128)(2,1)}, u32[]{:S(2)}, u32[]{:S(2)}) collective-permute-start(bf16[256,512]{1,0:T(8,128)(2,1)S(1)} %get-tuple-element.43.refs_8_.refs_4_), channel_id=1, source_target_pairs={{0,2},{2,4},{4,6},{6,7},{7,5},{5,3},{3,1},{1,0},{8,10},{10,12},{12... | collective-permute-start | bytes 786440 | tf_op jit(solution)/shard_map/ppermute | solution.py:372
  41.1 16.9 %collective-permute-start.18 = (bf16[256,512]{1,0:T(8,128)(2,1)S(1)}, bf16[256,512]{1,0:T(8,128)(2,1)}, u32[]{:S(2)}, u32[]{:S(2)}) collective-permute-start(bf16[256,512]{1,0:T(8,128)(2,1)S(1)} %get-tuple-element.44.refs_9_.refs_5_), channel_id=1, source_target_pairs={{2,0},{4,2},{6,4},{7,6},{5,7},{3,5},{1,3},{0,1},{10,8},{12,10},{14... | collective-permute-start | bytes 786440 | tf_op jit(solution)/shard_map/ppermute | solution.py:372
  41.5 4.8 %collective-permute-start.19 = (bf16[256,128]{1,0:T(8,128)(2,1)S(1)}, bf16[256,128]{1,0:T(8,128)(2,1)S(1)}, u32[]{:S(2)}, u32[]{:S(2)}) collective-permute-start(bf16[256,128]{1,0:T(8,128)(2,1)S(1)} %get-tuple-element.40.refs_4_.refs_0_), channel_id=1, source_target_pairs={{0,8},{8,0},{16,24},{24,16},{1,9},{9,1},{17,25},{25,17},{2,10},{10... | collective-permute-start | bytes 196616 | tf_op jit(solution)/shard_map/ppermute | solution.py:117
  41.5 5.2 %collective-permute-start.20 = (bf16[256,128]{1,0:T(8,128)(2,1)S(1)}, bf16[256,128]{1,0:T(8,128)(2,1)S(1)}, u32[]{:S(2)}, u32[]{:S(2)}) collective-permute-start(bf16[256,128]{1,0:T(8,128)(2,1)S(1)} %get-tuple-element.40.refs_4_.refs_0_), channel_id=1, source_target_pairs={{0,16},{8,24},{16,0},{24,8},{1,17},{9,25},{17,1},{25,9},{2,18},{10... | collective-permute-start | bytes 196616 | tf_op jit(solution)/shard_map/ppermute | solution.py:117
  44.1 11.8 %collective-permute-start.13 = (bf16[128,512]{1,0:T(8,128)(2,1)}, bf16[128,512]{1,0:T(8,128)(2,1)}, u32[]{:S(2)}, u32[]{:S(2)}) collective-permute-start(bf16[128,512]{1,0:T(8,128)(2,1)} %slice.8), channel_id=1, source_target_pairs={{0,2},{2,4},{4,6},{6,7},{7,5},{5,3},{3,1},{1,0},{8,10},{10,12},{12... | collective-permute-start | bytes 393224 | tf_op jit(solution)/shard_map/ppermute | solution.py:370
  46.3 9.6 %collective-permute-start.14 = (bf16[128,512]{1,0:T(8,128)(2,1)}, bf16[128,512]{1,0:T(8,128)(2,1)}, u32[]{:S(2)}, u32[]{:S(2)}) collective-permute-start(bf16[128,512]{1,0:T(8,128)(2,1)} %slice.9), channel_id=1, source_target_pairs={{2,0},{4,2},{6,4},{7,6},{5,7},{3,5},{1,3},{0,1},{10,8},{12,10},{14... | collective-permute-start | bytes 393224 | tf_op jit(solution)/shard_map/ppermute | solution.py:371
  47.4 4.3 %collective-permute-start.21 = (bf16[256,128]{1,0:T(8,128)(2,1)S(1)}, bf16[256,128]{1,0:T(8,128)(2,1)}, u32[]{:S(2)}, u32[]{:S(2)}) collective-permute-start(bf16[256,128]{1,0:T(8,128)(2,1)S(1)} %get-tuple-element.40.refs_4_.refs_0_), channel_id=1, source_target_pairs={{0,24},{8,16},{16,8},{24,0},{1,25},{9,17},{17,9},{25,1},{2,26},{10... | collective-permute-start | bytes 196616 | tf_op jit(solution)/shard_map/ppermute | solution.py:117
  (20 other events, 62.4 us)

commit v3 on v2

v3 whole, which is shorter than its diff:
```python
import functools

import jax
import jax.numpy as jnp
from jax import lax
from jax.experimental import pallas as pl
from jax.experimental.pallas import tpu as pltpu
from jax.sharding import PartitionSpec as P

BLOCK = 64

outer_rate = 0.7
outer_momentum = 0.9
scale_epsilon = 1e-06

F32 = jnp.float32
BF16 = jnp.bfloat16
LANES = 128
VMEM_BYTES = 8 * 2**20
PRODUCTS_BYTES = 8 * 2**20


def ring_order(size):
    return list(range(0, size, 2)) + list(range(1, size, 2))[::-1]


def ring_place(index, size):
    return jnp.where((index & 1) == 0, index >> 1, size - 1 - (index >> 1))


def ring_index(place, size):
    place = lax.rem(place + size, size)
    evens = (size + 1) // 2
    return jnp.where(place < evens, 2 * place, 2 * (size - 1 - place) + 1)


def block_start(offset, size, depth):
    start = ring_index(ring_place(lax.axis_index("fsdp"), size) + offset, size) * depth
    return pl.multiple_of(start, depth)


def vmem_call(kernel, out_shape, operands, flops, name, after=(), moved=None):
    def body(*refs):
        kernel(*refs[: len(operands)], *refs[len(operands) + len(after) :])

    moved = moved or sum(x.size * x.dtype.itemsize for x in operands)
    whole = pl.BlockSpec(memory_space=pltpu.VMEM)
    return pl.pallas_call(
        body,
        out_shape=out_shape,
        in_specs=[whole] * len(operands) + [pl.BlockSpec(memory_space=pl.ANY)] * len(after),
        out_specs=jax.tree.map(lambda _: whole, out_shape),
        compiler_params=pltpu.CompilerParams(vmem_limit_bytes=VMEM_BYTES),
        cost_estimate=pl.CostEstimate(flops=flops, bytes_accessed=moved, transcendentals=0),
        name=name,
    )(*operands, *after)


def shape_of(rows, columns, dtype):
    return jax.ShapeDtypeStruct((rows, columns), dtype)


def column_window(array, start, width):
    if isinstance(array, jax.Array):
        return lax.dynamic_slice_in_dim(array, start, width, array.ndim - 1)
    return array[..., pl.ds(pl.multiple_of(start, width), width)]


def outer_kernel(replicas, share_cols, *refs):
    *held_refs, global_ref, momentum_ref, share_ref, new_momentum_ref = refs
    rows, window = held_refs[-1].shape[-2:]
    me = lax.axis_index("replica")

    def windows_of(ref):
        here = me * share_cols // window * window % ref.shape[-1]
        return ref[...] if ref.shape[-1] == window else column_window(ref, here, window)

    old = windows_of(global_ref).astype(F32)
    lane = lax.broadcasted_iota(jnp.int32, (rows, window), 1) // BLOCK
    total = jnp.zeros((rows, window), F32)
    for held_ref in held_refs:
        held = windows_of(held_ref).astype(F32)
        for local in [held] if held.ndim == 2 else list(held):
            drift = old - local
            size = jnp.abs(drift)
            scale = jnp.zeros((rows, window), F32)
            for block in range(window // BLOCK):
                top = jnp.max(jnp.where(lane == block, size, 0.0), axis=1, keepdims=True)
                top = (top + scale_epsilon).astype(BF16).astype(F32)
                scale = jnp.where(lane == block, top, scale)
            total = total + (drift / scale).astype(BF16).astype(F32) * scale
    mean_grad = total / replicas
    shares = window // share_cols
    mean_here, old_here = mean_grad[:, :share_cols], old[:, :share_cols]
    mine = me % shares
    for share in range(1, shares):
        columns = slice(share * share_cols, (share + 1) * share_cols)
        mean_here = jnp.where(mine == share, mean_grad[:, columns], mean_here)
        old_here = jnp.where(mine == share, old[:, columns], old_here)
    new_momentum = outer_momentum * momentum_ref[...] + mean_here
    new_momentum_ref[...] = new_momentum
    share_ref[...] = (old_here - outer_rate * (mean_here + outer_momentum * new_momentum)).astype(BF16)


def swap(array, bits):
    return lax.ppermute(array, "replica", [(at, at ^ bits) for at in range(lax.axis_size("replica"))])


def partner_kernel(bits, share_cols, width, *refs):
    *held_refs, out_ref = refs
    start = (lax.axis_index("replica") ^ bits) * share_cols // width * width
    at = 0
    for held_ref in held_refs:
        part = column_window(held_ref, start % held_ref.shape[-1], width)
        count = 1 if part.ndim == 2 else part.shape[0]
        out_ref[at : at + count] = part.reshape((count,) + part.shape[-2:])
        at += count


def send_windows(held, bits, kv_width, after):
    replicas = lax.axis_size("replica")
    share_cols = kv_width // replicas
    width = max(bits * share_cols, BLOCK)
    rows = held[0].shape[-2]
    count = sum(1 if array.ndim == 2 else array.shape[0] for array in held)
    if width % LANES == 0:
        leaving = vmem_call(
            functools.partial(partner_kernel, bits, share_cols, width),
            jax.ShapeDtypeStruct((count, rows, width), BF16),
            held,
            0,
            "partner_columns",
            after,
        )
    else:
        start = (lax.axis_index("replica") ^ bits) * share_cols // width * width
        parts = [column_window(array, start % array.shape[-1], width).reshape(-1, rows, width) for array in held]
        leaving = jnp.concatenate(parts)
    return held + [swap(leaving, bits)]


def update_share(held, global_weights, momentum, after):
    rows, share_cols = momentum.shape
    replicas = lax.axis_size("replica")
    window = held[-1].shape[-1]
    if window % LANES:
        start = lax.axis_index("replica") * share_cols // window * window
        held = [column_window(array, start % array.shape[-1], window) for array in held]
        global_weights = column_window(global_weights, start, window)
    return vmem_call(
        functools.partial(outer_kernel, replicas, share_cols),
        (shape_of(rows, share_cols, BF16), shape_of(rows, share_cols, F32)),
        held + [global_weights, momentum],
        0,
        "outer_update",
        after,
    )


def join_kernel(bits, mine_ref, other_ref, out_ref):
    width = mine_ref.shape[1]
    first = (lax.axis_index("replica") & bits) == 0

    @pl.when(first)
    def _():
        out_ref[:, :width] = mine_ref[...]
        out_ref[:, width:] = other_ref[...]

    @pl.when(jnp.logical_not(first))
    def _():
        out_ref[:, :width] = other_ref[...]
        out_ref[:, width:] = mine_ref[...]


def join_shares(mine, bits, after):
    rows, width = mine.shape
    return vmem_call(
        functools.partial(join_kernel, bits),
        shape_of(rows, 2 * width, BF16),
        [mine, swap(mine, bits)],
        0,
        "join_shares",
        after,
    )


def distinct(arrays):
    found = []
    for array in arrays:
        if not any(array is other for other in found):
            found.append(array)
    return found


def positions(pieces, arrays):
    index = {id(array): at for at, array in enumerate(arrays)}
    return [(index[id(array)], row, place, half) for array, row, place, half in pieces]


def piece_columns(place, half, size, depth):
    cut = depth // 2
    return pl.ds(pl.multiple_of(block_start(place, size, depth) + half * cut, cut), cut)


def products_kernel(size, pieces, count, first, last, inputs_ref, cotangent_ref, *refs):
    piece_refs, refs = refs[:count], refs[count:]
    total_ref, refs = (None, refs) if first else (refs[0], refs[2:])
    rows_ref, grad_ref, mark_ref, held, sems = refs
    depth = inputs_ref.shape[1] // size
    copies = []
    for number, (at, row, place, half) in enumerate(pieces):
        piece = piece_refs[at][row : row + depth // 2]
        held[number] = lax.dot_general(
            cotangent_ref[...], piece, (((1,), (1,)), ((), ())), preferred_element_type=F32
        ).astype(BF16)
        columns = piece_columns(place, half, size, depth)
        copies.append(pltpu.make_async_copy(held.at[number], grad_ref.at[:, columns], sems.at[number]))
        copies[-1].start()
    total = jnp.zeros(rows_ref.shape, F32) if first else total_ref[...]
    for at, row, place, half in pieces:
        piece = piece_refs[at][row : row + depth // 2]
        columns = inputs_ref[:, piece_columns(place, half, size, depth)]
        total = total + jnp.dot(columns, piece, preferred_element_type=F32)
    rows_ref[...] = total.astype(rows_ref.dtype)
    mark_ref[...] = jnp.zeros_like(mark_ref)
    for copy in copies:
        copy.wait()


def products(inputs_here, cotangent, pieces, before, size, last=False):
    tokens, width = inputs_here.shape
    kv_width = cotangent.shape[1]
    depth = width // size
    arrays = distinct(array for array, *_ in pieces)
    first = before is None
    operands = [inputs_here, cotangent] + arrays + ([] if first else list(before[:2]))
    whole, anywhere = pl.BlockSpec(memory_space=pltpu.VMEM), pl.BlockSpec(memory_space=pl.ANY)
    return pl.pallas_call(
        functools.partial(products_kernel, size, positions(pieces, arrays), len(arrays), first, last),
        out_shape=(
            shape_of(tokens, kv_width, BF16 if last else F32),
            shape_of(tokens, width, BF16),
            shape_of(8, LANES, F32),
        ),
        in_specs=[whole] * (2 + len(arrays)) + ([] if first else [whole, anywhere]),
        out_specs=(whole, anywhere, whole),
        scratch_shapes=[
            pltpu.VMEM((len(pieces), tokens, depth // 2), BF16),
            pltpu.SemaphoreType.DMA((len(pieces),)),
        ],
        input_output_aliases={} if first else {len(operands) - 1: 1},
        compiler_params=pltpu.CompilerParams(vmem_limit_bytes=VMEM_BYTES),
        cost_estimate=pl.CostEstimate(
            flops=2 * tokens * depth * len(pieces) * kv_width, bytes_accessed=PRODUCTS_BYTES * (4 if last else 1), transcendentals=0
        ),
        name="last_products" if last else "products",
    )(*operands)


def all_products(inputs_here, cotangent, pieces, size):
    width = inputs_here.shape[1]
    depth = width // size
    here = ring_place(lax.axis_index("fsdp"), size)
    gathered = jnp.zeros((width, cotangent.shape[1]), BF16)
    for array, row, place, half in pieces:
        start = ring_index(here + place, size) * depth + half * (depth // 2)
        gathered = lax.dynamic_update_slice_in_dim(gathered, array[row : row + depth // 2], start, 0)
    rows = jnp.dot(inputs_here, gathered, preferred_element_type=F32).astype(BF16)
    grad = lax.dot_general(cotangent, gathered, (((1,), (1,)), ((), ())), preferred_element_type=F32)
    return rows, grad.astype(BF16)


def terms_kernel(size, offsets, token_weight, inputs_ref, cotangent_ref, *out_refs):
    depth = inputs_ref.shape[1] // size
    at = 0
    for offset in offsets:
        columns = inputs_ref[:, pl.ds(block_start(offset, size, depth), depth)]
        terms = (
            lax.dot_general(columns, cotangent_ref[...], (((0,), (0,)), ((), ())), preferred_element_type=F32)
            * token_weight
        )
        filled = 0
        while filled < depth:
            count = out_refs[at].shape[0]
            out_refs[at][...] = terms[filled : filled + count].astype(out_refs[at].dtype)
            filled += count
            at += 1


def token_terms(inputs_here, cotangent, size, offsets, out_shape, token_weight, name, after=()):
    tokens, width = inputs_here.shape
    kv_width = cotangent.shape[1]
    depth = width // size
    if depth % LANES == 0:
        return vmem_call(
            functools.partial(terms_kernel, size, offsets, token_weight),
            out_shape,
            [inputs_here, cotangent],
            2 * tokens * depth * len(offsets) * kv_width,
            name,
            after,
        )
    place = ring_place(lax.axis_index("fsdp"), size)
    out = []
    for offset in offsets:
        columns = lax.dynamic_slice_in_dim(inputs_here, ring_index(place + offset, size) * depth, depth, 1)
        terms = (
            lax.dot_general(columns, cotangent, (((0,), (0,)), ((), ())), preferred_element_type=F32) * token_weight
        )
        filled = 0
        while filled < depth:
            like = out_shape[len(out)]
            out.append(terms[filled : filled + like.shape[0]].astype(like.dtype))
            filled += like.shape[0]
    return out


def add_kernel(up_terms_ref, down_terms_ref, up_ref, down_ref, up_out, down_out):
    depth = up_terms_ref.shape[0]
    count = up_ref.shape[0]
    up_out[:count] = (up_terms_ref[:count] + up_ref[...].astype(F32)).astype(BF16)
    down_out[depth - count :] = (down_terms_ref[depth - count :] + down_ref[...].astype(F32)).astype(BF16)
    if count < depth:
        up_out[count:] = up_terms_ref[count:].astype(BF16)
        down_out[: depth - count] = down_terms_ref[: depth - count].astype(BF16)


def end_kernel(terms_ref, up_ref, down_ref, out_ref):
    count = up_ref.shape[0]
    if count == terms_ref.shape[0]:
        out_ref[...] = (terms_ref[...] + up_ref[...].astype(F32) + down_ref[...].astype(F32)).astype(BF16)
    else:
        out_ref[:count] = (terms_ref[:count] + up_ref[...].astype(F32)).astype(BF16)
        out_ref[count:] = (terms_ref[count:] + down_ref[...].astype(F32)).astype(BF16)


def per_device(local_weights, global_weights, momentum, activations, kv_cotangent):
    local_shard = local_weights[0]
    inputs_here = activations[0]
    cotangent = kv_cotangent[0]
    depth, kv_width = local_shard.shape
    size = lax.axis_size("fsdp")
    token_weight = 1.0 / (inputs_here.shape[0] * size)
    wide = depth % (2 * LANES) == 0
    order = ring_order(size)
    up = [(order[at], order[(at + 1) % size]) for at in range(size)]
    down = [(target, source) for source, target in up]
    far = size // 2
    cut = depth // 2
    whole, half = shape_of(depth, kv_width, F32), shape_of(cut, kv_width, BF16)

    from_below, from_above = lax.ppermute(local_shard, "fsdp", up), lax.ppermute(local_shard, "fsdp", down)
    farthest = token_terms(inputs_here, cotangent, size, [far], [half, half], token_weight, "farthest_terms")
    sum_up, sum_down = lax.ppermute(farthest[0], "fsdp", up), lax.ppermute(farthest[1], "fsdp", down)
    offsets = [sign * step for step in range(far - 1, 0, -1) for sign in (1, -1)] + [0]
    terms = [whole] * len(offsets)
    terms = token_terms(inputs_here, cotangent, size, offsets, terms, token_weight, "near_terms", farthest)
    terms = dict(zip(offsets, terms))

    bits = lax.axis_size("replica") // 2
    held = send_windows([local_shard], bits, kv_width, (terms[0],))
    pieces = [(local_shard, 0, 0, 0), (local_shard, cut, 0, 1)]
    made = None

    def around(step):
        return [
            (from_below, 0, -step, 0),
            (from_below, cut, 1 - step, 1),
            (from_above, 0, step - 1, 0),
            (from_above, cut, step, 1),
        ]

    for step in range(1, far):
        near = far - step
        if step == 1:
            latest = [
                (array, half * cut, place, half) for array, place in ((from_below, -1), (from_above, 1)) for half in (0, 1)
            ]
            upward, downward = from_below[:cut], from_above[cut:]
            behind_up, behind_down = from_below[cut:], from_above[:cut]
        elif step == 2:
            latest = [(from_below, 0, -2, 0), (from_above, 0, 2, 1)]
            upward, downward = jnp.concatenate([from_below, behind_up]), jnp.concatenate([behind_down, from_above])
        else:
            latest = around(step)
            upward, downward = from_below, from_above
        pieces += latest
        after = (from_below, from_above)
        if wide:
            made = products(inputs_here, cotangent, pieces if step == 1 else latest, made, size)
            after = (made[2],)
        if step == min(2, far - 1):
            new_share, new_momentum = update_share(held, global_weights, momentum, after)
            new_global = new_share
            after += (new_share,)
        elif step == min(3, far - 1):
            while new_global.shape[1] < kv_width // 2:
                new_global = join_shares(new_global, bits, after)
                bits *= 2
            after += (new_global,)
        sums = vmem_call(
            add_kernel,
            [shape_of(depth, kv_width, BF16)] * 2,
            [terms[near], terms[-near], sum_up, sum_down],
            0,
            "add_terms",
            after,
        )
        while step == 1 and bits > 1:
            bits //= 2
            held = send_windows(held, bits, kv_width, sums)
        from_below, from_above = lax.ppermute(upward, "fsdp", up), lax.ppermute(downward, "fsdp", down)
        sum_up, sum_down = lax.ppermute(sums[0], "fsdp", up), lax.ppermute(sums[1], "fsdp", down)
    latest = around(far)
    while new_global.shape[1] < kv_width:
        new_global = join_shares(new_global, bits, ())
        bits *= 2
    if wide:
        kv_rows, grad_in, mark = products(inputs_here, cotangent, latest, made, size, last=True)
        after = (mark,)
    else:
        kv_rows, grad_in = all_products(inputs_here, cotangent, pieces + latest, size)
        after = ()
    grad_rows = vmem_call(
        end_kernel,
        shape_of(depth, kv_width, BF16),
        [terms[0], sum_up, sum_down],
        0,
        "end_terms",
        after,
    )
    return kv_rows[None], grad_in[None], grad_rows[None], new_global, new_momentum


def solution(mesh):
    placed = (
        P("replica", "fsdp", None),
        P("fsdp", None),
        P("fsdp", "replica"),
        P("replica", "fsdp", None),
        P("replica", "fsdp", None),
    )
    return jax.shard_map(
        per_device,
        mesh=mesh,
        in_specs=placed,
        out_specs=(
            P("replica", "fsdp", None),
            P("replica", "fsdp", None),
            P("replica", "fsdp", None),
            P("fsdp", None),
            P("fsdp", "replica"),
        ),
        check_vma=False,
    )
```

time: 60.2 us -> 47.4 us (0.79)
  local copies, waits for them, and re-layouts: 7.14 us -> 2.46 us
  Pallas kernels: 12.9 us -> 9.22 us
  waiting for transfers between devices: 16.3 us -> 13.4 us
  starting transfers between devices: 22.7 us -> 21.2 us
    pallas_call x13 -> x11, Pallas kernels: 10.8 us -> 3.88 us  [vmem_call(): pl.pallas_call(body, out_shape=out_shape, in_specs=[whole] * len(operands...]
    ppermute x12, waiting for transfers between devices: 4.82 us -> 9.2 us  [the longest x3 4.48 us: per_device(): lax.ppermute(sums[1], 'fsdp', down)]
    ppermute x6 -> x4, waiting for transfers between devices: 7.58 us -> 3.6 us  [swap(): lax.ppermute(array, 'replica', [(at, at ^ bits) for at in range(lax.axis_...]
    unnamed x44 -> x14, local copies, waits for them, and re-layouts: 5.8 us -> 2.42 us
    pallas_call x1 -> x4, Pallas kernels: 2.12 us -> 5.35 us  [products(): pl.pallas_call(functools.partial(products_kernel, size, positions(pieces,...]
    ppermute x1, waiting for transfers between devices: 1.99 us -> 0.01 us  [per_device(): lax.ppermute(local_shard, 'fsdp', up)]
    ppermute x6 -> x4, starting transfers between devices: 4.99 us -> 3.29 us  [swap(): lax.ppermute(array, 'replica', [(at, at ^ bits) for at in range(lax.axis_...]
    slice x2, local copies, waits for them, and re-layouts: 1.31 us -> 0.04 us  [the longest x1 0.02 us: per_device(): upward, downward = (from_below[:cut], from_above[cut:])]
  transfers between devices with their start and end apart: 22 -> 20, of which waited for: 8 -> 8; matrix products, arithmetic and copies ran while one was open for 2% -> 0% of each run, Pallas kernels for 17% -> 18%
where the time goes in v3:
time: 47.4 us; the launch traced here: 47.2 us
  starting transfers between devices  21.2 us (45%)
  waiting for transfers between devices  13.4 us (28%)
  Pallas kernels  9.22 us (19%)
  local copies, waits for them, and re-layouts  2.46 us (5%)
  between operations  0.86 us (2%)
    ppermute x3, starting transfers between devices, per_device(): lax.ppermute(upward, 'fsdp', up)  6.03 us
    pallas_call x4, Pallas kernels, products(): pl.pallas_call(functools.partial(products_kernel, size, positions(pieces,...  5.35 us
    ppermute x3, starting transfers between devices, per_device(): lax.ppermute(sums[0], 'fsdp', up)  4.84 us
    ppermute x3, waiting for transfers between devices, per_device(): lax.ppermute(sums[1], 'fsdp', down)  4.48 us
    pallas_call x11, Pallas kernels, vmem_call(): pl.pallas_call(body, out_shape=out_shape, in_specs=[whole] * len(operands...  3.88 us
    ppermute x4, waiting for transfers between devices, swap(): lax.ppermute(array, 'replica', [(at, at ^ bits) for at in range(lax.axis_...  3.6 us
    ppermute x3, waiting for transfers between devices, per_device(): lax.ppermute(sums[0], 'fsdp', up)  3.51 us
    ppermute x4, starting transfers between devices, swap(): lax.ppermute(array, 'replica', [(at, at ^ bits) for at in range(lax.axis_...  3.29 us
  transfers between devices with their start and end apart: 20, of which 8 were waited for; matrix products, arithmetic and copies ran while one was open for 0% of the time, Pallas kernels for 18%

profile of v3, /device:TPU:0, one launch (start us, length us, event | category | flops | bytes accessed | tf_op | source)
XLA Modules:
  0.0 47.2 jit_solution(5657550684574450588)
XLA Ops:
  0.6 3.1 %collective-permute-start = (bf16[256,512]{1,0:T(8,128)(2,1)}, bf16[256,512]{1,0:T(8,128)(2,1)S(1)}, u32[]{:S(2)}, u32[]{:S(2)}) collective-permute-start(bf16[256,512]{1,0:T(8,128)(2,1)} %bitcast.18), channel_id=1, source_target_pairs={{0,2},{2,4},{4,6},{6,7},{7,5},{5,3},{3,1},{1,0},{8,10},{10,12},{12... | collective-permute-start | bytes 786440 | tf_op jit(solution)/shard_map/ppermute | solution.py:352
  3.7 1.2 %copy-done = bf16[1,256,2048]{2,1,0:T(8,128)(2,1)S(1)} copy-done((bf16[1,256,2048]{2,1,0:T(8,128)(2,1)S(1)}, bf16[1,256,2048]{2,1,0:T(8,128)(2,1)}, u32[]{:S(2)}) %copy-start) | copy-done | bytes 1048600
  4.9 0.9 %copy-done.2 = bf16[1,256,512]{2,1,0:T(8,128)(2,1)S(1)} copy-done((bf16[1,256,512]{2,1,0:T(8,128)(2,1)S(1)}, bf16[1,256,512]{2,1,0:T(8,128)(2,1)}, u32[]{:S(2)}) %copy-start.2) | copy-done | bytes 262168
  6.2 2.1 %collective-permute-start.8 = (bf16[128,512]{1,0:T(8,128)(2,1)S(1)}, bf16[128,512]{1,0:T(8,128)(2,1)S(1)}, u32[]{:S(2)}, u32[]{:S(2)}) collective-permute-start(bf16[128,512]{1,0:T(8,128)(2,1)S(1)} %get-tuple-element.42.refs_2_), channel_id=1, source_target_pairs={{0,2},{2,4},{4,6},{6,7},{7,5},{5,3},{3,1},{1,0},{8,10},{10,12},{12... | collective-permute-start | bytes 393224 | tf_op jit(solution)/shard_map/ppermute | solution.py:354
  9.2 1.8 %collective-permute-start.12 = (bf16[1,256,256]{2,1,0:T(8,128)(2,1)S(1)}, bf16[1,256,256]{2,1,0:T(8,128)(2,1)S(1)}, u32[]{:S(2)}, u32[]{:S(2)}) collective-permute-start(bf16[1,256,256]{2,1,0:T(8,128)(2,1)S(1)} %partner_columns.2), channel_id=1, source_target_pairs={{0,16},{8,24},{16,0},{24,8},{1,17},{9,25},{17,1},{25,9},{2,18},{10... | collective-permute-start | bytes 393224 | tf_op jit(solution)/shard_map/ppermute | solution.py:106
  11.1 2.1 %collective-permute-start.1 = (bf16[128,512]{1,0:T(8,128)(2,1)S(1)}, bf16[128,512]{1,0:T(8,128)(2,1)S(1)}, u32[]{:S(2)}, u32[]{:S(2)}) collective-permute-start(bf16[128,512]{1,0:T(8,128)(2,1)S(1)} %get-tuple-element.65), channel_id=1, source_target_pairs={{0,2},{2,4},{4,6},{6,7},{7,5},{5,3},{3,1},{1,0},{8,10},{10,12},{12... | collective-permute-start | bytes 393224 | tf_op jit(solution)/shard_map/ppermute | solution.py:412
  13.3 1.4 %products.3 = (f32[256,512]{1,0:T(8,128)S(1)}, bf16[256,2048]{1,0:T(8,128)(2,1)}, f32[8,128]{1,0:T(8,128)S(1)}) custom-call(bf16[256,2048]{1,0:T(8,128)(2,1)S(1)} %bitcast.8, bf16[256,512]{1,0:T(8,128)(2,1)S(1)} %bitcast.14, bf16[256,512]{1,0:T(8,128)(2,1)S(1)} %bitcast.21, bf16[256,512]{1,0:T(8,128)(2,1)S(1)} %collective-permute-done.refs_1_, ...), custom_call_target="tpu_custom_call" | custom-call | flops 402653184 | bytes 8388608 | tf_op jit(solution)/shard_map/products/pallas_call | solution.py:238
  15.4 1.6 %collective-permute-start.10 = (bf16[256,512]{1,0:T(8,128)(2,1)S(1)}, bf16[256,512]{1,0:T(8,128)(2,1)S(1)}, u32[]{:S(2)}, u32[]{:S(2)}) collective-permute-start(bf16[256,512]{1,0:T(8,128)(2,1)S(1)} %get-tuple-element.52.refs_2_), channel_id=1, source_target_pairs={{0,2},{2,4},{4,6},{6,7},{7,5},{5,3},{3,1},{1,0},{8,10},{10,12},{12... | collective-permute-start | bytes 786440 | tf_op jit(solution)/shard_map/ppermute | solution.py:413
  17.7 1.6 %collective-permute-start.2 = (bf16[256,512]{1,0:T(8,128)(2,1)S(1)}, bf16[256,512]{1,0:T(8,128)(2,1)S(1)}, u32[]{:S(2)}, u32[]{:S(2)}) collective-permute-start(bf16[256,512]{1,0:T(8,128)(2,1)S(1)} %pad_maximum_fusion), channel_id=1, source_target_pairs={{0,2},{2,4},{4,6},{6,7},{7,5},{5,3},{3,1},{1,0},{8,10},{10,12},{12... | collective-permute-start | bytes 786440 | tf_op jit(solution)/shard_map/ppermute | solution.py:412
  19.8 1.0 %products.4 = (f32[256,512]{1,0:T(8,128)S(1)}, bf16[256,2048]{1,0:T(8,128)(2,1)}, f32[8,128]{1,0:T(8,128)S(1)}) custom-call(bf16[256,2048]{1,0:T(8,128)(2,1)S(1)} %bitcast.9, bf16[256,512]{1,0:T(8,128)(2,1)S(1)} %bitcast.15, bf16[128,512]{1,0:T(8,128)(2,1)S(1)} %collective-permute-done.1.refs_0_, ...), custom_call_target="tpu_custom_call", output_to_operand_aliasing={{1}: (5, {})} | custom-call | flops 134217728 | bytes 8388608 | tf_op jit(solution)/shard_map/products/pallas_call | solution.py:238
  20.8 1.1 %outer_update.1 = (bf16[256,128]{1,0:T(8,128)(2,1)S(1)}, f32[256,128]{1,0:T(8,128)}) custom-call(bf16[256,512]{1,0:T(8,128)(2,1)S(1)} %bitcast.23, bf16[1,256,256]{2,1,0:T(8,128)(2,1)S(1)} %collective-permute-done.12.refs_1_, bf16[2,256,128]{2,1,0:T(8,128)(2,1)S(1)} %collective-permute-done.13.refs_2_, bf16[256,512]{1,0:T(8,128)(2,1)S(1)} %copy-done.5, ...), custom_call_target="tpu_custom_call" | custom-call | bytes 917504 | tf_op jit(solution)/shard_map/outer_update/pallas_call | solution.py:48
  21.9 0.9 %collective-permute-done.10.refs_2_ = bf16[256,512]{1,0:T(8,128)(2,1)S(1)} collective-permute-done((bf16[256,512]{1,0:T(8,128)(2,1)S(1)}, bf16[256,512]{1,0:T(8,128)(2,1)S(1)}, u32[]{:S(2)}, u32[]{:S(2)}) %collective-permute-start.10) | collective-permute-done | bytes 262176 | tf_op jit(solution)/shard_map/ppermute | solution.py:413
  22.9 2.6 %collective-permute-done.11.refs_3_ = bf16[256,512]{1,0:T(8,128)(2,1)S(1)} collective-permute-done((bf16[256,512]{1,0:T(8,128)(2,1)S(1)}, bf16[256,512]{1,0:T(8,128)(2,1)S(1)}, u32[]{:S(2)}, u32[]{:S(2)}) %collective-permute-start.11) | collective-permute-done | bytes 262176 | tf_op jit(solution)/shard_map/ppermute | solution.py:413
  25.6 1.6 %collective-permute-start.14 = (bf16[256,512]{1,0:T(8,128)(2,1)S(1)}, bf16[256,512]{1,0:T(8,128)(2,1)S(1)}, u32[]{:S(2)}, u32[]{:S(2)}) collective-permute-start(bf16[256,512]{1,0:T(8,128)(2,1)S(1)} %get-tuple-element.56), channel_id=1, source_target_pairs={{0,2},{2,4},{4,6},{6,7},{7,5},{5,3},{3,1},{1,0},{8,10},{10,12},{12... | collective-permute-start | bytes 786440 | tf_op jit(solution)/shard_map/ppermute | solution.py:413
  27.7 0.8 %collective-permute-done.2.refs_0_ = bf16[256,512]{1,0:T(8,128)(2,1)S(1)} collective-permute-done((bf16[256,512]{1,0:T(8,128)(2,1)S(1)}, bf16[256,512]{1,0:T(8,128)(2,1)S(1)}, u32[]{:S(2)}, u32[]{:S(2)}) %collective-permute-start.2) | collective-permute-done | bytes 262176 | tf_op jit(solution)/shard_map/ppermute | solution.py:412
  28.5 2.3 %collective-permute-start.3 = (bf16[256,512]{1,0:T(8,128)(2,1)S(1)}, bf16[256,512]{1,0:T(8,128)(2,1)S(1)}, u32[]{:S(2)}, u32[]{:S(2)}) collective-permute-start(bf16[256,512]{1,0:T(8,128)(2,1)S(1)} %collective-permute-done.2.refs_0_), channel_id=1, source_target_pairs={{0,2},{2,4},{4,6},{6,7},{7,5},{5,3},{3,1},{1,0},{8,10},{10,12},{12... | collective-permute-start | bytes 786440 | tf_op jit(solution)/shard_map/ppermute | solution.py:412
  31.1 1.1 %products.5 = (f32[256,512]{1,0:T(8,128)S(1)}, bf16[256,2048]{1,0:T(8,128)(2,1)}, f32[8,128]{1,0:T(8,128)S(1)}) custom-call(bf16[256,2048]{1,0:T(8,128)(2,1)S(1)} %bitcast.10, bf16[256,512]{1,0:T(8,128)(2,1)S(1)} %bitcast.16, bf16[256,512]{1,0:T(8,128)(2,1)S(1)} %collective-permute-done.2.refs_0_, ...), custom_call_target="tpu_custom_call", output_to_operand_aliasing={{1}: (5, {})} | custom-call | flops 268435456 | bytes 8388608 | tf_op jit(solution)/shard_map/products/pallas_call | solution.py:238
  32.3 2.6 %collective-permute-done.14.refs_2_ = bf16[256,512]{1,0:T(8,128)(2,1)S(1)} collective-permute-done((bf16[256,512]{1,0:T(8,128)(2,1)S(1)}, bf16[256,512]{1,0:T(8,128)(2,1)S(1)}, u32[]{:S(2)}, u32[]{:S(2)}) %collective-permute-start.14) | collective-permute-done | bytes 262176 | tf_op jit(solution)/shard_map/ppermute | solution.py:413
  34.9 1.8 %collective-permute-done.15.refs_3_ = bf16[256,512]{1,0:T(8,128)(2,1)S(1)} collective-permute-done((bf16[256,512]{1,0:T(8,128)(2,1)S(1)}, bf16[256,512]{1,0:T(8,128)(2,1)S(1)}, u32[]{:S(2)}, u32[]{:S(2)}) %collective-permute-start.15) | collective-permute-done | bytes 262176 | tf_op jit(solution)/shard_map/ppermute | solution.py:413
  36.8 1.6 %collective-permute-start.17 = (bf16[256,512]{1,0:T(8,128)(2,1)S(1)}, bf16[256,512]{1,0:T(8,128)(2,1)S(1)}, u32[]{:S(2)}, u32[]{:S(2)}) collective-permute-start(bf16[256,512]{1,0:T(8,128)(2,1)S(1)} %get-tuple-element.59), channel_id=1, source_target_pairs={{0,2},{2,4},{4,6},{6,7},{7,5},{5,3},{3,1},{1,0},{8,10},{10,12},{12... | collective-permute-start | bytes 786440 | tf_op jit(solution)/shard_map/ppermute | solution.py:413
  38.9 1.4 %collective-permute-start.19 = (bf16[256,256]{1,0:T(8,128)(2,1)S(1)}, bf16[256,256]{1,0:T(8,128)(2,1)S(1)}, u32[]{:S(2)}, u32[]{:S(2)}) collective-permute-start(bf16[256,256]{1,0:T(8,128)(2,1)S(1)} %join_shares.2.refs_5_.refs_0_), channel_id=1, source_target_pairs={{0,16},{8,24},{16,0},{24,8},{1,17},{9,25},{17,1},{25,9},{2,18},{10... | collective-permute-start | bytes 393224 | tf_op jit(solution)/shard_map/ppermute | solution.py:106
  40.3 3.6 %collective-permute-done.19.refs_1_ = bf16[256,256]{1,0:T(8,128)(2,1)S(1)} collective-permute-done((bf16[256,256]{1,0:T(8,128)(2,1)S(1)}, bf16[256,256]{1,0:T(8,128)(2,1)S(1)}, u32[]{:S(2)}, u32[]{:S(2)}) %collective-permute-start.19) | collective-permute-done | bytes 131104 | tf_op jit(solution)/shard_map/ppermute | solution.py:106
  44.6 1.8 %last_products.1 = (bf16[256,512]{1,0:T(8,128)(2,1)}, bf16[256,2048]{1,0:T(8,128)(2,1)}, f32[8,128]{1,0:T(8,128)S(1)}) custom-call(bf16[256,2048]{1,0:T(8,128)(2,1)S(1)} %bitcast.11, bf16[256,512]{1,0:T(8,128)(2,1)S(1)} %bitcast.17, bf16[256,512]{1,0:T(8,128)(2,1)S(1)} %collective-permute-done.3.refs_0_, ...), custom_call_target="tpu_custom_call", output_to_operand_aliasing={{1}: (5, {})} | custom-call | flops 268435456 | bytes 33554432 | tf_op jit(solution)/shard_map/last_products/pallas_call | solution.py:238
  46.4 0.8 %end_terms.1 = bf16[256,512]{1,0:T(8,128)(2,1)} custom-call(f32[256,512]{1,0:T(8,128)S(1)} %get-tuple-element.44.refs_1_.refs_0_, bf16[256,512]{1,0:T(8,128)(2,1)S(1)} %collective-permute-done.17.refs_1_, bf16[256,512]{1,0:T(8,128)(2,1)S(1)} %collective-permute-done.18.refs_2_, f32[8,128]{1,0:T(8,128)S(1)} %get-tuple-element.61.refs_3_), custom_call_target="tpu_custom_call" | custom-call | bytes 1048576 | tf_op jit(solution)/shard_map/end_terms/pallas_call | solution.py:48
  (49 shorter events, 5.4 us)
Async XLA Ops:
  0.6 10.4 %collective-permute-start = (bf16[256,512]{1,0:T(8,128)(2,1)}, bf16[256,512]{1,0:T(8,128)(2,1)S(1)}, u32[]{:S(2)}, u32[]{:S(2)}) collective-permute-start(bf16[256,512]{1,0:T(8,128)(2,1)} %bitcast.18), channel_id=1, source_target_pairs={{0,2},{2,4},{4,6},{6,7},{7,5},{5,3},{3,1},{1,0},{8,10},{10,12},{12... | collective-permute-start | bytes 786440 | tf_op jit(solution)/shard_map/ppermute | solution.py:352
  3.7 9.5 %collective-permute-start.4 = (bf16[256,512]{1,0:T(8,128)(2,1)}, bf16[256,512]{1,0:T(8,128)(2,1)S(1)}, u32[]{:S(2)}, u32[]{:S(2)}) collective-permute-start(bf16[256,512]{1,0:T(8,128)(2,1)} %bitcast.19), channel_id=1, source_target_pairs={{2,0},{4,2},{6,4},{7,6},{5,7},{3,5},{1,3},{0,1},{10,8},{12,10},{14... | collective-permute-start | bytes 786440 | tf_op jit(solution)/shard_map/ppermute | solution.py:352
  3.7 1.2 %copy-start = (bf16[1,256,2048]{2,1,0:T(8,128)(2,1)S(1)}, bf16[1,256,2048]{2,1,0:T(8,128)(2,1)}, u32[]{:S(2)}) copy-start(bf16[1,256,2048]{2,1,0:T(8,128)(2,1)} %param.8) | copy-start | bytes 3145732
  6.2 8.6 %collective-permute-start.8 = (bf16[128,512]{1,0:T(8,128)(2,1)S(1)}, bf16[128,512]{1,0:T(8,128)(2,1)S(1)}, u32[]{:S(2)}, u32[]{:S(2)}) collective-permute-start(bf16[128,512]{1,0:T(8,128)(2,1)S(1)} %get-tuple-element.42.refs_2_), channel_id=1, source_target_pairs={{0,2},{2,4},{4,6},{6,7},{7,5},{5,3},{3,1},{1,0},{8,10},{10,12},{12... | collective-permute-start | bytes 393224 | tf_op jit(solution)/shard_map/ppermute | solution.py:354
  8.2 7.1 %collective-permute-start.9 = (bf16[128,512]{1,0:T(8,128)(2,1)S(1)}, bf16[128,512]{1,0:T(8,128)(2,1)S(1)}, u32[]{:S(2)}, u32[]{:S(2)}) collective-permute-start(bf16[128,512]{1,0:T(8,128)(2,1)S(1)} %get-tuple-element.43.refs_3_), channel_id=1, source_target_pairs={{2,0},{4,2},{6,4},{7,6},{5,7},{3,5},{1,3},{0,1},{10,8},{12,10},{14... | collective-permute-start | bytes 393224 | tf_op jit(solution)/shard_map/ppermute | solution.py:354
  8.9 4.3 %copy-start.1 = (bf16[1,256,2048]{2,1,0:T(8,128)(2,1)S(1)}, bf16[1,256,2048]{2,1,0:T(8,128)(2,1)}, u32[]{:S(2)}) copy-start(bf16[1,256,2048]{2,1,0:T(8,128)(2,1)} %param.8) | copy-start | bytes 3145732
  9.2 8.3 %collective-permute-start.12 = (bf16[1,256,256]{2,1,0:T(8,128)(2,1)S(1)}, bf16[1,256,256]{2,1,0:T(8,128)(2,1)S(1)}, u32[]{:S(2)}, u32[]{:S(2)}) collective-permute-start(bf16[1,256,256]{2,1,0:T(8,128)(2,1)S(1)} %partner_columns.2), channel_id=1, source_target_pairs={{0,16},{8,24},{16,0},{24,8},{1,17},{9,25},{17,1},{25,9},{2,18},{10... | collective-permute-start | bytes 393224 | tf_op jit(solution)/shard_map/ppermute | solution.py:106
  11.1 2.2 %copy-start.3 = (bf16[1,256,512]{2,1,0:T(8,128)(2,1)S(1)}, bf16[1,256,512]{2,1,0:T(8,128)(2,1)}, u32[]{:S(2)}) copy-start(bf16[1,256,512]{2,1,0:T(8,128)(2,1)} %param.9) | copy-start | bytes 786436
  11.1 6.5 %collective-permute-start.1 = (bf16[128,512]{1,0:T(8,128)(2,1)S(1)}, bf16[128,512]{1,0:T(8,128)(2,1)S(1)}, u32[]{:S(2)}, u32[]{:S(2)}) collective-permute-start(bf16[128,512]{1,0:T(8,128)(2,1)S(1)} %get-tuple-element.65), channel_id=1, source_target_pairs={{0,2},{2,4},{4,6},{6,7},{7,5},{5,3},{3,1},{1,0},{8,10},{10,12},{12... | collective-permute-start | bytes 393224 | tf_op jit(solution)/shard_map/ppermute | solution.py:412
  13.2 6.1 %collective-permute-start.5 = (bf16[128,512]{1,0:T(8,128)(2,1)S(1)}, bf16[128,512]{1,0:T(8,128)(2,1)S(1)}, u32[]{:S(2)}, u32[]{:S(2)}) collective-permute-start(bf16[128,512]{1,0:T(8,128)(2,1)S(1)} %get-tuple-element.64), channel_id=1, source_target_pairs={{2,0},{4,2},{6,4},{7,6},{5,7},{3,5},{1,3},{0,1},{10,8},{12,10},{14... | collective-permute-start | bytes 393224 | tf_op jit(solution)/shard_map/ppermute | solution.py:412
  15.4 7.4 %collective-permute-start.10 = (bf16[256,512]{1,0:T(8,128)(2,1)S(1)}, bf16[256,512]{1,0:T(8,128)(2,1)S(1)}, u32[]{:S(2)}, u32[]{:S(2)}) collective-permute-start(bf16[256,512]{1,0:T(8,128)(2,1)S(1)} %get-tuple-element.52.refs_2_), channel_id=1, source_target_pairs={{0,2},{2,4},{4,6},{6,7},{7,5},{5,3},{3,1},{1,0},{8,10},{10,12},{12... | collective-permute-start | bytes 786440 | tf_op jit(solution)/shard_map/ppermute | solution.py:413
  17.1 8.4 %collective-permute-start.11 = (bf16[256,512]{1,0:T(8,128)(2,1)S(1)}, bf16[256,512]{1,0:T(8,128)(2,1)S(1)}, u32[]{:S(2)}, u32[]{:S(2)}) collective-permute-start(bf16[256,512]{1,0:T(8,128)(2,1)S(1)} %get-tuple-element.53.refs_3_), channel_id=1, source_target_pairs={{2,0},{4,2},{6,4},{7,6},{5,7},{3,5},{1,3},{0,1},{10,8},{12,10},{14... | collective-permute-start | bytes 786440 | tf_op jit(solution)/shard_map/ppermute | solution.py:413
  17.5 3.3 %collective-permute-start.13 = (bf16[2,256,128]{2,1,0:T(8,128)(2,1)S(1)}, bf16[2,256,128]{2,1,0:T(8,128)(2,1)S(1)}, u32[]{:S(2)}, u32[]{:S(2)}) collective-permute-start(bf16[2,256,128]{2,1,0:T(8,128)(2,1)S(1)} %partner_columns.3), channel_id=1, source_target_pairs={{0,8},{8,0},{16,24},{24,16},{1,9},{9,1},{17,25},{25,17},{2,10},{10... | collective-permute-start | bytes 393224 | tf_op jit(solution)/shard_map/ppermute | solution.py:106
  17.7 10.8 %collective-permute-start.2 = (bf16[256,512]{1,0:T(8,128)(2,1)S(1)}, bf16[256,512]{1,0:T(8,128)(2,1)S(1)}, u32[]{:S(2)}, u32[]{:S(2)}) collective-permute-start(bf16[256,512]{1,0:T(8,128)(2,1)S(1)} %pad_maximum_fusion), channel_id=1, source_target_pairs={{0,2},{2,4},{4,6},{6,7},{7,5},{5,3},{3,1},{1,0},{8,10},{10,12},{12... | collective-permute-start | bytes 786440 | tf_op jit(solution)/shard_map/ppermute | solution.py:412
  19.3 11.8 %collective-permute-start.6 = (bf16[256,512]{1,0:T(8,128)(2,1)S(1)}, bf16[256,512]{1,0:T(8,128)(2,1)S(1)}, u32[]{:S(2)}, u32[]{:S(2)}) collective-permute-start(bf16[256,512]{1,0:T(8,128)(2,1)S(1)} %pad_maximum_fusion.1), channel_id=1, source_target_pairs={{2,0},{4,2},{6,4},{7,6},{5,7},{3,5},{1,3},{0,1},{10,8},{12,10},{14... | collective-permute-start | bytes 786440 | tf_op jit(solution)/shard_map/ppermute | solution.py:412
  19.8 1.0 %copy-start.6 = (f32[256,128]{1,0:T(8,128)S(1)}, f32[256,128]{1,0:T(8,128)}, u32[]{:S(2)}) copy-start(f32[256,128]{1,0:T(8,128)} %refs_4_.1) | copy-start | bytes 393220
  25.6 9.3 %collective-permute-start.14 = (bf16[256,512]{1,0:T(8,128)(2,1)S(1)}, bf16[256,512]{1,0:T(8,128)(2,1)S(1)}, u32[]{:S(2)}, u32[]{:S(2)}) collective-permute-start(bf16[256,512]{1,0:T(8,128)(2,1)S(1)} %get-tuple-element.56), channel_id=1, source_target_pairs={{0,2},{2,4},{4,6},{6,7},{7,5},{5,3},{3,1},{1,0},{8,10},{10,12},{12... | collective-permute-start | bytes 786440 | tf_op jit(solution)/shard_map/ppermute | solution.py:413
  27.2 9.5 %collective-permute-start.15 = (bf16[256,512]{1,0:T(8,128)(2,1)S(1)}, bf16[256,512]{1,0:T(8,128)(2,1)S(1)}, u32[]{:S(2)}, u32[]{:S(2)}) collective-permute-start(bf16[256,512]{1,0:T(8,128)(2,1)S(1)} %get-tuple-element.57), channel_id=1, source_target_pairs={{2,0},{4,2},{6,4},{7,6},{5,7},{3,5},{1,3},{0,1},{10,8},{12,10},{14... | collective-permute-start | bytes 786440 | tf_op jit(solution)/shard_map/ppermute | solution.py:413
  27.7 4.6 %collective-permute-start.16 = (bf16[256,128]{1,0:T(8,128)(2,1)S(1)}, bf16[256,128]{1,0:T(8,128)(2,1)S(1)}, u32[]{:S(2)}, u32[]{:S(2)}) collective-permute-start(bf16[256,128]{1,0:T(8,128)(2,1)S(1)} %get-tuple-element.55.refs_5_.refs_0_), channel_id=1, source_target_pairs={{0,8},{8,0},{16,24},{24,16},{1,9},{9,1},{17,25},{25,17},{2,10},{10... | collective-permute-start | bytes 196616 | tf_op jit(solution)/shard_map/ppermute | solution.py:106
  28.5 16.1 %collective-permute-start.3 = (bf16[256,512]{1,0:T(8,128)(2,1)S(1)}, bf16[256,512]{1,0:T(8,128)(2,1)S(1)}, u32[]{:S(2)}, u32[]{:S(2)}) collective-permute-start(bf16[256,512]{1,0:T(8,128)(2,1)S(1)} %collective-permute-done.2.refs_0_), channel_id=1, source_target_pairs={{0,2},{2,4},{4,6},{6,7},{7,5},{5,3},{3,1},{1,0},{8,10},{10,12},{12... | collective-permute-start | bytes 786440 | tf_op jit(solution)/shard_map/ppermute | solution.py:412
  31.1 13.5 %collective-permute-start.7 = (bf16[256,512]{1,0:T(8,128)(2,1)S(1)}, bf16[256,512]{1,0:T(8,128)(2,1)S(1)}, u32[]{:S(2)}, u32[]{:S(2)}) collective-permute-start(bf16[256,512]{1,0:T(8,128)(2,1)S(1)} %collective-permute-done.6.refs_1_), channel_id=1, source_target_pairs={{2,0},{4,2},{6,4},{7,6},{5,7},{3,5},{1,3},{0,1},{10,8},{12,10},{14... | collective-permute-start | bytes 786440 | tf_op jit(solution)/shard_map/ppermute | solution.py:412
  36.8 9.6 %collective-permute-start.17 = (bf16[256,512]{1,0:T(8,128)(2,1)S(1)}, bf16[256,512]{1,0:T(8,128)(2,1)S(1)}, u32[]{:S(2)}, u32[]{:S(2)}) collective-permute-start(bf16[256,512]{1,0:T(8,128)(2,1)S(1)} %get-tuple-element.59), channel_id=1, source_target_pairs={{0,2},{2,4},{4,6},{6,7},{7,5},{5,3},{3,1},{1,0},{8,10},{10,12},{12... | collective-permute-start | bytes 786440 | tf_op jit(solution)/shard_map/ppermute | solution.py:413
  38.4 8.0 %collective-permute-start.18 = (bf16[256,512]{1,0:T(8,128)(2,1)S(1)}, bf16[256,512]{1,0:T(8,128)(2,1)S(1)}, u32[]{:S(2)}, u32[]{:S(2)}) collective-permute-start(bf16[256,512]{1,0:T(8,128)(2,1)S(1)} %get-tuple-element.60), channel_id=1, source_target_pairs={{2,0},{4,2},{6,4},{7,6},{5,7},{3,5},{1,3},{0,1},{10,8},{12,10},{14... | collective-permute-start | bytes 786440 | tf_op jit(solution)/shard_map/ppermute | solution.py:413
  38.9 5.0 %collective-permute-start.19 = (bf16[256,256]{1,0:T(8,128)(2,1)S(1)}, bf16[256,256]{1,0:T(8,128)(2,1)S(1)}, u32[]{:S(2)}, u32[]{:S(2)}) collective-permute-start(bf16[256,256]{1,0:T(8,128)(2,1)S(1)} %join_shares.2.refs_5_.refs_0_), channel_id=1, source_target_pairs={{0,16},{8,24},{16,0},{24,8},{1,17},{9,25},{17,1},{25,9},{2,18},{10... | collective-permute-start | bytes 393224 | tf_op jit(solution)/shard_map/ppermute | solution.py:106
  (3 other events, 2.9 us)

commit v4 on v3

--- a/solution.py
+++ b/solution.py
@@ -157,31 +157,31 @@
     )
 
 
-def join_kernel(bits, mine_ref, other_ref, out_ref):
-    width = mine_ref.shape[1]
-    first = (lax.axis_index("replica") & bits) == 0
-
-    @pl.when(first)
-    def _():
-        out_ref[:, :width] = mine_ref[...]
-        out_ref[:, width:] = other_ref[...]
-
-    @pl.when(jnp.logical_not(first))
-    def _():
-        out_ref[:, :width] = other_ref[...]
-        out_ref[:, width:] = mine_ref[...]
-
-
-def join_shares(mine, bits, after):
-    rows, width = mine.shape
-    return vmem_call(
-        functools.partial(join_kernel, bits),
-        shape_of(rows, 2 * width, BF16),
-        [mine, swap(mine, bits)],
-        0,
-        "join_shares",
-        after,
-    )
+def join_kernel(places, *refs):
+    *held_refs, out_ref = refs
+    width = out_ref.shape[1] // len(places)
+    me = lax.axis_index("replica")
+    at = 0
+    for held_ref in held_refs:
+        for start in range(0, held_ref.shape[1], width):
+            columns = pl.ds(pl.multiple_of((me ^ places[at]) * width, width), width)
+            out_ref[:, columns] = held_ref[:, start : start + width]
+            at += 1
+
+
+def join_shares(held, places, kv_width, after):
+    rows = held[0].shape[0]
+    width = kv_width // len(places)
+    if width % LANES == 0:
+        return vmem_call(
+            functools.partial(join_kernel, places), shape_of(rows, kv_width, BF16), held, 0, "join_shares", after
+        )
+    whole = jnp.concatenate(held, axis=1)
+    joined = jnp.zeros_like(whole)
+    for at, place in enumerate(places):
+        start = (lax.axis_index("replica") ^ place) * width
+        joined = lax.dynamic_update_slice_in_dim(joined, whole[:, at * width : (at + 1) * width], start, 1)
+    return joined
 
 
 def distinct(arrays):
@@ -391,13 +391,16 @@
             after = (made[2],)
         if step == min(2, far - 1):
             new_share, new_momentum = update_share(held, global_weights, momentum, after)
-            new_global = new_share
             after += (new_share,)
+            bits = lax.axis_size("replica") // 2
+            shares, places = [new_share, swap(new_share, bits)], [0, bits]
         elif step == min(3, far - 1):
-            while new_global.shape[1] < kv_width // 2:
-                new_global = join_shares(new_global, bits, after)
-                bits *= 2
-            after += (new_global,)
+            while bits > 1:
+                bits //= 2
+                shares = [jnp.concatenate(shares, axis=1)]
+                after += (shares[0],)
+                shares.append(swap(shares[0], bits))
+                places += [place ^ bits for place in places]
         sums = vmem_call(
             add_kernel,
             [shape_of(depth, kv_width, BF16)] * 2,
@@ -412,15 +415,13 @@
         from_below, from_above = lax.ppermute(upward, "fsdp", up), lax.ppermute(downward, "fsdp", down)
         sum_up, sum_down = lax.ppermute(sums[0], "fsdp", up), lax.ppermute(sums[1], "fsdp", down)
     latest = around(far)
-    while new_global.shape[1] < kv_width:
-        new_global = join_shares(new_global, bits, ())
-        bits *= 2
     if wide:
         kv_rows, grad_in, mark = products(inputs_here, cotangent, latest, made, size, last=True)
         after = (mark,)
     else:
         kv_rows, grad_in = all_products(inputs_here, cotangent, pieces + latest, size)
         after = ()
+    new_global = join_shares(shares, places, kv_width, after)
     grad_rows = vmem_call(
         end_kernel,
         shape_of(depth, kv_width, BF16),

time: 47.4 us -> 47.3 us (level)
    ppermute x3, waiting for transfers between devices: 3.51 us -> 0.95 us  [per_device(): lax.ppermute(sums[0], 'fsdp', up)]
    ppermute x3, waiting for transfers between devices: 0.82 us -> 2.24 us  [per_device(): lax.ppermute(upward, 'fsdp', up)]
    ppermute x3, waiting for transfers between devices: 0.4 us -> 1.71 us  [per_device(): lax.ppermute(downward, 'fsdp', down)]
    ppermute x4, waiting for transfers between devices: 3.6 us -> 2.89 us  [swap(): lax.ppermute(array, 'replica', [(at, at ^ bits) for at in range(lax.axis_...]
    ppermute x3, starting transfers between devices: 6.03 us -> 5.35 us  [per_device(): lax.ppermute(upward, 'fsdp', up)]
    ppermute x3, waiting for transfers between devices: 4.48 us -> 5.08 us  [per_device(): lax.ppermute(sums[1], 'fsdp', down)]
    unnamed x14 -> x15, local copies, waits for them, and re-layouts: 2.42 us -> 2.43 us
    pallas_call x11 -> x10, Pallas kernels: 3.88 us -> 3.88 us  [vmem_call(): pl.pallas_call(body, out_shape=out_shape, in_specs=[whole] * len(operands...]
where the time goes in v4:
time: 47.3 us; the launch traced here: 47.1 us
  starting transfers between devices  21 us (44%)
  waiting for transfers between devices  13.5 us (29%)
  Pallas kernels  9.22 us (19%)
  local copies, waits for them, and re-layouts  2.49 us (5%)
  between operations  0.85 us (2%)
    ppermute x3, starting transfers between devices, per_device(): lax.ppermute(upward, 'fsdp', up)  5.35 us
    pallas_call x4, Pallas kernels, products(): pl.pallas_call(functools.partial(products_kernel, size, positions(pieces,...  5.34 us
    ppermute x3, waiting for transfers between devices, per_device(): lax.ppermute(sums[1], 'fsdp', down)  5.08 us
    ppermute x3, starting transfers between devices, per_device(): lax.ppermute(sums[0], 'fsdp', up)  4.84 us
    pallas_call x10, Pallas kernels, vmem_call(): pl.pallas_call(body, out_shape=out_shape, in_specs=[whole] * len(operands...  3.88 us
    ppermute x4, starting transfers between devices, swap(): lax.ppermute(array, 'replica', [(at, at ^ bits) for at in range(lax.axis_...  3.29 us
    ppermute x1, starting transfers between devices, per_device(): lax.ppermute(local_shard, 'fsdp', up)  3.08 us
    ppermute x4, waiting for transfers between devices, swap(): lax.ppermute(array, 'replica', [(at, at ^ bits) for at in range(lax.axis_...  2.89 us
  transfers between devices with their start and end apart: 20, of which 8 were waited for; matrix products, arithmetic and copies ran while one was open for 0% of the time, Pallas kernels for 18%

profile of v4, /device:TPU:0, one launch (start us, length us, event | category | flops | bytes accessed | tf_op | source)
XLA Modules:
  0.0 47.1 jit_solution(17959736604885690040)
XLA Ops:
  0.6 3.1 %collective-permute-start = (bf16[256,512]{1,0:T(8,128)(2,1)}, bf16[256,512]{1,0:T(8,128)(2,1)S(1)}, u32[]{:S(2)}, u32[]{:S(2)}) collective-permute-start(bf16[256,512]{1,0:T(8,128)(2,1)} %bitcast.18), channel_id=1, source_target_pairs={{0,2},{2,4},{4,6},{6,7},{7,5},{5,3},{3,1},{1,0},{8,10},{10,12},{12... | collective-permute-start | bytes 786440 | tf_op jit(solution)/shard_map/ppermute | solution.py:352
  3.7 1.2 %copy-done = bf16[1,256,2048]{2,1,0:T(8,128)(2,1)S(1)} copy-done((bf16[1,256,2048]{2,1,0:T(8,128)(2,1)S(1)}, bf16[1,256,2048]{2,1,0:T(8,128)(2,1)}, u32[]{:S(2)}) %copy-start) | copy-done | bytes 1048600
  4.9 0.9 %copy-done.2 = bf16[1,256,512]{2,1,0:T(8,128)(2,1)S(1)} copy-done((bf16[1,256,512]{2,1,0:T(8,128)(2,1)S(1)}, bf16[1,256,512]{2,1,0:T(8,128)(2,1)}, u32[]{:S(2)}) %copy-start.2) | copy-done | bytes 262168
  6.2 2.1 %collective-permute-start.8 = (bf16[128,512]{1,0:T(8,128)(2,1)S(1)}, bf16[128,512]{1,0:T(8,128)(2,1)S(1)}, u32[]{:S(2)}, u32[]{:S(2)}) collective-permute-start(bf16[128,512]{1,0:T(8,128)(2,1)S(1)} %get-tuple-element.42.refs_2_), channel_id=1, source_target_pairs={{0,2},{2,4},{4,6},{6,7},{7,5},{5,3},{3,1},{1,0},{8,10},{10,12},{12... | collective-permute-start | bytes 393224 | tf_op jit(solution)/shard_map/ppermute | solution.py:354
  9.2 1.8 %collective-permute-start.12 = (bf16[1,256,256]{2,1,0:T(8,128)(2,1)S(1)}, bf16[1,256,256]{2,1,0:T(8,128)(2,1)S(1)}, u32[]{:S(2)}, u32[]{:S(2)}) collective-permute-start(bf16[1,256,256]{2,1,0:T(8,128)(2,1)S(1)} %partner_columns.2), channel_id=1, source_target_pairs={{0,16},{8,24},{16,0},{24,8},{1,17},{9,25},{17,1},{25,9},{2,18},{10... | collective-permute-start | bytes 393224 | tf_op jit(solution)/shard_map/ppermute | solution.py:106
  11.1 2.1 %collective-permute-start.1 = (bf16[128,512]{1,0:T(8,128)(2,1)S(1)}, bf16[128,512]{1,0:T(8,128)(2,1)S(1)}, u32[]{:S(2)}, u32[]{:S(2)}) collective-permute-start(bf16[128,512]{1,0:T(8,128)(2,1)S(1)} %get-tuple-element.65), channel_id=1, source_target_pairs={{0,2},{2,4},{4,6},{6,7},{7,5},{5,3},{3,1},{1,0},{8,10},{10,12},{12... | collective-permute-start | bytes 393224 | tf_op jit(solution)/shard_map/ppermute | solution.py:415
  13.3 1.4 %products.3 = (f32[256,512]{1,0:T(8,128)S(1)}, bf16[256,2048]{1,0:T(8,128)(2,1)}, f32[8,128]{1,0:T(8,128)S(1)}) custom-call(bf16[256,2048]{1,0:T(8,128)(2,1)S(1)} %bitcast.8, bf16[256,512]{1,0:T(8,128)(2,1)S(1)} %bitcast.14, bf16[256,512]{1,0:T(8,128)(2,1)S(1)} %bitcast.21, bf16[256,512]{1,0:T(8,128)(2,1)S(1)} %collective-permute-done.refs_1_, ...), custom_call_target="tpu_custom_call" | custom-call | flops 402653184 | bytes 8388608 | tf_op jit(solution)/shard_map/products/pallas_call | solution.py:238
  15.4 1.6 %collective-permute-start.10 = (bf16[256,512]{1,0:T(8,128)(2,1)S(1)}, bf16[256,512]{1,0:T(8,128)(2,1)S(1)}, u32[]{:S(2)}, u32[]{:S(2)}) collective-permute-start(bf16[256,512]{1,0:T(8,128)(2,1)S(1)} %get-tuple-element.52.refs_2_), channel_id=1, source_target_pairs={{0,2},{2,4},{4,6},{6,7},{7,5},{5,3},{3,1},{1,0},{8,10},{10,12},{12... | collective-permute-start | bytes 786440 | tf_op jit(solution)/shard_map/ppermute | solution.py:416
  17.7 1.6 %collective-permute-start.2 = (bf16[256,512]{1,0:T(8,128)(2,1)S(1)}, bf16[256,512]{1,0:T(8,128)(2,1)S(1)}, u32[]{:S(2)}, u32[]{:S(2)}) collective-permute-start(bf16[256,512]{1,0:T(8,128)(2,1)S(1)} %pad_maximum_fusion), channel_id=1, source_target_pairs={{0,2},{2,4},{4,6},{6,7},{7,5},{5,3},{3,1},{1,0},{8,10},{10,12},{12... | collective-permute-start | bytes 786440 | tf_op jit(solution)/shard_map/ppermute | solution.py:415
  19.8 1.0 %products.4 = (f32[256,512]{1,0:T(8,128)S(1)}, bf16[256,2048]{1,0:T(8,128)(2,1)}, f32[8,128]{1,0:T(8,128)S(1)}) custom-call(bf16[256,2048]{1,0:T(8,128)(2,1)S(1)} %bitcast.9, bf16[256,512]{1,0:T(8,128)(2,1)S(1)} %bitcast.15, bf16[128,512]{1,0:T(8,128)(2,1)S(1)} %collective-permute-done.1.refs_0_, ...), custom_call_target="tpu_custom_call", output_to_operand_aliasing={{1}: (5, {})} | custom-call | flops 134217728 | bytes 8388608 | tf_op jit(solution)/shard_map/products/pallas_call | solution.py:238
  20.8 1.1 %outer_update.1 = (bf16[256,128]{1,0:T(8,128)(2,1)S(1)}, f32[256,128]{1,0:T(8,128)}) custom-call(bf16[256,512]{1,0:T(8,128)(2,1)S(1)} %bitcast.23, bf16[1,256,256]{2,1,0:T(8,128)(2,1)S(1)} %collective-permute-done.12.refs_1_, bf16[2,256,128]{2,1,0:T(8,128)(2,1)S(1)} %collective-permute-done.13.refs_2_, bf16[256,512]{1,0:T(8,128)(2,1)S(1)} %copy-done.5, ...), custom_call_target="tpu_custom_call" | custom-call | bytes 917504 | tf_op jit(solution)/shard_map/outer_update/pallas_call | solution.py:48
  21.9 0.9 %collective-permute-done.10.refs_2_ = bf16[256,512]{1,0:T(8,128)(2,1)S(1)} collective-permute-done((bf16[256,512]{1,0:T(8,128)(2,1)S(1)}, bf16[256,512]{1,0:T(8,128)(2,1)S(1)}, u32[]{:S(2)}, u32[]{:S(2)}) %collective-permute-start.10) | collective-permute-done | bytes 262176 | tf_op jit(solution)/shard_map/ppermute | solution.py:416
  22.9 2.6 %collective-permute-done.11.refs_3_ = bf16[256,512]{1,0:T(8,128)(2,1)S(1)} collective-permute-done((bf16[256,512]{1,0:T(8,128)(2,1)S(1)}, bf16[256,512]{1,0:T(8,128)(2,1)S(1)}, u32[]{:S(2)}, u32[]{:S(2)}) %collective-permute-start.11) | collective-permute-done | bytes 262176 | tf_op jit(solution)/shard_map/ppermute | solution.py:416
  25.6 1.6 %collective-permute-start.14 = (bf16[256,512]{1,0:T(8,128)(2,1)S(1)}, bf16[256,512]{1,0:T(8,128)(2,1)S(1)}, u32[]{:S(2)}, u32[]{:S(2)}) collective-permute-start(bf16[256,512]{1,0:T(8,128)(2,1)S(1)} %get-tuple-element.56), channel_id=1, source_target_pairs={{0,2},{2,4},{4,6},{6,7},{7,5},{5,3},{3,1},{1,0},{8,10},{10,12},{12... | collective-permute-start | bytes 786440 | tf_op jit(solution)/shard_map/ppermute | solution.py:416
  27.7 1.4 %collective-permute-start.16 = (bf16[256,128]{1,0:T(8,128)(2,1)S(1)}, bf16[256,128]{1,0:T(8,128)(2,1)S(1)}, u32[]{:S(2)}, u32[]{:S(2)}) collective-permute-start(bf16[256,128]{1,0:T(8,128)(2,1)S(1)} %get-tuple-element.55.refs_5_), channel_id=1, source_target_pairs={{0,16},{8,24},{16,0},{24,8},{1,17},{9,25},{17,1},{25,9},{2,18},{10... | collective-permute-start | bytes 196616 | tf_op jit(solution)/shard_map/ppermute | solution.py:106
  29.0 2.9 %collective-permute-done.16 = bf16[256,128]{1,0:T(8,128)(2,1)S(1)} collective-permute-done((bf16[256,128]{1,0:T(8,128)(2,1)S(1)}, bf16[256,128]{1,0:T(8,128)(2,1)S(1)}, u32[]{:S(2)}, u32[]{:S(2)}) %collective-permute-start.16) | collective-permute-done | bytes 65568 | tf_op jit(solution)/shard_map/ppermute | solution.py:106
  32.0 1.6 %collective-permute-start.3 = (bf16[256,512]{1,0:T(8,128)(2,1)S(1)}, bf16[256,512]{1,0:T(8,128)(2,1)S(1)}, u32[]{:S(2)}, u32[]{:S(2)}) collective-permute-start(bf16[256,512]{1,0:T(8,128)(2,1)S(1)} %collective-permute-done.2.refs_0_), channel_id=1, source_target_pairs={{0,2},{2,4},{4,6},{6,7},{7,5},{5,3},{3,1},{1,0},{8,10},{10,12},{12... | collective-permute-start | bytes 786440 | tf_op jit(solution)/shard_map/ppermute | solution.py:415
  34.0 1.1 %products.5 = (f32[256,512]{1,0:T(8,128)S(1)}, bf16[256,2048]{1,0:T(8,128)(2,1)}, f32[8,128]{1,0:T(8,128)S(1)}) custom-call(bf16[256,2048]{1,0:T(8,128)(2,1)S(1)} %bitcast.10, bf16[256,512]{1,0:T(8,128)(2,1)S(1)} %bitcast.16, bf16[256,512]{1,0:T(8,128)(2,1)S(1)} %collective-permute-done.2.refs_0_, ...), custom_call_target="tpu_custom_call", output_to_operand_aliasing={{1}: (5, {})} | custom-call | flops 268435456 | bytes 8388608 | tf_op jit(solution)/shard_map/products/pallas_call | solution.py:238
  35.2 1.5 %collective-permute-done.15.refs_3_ = bf16[256,512]{1,0:T(8,128)(2,1)S(1)} collective-permute-done((bf16[256,512]{1,0:T(8,128)(2,1)S(1)}, bf16[256,512]{1,0:T(8,128)(2,1)S(1)}, u32[]{:S(2)}, u32[]{:S(2)}) %collective-permute-start.15) | collective-permute-done | bytes 262176 | tf_op jit(solution)/shard_map/ppermute | solution.py:416
  36.8 1.6 %collective-permute-start.17 = (bf16[256,512]{1,0:T(8,128)(2,1)S(1)}, bf16[256,512]{1,0:T(8,128)(2,1)S(1)}, u32[]{:S(2)}, u32[]{:S(2)}) collective-permute-start(bf16[256,512]{1,0:T(8,128)(2,1)S(1)} %get-tuple-element.59), channel_id=1, source_target_pairs={{0,2},{2,4},{4,6},{6,7},{7,5},{5,3},{3,1},{1,0},{8,10},{10,12},{12... | collective-permute-start | bytes 786440 | tf_op jit(solution)/shard_map/ppermute | solution.py:416
  38.9 2.2 %collective-permute-done.3.refs_0_ = bf16[256,512]{1,0:T(8,128)(2,1)S(1)} collective-permute-done((bf16[256,512]{1,0:T(8,128)(2,1)S(1)}, bf16[256,512]{1,0:T(8,128)(2,1)S(1)}, u32[]{:S(2)}, u32[]{:S(2)}) %collective-permute-start.3) | collective-permute-done | bytes 262176 | tf_op jit(solution)/shard_map/ppermute | solution.py:415
  41.1 1.7 %collective-permute-done.7.refs_1_ = bf16[256,512]{1,0:T(8,128)(2,1)S(1)} collective-permute-done((bf16[256,512]{1,0:T(8,128)(2,1)S(1)}, bf16[256,512]{1,0:T(8,128)(2,1)S(1)}, u32[]{:S(2)}, u32[]{:S(2)}) %collective-permute-start.7) | collective-permute-done | bytes 262176 | tf_op jit(solution)/shard_map/ppermute | solution.py:415
  42.8 1.8 %last_products.1 = (bf16[256,512]{1,0:T(8,128)(2,1)}, bf16[256,2048]{1,0:T(8,128)(2,1)}, f32[8,128]{1,0:T(8,128)S(1)}) custom-call(bf16[256,2048]{1,0:T(8,128)(2,1)S(1)} %bitcast.11, bf16[256,512]{1,0:T(8,128)(2,1)S(1)} %bitcast.17, bf16[256,512]{1,0:T(8,128)(2,1)S(1)} %collective-permute-done.3.refs_0_, ...), custom_call_target="tpu_custom_call", output_to_operand_aliasing={{1}: (5, {})} | custom-call | flops 268435456 | bytes 33554432 | tf_op jit(solution)/shard_map/last_products/pallas_call | solution.py:238
  45.4 0.9 %collective-permute-done.18.refs_2_ = bf16[256,512]{1,0:T(8,128)(2,1)S(1)} collective-permute-done((bf16[256,512]{1,0:T(8,128)(2,1)S(1)}, bf16[256,512]{1,0:T(8,128)(2,1)S(1)}, u32[]{:S(2)}, u32[]{:S(2)}) %collective-permute-start.18) | collective-permute-done | bytes 262176 | tf_op jit(solution)/shard_map/ppermute | solution.py:416
  (50 shorter events, 6.3 us)
Async XLA Ops:
  0.6 10.4 %collective-permute-start = (bf16[256,512]{1,0:T(8,128)(2,1)}, bf16[256,512]{1,0:T(8,128)(2,1)S(1)}, u32[]{:S(2)}, u32[]{:S(2)}) collective-permute-start(bf16[256,512]{1,0:T(8,128)(2,1)} %bitcast.18), channel_id=1, source_target_pairs={{0,2},{2,4},{4,6},{6,7},{7,5},{5,3},{3,1},{1,0},{8,10},{10,12},{12... | collective-permute-start | bytes 786440 | tf_op jit(solution)/shard_map/ppermute | solution.py:352
  3.7 9.5 %collective-permute-start.4 = (bf16[256,512]{1,0:T(8,128)(2,1)}, bf16[256,512]{1,0:T(8,128)(2,1)S(1)}, u32[]{:S(2)}, u32[]{:S(2)}) collective-permute-start(bf16[256,512]{1,0:T(8,128)(2,1)} %bitcast.19), channel_id=1, source_target_pairs={{2,0},{4,2},{6,4},{7,6},{5,7},{3,5},{1,3},{0,1},{10,8},{12,10},{14... | collective-permute-start | bytes 786440 | tf_op jit(solution)/shard_map/ppermute | solution.py:352
  3.7 1.2 %copy-start = (bf16[1,256,2048]{2,1,0:T(8,128)(2,1)S(1)}, bf16[1,256,2048]{2,1,0:T(8,128)(2,1)}, u32[]{:S(2)}) copy-start(bf16[1,256,2048]{2,1,0:T(8,128)(2,1)} %param.8) | copy-start | bytes 3145732
  6.2 8.6 %collective-permute-start.8 = (bf16[128,512]{1,0:T(8,128)(2,1)S(1)}, bf16[128,512]{1,0:T(8,128)(2,1)S(1)}, u32[]{:S(2)}, u32[]{:S(2)}) collective-permute-start(bf16[128,512]{1,0:T(8,128)(2,1)S(1)} %get-tuple-element.42.refs_2_), channel_id=1, source_target_pairs={{0,2},{2,4},{4,6},{6,7},{7,5},{5,3},{3,1},{1,0},{8,10},{10,12},{12... | collective-permute-start | bytes 393224 | tf_op jit(solution)/shard_map/ppermute | solution.py:354
  8.2 7.1 %collective-permute-start.9 = (bf16[128,512]{1,0:T(8,128)(2,1)S(1)}, bf16[128,512]{1,0:T(8,128)(2,1)S(1)}, u32[]{:S(2)}, u32[]{:S(2)}) collective-permute-start(bf16[128,512]{1,0:T(8,128)(2,1)S(1)} %get-tuple-element.43.refs_3_), channel_id=1, source_target_pairs={{2,0},{4,2},{6,4},{7,6},{5,7},{3,5},{1,3},{0,1},{10,8},{12,10},{14... | collective-permute-start | bytes 393224 | tf_op jit(solution)/shard_map/ppermute | solution.py:354
  8.9 4.3 %copy-start.1 = (bf16[1,256,2048]{2,1,0:T(8,128)(2,1)S(1)}, bf16[1,256,2048]{2,1,0:T(8,128)(2,1)}, u32[]{:S(2)}) copy-start(bf16[1,256,2048]{2,1,0:T(8,128)(2,1)} %param.8) | copy-start | bytes 3145732
  9.2 8.3 %collective-permute-start.12 = (bf16[1,256,256]{2,1,0:T(8,128)(2,1)S(1)}, bf16[1,256,256]{2,1,0:T(8,128)(2,1)S(1)}, u32[]{:S(2)}, u32[]{:S(2)}) collective-permute-start(bf16[1,256,256]{2,1,0:T(8,128)(2,1)S(1)} %partner_columns.2), channel_id=1, source_target_pairs={{0,16},{8,24},{16,0},{24,8},{1,17},{9,25},{17,1},{25,9},{2,18},{10... | collective-permute-start | bytes 393224 | tf_op jit(solution)/shard_map/ppermute | solution.py:106
  11.1 2.2 %copy-start.3 = (bf16[1,256,512]{2,1,0:T(8,128)(2,1)S(1)}, bf16[1,256,512]{2,1,0:T(8,128)(2,1)}, u32[]{:S(2)}) copy-start(bf16[1,256,512]{2,1,0:T(8,128)(2,1)} %param.9) | copy-start | bytes 786436
  11.1 6.5 %collective-permute-start.1 = (bf16[128,512]{1,0:T(8,128)(2,1)S(1)}, bf16[128,512]{1,0:T(8,128)(2,1)S(1)}, u32[]{:S(2)}, u32[]{:S(2)}) collective-permute-start(bf16[128,512]{1,0:T(8,128)(2,1)S(1)} %get-tuple-element.65), channel_id=1, source_target_pairs={{0,2},{2,4},{4,6},{6,7},{7,5},{5,3},{3,1},{1,0},{8,10},{10,12},{12... | collective-permute-start | bytes 393224 | tf_op jit(solution)/shard_map/ppermute | solution.py:415
  13.2 6.1 %collective-permute-start.5 = (bf16[128,512]{1,0:T(8,128)(2,1)S(1)}, bf16[128,512]{1,0:T(8,128)(2,1)S(1)}, u32[]{:S(2)}, u32[]{:S(2)}) collective-permute-start(bf16[128,512]{1,0:T(8,128)(2,1)S(1)} %get-tuple-element.64), channel_id=1, source_target_pairs={{2,0},{4,2},{6,4},{7,6},{5,7},{3,5},{1,3},{0,1},{10,8},{12,10},{14... | collective-permute-start | bytes 393224 | tf_op jit(solution)/shard_map/ppermute | solution.py:415
  15.4 7.4 %collective-permute-start.10 = (bf16[256,512]{1,0:T(8,128)(2,1)S(1)}, bf16[256,512]{1,0:T(8,128)(2,1)S(1)}, u32[]{:S(2)}, u32[]{:S(2)}) collective-permute-start(bf16[256,512]{1,0:T(8,128)(2,1)S(1)} %get-tuple-element.52.refs_2_), channel_id=1, source_target_pairs={{0,2},{2,4},{4,6},{6,7},{7,5},{5,3},{3,1},{1,0},{8,10},{10,12},{12... | collective-permute-start | bytes 786440 | tf_op jit(solution)/shard_map/ppermute | solution.py:416
  17.1 8.4 %collective-permute-start.11 = (bf16[256,512]{1,0:T(8,128)(2,1)S(1)}, bf16[256,512]{1,0:T(8,128)(2,1)S(1)}, u32[]{:S(2)}, u32[]{:S(2)}) collective-permute-start(bf16[256,512]{1,0:T(8,128)(2,1)S(1)} %get-tuple-element.53.refs_3_), channel_id=1, source_target_pairs={{2,0},{4,2},{6,4},{7,6},{5,7},{3,5},{1,3},{0,1},{10,8},{12,10},{14... | collective-permute-start | bytes 786440 | tf_op jit(solution)/shard_map/ppermute | solution.py:416
  17.5 3.3 %collective-permute-start.13 = (bf16[2,256,128]{2,1,0:T(8,128)(2,1)S(1)}, bf16[2,256,128]{2,1,0:T(8,128)(2,1)S(1)}, u32[]{:S(2)}, u32[]{:S(2)}) collective-permute-start(bf16[2,256,128]{2,1,0:T(8,128)(2,1)S(1)} %partner_columns.3), channel_id=1, source_target_pairs={{0,8},{8,0},{16,24},{24,16},{1,9},{9,1},{17,25},{25,17},{2,10},{10... | collective-permute-start | bytes 393224 | tf_op jit(solution)/shard_map/ppermute | solution.py:106
  17.7 14.3 %collective-permute-start.2 = (bf16[256,512]{1,0:T(8,128)(2,1)S(1)}, bf16[256,512]{1,0:T(8,128)(2,1)S(1)}, u32[]{:S(2)}, u32[]{:S(2)}) collective-permute-start(bf16[256,512]{1,0:T(8,128)(2,1)S(1)} %pad_maximum_fusion), channel_id=1, source_target_pairs={{0,2},{2,4},{4,6},{6,7},{7,5},{5,3},{3,1},{1,0},{8,10},{10,12},{12... | collective-permute-start | bytes 786440 | tf_op jit(solution)/shard_map/ppermute | solution.py:415
  19.3 14.2 %collective-permute-start.6 = (bf16[256,512]{1,0:T(8,128)(2,1)S(1)}, bf16[256,512]{1,0:T(8,128)(2,1)S(1)}, u32[]{:S(2)}, u32[]{:S(2)}) collective-permute-start(bf16[256,512]{1,0:T(8,128)(2,1)S(1)} %pad_maximum_fusion.1), channel_id=1, source_target_pairs={{2,0},{4,2},{6,4},{7,6},{5,7},{3,5},{1,3},{0,1},{10,8},{12,10},{14... | collective-permute-start | bytes 786440 | tf_op jit(solution)/shard_map/ppermute | solution.py:415
  19.8 1.0 %copy-start.6 = (f32[256,128]{1,0:T(8,128)S(1)}, f32[256,128]{1,0:T(8,128)}, u32[]{:S(2)}) copy-start(f32[256,128]{1,0:T(8,128)} %refs_4_.1) | copy-start | bytes 393220
  25.6 9.6 %collective-permute-start.14 = (bf16[256,512]{1,0:T(8,128)(2,1)S(1)}, bf16[256,512]{1,0:T(8,128)(2,1)S(1)}, u32[]{:S(2)}, u32[]{:S(2)}) collective-permute-start(bf16[256,512]{1,0:T(8,128)(2,1)S(1)} %get-tuple-element.56), channel_id=1, source_target_pairs={{0,2},{2,4},{4,6},{6,7},{7,5},{5,3},{3,1},{1,0},{8,10},{10,12},{12... | collective-permute-start | bytes 786440 | tf_op jit(solution)/shard_map/ppermute | solution.py:416
  27.2 9.5 %collective-permute-start.15 = (bf16[256,512]{1,0:T(8,128)(2,1)S(1)}, bf16[256,512]{1,0:T(8,128)(2,1)S(1)}, u32[]{:S(2)}, u32[]{:S(2)}) collective-permute-start(bf16[256,512]{1,0:T(8,128)(2,1)S(1)} %get-tuple-element.57), channel_id=1, source_target_pairs={{2,0},{4,2},{6,4},{7,6},{5,7},{3,5},{1,3},{0,1},{10,8},{12,10},{14... | collective-permute-start | bytes 786440 | tf_op jit(solution)/shard_map/ppermute | solution.py:416
  27.7 4.3 %collective-permute-start.16 = (bf16[256,128]{1,0:T(8,128)(2,1)S(1)}, bf16[256,128]{1,0:T(8,128)(2,1)S(1)}, u32[]{:S(2)}, u32[]{:S(2)}) collective-permute-start(bf16[256,128]{1,0:T(8,128)(2,1)S(1)} %get-tuple-element.55.refs_5_), channel_id=1, source_target_pairs={{0,16},{8,24},{16,0},{24,8},{1,17},{9,25},{17,1},{25,9},{2,18},{10... | collective-permute-start | bytes 196616 | tf_op jit(solution)/shard_map/ppermute | solution.py:106
  32.0 9.2 %collective-permute-start.3 = (bf16[256,512]{1,0:T(8,128)(2,1)S(1)}, bf16[256,512]{1,0:T(8,128)(2,1)S(1)}, u32[]{:S(2)}, u32[]{:S(2)}) collective-permute-start(bf16[256,512]{1,0:T(8,128)(2,1)S(1)} %collective-permute-done.2.refs_0_), channel_id=1, source_target_pairs={{0,2},{2,4},{4,6},{6,7},{7,5},{5,3},{3,1},{1,0},{8,10},{10,12},{12... | collective-permute-start | bytes 786440 | tf_op jit(solution)/shard_map/ppermute | solution.py:415
  33.6 9.2 %collective-permute-start.7 = (bf16[256,512]{1,0:T(8,128)(2,1)S(1)}, bf16[256,512]{1,0:T(8,128)(2,1)S(1)}, u32[]{:S(2)}, u32[]{:S(2)}) collective-permute-start(bf16[256,512]{1,0:T(8,128)(2,1)S(1)} %collective-permute-done.6.refs_1_), channel_id=1, source_target_pairs={{2,0},{4,2},{6,4},{7,6},{5,7},{3,5},{1,3},{0,1},{10,8},{12,10},{14... | collective-permute-start | bytes 786440 | tf_op jit(solution)/shard_map/ppermute | solution.py:415
  36.8 8.6 %collective-permute-start.17 = (bf16[256,512]{1,0:T(8,128)(2,1)S(1)}, bf16[256,512]{1,0:T(8,128)(2,1)S(1)}, u32[]{:S(2)}, u32[]{:S(2)}) collective-permute-start(bf16[256,512]{1,0:T(8,128)(2,1)S(1)} %get-tuple-element.59), channel_id=1, source_target_pairs={{0,2},{2,4},{4,6},{6,7},{7,5},{5,3},{3,1},{1,0},{8,10},{10,12},{12... | collective-permute-start | bytes 786440 | tf_op jit(solution)/shard_map/ppermute | solution.py:416
  38.4 7.9 %collective-permute-start.18 = (bf16[256,512]{1,0:T(8,128)(2,1)S(1)}, bf16[256,512]{1,0:T(8,128)(2,1)S(1)}, u32[]{:S(2)}, u32[]{:S(2)}) collective-permute-start(bf16[256,512]{1,0:T(8,128)(2,1)S(1)} %get-tuple-element.60), channel_id=1, source_target_pairs={{2,0},{4,2},{6,4},{7,6},{5,7},{3,5},{1,3},{0,1},{10,8},{12,10},{14... | collective-permute-start | bytes 786440 | tf_op jit(solution)/shard_map/ppermute | solution.py:416
  38.9 5.7 %collective-permute-start.19 = (bf16[256,256]{1,0:T(8,128)(2,1)S(1)}, bf16[256,256]{1,0:T(8,128)(2,1)S(1)}, u32[]{:S(2)}, u32[]{:S(2)}) collective-permute-start(bf16[256,256]{1,0:T(8,128)(2,1)S(1)} %constant_dynamic-update-slice_fusion.refs_5_.refs_0_), channel_id=1, source_target_pairs={{0,8},{8,0},{16,24},{24,16},{1,9},{9,1},{17,25},{25,17},{2,10},{10... | collective-permute-start | bytes 393224 | tf_op jit(solution)/shard_map/ppermute | solution.py:106
  (3 other events, 2.9 us)

commit v5 on v4

v5 whole, which is shorter than its diff:
```python
import functools

import jax
import jax.numpy as jnp
from jax import lax
from jax.experimental import pallas as pl
from jax.experimental.pallas import tpu as pltpu
from jax.sharding import PartitionSpec as P

BLOCK = 64

outer_rate = 0.7
outer_momentum = 0.9
scale_epsilon = 1e-06

F32 = jnp.float32
BF16 = jnp.bfloat16
LANES = 128
VMEM_BYTES = 8 * 2**20
PRODUCTS_BYTES = 8 * 2**20


def ring_order(size):
    return list(range(0, size, 2)) + list(range(1, size, 2))[::-1]


def ring_place(index, size):
    return jnp.where((index & 1) == 0, index >> 1, size - 1 - (index >> 1))


def ring_index(place, size):
    place = lax.rem(place + size, size)
    evens = (size + 1) // 2
    return jnp.where(place < evens, 2 * place, 2 * (size - 1 - place) + 1)


def block_start(offset, size, depth):
    start = ring_index(ring_place(lax.axis_index("fsdp"), size) + offset, size) * depth
    return pl.multiple_of(start, depth)


def vmem_call(kernel, out_shape, operands, flops, name, after=(), moved=None):
    def body(*refs):
        kernel(*refs[: len(operands)], *refs[len(operands) + len(after) :])

    moved = moved or sum(x.size * x.dtype.itemsize for x in operands)
    whole = pl.BlockSpec(memory_space=pltpu.VMEM)
    return pl.pallas_call(
        body,
        out_shape=out_shape,
        in_specs=[whole] * len(operands) + [pl.BlockSpec(memory_space=pl.ANY)] * len(after),
        out_specs=jax.tree.map(lambda _: whole, out_shape),
        compiler_params=pltpu.CompilerParams(vmem_limit_bytes=VMEM_BYTES),
        cost_estimate=pl.CostEstimate(flops=flops, bytes_accessed=moved, transcendentals=0),
        name=name,
    )(*operands, *after)


def shape_of(rows, columns, dtype):
    return jax.ShapeDtypeStruct((rows, columns), dtype)


def column_window(array, start, width):
    if isinstance(array, jax.Array):
        return lax.dynamic_slice_in_dim(array, start, width, array.ndim - 1)
    return array[..., pl.ds(pl.multiple_of(start, width), width)]


def outer_kernel(replicas, share_cols, *refs):
    *held_refs, global_ref, momentum_ref, share_ref, new_momentum_ref = refs
    rows, window = held_refs[-1].shape[-2:]
    me = lax.axis_index("replica")

    def windows_of(ref):
        here = me * share_cols // window * window % ref.shape[-1]
        return ref[...] if ref.shape[-1] == window else column_window(ref, here, window)

    old = windows_of(global_ref).astype(F32)
    lane = lax.broadcasted_iota(jnp.int32, (rows, window), 1) // BLOCK
    total = jnp.zeros((rows, window), F32)
    for held_ref in held_refs:
        held = windows_of(held_ref).astype(F32)
        for local in [held] if held.ndim == 2 else list(held):
            drift = old - local
            size = jnp.abs(drift)
            scale = jnp.zeros((rows, window), F32)
            for block in range(window // BLOCK):
                top = jnp.max(jnp.where(lane == block, size, 0.0), axis=1, keepdims=True)
                top = (top + scale_epsilon).astype(BF16).astype(F32)
                scale = jnp.where(lane == block, top, scale)
            total = total + (drift / scale).astype(BF16).astype(F32) * scale
    mean_grad = total / replicas
    shares = window // share_cols
    mean_here, old_here = mean_grad[:, :share_cols], old[:, :share_cols]
    mine = me % shares
    for share in range(1, shares):
        columns = slice(share * share_cols, (share + 1) * share_cols)
        mean_here = jnp.where(mine == share, mean_grad[:, columns], mean_here)
        old_here = jnp.where(mine == share, old[:, columns], old_here)
    new_momentum = outer_momentum * momentum_ref[...] + mean_here
    new_momentum_ref[...] = new_momentum
    share_ref[...] = (old_here - outer_rate * (mean_here + outer_momentum * new_momentum)).astype(BF16)


def swap(array, bits):
    return lax.ppermute(array, "replica", [(at, at ^ bits) for at in range(lax.axis_size("replica"))])


def partner_kernel(bits, share_cols, width, *refs):
    *held_refs, out_ref = refs
    start = (lax.axis_index("replica") ^ bits) * share_cols // width * width
    at = 0
    for held_ref in held_refs:
        part = column_window(held_ref, start % held_ref.shape[-1], width)
        count = 1 if part.ndim == 2 else part.shape[0]
        out_ref[at : at + count] = part.reshape((count,) + part.shape[-2:])
        at += count


def send_windows(held, bits, kv_width, after):
    replicas = lax.axis_size("replica")
    share_cols = kv_width // replicas
    width = max(bits * share_cols, BLOCK)
    rows = held[0].shape[-2]
    count = sum(1 if array.ndim == 2 else array.shape[0] for array in held)
    if width % LANES == 0:
        leaving = vmem_call(
            functools.partial(partner_kernel, bits, share_cols, width),
            jax.ShapeDtypeStruct((count, rows, width), BF16),
            held,
            0,
            "partner_columns",
            after,
        )
    else:
        start = (lax.axis_index("replica") ^ bits) * share_cols // width * width
        parts = [column_window(array, start % array.shape[-1], width).reshape(-1, rows, width) for array in held]
        leaving = jnp.concatenate(parts)
    return held + [swap(leaving, bits)]


def update_share(held, global_weights, momentum, after):
    rows, share_cols = momentum.shape
    replicas = lax.axis_size("replica")
    window = held[-1].shape[-1]
    if window % LANES:
        start = lax.axis_index("replica") * share_cols // window * window
        held = [column_window(array, start % array.shape[-1], window) for array in held]
        global_weights = column_window(global_weights, start, window)
    return vmem_call(
        functools.partial(outer_kernel, replicas, share_cols),
        (shape_of(rows, share_cols, BF16), shape_of(rows, share_cols, F32)),
        held + [global_weights, momentum],
        0,
        "outer_update",
        after,
    )


def join_kernel(places, *refs):
    *held_refs, out_ref = refs
    width = out_ref.shape[1] // len(places)
    me = lax.axis_index("replica")
    at = 0
    for held_ref in held_refs:
        for start in range(0, held_ref.shape[1], width):
            columns = pl.ds(pl.multiple_of((me ^ places[at]) * width, width), width)
            out_ref[:, columns] = held_ref[:, start : start + width]
            at += 1


def join_shares(held, places, kv_width, after):
    rows = held[0].shape[0]
    width = kv_width // len(places)
    if width % LANES == 0:
        return vmem_call(
            functools.partial(join_kernel, places), shape_of(rows, kv_width, BF16), held, 0, "join_shares", after
        )
    whole = jnp.concatenate(held, axis=1)
    joined = jnp.zeros_like(whole)
    for at, place in enumerate(places):
        start = (lax.axis_index("replica") ^ place) * width
        joined = lax.dynamic_update_slice_in_dim(joined, whole[:, at * width : (at + 1) * width], start, 1)
    return joined


def products_kernel(size, places, first, inputs_ref, cotangent_ref, *refs):
    block_refs, refs = refs[: len(places)], refs[len(places) :]
    total_ref = None if first else refs[0]
    rows_ref, grad_ref, mark_ref, held, sems = refs[-5:]
    depth = inputs_ref.shape[1] // size
    copies = []
    for number, (place, block_ref) in enumerate(zip(places, block_refs)):
        held[number] = lax.dot_general(
            cotangent_ref[...], block_ref[...], (((1,), (1,)), ((), ())), preferred_element_type=F32
        ).astype(BF16)
        columns = pl.ds(block_start(place, size, depth), depth)
        copies.append(pltpu.make_async_copy(held.at[number], grad_ref.at[:, columns], sems.at[number]))
        copies[-1].start()
    total = jnp.zeros(rows_ref.shape, F32) if first else total_ref[...]
    for place, block_ref in zip(places, block_refs):
        columns = inputs_ref[:, pl.ds(block_start(place, size, depth), depth)]
        total = total + jnp.dot(columns, block_ref[...], preferred_element_type=F32)
    rows_ref[...] = total.astype(rows_ref.dtype)
    mark_ref[...] = jnp.zeros_like(mark_ref)
    for copy in copies:
        copy.wait()


def products(inputs_here, cotangent, blocks, before, size, last=False, after=()):
    tokens, width = inputs_here.shape
    kv_width = cotangent.shape[1]
    depth = width // size
    first = before is None
    operands = [inputs_here, cotangent] + list(blocks.values()) + ([] if first else list(before[:2]))
    whole, anywhere = pl.BlockSpec(memory_space=pltpu.VMEM), pl.BlockSpec(memory_space=pl.ANY)
    return pl.pallas_call(
        functools.partial(products_kernel, size, list(blocks), first),
        out_shape=(
            shape_of(tokens, kv_width, BF16 if last else F32),
            shape_of(tokens, width, BF16),
            shape_of(8, LANES, F32),
        ),
        in_specs=[whole] * (2 + len(blocks)) + ([] if first else [whole, anywhere]) + [anywhere] * len(after),
        out_specs=(whole, anywhere, whole),
        scratch_shapes=[
            pltpu.VMEM((len(blocks), tokens, depth), BF16),
            pltpu.SemaphoreType.DMA((len(blocks),)),
        ],
        input_output_aliases={} if first else {len(operands) - 1: 1},
        compiler_params=pltpu.CompilerParams(vmem_limit_bytes=VMEM_BYTES),
        cost_estimate=pl.CostEstimate(
            flops=4 * tokens * depth * len(blocks) * kv_width,
            bytes_accessed=PRODUCTS_BYTES * (4 if last else 1),
            transcendentals=0,
        ),
        name="last_products" if last else "products",
    )(*operands, *after)


def all_products(inputs_here, cotangent, blocks, size):
    width = inputs_here.shape[1]
    depth = width // size
    here = ring_place(lax.axis_index("fsdp"), size)
    gathered = jnp.zeros((width, cotangent.shape[1]), BF16)
    for place, block in blocks.items():
        gathered = lax.dynamic_update_slice_in_dim(gathered, block, ring_index(here + place, size) * depth, 0)
    rows = jnp.dot(inputs_here, gathered, preferred_element_type=F32).astype(BF16)
    grad = lax.dot_general(cotangent, gathered, (((1,), (1,)), ((), ())), preferred_element_type=F32)
    return rows, grad.astype(BF16)


def own_terms(columns, cotangent, token_weight):
    return (
        lax.dot_general(columns, cotangent, (((0,), (0,)), ((), ())), preferred_element_type=F32) * token_weight
    )


def terms_kernel(size, places, token_weight, inputs_ref, cotangent_ref, *out_refs):
    depth = inputs_ref.shape[1] // size
    for place, out_ref in zip(places, out_refs):
        columns = inputs_ref[:, pl.ds(block_start(place, size, depth), depth)]
        out_ref[...] = own_terms(columns, cotangent_ref[...], token_weight).astype(out_ref.dtype)


def token_terms(inputs_here, cotangent, size, places, dtypes, token_weight):
    tokens, width = inputs_here.shape
    kv_width = cotangent.shape[1]
    depth = width // size
    if depth % LANES == 0:
        return vmem_call(
            functools.partial(terms_kernel, size, places, token_weight),
            [shape_of(depth, kv_width, dtype) for dtype in dtypes],
            [inputs_here, cotangent],
            2 * tokens * depth * len(places) * kv_width,
            "token_terms",
        )
    here = ring_place(lax.axis_index("fsdp"), size)
    out = []
    for place, dtype in zip(places, dtypes):
        columns = lax.dynamic_slice_in_dim(inputs_here, ring_index(here + place, size) * depth, depth, 1)
        out.append(own_terms(columns, cotangent, token_weight).astype(dtype))
    return out


def add_kernel(count, *refs):
    for one_ref, other_ref, out_ref in zip(refs[:count], refs[count : 2 * count], refs[2 * count :]):
        out_ref[...] = (one_ref[...] + other_ref[...].astype(F32)).astype(BF16)


def add_terms(terms, sums, after):
    rows, columns = terms[0].shape
    shapes = [shape_of(rows, columns, BF16)] * len(sums)
    return vmem_call(functools.partial(add_kernel, len(sums)), shapes, terms + sums, 0, "add_terms", after)


def end_kernel(terms_ref, up_ref, down_ref, out_ref):
    out_ref[...] = (terms_ref[...] + up_ref[...].astype(F32) + down_ref[...].astype(F32)).astype(BF16)


def per_device(local_weights, global_weights, momentum, activations, kv_cotangent):
    local_shard = local_weights[0]
    inputs_here = activations[0]
    cotangent = kv_cotangent[0]
    depth, kv_width = local_shard.shape
    size = lax.axis_size("fsdp")
    token_weight = 1.0 / (inputs_here.shape[0] * size)
    wide = depth % LANES == 0
    order = ring_order(size)
    far = size // 2

    def upward(array):
        return lax.ppermute(array, "fsdp", [(order[at - 1], order[at]) for at in range(size)])

    def downward(array):
        return lax.ppermute(array, "fsdp", [(order[at], order[at - 1]) for at in range(size)])

    from_below, from_above = upward(local_shard), downward(local_shard)
    places = [-far, far - 1] + [1 - far] + [sign * step for step in range(far - 2, 0, -1) for sign in (1, -1)] + [0]
    dtypes = [BF16] * 2 + [F32] * (len(places) - 2)
    terms = dict(zip(places, token_terms(inputs_here, cotangent, size, places, dtypes, token_weight)))
    sum_down, sum_up = downward(terms[-far]), upward(terms[far - 1])

    bits = lax.axis_size("replica") // 2
    held = send_windows([local_shard], bits, kv_width, (terms[0],))
    blocks = {0: local_shard}
    made = None
    for step in range(1, far):
        near = far - step
        latest = {-step: from_below, step: from_above}
        blocks.update(latest)
        after = (from_below, from_above)
        order_after = ()
        if step == min(3, far - 1):
            while bits > 1:
                bits //= 2
                shares = [jnp.concatenate(shares, axis=1)]
                shares.append(swap(shares[0], bits))
                joined += [place ^ bits for place in joined]
            order_after = (shares[0],)
        if wide:
            made = products(inputs_here, cotangent, blocks if step == 1 else latest, made, size, after=order_after)
            after = (made[2],)
        if step == min(2, far - 1):
            new_share, new_momentum = update_share(held, global_weights, momentum, after)
            bits = lax.axis_size("replica") // 2
            shares, joined = [new_share, swap(new_share, bits)], [0, bits]
            after += (new_share,)
        if near > 1:
            from_below, from_above = upward(from_below), downward(from_above)
            totals = add_terms([terms[near - 1], terms[-near]], [sum_up, sum_down], after)
            sum_up, sum_down = upward(totals[0]), downward(totals[1])
        else:
            from_below = upward(from_below)
            totals = add_terms([terms[-near]], [sum_down], after)
            sum_down = downward(totals[0])
        while step == 1 and bits > 1:
            bits //= 2
            held = send_windows(held, bits, kv_width, totals)
    latest = {-far: from_below}
    if wide:
        kv_rows, grad_in, mark = products(inputs_here, cotangent, latest, made, size, last=True)
        after = (mark,)
    else:
        kv_rows, grad_in = all_products(inputs_here, cotangent, {**blocks, **latest}, size)
        after = ()
    new_global = join_shares(shares, joined, kv_width, after)
    grad_rows = vmem_call(
        end_kernel, shape_of(depth, kv_width, BF16), [terms[0], sum_up, sum_down], 0, "end_terms", after
    )
    return kv_rows[None], grad_in[None], grad_rows[None], new_global, new_momentum


def solution(mesh):
    placed = (
        P("replica", "fsdp", None),
        P("fsdp", None),
        P("fsdp", "replica"),
        P("replica", "fsdp", None),
        P("replica", "fsdp", None),
    )
    return jax.shard_map(
        per_device,
        mesh=mesh,
        in_specs=placed,
        out_specs=(
            P("replica", "fsdp", None),
            P("replica", "fsdp", None),
            P("replica", "fsdp", None),
            P("fsdp", None),
            P("fsdp", "replica"),
        ),
        check_vma=False,
    )
```

time: 47.3 us -> 47.9 us (1.013)
  waiting for transfers between devices: 13.5 us -> 16.4 us
  starting transfers between devices: 21 us -> 19.6 us
    ppermute x16 -> x14, waiting for transfers between devices: 10.6 us -> 15.5 us  [the longest x7 8.69 us: upward(): lax.ppermute(array, 'fsdp', [(order[at - 1], order[at]) for at in range(s...]
    ppermute x16 -> x14, starting transfers between devices: 17.7 us -> 15.7 us  [the longest x7 14.5 us: upward(): lax.ppermute(array, 'fsdp', [(order[at - 1], order[at]) for at in range(s...]
    ppermute x4, waiting for transfers between devices: 2.89 us -> 0.89 us  [swap(): lax.ppermute(array, 'replica', [(at, at ^ bits) for at in range(lax.axis_...]
    ppermute x4, starting transfers between devices: 3.29 us -> 3.9 us  [swap(): lax.ppermute(array, 'replica', [(at, at ^ bits) for at in range(lax.axis_...]
    pallas_call x10 -> x9, Pallas kernels: 3.88 us -> 3.77 us  [vmem_call(): pl.pallas_call(body, out_shape=out_shape, in_specs=[whole] * len(operands...]
  transfers between devices with their start and end apart: 20 -> 18, of which waited for: 8 -> 10; matrix products, arithmetic and copies ran while one was open for 0% -> 0% of each run, Pallas kernels for 18% -> 17%
where the time goes in v5:
time: 47.9 us; the launch traced here: 47.7 us
  starting transfers between devices  19.6 us (41%)
  waiting for transfers between devices  16.4 us (34%)
  Pallas kernels  8.85 us (18%)
  local copies, waits for them, and re-layouts  2.22 us (5%)
  between operations  0.76 us (2%)
    ppermute x7, starting transfers between devices, upward(): lax.ppermute(array, 'fsdp', [(order[at - 1], order[at]) for at in range(s...  14.5 us
    ppermute x7, waiting for transfers between devices, upward(): lax.ppermute(array, 'fsdp', [(order[at - 1], order[at]) for at in range(s...  8.69 us
    ppermute x7, waiting for transfers between devices, downward(): lax.ppermute(array, 'fsdp', [(order[at], order[at - 1]) for at in range(s...  6.78 us
    pallas_call x4, Pallas kernels, products(): pl.pallas_call(functools.partial(products_kernel, size, list(blocks), fir...  5.08 us
    ppermute x4, starting transfers between devices, swap(): lax.ppermute(array, 'replica', [(at, at ^ bits) for at in range(lax.axis_...  3.9 us
    pallas_call x9, Pallas kernels, vmem_call(): pl.pallas_call(body, out_shape=out_shape, in_specs=[whole] * len(operands...  3.77 us
    unnamed x15, local copies, waits for them, and re-layouts  2.2 us
    ppermute x7, starting transfers between devices, downward(): lax.ppermute(array, 'fsdp', [(order[at], order[at - 1]) for at in range(s...  1.12 us
  transfers between devices with their start and end apart: 18, of which 10 were waited for; matrix products, arithmetic and copies ran while one was open for 0% of the time, Pallas kernels for 17%

profile of v5, /device:TPU:0, one launch (start us, length us, event | category | flops | bytes accessed | tf_op | source)
XLA Modules:
  0.0 47.7 jit_solution(11142523137490616475)
XLA Ops:
  0.6 3.1 %collective-permute-start = (bf16[256,512]{1,0:T(8,128)(2,1)}, bf16[256,512]{1,0:T(8,128)(2,1)S(1)}, u32[]{:S(2)}, u32[]{:S(2)}) collective-permute-start(bf16[256,512]{1,0:T(8,128)(2,1)} %bitcast.11), channel_id=1, source_target_pairs={{1,0},{0,2},{2,4},{4,6},{6,7},{7,5},{5,3},{3,1},{9,8},{8,10},{10,1... | collective-permute-start | bytes 786440 | tf_op jit(solution)/shard_map/ppermute | solution.py:313
  3.7 1.2 %copy-done = bf16[1,256,2048]{2,1,0:T(8,128)(2,1)S(1)} copy-done((bf16[1,256,2048]{2,1,0:T(8,128)(2,1)S(1)}, bf16[1,256,2048]{2,1,0:T(8,128)(2,1)}, u32[]{:S(2)}) %copy-start) | copy-done | bytes 1048600
  4.9 0.9 %copy-done.3 = bf16[1,256,512]{2,1,0:T(8,128)(2,1)S(1)} copy-done((bf16[1,256,512]{2,1,0:T(8,128)(2,1)S(1)}, bf16[1,256,512]{2,1,0:T(8,128)(2,1)}, u32[]{:S(2)}) %copy-start.3) | copy-done | bytes 262168
  6.7 2.1 %collective-permute-start.8 = (bf16[256,512]{1,0:T(8,128)(2,1)S(1)}, bf16[256,512]{1,0:T(8,128)(2,1)S(1)}, u32[]{:S(2)}, u32[]{:S(2)}) collective-permute-start(bf16[256,512]{1,0:T(8,128)(2,1)S(1)} %get-tuple-element.38), channel_id=1, source_target_pairs={{1,0},{0,2},{2,4},{4,6},{6,7},{7,5},{5,3},{3,1},{9,8},{8,10},{10,1... | collective-permute-start | bytes 786440 | tf_op jit(solution)/shard_map/ppermute | solution.py:313
  8.8 2.0 %collective-permute-start.7 = (bf16[1,256,256]{2,1,0:T(8,128)(2,1)S(1)}, bf16[1,256,256]{2,1,0:T(8,128)(2,1)S(1)}, u32[]{:S(2)}, u32[]{:S(2)}) collective-permute-start(bf16[1,256,256]{2,1,0:T(8,128)(2,1)S(1)} %partner_columns.2), channel_id=1, source_target_pairs={{0,16},{8,24},{16,0},{24,8},{1,17},{9,25},{17,1},{25,9},{2,18},{10... | collective-permute-start | bytes 393224 | tf_op jit(solution)/shard_map/ppermute | solution.py:106
  11.0 2.1 %collective-permute-start.1 = (bf16[256,512]{1,0:T(8,128)(2,1)S(1)}, bf16[256,512]{1,0:T(8,128)(2,1)S(1)}, u32[]{:S(2)}, u32[]{:S(2)}) collective-permute-start(bf16[256,512]{1,0:T(8,128)(2,1)S(1)} %collective-permute-done.refs_1_), channel_id=1, source_target_pairs={{1,0},{0,2},{2,4},{4,6},{6,7},{7,5},{5,3},{3,1},{9,8},{8,10},{10,1... | collective-permute-start | bytes 786440 | tf_op jit(solution)/shard_map/ppermute | solution.py:313
  13.1 1.3 %products.3 = (f32[256,512]{1,0:T(8,128)S(1)}, bf16[256,2048]{1,0:T(8,128)(2,1)}, f32[8,128]{1,0:T(8,128)S(1)}) custom-call(bf16[256,2048]{1,0:T(8,128)(2,1)S(1)} %bitcast.7, bf16[256,512]{1,0:T(8,128)(2,1)S(1)} %bitcast.18, bf16[256,512]{1,0:T(8,128)(2,1)S(1)} %bitcast.14, bf16[256,512]{1,0:T(8,128)(2,1)S(1)} %collective-permute-done.refs_1_, ...), custom_call_target="tpu_custom_call" | custom-call | flops 402653184 | bytes 8388608 | tf_op jit(solution)/shard_map/products/pallas_call | solution.py:217
  14.4 2.1 %collective-permute-done.8.refs_2_ = bf16[256,512]{1,0:T(8,128)(2,1)S(1)} collective-permute-done((bf16[256,512]{1,0:T(8,128)(2,1)S(1)}, bf16[256,512]{1,0:T(8,128)(2,1)S(1)}, u32[]{:S(2)}, u32[]{:S(2)}) %collective-permute-start.8) | collective-permute-done | bytes 262176 | tf_op jit(solution)/shard_map/ppermute | solution.py:313
  16.6 2.0 %collective-permute-done.9.refs_3_ = bf16[256,512]{1,0:T(8,128)(2,1)S(1)} collective-permute-done((bf16[256,512]{1,0:T(8,128)(2,1)S(1)}, bf16[256,512]{1,0:T(8,128)(2,1)S(1)}, u32[]{:S(2)}, u32[]{:S(2)}) %collective-permute-start.9) | collective-permute-done | bytes 262176 | tf_op jit(solution)/shard_map/ppermute | solution.py:316
  18.7 1.6 %collective-permute-start.12 = (bf16[256,512]{1,0:T(8,128)(2,1)S(1)}, bf16[256,512]{1,0:T(8,128)(2,1)S(1)}, u32[]{:S(2)}, u32[]{:S(2)}) collective-permute-start(bf16[256,512]{1,0:T(8,128)(2,1)S(1)} %get-tuple-element.41.refs_2_), channel_id=1, source_target_pairs={{1,0},{0,2},{2,4},{4,6},{6,7},{7,5},{5,3},{3,1},{9,8},{8,10},{10,1... | collective-permute-start | bytes 786440 | tf_op jit(solution)/shard_map/ppermute | solution.py:313
  20.9 1.3 %collective-permute-done.1.refs_0_ = bf16[256,512]{1,0:T(8,128)(2,1)S(1)} collective-permute-done((bf16[256,512]{1,0:T(8,128)(2,1)S(1)}, bf16[256,512]{1,0:T(8,128)(2,1)S(1)}, u32[]{:S(2)}, u32[]{:S(2)}) %collective-permute-start.1) | collective-permute-done | bytes 262176 | tf_op jit(solution)/shard_map/ppermute | solution.py:313
  22.2 2.1 %collective-permute-start.2 = (bf16[256,512]{1,0:T(8,128)(2,1)S(1)}, bf16[256,512]{1,0:T(8,128)(2,1)S(1)}, u32[]{:S(2)}, u32[]{:S(2)}) collective-permute-start(bf16[256,512]{1,0:T(8,128)(2,1)S(1)} %collective-permute-done.1.refs_0_), channel_id=1, source_target_pairs={{1,0},{0,2},{2,4},{4,6},{6,7},{7,5},{5,3},{3,1},{9,8},{8,10},{10,1... | collective-permute-start | bytes 786440 | tf_op jit(solution)/shard_map/ppermute | solution.py:313
  24.4 1.1 %products.4 = (f32[256,512]{1,0:T(8,128)S(1)}, bf16[256,2048]{1,0:T(8,128)(2,1)}, f32[8,128]{1,0:T(8,128)S(1)}) custom-call(bf16[256,2048]{1,0:T(8,128)(2,1)S(1)} %bitcast.8, bf16[256,512]{1,0:T(8,128)(2,1)S(1)} %bitcast.19, bf16[256,512]{1,0:T(8,128)(2,1)S(1)} %collective-permute-done.1.refs_0_, ...), custom_call_target="tpu_custom_call", output_to_operand_aliasing={{1}: (5, {})} | custom-call | flops 268435456 | bytes 8388608 | tf_op jit(solution)/shard_map/products/pallas_call | solution.py:217
  25.5 1.1 %outer_update.1 = (bf16[256,128]{1,0:T(8,128)(2,1)S(1)}, f32[256,128]{1,0:T(8,128)}) custom-call(bf16[256,512]{1,0:T(8,128)(2,1)S(1)} %bitcast.16, bf16[1,256,256]{2,1,0:T(8,128)(2,1)S(1)} %collective-permute-done.7.refs_1_, bf16[2,256,128]{2,1,0:T(8,128)(2,1)S(1)} %collective-permute-done.10.refs_2_, bf16[256,512]{1,0:T(8,128)(2,1)S(1)} %copy-done.5, ...), custom_call_target="tpu_custom_call" | custom-call | bytes 917504 | tf_op jit(solution)/shard_map/outer_update/pallas_call | solution.py:48
  26.6 1.4 %collective-permute-done.12.refs_2_ = bf16[256,512]{1,0:T(8,128)(2,1)S(1)} collective-permute-done((bf16[256,512]{1,0:T(8,128)(2,1)S(1)}, bf16[256,512]{1,0:T(8,128)(2,1)S(1)}, u32[]{:S(2)}, u32[]{:S(2)}) %collective-permute-start.12) | collective-permute-done | bytes 262176 | tf_op jit(solution)/shard_map/ppermute | solution.py:313
  28.0 1.8 %collective-permute-done.13.refs_3_ = bf16[256,512]{1,0:T(8,128)(2,1)S(1)} collective-permute-done((bf16[256,512]{1,0:T(8,128)(2,1)S(1)}, bf16[256,512]{1,0:T(8,128)(2,1)S(1)}, u32[]{:S(2)}, u32[]{:S(2)}) %collective-permute-start.13) | collective-permute-done | bytes 262176 | tf_op jit(solution)/shard_map/ppermute | solution.py:316
  30.2 1.8 %collective-permute-start.11 = (bf16[256,128]{1,0:T(8,128)(2,1)S(1)}, bf16[256,128]{1,0:T(8,128)(2,1)S(1)}, u32[]{:S(2)}, u32[]{:S(2)}) collective-permute-start(bf16[256,128]{1,0:T(8,128)(2,1)S(1)} %get-tuple-element.44.refs_5_), channel_id=1, source_target_pairs={{0,16},{8,24},{16,0},{24,8},{1,17},{9,25},{17,1},{25,9},{2,18},{10... | collective-permute-start | bytes 196616 | tf_op jit(solution)/shard_map/ppermute | solution.py:106
  32.0 1.6 %collective-permute-start.14 = (bf16[256,512]{1,0:T(8,128)(2,1)S(1)}, bf16[256,512]{1,0:T(8,128)(2,1)S(1)}, u32[]{:S(2)}, u32[]{:S(2)}) collective-permute-start(bf16[256,512]{1,0:T(8,128)(2,1)S(1)} %get-tuple-element.51), channel_id=1, source_target_pairs={{1,0},{0,2},{2,4},{4,6},{6,7},{7,5},{5,3},{3,1},{9,8},{8,10},{10,1... | collective-permute-start | bytes 786440 | tf_op jit(solution)/shard_map/ppermute | solution.py:313
  33.6 0.9 %collective-permute-done.11 = bf16[256,128]{1,0:T(8,128)(2,1)S(1)} collective-permute-done((bf16[256,128]{1,0:T(8,128)(2,1)S(1)}, bf16[256,128]{1,0:T(8,128)(2,1)S(1)}, u32[]{:S(2)}, u32[]{:S(2)}) %collective-permute-start.11) | collective-permute-done | bytes 65568 | tf_op jit(solution)/shard_map/ppermute | solution.py:106
  34.5 1.9 %collective-permute-start.3 = (bf16[256,512]{1,0:T(8,128)(2,1)S(1)}, bf16[256,512]{1,0:T(8,128)(2,1)S(1)}, u32[]{:S(2)}, u32[]{:S(2)}) collective-permute-start(bf16[256,512]{1,0:T(8,128)(2,1)S(1)} %collective-permute-done.2.refs_0_), channel_id=1, source_target_pairs={{1,0},{0,2},{2,4},{4,6},{6,7},{7,5},{5,3},{3,1},{9,8},{8,10},{10,1... | collective-permute-start | bytes 786440 | tf_op jit(solution)/shard_map/ppermute | solution.py:313
  36.4 1.1 %products.5 = (f32[256,512]{1,0:T(8,128)S(1)}, bf16[256,2048]{1,0:T(8,128)(2,1)}, f32[8,128]{1,0:T(8,128)S(1)}) custom-call(bf16[256,2048]{1,0:T(8,128)(2,1)S(1)} %bitcast.9, bf16[256,512]{1,0:T(8,128)(2,1)S(1)} %bitcast.20, bf16[256,512]{1,0:T(8,128)(2,1)S(1)} %collective-permute-done.2.refs_0_, ...), custom_call_target="tpu_custom_call", output_to_operand_aliasing={{1}: (5, {})} | custom-call | flops 268435456 | bytes 8388608 | tf_op jit(solution)/shard_map/products/pallas_call | solution.py:217
  37.4 2.3 %collective-permute-done.15.refs_1_ = bf16[256,512]{1,0:T(8,128)(2,1)S(1)} collective-permute-done((bf16[256,512]{1,0:T(8,128)(2,1)S(1)}, bf16[256,512]{1,0:T(8,128)(2,1)S(1)}, u32[]{:S(2)}, u32[]{:S(2)}) %collective-permute-start.15) | collective-permute-done | bytes 262176 | tf_op jit(solution)/shard_map/ppermute | solution.py:316
  40.2 3.6 %collective-permute-done.3.refs_0_ = bf16[256,512]{1,0:T(8,128)(2,1)S(1)} collective-permute-done((bf16[256,512]{1,0:T(8,128)(2,1)S(1)}, bf16[256,512]{1,0:T(8,128)(2,1)S(1)}, u32[]{:S(2)}, u32[]{:S(2)}) %collective-permute-start.3) | collective-permute-done | bytes 262176 | tf_op jit(solution)/shard_map/ppermute | solution.py:313
  43.8 1.7 %last_products.1 = (bf16[256,512]{1,0:T(8,128)(2,1)}, bf16[256,2048]{1,0:T(8,128)(2,1)}, f32[8,128]{1,0:T(8,128)S(1)}) custom-call(bf16[256,2048]{1,0:T(8,128)(2,1)S(1)} %bitcast.10, bf16[256,512]{1,0:T(8,128)(2,1)S(1)} %bitcast.21, bf16[256,512]{1,0:T(8,128)(2,1)S(1)} %collective-permute-done.3.refs_0_, ...), custom_call_target="tpu_custom_call", output_to_operand_aliasing={{1}: (4, {})} | custom-call | flops 134217728 | bytes 33554432 | tf_op jit(solution)/shard_map/last_products/pallas_call | solution.py:217
  (41 shorter events, 4.7 us)
Async XLA Ops:
  0.6 10.3 %collective-permute-start = (bf16[256,512]{1,0:T(8,128)(2,1)}, bf16[256,512]{1,0:T(8,128)(2,1)S(1)}, u32[]{:S(2)}, u32[]{:S(2)}) collective-permute-start(bf16[256,512]{1,0:T(8,128)(2,1)} %bitcast.11), channel_id=1, source_target_pairs={{1,0},{0,2},{2,4},{4,6},{6,7},{7,5},{5,3},{3,1},{9,8},{8,10},{10,1... | collective-permute-start | bytes 786440 | tf_op jit(solution)/shard_map/ppermute | solution.py:313
  3.7 9.4 %collective-permute-start.4 = (bf16[256,512]{1,0:T(8,128)(2,1)}, bf16[256,512]{1,0:T(8,128)(2,1)S(1)}, u32[]{:S(2)}, u32[]{:S(2)}) collective-permute-start(bf16[256,512]{1,0:T(8,128)(2,1)} %bitcast.12), channel_id=1, source_target_pairs={{0,1},{2,0},{4,2},{6,4},{7,6},{5,7},{3,5},{1,3},{8,9},{10,8},{12,1... | collective-permute-start | bytes 786440 | tf_op jit(solution)/shard_map/ppermute | solution.py:316
  3.7 1.2 %copy-start = (bf16[1,256,2048]{2,1,0:T(8,128)(2,1)S(1)}, bf16[1,256,2048]{2,1,0:T(8,128)(2,1)}, u32[]{:S(2)}) copy-start(bf16[1,256,2048]{2,1,0:T(8,128)(2,1)} %param.8) | copy-start | bytes 3145732
  5.9 2.9 %copy-start.2 = (bf16[1,256,512]{2,1,0:T(8,128)(2,1)S(1)}, bf16[1,256,512]{2,1,0:T(8,128)(2,1)}, u32[]{:S(2)}) copy-start(bf16[1,256,512]{2,1,0:T(8,128)(2,1)} %param.5) | copy-start | bytes 786436
  5.9 7.3 %copy-start.1 = (bf16[1,256,2048]{2,1,0:T(8,128)(2,1)S(1)}, bf16[1,256,2048]{2,1,0:T(8,128)(2,1)}, u32[]{:S(2)}) copy-start(bf16[1,256,2048]{2,1,0:T(8,128)(2,1)} %param.8) | copy-start | bytes 3145732
  6.7 9.9 %collective-permute-start.8 = (bf16[256,512]{1,0:T(8,128)(2,1)S(1)}, bf16[256,512]{1,0:T(8,128)(2,1)S(1)}, u32[]{:S(2)}, u32[]{:S(2)}) collective-permute-start(bf16[256,512]{1,0:T(8,128)(2,1)S(1)} %get-tuple-element.38), channel_id=1, source_target_pairs={{1,0},{0,2},{2,4},{4,6},{6,7},{7,5},{5,3},{3,1},{9,8},{8,10},{10,1... | collective-permute-start | bytes 786440 | tf_op jit(solution)/shard_map/ppermute | solution.py:313
  8.7 9.8 %collective-permute-start.9 = (bf16[256,512]{1,0:T(8,128)(2,1)S(1)}, bf16[256,512]{1,0:T(8,128)(2,1)S(1)}, u32[]{:S(2)}, u32[]{:S(2)}) collective-permute-start(bf16[256,512]{1,0:T(8,128)(2,1)S(1)} %get-tuple-element.39), channel_id=1, source_target_pairs={{0,1},{2,0},{4,2},{6,4},{7,6},{5,7},{3,5},{1,3},{8,9},{10,8},{12,1... | collective-permute-start | bytes 786440 | tf_op jit(solution)/shard_map/ppermute | solution.py:316
  8.8 12.0 %collective-permute-start.7 = (bf16[1,256,256]{2,1,0:T(8,128)(2,1)S(1)}, bf16[1,256,256]{2,1,0:T(8,128)(2,1)S(1)}, u32[]{:S(2)}, u32[]{:S(2)}) collective-permute-start(bf16[1,256,256]{2,1,0:T(8,128)(2,1)S(1)} %partner_columns.2), channel_id=1, source_target_pairs={{0,16},{8,24},{16,0},{24,8},{1,17},{9,25},{17,1},{25,9},{2,18},{10... | collective-permute-start | bytes 393224 | tf_op jit(solution)/shard_map/ppermute | solution.py:106
  11.0 11.2 %collective-permute-start.1 = (bf16[256,512]{1,0:T(8,128)(2,1)S(1)}, bf16[256,512]{1,0:T(8,128)(2,1)S(1)}, u32[]{:S(2)}, u32[]{:S(2)}) collective-permute-start(bf16[256,512]{1,0:T(8,128)(2,1)S(1)} %collective-permute-done.refs_1_), channel_id=1, source_target_pairs={{1,0},{0,2},{2,4},{4,6},{6,7},{7,5},{5,3},{3,1},{9,8},{8,10},{10,1... | collective-permute-start | bytes 786440 | tf_op jit(solution)/shard_map/ppermute | solution.py:313
  13.1 11.2 %collective-permute-start.5 = (bf16[256,512]{1,0:T(8,128)(2,1)S(1)}, bf16[256,512]{1,0:T(8,128)(2,1)S(1)}, u32[]{:S(2)}, u32[]{:S(2)}) collective-permute-start(bf16[256,512]{1,0:T(8,128)(2,1)S(1)} %collective-permute-done.4.refs_2_), channel_id=1, source_target_pairs={{0,1},{2,0},{4,2},{6,4},{7,6},{5,7},{3,5},{1,3},{8,9},{10,8},{12,1... | collective-permute-start | bytes 786440 | tf_op jit(solution)/shard_map/ppermute | solution.py:316
  18.7 9.3 %collective-permute-start.12 = (bf16[256,512]{1,0:T(8,128)(2,1)S(1)}, bf16[256,512]{1,0:T(8,128)(2,1)S(1)}, u32[]{:S(2)}, u32[]{:S(2)}) collective-permute-start(bf16[256,512]{1,0:T(8,128)(2,1)S(1)} %get-tuple-element.41.refs_2_), channel_id=1, source_target_pairs={{1,0},{0,2},{2,4},{4,6},{6,7},{7,5},{5,3},{3,1},{9,8},{8,10},{10,1... | collective-permute-start | bytes 786440 | tf_op jit(solution)/shard_map/ppermute | solution.py:313
  20.3 4.1 %copy-start.4 = (bf16[1,256,512]{2,1,0:T(8,128)(2,1)S(1)}, bf16[1,256,512]{2,1,0:T(8,128)(2,1)}, u32[]{:S(2)}) copy-start(bf16[1,256,512]{2,1,0:T(8,128)(2,1)} %param.9) | copy-start | bytes 786436
  20.3 9.5 %collective-permute-start.13 = (bf16[256,512]{1,0:T(8,128)(2,1)S(1)}, bf16[256,512]{1,0:T(8,128)(2,1)S(1)}, u32[]{:S(2)}, u32[]{:S(2)}) collective-permute-start(bf16[256,512]{1,0:T(8,128)(2,1)S(1)} %get-tuple-element.42.refs_3_), channel_id=1, source_target_pairs={{0,1},{2,0},{4,2},{6,4},{7,6},{5,7},{3,5},{1,3},{8,9},{10,8},{12,1... | collective-permute-start | bytes 786440 | tf_op jit(solution)/shard_map/ppermute | solution.py:316
  20.8 4.7 %collective-permute-start.10 = (bf16[2,256,128]{2,1,0:T(8,128)(2,1)S(1)}, bf16[2,256,128]{2,1,0:T(8,128)(2,1)S(1)}, u32[]{:S(2)}, u32[]{:S(2)}) collective-permute-start(bf16[2,256,128]{2,1,0:T(8,128)(2,1)S(1)} %partner_columns.3), channel_id=1, source_target_pairs={{0,8},{8,0},{16,24},{24,16},{1,9},{9,1},{17,25},{25,17},{2,10},{10... | collective-permute-start | bytes 393224 | tf_op jit(solution)/shard_map/ppermute | solution.py:106
  22.2 12.3 %collective-permute-start.2 = (bf16[256,512]{1,0:T(8,128)(2,1)S(1)}, bf16[256,512]{1,0:T(8,128)(2,1)S(1)}, u32[]{:S(2)}, u32[]{:S(2)}) collective-permute-start(bf16[256,512]{1,0:T(8,128)(2,1)S(1)} %collective-permute-done.1.refs_0_), channel_id=1, source_target_pairs={{1,0},{0,2},{2,4},{4,6},{6,7},{7,5},{5,3},{3,1},{9,8},{8,10},{10,1... | collective-permute-start | bytes 786440 | tf_op jit(solution)/shard_map/ppermute | solution.py:313
  24.3 12.0 %collective-permute-start.6 = (bf16[256,512]{1,0:T(8,128)(2,1)S(1)}, bf16[256,512]{1,0:T(8,128)(2,1)S(1)}, u32[]{:S(2)}, u32[]{:S(2)}) collective-permute-start(bf16[256,512]{1,0:T(8,128)(2,1)S(1)} %collective-permute-done.5.refs_1_), channel_id=1, source_target_pairs={{0,1},{2,0},{4,2},{6,4},{7,6},{5,7},{3,5},{1,3},{8,9},{10,8},{12,1... | collective-permute-start | bytes 786440 | tf_op jit(solution)/shard_map/ppermute | solution.py:316
  24.4 1.1 %copy-start.5 = (bf16[256,512]{1,0:T(8,128)(2,1)S(1)}, bf16[256,512]{1,0:T(8,128)(2,1)}, u32[]{:S(2)}) copy-start(bf16[256,512]{1,0:T(8,128)(2,1)} %refs_3_.1) | copy-start | bytes 786436
  24.4 1.1 %copy-start.6 = (f32[256,128]{1,0:T(8,128)S(1)}, f32[256,128]{1,0:T(8,128)}, u32[]{:S(2)}) copy-start(f32[256,128]{1,0:T(8,128)} %refs_4_.1) | copy-start | bytes 393220
  29.9 9.8 %collective-permute-start.15 = (bf16[256,512]{1,0:T(8,128)(2,1)S(1)}, bf16[256,512]{1,0:T(8,128)(2,1)S(1)}, u32[]{:S(2)}, u32[]{:S(2)}) collective-permute-start(bf16[256,512]{1,0:T(8,128)(2,1)S(1)} %get-tuple-element.53), channel_id=1, source_target_pairs={{0,1},{2,0},{4,2},{6,4},{7,6},{5,7},{3,5},{1,3},{8,9},{10,8},{12,1... | collective-permute-start | bytes 786440 | tf_op jit(solution)/shard_map/ppermute | solution.py:316
  30.2 4.3 %collective-permute-start.11 = (bf16[256,128]{1,0:T(8,128)(2,1)S(1)}, bf16[256,128]{1,0:T(8,128)(2,1)S(1)}, u32[]{:S(2)}, u32[]{:S(2)}) collective-permute-start(bf16[256,128]{1,0:T(8,128)(2,1)S(1)} %get-tuple-element.44.refs_5_), channel_id=1, source_target_pairs={{0,16},{8,24},{16,0},{24,8},{1,17},{9,25},{17,1},{25,9},{2,18},{10... | collective-permute-start | bytes 196616 | tf_op jit(solution)/shard_map/ppermute | solution.py:106
  32.0 14.3 %collective-permute-start.14 = (bf16[256,512]{1,0:T(8,128)(2,1)S(1)}, bf16[256,512]{1,0:T(8,128)(2,1)S(1)}, u32[]{:S(2)}, u32[]{:S(2)}) collective-permute-start(bf16[256,512]{1,0:T(8,128)(2,1)S(1)} %get-tuple-element.51), channel_id=1, source_target_pairs={{1,0},{0,2},{2,4},{4,6},{6,7},{7,5},{5,3},{3,1},{9,8},{8,10},{10,1... | collective-permute-start | bytes 786440 | tf_op jit(solution)/shard_map/ppermute | solution.py:313
  34.5 9.4 %collective-permute-start.3 = (bf16[256,512]{1,0:T(8,128)(2,1)S(1)}, bf16[256,512]{1,0:T(8,128)(2,1)S(1)}, u32[]{:S(2)}, u32[]{:S(2)}) collective-permute-start(bf16[256,512]{1,0:T(8,128)(2,1)S(1)} %collective-permute-done.2.refs_0_), channel_id=1, source_target_pairs={{1,0},{0,2},{2,4},{4,6},{6,7},{7,5},{5,3},{3,1},{9,8},{8,10},{10,1... | collective-permute-start | bytes 786440 | tf_op jit(solution)/shard_map/ppermute | solution.py:313
  39.8 7.1 %collective-permute-start.16 = (bf16[256,512]{1,0:T(8,128)(2,1)S(1)}, bf16[256,512]{1,0:T(8,128)(2,1)S(1)}, u32[]{:S(2)}, u32[]{:S(2)}) collective-permute-start(bf16[256,512]{1,0:T(8,128)(2,1)S(1)} %add_terms.5), channel_id=1, source_target_pairs={{0,1},{2,0},{4,2},{6,4},{7,6},{5,7},{3,5},{1,3},{8,9},{10,8},{12,1... | collective-permute-start | bytes 786440 | tf_op jit(solution)/shard_map/ppermute | solution.py:316
  40.2 5.3 %collective-permute-start.17 = (bf16[256,256]{1,0:T(8,128)(2,1)S(1)}, bf16[256,256]{1,0:T(8,128)(2,1)S(1)}, u32[]{:S(2)}, u32[]{:S(2)}) collective-permute-start(bf16[256,256]{1,0:T(8,128)(2,1)S(1)} %constant_dynamic-update-slice_fusion.refs_4_.refs_0_), channel_id=1, source_target_pairs={{0,8},{8,0},{16,24},{24,16},{1,9},{9,1},{17,25},{25,17},{2,10},{10... | collective-permute-start | bytes 393224 | tf_op jit(solution)/shard_map/ppermute | solution.py:106
  (1 other events, 0.9 us)

commit v6 on v5

v6 whole, which is shorter than its diff:
```python
import functools

import jax
import jax.numpy as jnp
from jax import lax
from jax.experimental import pallas as pl
from jax.experimental.pallas import tpu as pltpu
from jax.sharding import PartitionSpec as P

BLOCK = 64

outer_rate = 0.7
outer_momentum = 0.9
scale_epsilon = 1e-06

F32 = jnp.float32
BF16 = jnp.bfloat16
LANES = 128
VMEM_BYTES = 8 * 2**20
PRODUCTS_BYTES = 8 * 2**20


def ring_order(size):
    return list(range(0, size, 2)) + list(range(1, size, 2))[::-1]


def ring_place(index, size):
    return jnp.where((index & 1) == 0, index >> 1, size - 1 - (index >> 1))


def ring_index(place, size):
    place = lax.rem(place + size, size)
    evens = (size + 1) // 2
    return jnp.where(place < evens, 2 * place, 2 * (size - 1 - place) + 1)


def block_start(offset, size, depth, other=0):
    me = lax.axis_index("fsdp")
    row = ring_index(ring_place(me >> 1, size // 2) + offset, size // 2)
    return pl.multiple_of((2 * row + ((me & 1) ^ other)) * depth, depth)


def vmem_call(kernel, out_shape, operands, flops, name, after=(), moved=None):
    def body(*refs):
        kernel(*refs[: len(operands)], *refs[len(operands) + len(after) :])

    moved = moved or sum(x.size * x.dtype.itemsize for x in operands)
    whole = pl.BlockSpec(memory_space=pltpu.VMEM)
    return pl.pallas_call(
        body,
        out_shape=out_shape,
        in_specs=[whole] * len(operands) + [pl.BlockSpec(memory_space=pl.ANY)] * len(after),
        out_specs=jax.tree.map(lambda _: whole, out_shape),
        compiler_params=pltpu.CompilerParams(vmem_limit_bytes=VMEM_BYTES),
        cost_estimate=pl.CostEstimate(flops=flops, bytes_accessed=moved, transcendentals=0),
        name=name,
    )(*operands, *after)


def shape_of(rows, columns, dtype):
    return jax.ShapeDtypeStruct((rows, columns), dtype)


def column_window(array, start, width):
    if isinstance(array, jax.Array):
        return lax.dynamic_slice_in_dim(array, start, width, array.ndim - 1)
    return array[..., pl.ds(pl.multiple_of(start, width), width)]


def outer_kernel(replicas, share_cols, *refs):
    *held_refs, global_ref, momentum_ref, share_ref, new_momentum_ref = refs
    rows, window = held_refs[-1].shape[-2:]
    me = lax.axis_index("replica")

    def windows_of(ref):
        here = me * share_cols // window * window % ref.shape[-1]
        return ref[...] if ref.shape[-1] == window else column_window(ref, here, window)

    old = windows_of(global_ref).astype(F32)
    lane = lax.broadcasted_iota(jnp.int32, (rows, window), 1) // BLOCK
    total = jnp.zeros((rows, window), F32)
    for held_ref in held_refs:
        held = windows_of(held_ref).astype(F32)
        for local in [held] if held.ndim == 2 else list(held):
            drift = old - local
            size = jnp.abs(drift)
            scale = jnp.zeros((rows, window), F32)
            for block in range(window // BLOCK):
                top = jnp.max(jnp.where(lane == block, size, 0.0), axis=1, keepdims=True)
                top = (top + scale_epsilon).astype(BF16).astype(F32)
                scale = jnp.where(lane == block, top, scale)
            total = total + (drift / scale).astype(BF16).astype(F32) * scale
    mean_grad = total / replicas
    shares = window // share_cols
    mean_here, old_here = mean_grad[:, :share_cols], old[:, :share_cols]
    mine = me % shares
    for share in range(1, shares):
        columns = slice(share * share_cols, (share + 1) * share_cols)
        mean_here = jnp.where(mine == share, mean_grad[:, columns], mean_here)
        old_here = jnp.where(mine == share, old[:, columns], old_here)
    new_momentum = outer_momentum * momentum_ref[...] + mean_here
    new_momentum_ref[...] = new_momentum
    share_ref[...] = (old_here - outer_rate * (mean_here + outer_momentum * new_momentum)).astype(BF16)


def swap(array, bits):
    return lax.ppermute(array, "replica", [(at, at ^ bits) for at in range(lax.axis_size("replica"))])


def partner_kernel(bits, share_cols, width, *refs):
    *held_refs, out_ref = refs
    start = (lax.axis_index("replica") ^ bits) * share_cols // width * width
    at = 0
    for held_ref in held_refs:
        part = column_window(held_ref, start % held_ref.shape[-1], width)
        count = 1 if part.ndim == 2 else part.shape[0]
        out_ref[at : at + count] = part.reshape((count,) + part.shape[-2:])
        at += count


def send_windows(held, bits, kv_width, after):
    replicas = lax.axis_size("replica")
    share_cols = kv_width // replicas
    width = max(bits * share_cols, BLOCK)
    rows = held[0].shape[-2]
    count = sum(1 if array.ndim == 2 else array.shape[0] for array in held)
    if width % LANES == 0:
        leaving = vmem_call(
            functools.partial(partner_kernel, bits, share_cols, width),
            jax.ShapeDtypeStruct((count, rows, width), BF16),
            held,
            0,
            "partner_columns",
            after,
        )
    else:
        start = (lax.axis_index("replica") ^ bits) * share_cols // width * width
        parts = [column_window(array, start % array.shape[-1], width).reshape(-1, rows, width) for array in held]
        leaving = jnp.concatenate(parts)
    return held + [swap(leaving, bits)]


def update_share(held, global_weights, momentum, after):
    rows, share_cols = momentum.shape
    replicas = lax.axis_size("replica")
    window = held[-1].shape[-1]
    if window % LANES:
        start = lax.axis_index("replica") * share_cols // window * window
        held = [column_window(array, start % array.shape[-1], window) for array in held]
        global_weights = column_window(global_weights, start, window)
    return vmem_call(
        functools.partial(outer_kernel, replicas, share_cols),
        (shape_of(rows, share_cols, BF16), shape_of(rows, share_cols, F32)),
        held + [global_weights, momentum],
        0,
        "outer_update",
        after,
    )


def join_kernel(places, *refs):
    *held_refs, out_ref = refs
    width = out_ref.shape[1] // len(places)
    me = lax.axis_index("replica")
    at = 0
    for held_ref in held_refs:
        for start in range(0, held_ref.shape[1], width):
            columns = pl.ds(pl.multiple_of((me ^ places[at]) * width, width), width)
            out_ref[:, columns] = held_ref[:, start : start + width]
            at += 1


def join_shares(held, places, kv_width, after):
    rows = held[0].shape[0]
    width = kv_width // len(places)
    if width % LANES == 0:
        return vmem_call(
            functools.partial(join_kernel, places), shape_of(rows, kv_width, BF16), held, 0, "join_shares", after
        )
    whole = jnp.concatenate(held, axis=1)
    joined = jnp.zeros_like(whole)
    for at, place in enumerate(places):
        start = (lax.axis_index("replica") ^ place) * width
        joined = lax.dynamic_update_slice_in_dim(joined, whole[:, at * width : (at + 1) * width], start, 1)
    return joined


PARTNER = {2: (0, 0), 1: (0, 1), 3: (1, 0), 0: (1, 1)}


def pack_kernel(size, inputs_ref, *out_refs):
    depth = inputs_ref.shape[1] // size
    for offset, (at, slot) in PARTNER.items():
        out_refs[at][slot] = inputs_ref[:, pl.ds(block_start(offset, size, depth, 1), depth)]


def pack(inputs_here, size):
    tokens, width = inputs_here.shape
    shapes = [jax.ShapeDtypeStruct((2, tokens, width // size), BF16)] * 2
    return vmem_call(functools.partial(pack_kernel, size), shapes, [inputs_here], 0, "pack_columns")


def terms_kernel(size, offsets, token_weight, inputs_ref, cotangent_ref, partner_ref, partner_cotangent_ref, *out_refs):
    depth = inputs_ref.shape[1] // size
    for offset, out_ref in zip(offsets, out_refs):
        here = inputs_ref[:, pl.ds(block_start(offset, size, depth), depth)]
        there = partner_ref[PARTNER[offset][1]]
        total = 0.0
        for columns, cotangent in ((here, cotangent_ref[...]), (there, partner_cotangent_ref[...])):
            total = total + lax.dot_general(
                columns, cotangent, (((0,), (0,)), ((), ())), preferred_element_type=F32
            )
        out_ref[...] = (total * token_weight).astype(out_ref.dtype)


def token_terms(operands, size, offsets, dtype, token_weight, after=()):
    tokens, width = operands[0].shape
    kv_width = operands[1].shape[1]
    depth = width // size
    return vmem_call(
        functools.partial(terms_kernel, size, offsets, token_weight),
        [shape_of(depth, kv_width, dtype)] * len(offsets),
        operands,
        4 * tokens * depth * len(offsets) * kv_width,
        "token_terms",
        after,
    )


def add_kernel(terms_ref, sum_ref, out_ref):
    out_ref[...] = (terms_ref[...] + sum_ref[...].astype(F32)).astype(BF16)


def end_kernel(terms_ref, up_ref, down_ref, out_ref):
    out_ref[...] = (terms_ref[...] + up_ref[...].astype(F32) + down_ref[...].astype(F32)).astype(BF16)


def products_kernel(size, offsets, last, inputs_ref, cotangent_ref, partner_cotangent_ref, *refs):
    partner_refs, block_refs, refs = refs[:2], refs[2 : 2 + len(offsets)], refs[2 + len(offsets) :]
    total_refs = refs[:2] if last else ()
    here_ref, there_ref, leaving_ref, grad_ref, mark_ref, held, sems = refs[-7:]
    depth = inputs_ref.shape[1] // size
    copies = []
    for number, (offset, block_ref) in enumerate(zip(offsets, block_refs)):
        for cotangent, out_ref in ((partner_cotangent_ref, leaving_ref), (cotangent_ref, held)):
            out_ref[number] = lax.dot_general(
                cotangent[...], block_ref[...], (((1,), (1,)), ((), ())), preferred_element_type=F32
            ).astype(BF16)
        columns = pl.ds(block_start(offset, size, depth), depth)
        copies.append(pltpu.make_async_copy(held.at[number], grad_ref.at[:, columns], sems.at[number]))
        copies[-1].start()
    there, here = (total_refs[1][...], total_refs[0][...]) if last else (0.0, 0.0)
    for offset, block_ref in zip(offsets, block_refs):
        at, slot = PARTNER[offset]
        there = there + jnp.dot(partner_refs[at][slot], block_ref[...], preferred_element_type=F32)
        columns = inputs_ref[:, pl.ds(block_start(offset, size, depth), depth)]
        here = here + jnp.dot(columns, block_ref[...], preferred_element_type=F32)
    here_ref[...] = here
    if last:
        for part in range(there.shape[1] // depth):
            leaving_ref[len(offsets) + part] = there[:, part * depth : (part + 1) * depth].astype(BF16)
    else:
        there_ref[...] = there
    mark_ref[...] = jnp.zeros_like(mark_ref)
    for copy in copies:
        copy.wait()


def products(inputs_here, cotangent, partner_cotangent, partner_inputs, blocks, size, before=None):
    tokens, width = inputs_here.shape
    kv_width = cotangent.shape[1]
    depth = width // size
    last = before is not None
    leaving = len(blocks) + (kv_width // depth if last else 0)
    operands = [inputs_here, cotangent, partner_cotangent, *partner_inputs, *blocks.values()]
    operands += [before[0], before[1], before[3]] if last else []
    whole, anywhere = pl.BlockSpec(memory_space=pltpu.VMEM), pl.BlockSpec(memory_space=pl.ANY)
    total = shape_of(tokens, kv_width, F32)
    mark = shape_of(8, LANES, F32)
    return pl.pallas_call(
        functools.partial(products_kernel, size, list(blocks), last),
        out_shape=(
            total,
            mark if last else total,
            jax.ShapeDtypeStruct((leaving, tokens, depth), BF16),
            shape_of(tokens, width, BF16),
            mark,
        ),
        in_specs=[whole] * (5 + len(blocks)) + ([whole, whole, anywhere] if last else []),
        out_specs=(whole, whole, whole, anywhere, whole),
        scratch_shapes=[
            pltpu.VMEM((len(blocks), tokens, depth), BF16),
            pltpu.SemaphoreType.DMA((len(blocks),)),
        ],
        input_output_aliases={len(operands) - 1: 3} if last else {},
        compiler_params=pltpu.CompilerParams(vmem_limit_bytes=VMEM_BYTES),
        cost_estimate=pl.CostEstimate(
            flops=8 * tokens * depth * len(blocks) * kv_width, bytes_accessed=PRODUCTS_BYTES, transcendentals=0
        ),
        name="last_products" if last else "products",
    )(*operands)


def collect_kernel(size, offsets, total_ref, early_ref, late_ref, _, rows_ref, grad_ref, mark_ref, sems):
    depth = early_ref.shape[-1]
    parts = total_ref.shape[1] // depth
    copies = []
    for number, offset in enumerate(offsets):
        late = number - early_ref.shape[0]
        source = early_ref.at[number] if late < 0 else late_ref.at[late]
        columns = pl.ds(block_start(offset, size, depth, 1), depth)
        copies.append(pltpu.make_async_copy(source, grad_ref.at[:, columns], sems.at[number]))
        copies[-1].start()
    for part in range(parts):
        columns = slice(part * depth, (part + 1) * depth)
        arrived = late_ref[late_ref.shape[0] - parts + part].astype(F32)
        rows_ref[:, columns] = (total_ref[:, columns] + arrived).astype(BF16)
    mark_ref[...] = jnp.zeros_like(mark_ref)
    for copy in copies:
        copy.wait()


def collect(total, early, late, grad, offsets, size):
    tokens, kv_width = total.shape
    whole, anywhere = pl.BlockSpec(memory_space=pltpu.VMEM), pl.BlockSpec(memory_space=pl.ANY)
    return pl.pallas_call(
        functools.partial(collect_kernel, size, offsets),
        out_shape=(shape_of(tokens, kv_width, BF16), shape_of(*grad.shape, BF16), shape_of(8, LANES, F32)),
        in_specs=[whole] * 3 + [anywhere],
        out_specs=(whole, anywhere, whole),
        scratch_shapes=[pltpu.SemaphoreType.DMA((len(offsets),))],
        input_output_aliases={3: 1},
        compiler_params=pltpu.CompilerParams(vmem_limit_bytes=VMEM_BYTES),
        cost_estimate=pl.CostEstimate(flops=tokens * kv_width, bytes_accessed=PRODUCTS_BYTES, transcendentals=0),
        name="collect",
    )(total, early, late, grad)


def inner_and_outer(local_shard, global_weights, momentum, inputs_here, cotangent):
    depth, kv_width = local_shard.shape
    size = lax.axis_size("fsdp")
    ring = size // 2
    token_weight = 1.0 / (inputs_here.shape[0] * size)
    order = ring_order(ring)
    pairs = [(2 * order[at - 1] + side, 2 * order[at] + side) for at in range(ring) for side in (0, 1)]

    def upward(array):
        return lax.ppermute(array, "fsdp", pairs)

    def downward(array):
        return lax.ppermute(array, "fsdp", [(target, source) for source, target in pairs])

    def across(array):
        return lax.ppermute(array, "fsdp", [(at, at ^ 1) for at in range(size)])

    from_below, from_above = upward(local_shard), downward(local_shard)
    partner_cotangent = across(cotangent)
    packed = pack(inputs_here, size)
    partner_inputs = [across(part) for part in packed]

    bits = lax.axis_size("replica") // 2
    held = send_windows([local_shard], bits, kv_width, packed)

    blocks = {0: local_shard, 3: from_below, 1: from_above}
    operands = [inputs_here, cotangent, partner_inputs[0], partner_cotangent]
    first = token_terms(operands, size, [2, 1], BF16, token_weight)
    sum_down, sum_up = downward(first[0]), upward(first[1])
    farthest = upward(from_below)
    while bits > 1:
        bits //= 2
        held = send_windows(held, bits, kv_width, first)
    operands[2] = partner_inputs[1]
    terms = token_terms(operands, size, [3, 0], F32, token_weight)
    made = products(inputs_here, cotangent, partner_cotangent, partner_inputs, blocks, size)
    early = across(made[2])
    new_share, new_momentum = update_share(held, global_weights, momentum, (made[4],))
    bits = lax.axis_size("replica") // 2
    shares, joined = [new_share, swap(new_share, bits)], [0, bits]
    total_down = vmem_call(
        add_kernel, shape_of(depth, kv_width, BF16), [terms[0], sum_down], 0, "add_terms", (new_share,)
    )
    sum_down = downward(total_down)
    made = products(inputs_here, cotangent, partner_cotangent, partner_inputs, {2: farthest}, size, made)
    late = across(made[2])
    while bits > 1:
        bits //= 2
        shares = [jnp.concatenate(shares, axis=1)]
        shares.append(swap(shares[0], bits))
        joined += [place ^ bits for place in joined]
    new_global = join_shares(shares, joined, kv_width, (made[4],))
    grad_rows = vmem_call(
        end_kernel, shape_of(depth, kv_width, BF16), [terms[1], sum_up, sum_down], 0, "end_terms", ()
    )
    kv_rows, grad_in, mark = collect(made[0], early, late, made[3], [*blocks, 2], size)
    return kv_rows, grad_in, grad_rows, new_global, new_momentum


def plain_inner_and_outer(local_shard, global_weights, momentum, inputs_here, cotangent):
    depth, kv_width = local_shard.shape
    token_weight = 1.0 / (inputs_here.shape[0] * lax.axis_size("fsdp"))
    gathered = lax.all_gather(local_shard, "fsdp", axis=0, tiled=True)
    kv_rows = jnp.dot(inputs_here, gathered, preferred_element_type=F32).astype(BF16)
    grad_in = lax.dot_general(cotangent, gathered, (((1,), (1,)), ((), ())), preferred_element_type=F32).astype(BF16)
    terms = lax.dot_general(inputs_here, cotangent, (((0,), (0,)), ((), ())), preferred_element_type=F32)
    grad_rows = lax.psum_scatter(terms * token_weight, "fsdp", scatter_dimension=0, tiled=True).astype(BF16)
    bits = lax.axis_size("replica")
    held = [local_shard]
    while bits > 1:
        bits //= 2
        held = send_windows(held, bits, kv_width, ())
    new_share, new_momentum = update_share(held, global_weights, momentum, ())
    shares, joined = [new_share], [0]
    bits = lax.axis_size("replica")
    while bits > 1:
        bits //= 2
        shares = [jnp.concatenate(shares, axis=1)]
        shares.append(swap(shares[0], bits))
        joined += [place ^ bits for place in joined]
    return kv_rows, grad_in, grad_rows, join_shares(shares, joined, kv_width, ()), new_momentum


def per_device(local_weights, global_weights, momentum, activations, kv_cotangent):
    depth = local_weights.shape[1]
    pairs_fit = lax.axis_size("fsdp") == 8 and depth % LANES == 0 and local_weights.shape[2] % depth == 0
    step = inner_and_outer if pairs_fit else plain_inner_and_outer
    kv_rows, grad_in, grad_rows, new_global, new_momentum = step(
        local_weights[0], global_weights, momentum, activations[0], kv_cotangent[0]
    )
    return kv_rows[None], grad_in[None], grad_rows[None], new_global, new_momentum


def solution(mesh):
    placed = (
        P("replica", "fsdp", None),
        P("fsdp", None),
        P("fsdp", "replica"),
        P("replica", "fsdp", None),
        P("replica", "fsdp", None),
    )
    return jax.shard_map(
        per_device,
        mesh=mesh,
        in_specs=placed,
        out_specs=(
            P("replica", "fsdp", None),
            P("replica", "fsdp", None),
            P("replica", "fsdp", None),
            P("fsdp", None),
            P("fsdp", "replica"),
        ),
        check_vma=False,
    )
```

time: 47.9 us -> 45.3 us (0.946)
  starting transfers between devices: 19.6 us -> 18.5 us
  waiting for transfers between devices: 16.4 us -> 15.3 us
  Pallas kernels: 8.85 us -> 8.37 us
    ppermute x14 -> x11, waiting for transfers between devices: 15.5 us -> 11.1 us  [the longest x5 5.81 us: across(): return lax.ppermute(array, 'fsdp', [(at, at ^ 1) for at in range(size)])]
    ppermute x4, waiting for transfers between devices: 0.89 us -> 4.21 us  [swap(): lax.ppermute(array, 'replica', [(at, at ^ bits) for at in range(lax.axis_...]
    ppermute x4, starting transfers between devices: 3.9 us -> 3.25 us  [swap(): lax.ppermute(array, 'replica', [(at, at ^ bits) for at in range(lax.axis_...]
    pallas_call x4 -> x3, Pallas kernels: 5.08 us -> 4.65 us  [the longest x2 3.1 us: products(): pl.pallas_call(functools.partial(products_kernel, size, list(blocks), las...]
    ppermute x14 -> x11, starting transfers between devices: 15.7 us -> 15.3 us  [the longest x3 8.93 us: upward(): return lax.ppermute(array, 'fsdp', pairs)]
  transfers between devices with their start and end apart: 18 -> 15, of which waited for: 10 -> 8; matrix products, arithmetic and copies ran while one was open for 0% -> 0% of each run, Pallas kernels for 17% -> 15%
where the time goes in v6:
time: 45.3 us; the launch traced here: 45.2 us
  starting transfers between devices  18.5 us (41%)
  waiting for transfers between devices  15.3 us (34%)
  Pallas kernels  8.37 us (18%)
  local copies, waits for them, and re-layouts  2.23 us (5%)
  between operations  0.78 us (2%)
    ppermute x3, starting transfers between devices, upward(): return lax.ppermute(array, 'fsdp', pairs)  8.93 us
    ppermute x5, waiting for transfers between devices, across(): return lax.ppermute(array, 'fsdp', [(at, at ^ 1) for at in range(size)])  5.81 us
    ppermute x5, starting transfers between devices, across(): return lax.ppermute(array, 'fsdp', [(at, at ^ 1) for at in range(size)])  5.75 us
    ppermute x4, waiting for transfers between devices, swap(): lax.ppermute(array, 'replica', [(at, at ^ bits) for at in range(lax.axis_...  4.21 us
    pallas_call x9, Pallas kernels, vmem_call(): pl.pallas_call(body, out_shape=out_shape, in_specs=[whole] * len(operands...  3.72 us
    ppermute x4, starting transfers between devices, swap(): lax.ppermute(array, 'replica', [(at, at ^ bits) for at in range(lax.axis_...  3.25 us
    ppermute x3, waiting for transfers between devices, downward(): lax.ppermute(array, 'fsdp', [(target, source) for source, target in pairs])  3.11 us
    pallas_call x2, Pallas kernels, products(): pl.pallas_call(functools.partial(products_kernel, size, list(blocks), las...  3.1 us
  transfers between devices with their start and end apart: 15, of which 8 were waited for; matrix products, arithmetic and copies ran while one was open for 0% of the time, Pallas kernels for 15%

profile of v6, /device:TPU:0, one launch (start us, length us, event | category | flops | bytes accessed | tf_op | source)
XLA Modules:
  0.0 45.2 jit_solution(6097484536774994649)
XLA Ops:
  0.6 4.1 %collective-permute-start.3 = (bf16[256,512]{1,0:T(8,128)(2,1)}, bf16[256,512]{1,0:T(8,128)(2,1)S(1)}, u32[]{:S(2)}, u32[]{:S(2)}) collective-permute-start(bf16[256,512]{1,0:T(8,128)(2,1)} %bitcast.16), channel_id=1, source_target_pairs={{2,0},{3,1},{0,4},{1,5},{4,6},{5,7},{6,2},{7,3},{10,8},{11,9},{8,1... | collective-permute-start | bytes 786440 | tf_op jit(solution)/shard_map/ppermute | solution.py:348
  4.7 1.5 %collective-permute-start = (bf16[256,512]{1,0:T(8,128)(2,1)}, bf16[256,512]{1,0:T(8,128)(2,1)S(1)}, u32[]{:S(2)}, u32[]{:S(2)}) collective-permute-start(bf16[256,512]{1,0:T(8,128)(2,1)} %bitcast.11), channel_id=1, source_target_pairs={{0,1},{1,0},{2,3},{3,2},{4,5},{5,4},{6,7},{7,6},{8,9},{9,8},{10,11... | collective-permute-start | bytes 786440 | tf_op jit(solution)/shard_map/ppermute | solution.py:354
  6.2 1.2 %copy-done = bf16[1,256,2048]{2,1,0:T(8,128)(2,1)S(1)} copy-done((bf16[1,256,2048]{2,1,0:T(8,128)(2,1)S(1)}, bf16[1,256,2048]{2,1,0:T(8,128)(2,1)}, u32[]{:S(2)}) %copy-start) | copy-done | bytes 1048600
  8.1 1.5 %collective-permute-start.2 = (bf16[2,256,256]{2,1,0:T(8,128)(2,1)S(1)}, bf16[2,256,256]{2,1,0:T(8,128)(2,1)S(1)}, u32[]{:S(2)}, u32[]{:S(2)}) collective-permute-start(bf16[2,256,256]{2,1,0:T(8,128)(2,1)S(1)} %get-tuple-element.25.refs_2_), channel_id=1, source_target_pairs={{0,1},{1,0},{2,3},{3,2},{4,5},{5,4},{6,7},{7,6},{8,9},{9,8},{10,11... | collective-permute-start | bytes 786440 | tf_op jit(solution)/shard_map/ppermute | solution.py:354
  9.6 2.1 %collective-permute-done.3.refs_3_ = bf16[256,512]{1,0:T(8,128)(2,1)S(1)} collective-permute-done((bf16[256,512]{1,0:T(8,128)(2,1)}, bf16[256,512]{1,0:T(8,128)(2,1)S(1)}, u32[]{:S(2)}, u32[]{:S(2)}) %collective-permute-start.3) | collective-permute-done | bytes 262176 | tf_op jit(solution)/shard_map/ppermute | solution.py:348
  11.7 3.3 %collective-permute-start.4 = (bf16[256,512]{1,0:T(8,128)(2,1)S(1)}, bf16[256,512]{1,0:T(8,128)(2,1)S(1)}, u32[]{:S(2)}, u32[]{:S(2)}) collective-permute-start(bf16[256,512]{1,0:T(8,128)(2,1)S(1)} %collective-permute-done.3.refs_3_), channel_id=1, source_target_pairs={{2,0},{3,1},{0,4},{1,5},{4,6},{5,7},{6,2},{7,3},{10,8},{11,9},{8,1... | collective-permute-start | bytes 786440 | tf_op jit(solution)/shard_map/ppermute | solution.py:348
  15.0 0.9 %copy-done.3 = bf16[1,256,512]{2,1,0:T(8,128)(2,1)S(1)} copy-done((bf16[1,256,512]{2,1,0:T(8,128)(2,1)S(1)}, bf16[1,256,512]{2,1,0:T(8,128)(2,1)}, u32[]{:S(2)}) %copy-start.3) | copy-done | bytes 262168
  16.0 1.6 %collective-permute-start.10 = (bf16[1,256,256]{2,1,0:T(8,128)(2,1)S(1)}, bf16[1,256,256]{2,1,0:T(8,128)(2,1)S(1)}, u32[]{:S(2)}, u32[]{:S(2)}) collective-permute-start(bf16[1,256,256]{2,1,0:T(8,128)(2,1)S(1)} %partner_columns.2), channel_id=1, source_target_pairs={{0,16},{8,24},{16,0},{24,8},{1,17},{9,25},{17,1},{25,9},{2,18},{10... | collective-permute-start | bytes 393224 | tf_op jit(solution)/shard_map/ppermute | solution.py:107
  17.6 2.2 %collective-permute-done.1.refs_0_.refs_2_ = bf16[2,256,256]{2,1,0:T(8,128)(2,1)S(1)} collective-permute-done((bf16[2,256,256]{2,1,0:T(8,128)(2,1)S(1)}, bf16[2,256,256]{2,1,0:T(8,128)(2,1)S(1)}, u32[]{:S(2)}, u32[]{:S(2)}) %collective-permute-start.1) | collective-permute-done | bytes 262176 | tf_op jit(solution)/shard_map/ppermute | solution.py:354
  20.3 0.7 %collective-permute-done.10.refs_1_ = bf16[1,256,256]{2,1,0:T(8,128)(2,1)S(1)} collective-permute-done((bf16[1,256,256]{2,1,0:T(8,128)(2,1)S(1)}, bf16[1,256,256]{2,1,0:T(8,128)(2,1)S(1)}, u32[]{:S(2)}, u32[]{:S(2)}) %collective-permute-start.10) | collective-permute-done | bytes 131104 | tf_op jit(solution)/shard_map/ppermute | solution.py:107
  21.2 2.8 %collective-permute-done.2.refs_1_.refs_2_ = bf16[2,256,256]{2,1,0:T(8,128)(2,1)S(1)} collective-permute-done((bf16[2,256,256]{2,1,0:T(8,128)(2,1)S(1)}, bf16[2,256,256]{2,1,0:T(8,128)(2,1)S(1)}, u32[]{:S(2)}, u32[]{:S(2)}) %collective-permute-start.2) | collective-permute-done | bytes 262176 | tf_op jit(solution)/shard_map/ppermute | solution.py:354
  23.9 1.5 %products.1 = (f32[256,512]{1,0:T(8,128)S(1)}, f32[256,512]{1,0:T(8,128)S(1)}, bf16[3,256,256]{2,1,0:T(8,128)(2,1)S(1)}, bf16[256,2048]{1,0:T(8,128)(2,1)}, f32[8,128]{1,0:T(8,128)S(1)}) custom-call(bf16[256,2048]{1,0:T(8,128)(2,1)S(1)} %bitcast.8, bf16[256,512]{1,0:T(8,128)(2,1)S(1)} %bitcast.13, ...), custom_call_target="tpu_custom_call" | custom-call | flops 805306368 | bytes 8388608 | tf_op jit(solution)/shard_map/products/pallas_call | solution.py:280
  25.4 1.6 %collective-permute-start.6 = (bf16[3,256,256]{2,1,0:T(8,128)(2,1)S(1)}, bf16[3,256,256]{2,1,0:T(8,128)(2,1)S(1)}, u32[]{:S(2)}, u32[]{:S(2)}) collective-permute-start(bf16[3,256,256]{2,1,0:T(8,128)(2,1)S(1)} %get-tuple-element.30), channel_id=1, source_target_pairs={{0,1},{1,0},{2,3},{3,2},{4,5},{5,4},{6,7},{7,6},{8,9},{9,8},{10,11... | collective-permute-start | bytes 1179656 | tf_op jit(solution)/shard_map/ppermute | solution.py:354
  27.0 1.6 %last_products.1 = (f32[256,512]{1,0:T(8,128)S(1)}, f32[8,128]{1,0:T(8,128)}, bf16[3,256,256]{2,1,0:T(8,128)(2,1)S(1)}, bf16[256,2048]{1,0:T(8,128)(2,1)}, f32[8,128]{1,0:T(8,128)S(1)}) custom-call(bf16[256,2048]{1,0:T(8,128)(2,1)S(1)} %bitcast.9, bf16[256,512]{1,0:T(8,128)(2,1)S(1)} %bitcast.14, ...), custom_call_target="tpu_custom_call", output_to_operand_aliasing={{3}: (8, {})} | custom-call | flops 268435456 | bytes 8388608 | tf_op jit(solution)/shard_map/last_products/pallas_call | solution.py:280
  29.2 1.6 %collective-permute-start.8 = (bf16[256,512]{1,0:T(8,128)(2,1)S(1)}, bf16[256,512]{1,0:T(8,128)(2,1)S(1)}, u32[]{:S(2)}, u32[]{:S(2)}) collective-permute-start(bf16[256,512]{1,0:T(8,128)(2,1)S(1)} %get-tuple-element.36.refs_3_), channel_id=1, source_target_pairs={{2,0},{3,1},{0,4},{1,5},{4,6},{5,7},{6,2},{7,3},{10,8},{11,9},{8,1... | collective-permute-start | bytes 786440 | tf_op jit(solution)/shard_map/ppermute | solution.py:348
  31.3 1.1 %outer_update.1 = (bf16[256,128]{1,0:T(8,128)(2,1)S(1)}, f32[256,128]{1,0:T(8,128)}) custom-call(bf16[256,512]{1,0:T(8,128)(2,1)S(1)} %bitcast.21, bf16[1,256,256]{2,1,0:T(8,128)(2,1)S(1)} %collective-permute-done.10.refs_1_, bf16[2,256,128]{2,1,0:T(8,128)(2,1)S(1)} %collective-permute-done.11.refs_2_, bf16[256,512]{1,0:T(8,128)(2,1)S(1)} %copy-done.5, ...), custom_call_target="tpu_custom_call" | custom-call | bytes 917504 | tf_op jit(solution)/shard_map/outer_update/pallas_call | solution.py:49
  32.4 1.5 %collective-permute-start.13 = (bf16[256,128]{1,0:T(8,128)(2,1)S(1)}, bf16[256,128]{1,0:T(8,128)(2,1)S(1)}, u32[]{:S(2)}, u32[]{:S(2)}) collective-permute-start(bf16[256,128]{1,0:T(8,128)(2,1)S(1)} %get-tuple-element.40.refs_2_), channel_id=1, source_target_pairs={{0,16},{8,24},{16,0},{24,8},{1,17},{9,25},{17,1},{25,9},{2,18},{10... | collective-permute-start | bytes 196616 | tf_op jit(solution)/shard_map/ppermute | solution.py:107
  34.5 2.1 %collective-permute-done.13 = bf16[256,128]{1,0:T(8,128)(2,1)S(1)} collective-permute-done((bf16[256,128]{1,0:T(8,128)(2,1)S(1)}, bf16[256,128]{1,0:T(8,128)(2,1)S(1)}, u32[]{:S(2)}, u32[]{:S(2)}) %collective-permute-start.13) | collective-permute-done | bytes 65568 | tf_op jit(solution)/shard_map/ppermute | solution.py:107
  36.8 1.3 %collective-permute-done.14.refs_1_ = bf16[256,256]{1,0:T(8,128)(2,1)S(1)} collective-permute-done((bf16[256,256]{1,0:T(8,128)(2,1)S(1)}, bf16[256,256]{1,0:T(8,128)(2,1)S(1)}, u32[]{:S(2)}, u32[]{:S(2)}) %collective-permute-start.14) | collective-permute-done | bytes 131104 | tf_op jit(solution)/shard_map/ppermute | solution.py:107
  38.1 0.8 %join_shares.1 = bf16[256,512]{1,0:T(8,128)(2,1)} custom-call(bf16[256,256]{1,0:T(8,128)(2,1)S(1)} %constant_dynamic-update-slice_fusion.refs_0_, bf16[256,256]{1,0:T(8,128)(2,1)S(1)} %collective-permute-done.14.refs_1_, f32[8,128]{1,0:T(8,128)S(1)} %get-tuple-element.41.refs_2_), custom_call_target="tpu_custom_call" | custom-call | bytes 262144 | tf_op jit(solution)/shard_map/join_shares/pallas_call | solution.py:49
  38.9 3.1 %collective-permute-done.12.refs_2_ = bf16[256,512]{1,0:T(8,128)(2,1)S(1)} collective-permute-done((bf16[256,512]{1,0:T(8,128)(2,1)S(1)}, bf16[256,512]{1,0:T(8,128)(2,1)S(1)}, u32[]{:S(2)}, u32[]{:S(2)}) %collective-permute-start.12) | collective-permute-done | bytes 262176 | tf_op jit(solution)/shard_map/ppermute | solution.py:351
  42.0 0.8 %end_terms.1 = bf16[256,512]{1,0:T(8,128)(2,1)} custom-call(f32[256,512]{1,0:T(8,128)S(1)} %get-tuple-element.35.refs_0_, bf16[256,512]{1,0:T(8,128)(2,1)S(1)} %collective-permute-done.8.refs_1_, bf16[256,512]{1,0:T(8,128)(2,1)S(1)} %collective-permute-done.12.refs_2_), custom_call_target="tpu_custom_call" | custom-call | bytes 1048576 | tf_op jit(solution)/shard_map/end_terms/pallas_call | solution.py:49
  42.8 0.8 %collective-permute-done.7.late_ref = bf16[3,256,256]{2,1,0:T(8,128)(2,1)S(1)} collective-permute-done((bf16[3,256,256]{2,1,0:T(8,128)(2,1)S(1)}, bf16[3,256,256]{2,1,0:T(8,128)(2,1)S(1)}, u32[]{:S(2)}, u32[]{:S(2)}) %collective-permute-start.7) | collective-permute-done | bytes 393248 | tf_op jit(solution)/shard_map/ppermute | solution.py:354
  43.6 1.6 %collect.1 = (bf16[256,512]{1,0:T(8,128)(2,1)}, bf16[256,2048]{1,0:T(8,128)(2,1)}, f32[8,128]{1,0:T(8,128)}) custom-call(f32[256,512]{1,0:T(8,128)S(1)} %get-tuple-element.29.total_ref, bf16[3,256,256]{2,1,0:T(8,128)(2,1)S(1)} %collective-permute-done.6.early_ref, ...), custom_call_target="tpu_custom_call", output_to_operand_aliasing={{1}: (3, {})} | custom-call | flops 131072 | bytes 8388608 | tf_op jit(solution)/shard_map/collect/pallas_call | solution.py:326
  (34 shorter events, 3.1 us)
Async XLA Ops:
  0.6 11.1 %collective-permute-start.3 = (bf16[256,512]{1,0:T(8,128)(2,1)}, bf16[256,512]{1,0:T(8,128)(2,1)S(1)}, u32[]{:S(2)}, u32[]{:S(2)}) collective-permute-start(bf16[256,512]{1,0:T(8,128)(2,1)} %bitcast.16), channel_id=1, source_target_pairs={{2,0},{3,1},{0,4},{1,5},{4,6},{5,7},{6,2},{7,3},{10,8},{11,9},{8,1... | collective-permute-start | bytes 786440 | tf_op jit(solution)/shard_map/ppermute | solution.py:348
  4.7 11.3 %collective-permute-start = (bf16[256,512]{1,0:T(8,128)(2,1)}, bf16[256,512]{1,0:T(8,128)(2,1)S(1)}, u32[]{:S(2)}, u32[]{:S(2)}) collective-permute-start(bf16[256,512]{1,0:T(8,128)(2,1)} %bitcast.11), channel_id=1, source_target_pairs={{0,1},{1,0},{2,3},{3,2},{4,5},{5,4},{6,7},{7,6},{8,9},{9,8},{10,11... | collective-permute-start | bytes 786440 | tf_op jit(solution)/shard_map/ppermute | solution.py:354
  6.2 1.2 %copy-start = (bf16[1,256,2048]{2,1,0:T(8,128)(2,1)S(1)}, bf16[1,256,2048]{2,1,0:T(8,128)(2,1)}, u32[]{:S(2)}) copy-start(bf16[1,256,2048]{2,1,0:T(8,128)(2,1)} %param.8) | copy-start | bytes 3145732
  7.4 12.3 %copy-start.1 = (bf16[1,256,2048]{2,1,0:T(8,128)(2,1)S(1)}, bf16[1,256,2048]{2,1,0:T(8,128)(2,1)}, u32[]{:S(2)}) copy-start(bf16[1,256,2048]{2,1,0:T(8,128)(2,1)} %param.8) | copy-start | bytes 3145732
  7.5 12.3 %collective-permute-start.1 = (bf16[2,256,256]{2,1,0:T(8,128)(2,1)S(1)}, bf16[2,256,256]{2,1,0:T(8,128)(2,1)S(1)}, u32[]{:S(2)}, u32[]{:S(2)}) collective-permute-start(bf16[2,256,256]{2,1,0:T(8,128)(2,1)S(1)} %get-tuple-element.24.refs_1_), channel_id=1, source_target_pairs={{0,1},{1,0},{2,3},{3,2},{4,5},{5,4},{6,7},{7,6},{8,9},{9,8},{10,11... | collective-permute-start | bytes 786440 | tf_op jit(solution)/shard_map/ppermute | solution.py:354
  8.1 11.7 %copy-start.2 = (bf16[1,256,512]{2,1,0:T(8,128)(2,1)S(1)}, bf16[1,256,512]{2,1,0:T(8,128)(2,1)}, u32[]{:S(2)}) copy-start(bf16[1,256,512]{2,1,0:T(8,128)(2,1)} %param.9) | copy-start | bytes 786436
  8.1 15.8 %collective-permute-start.2 = (bf16[2,256,256]{2,1,0:T(8,128)(2,1)S(1)}, bf16[2,256,256]{2,1,0:T(8,128)(2,1)S(1)}, u32[]{:S(2)}, u32[]{:S(2)}) collective-permute-start(bf16[2,256,256]{2,1,0:T(8,128)(2,1)S(1)} %get-tuple-element.25.refs_2_), channel_id=1, source_target_pairs={{0,1},{1,0},{2,3},{3,2},{4,5},{5,4},{6,7},{7,6},{8,9},{9,8},{10,11... | collective-permute-start | bytes 786440 | tf_op jit(solution)/shard_map/ppermute | solution.py:354
  9.6 14.3 %collective-permute-start.5 = (bf16[256,512]{1,0:T(8,128)(2,1)}, bf16[256,512]{1,0:T(8,128)(2,1)S(1)}, u32[]{:S(2)}, u32[]{:S(2)}) collective-permute-start(bf16[256,512]{1,0:T(8,128)(2,1)} %bitcast.17), channel_id=1, source_target_pairs={{0,2},{1,3},{4,0},{5,1},{6,4},{7,5},{2,6},{3,7},{8,10},{9,11},{12,... | collective-permute-start | bytes 786440 | tf_op jit(solution)/shard_map/ppermute | solution.py:351
  11.7 15.3 %collective-permute-start.4 = (bf16[256,512]{1,0:T(8,128)(2,1)S(1)}, bf16[256,512]{1,0:T(8,128)(2,1)S(1)}, u32[]{:S(2)}, u32[]{:S(2)}) collective-permute-start(bf16[256,512]{1,0:T(8,128)(2,1)S(1)} %collective-permute-done.3.refs_3_), channel_id=1, source_target_pairs={{2,0},{3,1},{0,4},{1,5},{4,6},{5,7},{6,2},{7,3},{10,8},{11,9},{8,1... | collective-permute-start | bytes 786440 | tf_op jit(solution)/shard_map/ppermute | solution.py:348
  15.0 0.9 %copy-start.3 = (bf16[1,256,512]{2,1,0:T(8,128)(2,1)S(1)}, bf16[1,256,512]{2,1,0:T(8,128)(2,1)}, u32[]{:S(2)}) copy-start(bf16[1,256,512]{2,1,0:T(8,128)(2,1)} %param.5) | copy-start | bytes 786436
  16.0 5.1 %copy-start.4 = (bf16[1,256,512]{2,1,0:T(8,128)(2,1)S(1)}, bf16[1,256,512]{2,1,0:T(8,128)(2,1)}, u32[]{:S(2)}) copy-start(bf16[1,256,512]{2,1,0:T(8,128)(2,1)} %param.5) | copy-start | bytes 786436
  16.0 5.0 %collective-permute-start.10 = (bf16[1,256,256]{2,1,0:T(8,128)(2,1)S(1)}, bf16[1,256,256]{2,1,0:T(8,128)(2,1)S(1)}, u32[]{:S(2)}, u32[]{:S(2)}) collective-permute-start(bf16[1,256,256]{2,1,0:T(8,128)(2,1)S(1)} %partner_columns.2), channel_id=1, source_target_pairs={{0,16},{8,24},{16,0},{24,8},{1,17},{9,25},{17,1},{25,9},{2,18},{10... | collective-permute-start | bytes 393224 | tf_op jit(solution)/shard_map/ppermute | solution.py:107
  20.3 13.7 %collective-permute-start.9 = (bf16[256,512]{1,0:T(8,128)(2,1)S(1)}, bf16[256,512]{1,0:T(8,128)(2,1)S(1)}, u32[]{:S(2)}, u32[]{:S(2)}) collective-permute-start(bf16[256,512]{1,0:T(8,128)(2,1)S(1)} %get-tuple-element.38.refs_2_), channel_id=1, source_target_pairs={{0,2},{1,3},{4,0},{5,1},{6,4},{7,5},{2,6},{3,7},{8,10},{9,11},{12,... | collective-permute-start | bytes 786440 | tf_op jit(solution)/shard_map/ppermute | solution.py:351
  21.1 10.2 %collective-permute-start.11 = (bf16[2,256,128]{2,1,0:T(8,128)(2,1)S(1)}, bf16[2,256,128]{2,1,0:T(8,128)(2,1)S(1)}, u32[]{:S(2)}, u32[]{:S(2)}) collective-permute-start(bf16[2,256,128]{2,1,0:T(8,128)(2,1)S(1)} %partner_columns.3), channel_id=1, source_target_pairs={{0,8},{8,0},{16,24},{24,16},{1,9},{9,1},{17,25},{25,17},{2,10},{10... | collective-permute-start | bytes 393224 | tf_op jit(solution)/shard_map/ppermute | solution.py:107
  25.4 17.3 %collective-permute-start.6 = (bf16[3,256,256]{2,1,0:T(8,128)(2,1)S(1)}, bf16[3,256,256]{2,1,0:T(8,128)(2,1)S(1)}, u32[]{:S(2)}, u32[]{:S(2)}) collective-permute-start(bf16[3,256,256]{2,1,0:T(8,128)(2,1)S(1)} %get-tuple-element.30), channel_id=1, source_target_pairs={{0,1},{1,0},{2,3},{3,2},{4,5},{5,4},{6,7},{7,6},{8,9},{9,8},{10,11... | collective-permute-start | bytes 1179656 | tf_op jit(solution)/shard_map/ppermute | solution.py:354
  28.6 2.7 %copy-start.5 = (bf16[256,512]{1,0:T(8,128)(2,1)S(1)}, bf16[256,512]{1,0:T(8,128)(2,1)}, u32[]{:S(2)}) copy-start(bf16[256,512]{1,0:T(8,128)(2,1)} %refs_3_.1) | copy-start | bytes 786436
  28.6 2.7 %copy-start.6 = (f32[256,128]{1,0:T(8,128)S(1)}, f32[256,128]{1,0:T(8,128)}, u32[]{:S(2)}) copy-start(f32[256,128]{1,0:T(8,128)} %refs_4_.1) | copy-start | bytes 393220
  28.6 15.0 %collective-permute-start.7 = (bf16[3,256,256]{2,1,0:T(8,128)(2,1)S(1)}, bf16[3,256,256]{2,1,0:T(8,128)(2,1)S(1)}, u32[]{:S(2)}, u32[]{:S(2)}) collective-permute-start(bf16[3,256,256]{2,1,0:T(8,128)(2,1)S(1)} %get-tuple-element.31), channel_id=1, source_target_pairs={{0,1},{1,0},{2,3},{3,2},{4,5},{5,4},{6,7},{7,6},{8,9},{9,8},{10,11... | collective-permute-start | bytes 1179656 | tf_op jit(solution)/shard_map/ppermute | solution.py:354
  29.2 9.6 %collective-permute-start.8 = (bf16[256,512]{1,0:T(8,128)(2,1)S(1)}, bf16[256,512]{1,0:T(8,128)(2,1)S(1)}, u32[]{:S(2)}, u32[]{:S(2)}) collective-permute-start(bf16[256,512]{1,0:T(8,128)(2,1)S(1)} %get-tuple-element.36.refs_3_), channel_id=1, source_target_pairs={{2,0},{3,1},{0,4},{1,5},{4,6},{5,7},{6,2},{7,3},{10,8},{11,9},{8,1... | collective-permute-start | bytes 786440 | tf_op jit(solution)/shard_map/ppermute | solution.py:348
  32.4 4.3 %collective-permute-start.13 = (bf16[256,128]{1,0:T(8,128)(2,1)S(1)}, bf16[256,128]{1,0:T(8,128)(2,1)S(1)}, u32[]{:S(2)}, u32[]{:S(2)}) collective-permute-start(bf16[256,128]{1,0:T(8,128)(2,1)S(1)} %get-tuple-element.40.refs_2_), channel_id=1, source_target_pairs={{0,16},{8,24},{16,0},{24,8},{1,17},{9,25},{17,1},{25,9},{2,18},{10... | collective-permute-start | bytes 196616 | tf_op jit(solution)/shard_map/ppermute | solution.py:107
  34.0 8.0 %collective-permute-start.12 = (bf16[256,512]{1,0:T(8,128)(2,1)S(1)}, bf16[256,512]{1,0:T(8,128)(2,1)S(1)}, u32[]{:S(2)}, u32[]{:S(2)}) collective-permute-start(bf16[256,512]{1,0:T(8,128)(2,1)S(1)} %add_terms.1), channel_id=1, source_target_pairs={{0,2},{1,3},{4,0},{5,1},{6,4},{7,5},{2,6},{3,7},{8,10},{9,11},{12,... | collective-permute-start | bytes 786440 | tf_op jit(solution)/shard_map/ppermute | solution.py:351
  36.7 1.4 %collective-permute-start.14 = (bf16[256,256]{1,0:T(8,128)(2,1)S(1)}, bf16[256,256]{1,0:T(8,128)(2,1)S(1)}, u32[]{:S(2)}, u32[]{:S(2)}) collective-permute-start(bf16[256,256]{1,0:T(8,128)(2,1)S(1)} %constant_dynamic-update-slice_fusion.refs_0_), channel_id=1, source_target_pairs={{0,8},{8,0},{16,24},{24,16},{1,9},{9,1},{17,25},{25,17},{2,10},{10... | collective-permute-start | bytes 393224 | tf_op jit(solution)/shard_map/ppermute | solution.py:107

commit v7 on v6

--- a/solution.py
+++ b/solution.py
@@ -17,7 +17,6 @@
 BF16 = jnp.bfloat16
 LANES = 128
 VMEM_BYTES = 8 * 2**20
-PRODUCTS_BYTES = 8 * 2**20
 
 
 def ring_order(size):
@@ -188,16 +187,17 @@
 PARTNER = {2: (0, 0), 1: (0, 1), 3: (1, 0), 0: (1, 1)}
 
 
-def pack_kernel(size, inputs_ref, *out_refs):
+def pack_kernel(size, part, inputs_ref, out_ref):
     depth = inputs_ref.shape[1] // size
     for offset, (at, slot) in PARTNER.items():
-        out_refs[at][slot] = inputs_ref[:, pl.ds(block_start(offset, size, depth, 1), depth)]
-
-
-def pack(inputs_here, size):
+        if at == part:
+            out_ref[slot] = inputs_ref[:, pl.ds(block_start(offset, size, depth, 1), depth)]
+
+
+def pack(inputs_here, size, part, after=()):
     tokens, width = inputs_here.shape
-    shapes = [jax.ShapeDtypeStruct((2, tokens, width // size), BF16)] * 2
-    return vmem_call(functools.partial(pack_kernel, size), shapes, [inputs_here], 0, "pack_columns")
+    shape = jax.ShapeDtypeStruct((2, tokens, width // size), BF16)
+    return vmem_call(functools.partial(pack_kernel, size, part), shape, [inputs_here], 0, "pack_columns", after)
 
 
 def terms_kernel(size, offsets, token_weight, inputs_ref, cotangent_ref, partner_ref, partner_cotangent_ref, *out_refs):
@@ -235,112 +235,135 @@
     out_ref[...] = (terms_ref[...] + up_ref[...].astype(F32) + down_ref[...].astype(F32)).astype(BF16)
 
 
-def products_kernel(size, offsets, last, inputs_ref, cotangent_ref, partner_cotangent_ref, *refs):
-    partner_refs, block_refs, refs = refs[:2], refs[2 : 2 + len(offsets)], refs[2 + len(offsets) :]
-    total_refs = refs[:2] if last else ()
-    here_ref, there_ref, leaving_ref, grad_ref, mark_ref, held, sems = refs[-7:]
+def back_product(cotangent, block):
+    return lax.dot_general(cotangent, block, (((1,), (1,)), ((), ())), preferred_element_type=F32).astype(BF16)
+
+
+def grads_kernel(cotangent_ref, partner_cotangent_ref, *refs):
+    *block_refs, here_ref, leaving_ref = refs
+    for number, block_ref in enumerate(block_refs):
+        here_ref[number] = back_product(cotangent_ref[...], block_ref[...])
+        leaving_ref[number] = back_product(partner_cotangent_ref[...], block_ref[...])
+
+
+def near_grads(cotangent, partner_cotangent, blocks, after):
+    tokens, kv_width = cotangent.shape
+    depth = blocks[0].shape[0]
+    shape = jax.ShapeDtypeStruct((len(blocks), tokens, depth), BF16)
+    operands = [cotangent, partner_cotangent, *blocks.values()]
+    flops = 4 * tokens * depth * len(blocks) * kv_width
+    return vmem_call(grads_kernel, [shape] * 2, operands, flops, "near_grads", after)
+
+
+def rows_kernel(size, offsets, inputs_ref, *refs):
+    partner_refs, block_refs, (here_ref, there_ref) = refs[:2], refs[2:-2], refs[-2:]
     depth = inputs_ref.shape[1] // size
-    copies = []
-    for number, (offset, block_ref) in enumerate(zip(offsets, block_refs)):
-        for cotangent, out_ref in ((partner_cotangent_ref, leaving_ref), (cotangent_ref, held)):
-            out_ref[number] = lax.dot_general(
-                cotangent[...], block_ref[...], (((1,), (1,)), ((), ())), preferred_element_type=F32
-            ).astype(BF16)
-        columns = pl.ds(block_start(offset, size, depth), depth)
-        copies.append(pltpu.make_async_copy(held.at[number], grad_ref.at[:, columns], sems.at[number]))
-        copies[-1].start()
-    there, here = (total_refs[1][...], total_refs[0][...]) if last else (0.0, 0.0)
+    here = there = 0.0
     for offset, block_ref in zip(offsets, block_refs):
         at, slot = PARTNER[offset]
-        there = there + jnp.dot(partner_refs[at][slot], block_ref[...], preferred_element_type=F32)
         columns = inputs_ref[:, pl.ds(block_start(offset, size, depth), depth)]
         here = here + jnp.dot(columns, block_ref[...], preferred_element_type=F32)
-    here_ref[...] = here
-    if last:
-        for part in range(there.shape[1] // depth):
-            leaving_ref[len(offsets) + part] = there[:, part * depth : (part + 1) * depth].astype(BF16)
-    else:
-        there_ref[...] = there
+        there = there + jnp.dot(partner_refs[at][slot], block_ref[...], preferred_element_type=F32)
+    here_ref[...], there_ref[...] = here, there
+
+
+def near_rows(inputs_here, partner_inputs, blocks, size, after):
+    tokens, kv_width = inputs_here.shape[0], blocks[0].shape[1]
+    return vmem_call(
+        functools.partial(rows_kernel, size, list(blocks)),
+        [shape_of(tokens, kv_width, F32)] * 2,
+        [inputs_here, *partner_inputs, *blocks.values()],
+        4 * tokens * blocks[0].shape[0] * len(blocks) * kv_width,
+        "near_rows",
+        after,
+    )
+
+
+def last_kernel(
+    size, offset, inputs_ref, cotangent_ref, partner_ref, partner_cotangent_ref, block_ref, here_ref, there_ref, *outs
+):
+    rows_ref, grad_ref, leaving_ref = outs
+    depth = block_ref.shape[0]
+    leaving_ref[0] = back_product(partner_cotangent_ref[...], block_ref[...])
+    there = there_ref[...] + jnp.dot(
+        partner_ref[PARTNER[offset][1]], block_ref[...], preferred_element_type=F32
+    )
+    for part in range(there.shape[1] // depth):
+        leaving_ref[1 + part] = there[:, part * depth : (part + 1) * depth].astype(BF16)
+    grad_ref[0] = back_product(cotangent_ref[...], block_ref[...])
+    columns = inputs_ref[:, pl.ds(block_start(offset, size, depth), depth)]
+    rows_ref[...] = here_ref[...] + jnp.dot(columns, block_ref[...], preferred_element_type=F32)
+
+
+def last_products(inputs_here, cotangent, partner_inputs, partner_cotangent, block, totals, size, offset):
+    tokens = inputs_here.shape[0]
+    depth, kv_width = block.shape
+    return vmem_call(
+        functools.partial(last_kernel, size, offset),
+        [
+            shape_of(tokens, kv_width, F32),
+            jax.ShapeDtypeStruct((1, tokens, depth), BF16),
+            jax.ShapeDtypeStruct((1 + kv_width // depth, tokens, depth), BF16),
+        ],
+        [inputs_here, cotangent, partner_inputs[PARTNER[offset][0]], partner_cotangent, block, *totals],
+        8 * tokens * depth * kv_width,
+        "last_products",
+    )
+
+
+def write_columns(size, sources, grad_ref, sems):
+    depth = grad_ref.shape[1] // size
+    copies = []
+    for source_ref, number, offset, other in sources:
+        columns = pl.ds(block_start(offset, size, depth, other), depth)
+        copies.append(pltpu.make_async_copy(source_ref.at[number], grad_ref.at[:, columns], sems.at[len(copies)]))
+        copies[-1].start()
+    return copies
+
+
+def collect_kernel(size, offsets, near_ref, last_ref, early_ref, *refs):
+    grad_ref, mark_ref, sems = refs[-3:]
+    sources = [(near_ref, number, offset, 0) for number, offset in enumerate(offsets[:-1])]
+    sources += [(last_ref, 0, offsets[-1], 0)]
+    sources += [(early_ref, number, offset, 1) for number, offset in enumerate(offsets[:-1])]
+    copies = write_columns(size, sources, grad_ref, sems)
     mark_ref[...] = jnp.zeros_like(mark_ref)
     for copy in copies:
         copy.wait()
 
 
-def products(inputs_here, cotangent, partner_cotangent, partner_inputs, blocks, size, before=None):
-    tokens, width = inputs_here.shape
-    kv_width = cotangent.shape[1]
-    depth = width // size
-    last = before is not None
-    leaving = len(blocks) + (kv_width // depth if last else 0)
-    operands = [inputs_here, cotangent, partner_cotangent, *partner_inputs, *blocks.values()]
-    operands += [before[0], before[1], before[3]] if last else []
-    whole, anywhere = pl.BlockSpec(memory_space=pltpu.VMEM), pl.BlockSpec(memory_space=pl.ANY)
-    total = shape_of(tokens, kv_width, F32)
-    mark = shape_of(8, LANES, F32)
-    return pl.pallas_call(
-        functools.partial(products_kernel, size, list(blocks), last),
-        out_shape=(
-            total,
-            mark if last else total,
-            jax.ShapeDtypeStruct((leaving, tokens, depth), BF16),
-            shape_of(tokens, width, BF16),
-            mark,
-        ),
-        in_specs=[whole] * (5 + len(blocks)) + ([whole, whole, anywhere] if last else []),
-        out_specs=(whole, whole, whole, anywhere, whole),
-        scratch_shapes=[
-            pltpu.VMEM((len(blocks), tokens, depth), BF16),
-            pltpu.SemaphoreType.DMA((len(blocks),)),
-        ],
-        input_output_aliases={len(operands) - 1: 3} if last else {},
-        compiler_params=pltpu.CompilerParams(vmem_limit_bytes=VMEM_BYTES),
-        cost_estimate=pl.CostEstimate(
-            flops=8 * tokens * depth * len(blocks) * kv_width, bytes_accessed=PRODUCTS_BYTES, transcendentals=0
-        ),
-        name="last_products" if last else "products",
-    )(*operands)
-
-
-def collect_kernel(size, offsets, total_ref, early_ref, late_ref, _, rows_ref, grad_ref, mark_ref, sems):
-    depth = early_ref.shape[-1]
-    parts = total_ref.shape[1] // depth
-    copies = []
-    for number, offset in enumerate(offsets):
-        late = number - early_ref.shape[0]
-        source = early_ref.at[number] if late < 0 else late_ref.at[late]
-        columns = pl.ds(block_start(offset, size, depth, 1), depth)
-        copies.append(pltpu.make_async_copy(source, grad_ref.at[:, columns], sems.at[number]))
-        copies[-1].start()
-    for part in range(parts):
+def collect_last_kernel(size, offset, total_ref, late_ref, _, rows_ref, grad_ref, sems):
+    copies = write_columns(size, [(late_ref, 0, offset, 1)], grad_ref, sems)
+    depth = late_ref.shape[-1]
+    for part in range(total_ref.shape[1] // depth):
         columns = slice(part * depth, (part + 1) * depth)
-        arrived = late_ref[late_ref.shape[0] - parts + part].astype(F32)
-        rows_ref[:, columns] = (total_ref[:, columns] + arrived).astype(BF16)
-    mark_ref[...] = jnp.zeros_like(mark_ref)
+        rows_ref[:, columns] = (total_ref[:, columns] + late_ref[1 + part].astype(F32)).astype(BF16)
     for copy in copies:
         copy.wait()
 
 
-def collect(total, early, late, grad, offsets, size):
-    tokens, kv_width = total.shape
+def collect(kernel, out_shape, operands, grad, count, name, after=()):
     whole, anywhere = pl.BlockSpec(memory_space=pltpu.VMEM), pl.BlockSpec(memory_space=pl.ANY)
+    given = [] if grad is None else [grad]
     return pl.pallas_call(
-        functools.partial(collect_kernel, size, offsets),
-        out_shape=(shape_of(tokens, kv_width, BF16), shape_of(*grad.shape, BF16), shape_of(8, LANES, F32)),
-        in_specs=[whole] * 3 + [anywhere],
-        out_specs=(whole, anywhere, whole),
-        scratch_shapes=[pltpu.SemaphoreType.DMA((len(offsets),))],
-        input_output_aliases={3: 1},
+        kernel,
+        out_shape=out_shape,
+        in_specs=[whole] * len(operands) + [anywhere] * (len(given) + len(after)),
+        out_specs=(anywhere, whole) if grad is None else (whole, anywhere),
+        scratch_shapes=[pltpu.SemaphoreType.DMA((count,))],
+        input_output_aliases={} if grad is None else {len(operands): 1},
         compiler_params=pltpu.CompilerParams(vmem_limit_bytes=VMEM_BYTES),
-        cost_estimate=pl.CostEstimate(flops=tokens * kv_width, bytes_accessed=PRODUCTS_BYTES, transcendentals=0),
-        name="collect",
-    )(total, early, late, grad)
+        cost_estimate=pl.CostEstimate(flops=0, bytes_accessed=2**20, transcendentals=0),
+        name=name,
+    )(*operands, *given, *after)
 
 
 def inner_and_outer(local_shard, global_weights, momentum, inputs_here, cotangent):
     depth, kv_width = local_shard.shape
+    tokens, width = inputs_here.shape
     size = lax.axis_size("fsdp")
     ring = size // 2
-    token_weight = 1.0 / (inputs_here.shape[0] * size)
+    token_weight = 1.0 / (tokens * size)
     order = ring_order(ring)
     pairs = [(2 * order[at - 1] + side, 2 * order[at] + side) for at in range(ring) for side in (0, 1)]
 
@@ -355,43 +378,62 @@
 
     from_below, from_above = upward(local_shard), downward(local_shard)
     partner_cotangent = across(cotangent)
-    packed = pack(inputs_here, size)
-    partner_inputs = [across(part) for part in packed]
+    packed = pack(inputs_here, size, 0)
+    partner_inputs = [across(packed), across(pack(inputs_here, size, 1, (partner_cotangent,)))]
 
     bits = lax.axis_size("replica") // 2
-    held = send_windows([local_shard], bits, kv_width, packed)
+    held = send_windows([local_shard], bits, kv_width, (packed,))
 
     blocks = {0: local_shard, 3: from_below, 1: from_above}
+    farthest = upward(from_below)
     operands = [inputs_here, cotangent, partner_inputs[0], partner_cotangent]
     first = token_terms(operands, size, [2, 1], BF16, token_weight)
     sum_down, sum_up = downward(first[0]), upward(first[1])
-    farthest = upward(from_below)
     while bits > 1:
         bits //= 2
         held = send_windows(held, bits, kv_width, first)
+    grads, leaving = near_grads(cotangent, partner_cotangent, blocks, first)
+    early = across(leaving)
     operands[2] = partner_inputs[1]
-    terms = token_terms(operands, size, [3, 0], F32, token_weight)
-    made = products(inputs_here, cotangent, partner_cotangent, partner_inputs, blocks, size)
-    early = across(made[2])
-    new_share, new_momentum = update_share(held, global_weights, momentum, (made[4],))
-    bits = lax.axis_size("replica") // 2
-    shares, joined = [new_share, swap(new_share, bits)], [0, bits]
+    terms = token_terms(operands, size, [3, 0], F32, token_weight, (leaving,))
+    totals = near_rows(inputs_here, partner_inputs, blocks, size, (leaving,))
+    rows, last_grads, leaving = last_products(
+        inputs_here, cotangent, partner_inputs, partner_cotangent, farthest, totals, size, 2
+    )
+    late = across(leaving)
     total_down = vmem_call(
-        add_kernel, shape_of(depth, kv_width, BF16), [terms[0], sum_down], 0, "add_terms", (new_share,)
+        add_kernel, shape_of(depth, kv_width, BF16), [terms[0], sum_down], 0, "add_terms", (leaving,)
     )
     sum_down = downward(total_down)
-    made = products(inputs_here, cotangent, partner_cotangent, partner_inputs, {2: farthest}, size, made)
-    late = across(made[2])
+    new_share, new_momentum = update_share(held, global_weights, momentum, (total_down,))
+    bits = lax.axis_size("replica")
+    shares, joined = [new_share], [0]
     while bits > 1:
         bits //= 2
-        shares = [jnp.concatenate(shares, axis=1)]
+        shares = [shares[0] if len(shares) == 1 else jnp.concatenate(shares, axis=1)]
         shares.append(swap(shares[0], bits))
         joined += [place ^ bits for place in joined]
-    new_global = join_shares(shares, joined, kv_width, (made[4],))
+    offsets = [*blocks, 2]
+    grad, mark = collect(
+        functools.partial(collect_kernel, size, offsets),
+        (shape_of(tokens, width, BF16), shape_of(8, LANES, F32)),
+        [grads, last_grads, early],
+        None,
+        2 * len(offsets) - 1,
+        "collect",
+    )
+    new_global = join_shares(shares, joined, kv_width, (mark,))
     grad_rows = vmem_call(
         end_kernel, shape_of(depth, kv_width, BF16), [terms[1], sum_up, sum_down], 0, "end_terms", ()
     )
-    kv_rows, grad_in, mark = collect(made[0], early, late, made[3], [*blocks, 2], size)
+    kv_rows, grad_in = collect(
+        functools.partial(collect_last_kernel, size, offsets[-1]),
+        (shape_of(tokens, kv_width, BF16), shape_of(tokens, width, BF16)),
+        [rows, late],
+        grad,
+        1,
+        "collect_last",
+    )
     return kv_rows, grad_in, grad_rows, new_global, new_momentum
 
 

time: 45.3 us -> 44 us (0.971)
  waiting for transfers between devices: 15.3 us -> 14.3 us
  starting transfers between devices: 18.5 us -> 19.4 us
  Pallas kernels: 8.37 us -> 7.67 us
  local copies, waits for them, and re-layouts: 2.23 us -> 1.72 us
    ppermute x5, waiting for transfers between devices: 5.81 us -> 2.41 us  [across(): return lax.ppermute(array, 'fsdp', [(at, at ^ 1) for at in range(size)])]
    ppermute x3, waiting for transfers between devices: 3.11 us -> 6.27 us  [downward(): lax.ppermute(array, 'fsdp', [(target, source) for source, target in pairs])]
    ppermute x5, starting transfers between devices: 5.75 us -> 8.07 us  [across(): return lax.ppermute(array, 'fsdp', [(at, at ^ 1) for at in range(size)])]
    pallas_call x3 -> x2, Pallas kernels: 4.65 us -> 2.38 us  [collect(): pl.pallas_call(kernel, out_shape=out_shape, in_specs=[whole] * len(operan...]
    ppermute x3, starting transfers between devices: 8.93 us -> 6.7 us  [upward(): return lax.ppermute(array, 'fsdp', pairs)]
    ppermute x3, waiting for transfers between devices: 2.14 us -> 0.18 us  [upward(): return lax.ppermute(array, 'fsdp', pairs)]
    pallas_call x9 -> x13, Pallas kernels: 3.72 us -> 5.29 us  [vmem_call(): pl.pallas_call(body, out_shape=out_shape, in_specs=[whole] * len(operands...]
    ppermute x4, waiting for transfers between devices: 4.21 us -> 5.45 us  [swap(): lax.ppermute(array, 'replica', [(at, at ^ bits) for at in range(lax.axis_...]
  transfers between devices with their start and end apart: 15 -> 15, of which waited for: 8 -> 8; matrix products, arithmetic and copies ran while one was open for 0% -> 0% of each run, Pallas kernels for 15% -> 14%
where the time goes in v7:
time: 44 us; the launch traced here: 43.8 us
  starting transfers between devices  19.4 us (44%)
  waiting for transfers between devices  14.3 us (32%)
  Pallas kernels  7.67 us (17%)
  local copies, waits for them, and re-layouts  1.72 us (4%)
  between operations  0.77 us (2%)
    ppermute x5, starting transfers between devices, across(): return lax.ppermute(array, 'fsdp', [(at, at ^ 1) for at in range(size)])  8.07 us
    ppermute x3, starting transfers between devices, upward(): return lax.ppermute(array, 'fsdp', pairs)  6.7 us
    ppermute x3, waiting for transfers between devices, downward(): lax.ppermute(array, 'fsdp', [(target, source) for source, target in pairs])  6.27 us
    ppermute x4, waiting for transfers between devices, swap(): lax.ppermute(array, 'replica', [(at, at ^ bits) for at in range(lax.axis_...  5.45 us
    pallas_call x13, Pallas kernels, vmem_call(): pl.pallas_call(body, out_shape=out_shape, in_specs=[whole] * len(operands...  5.29 us
    ppermute x4, starting transfers between devices, swap(): lax.ppermute(array, 'replica', [(at, at ^ bits) for at in range(lax.axis_...  3.25 us
    ppermute x5, waiting for transfers between devices, across(): return lax.ppermute(array, 'fsdp', [(at, at ^ 1) for at in range(size)])  2.41 us
    pallas_call x2, Pallas kernels, collect(): pl.pallas_call(kernel, out_shape=out_shape, in_specs=[whole] * len(operan...  2.38 us
  transfers between devices with their start and end apart: 15, of which 8 were waited for; matrix products, arithmetic and copies ran while one was open for 0% of the time, Pallas kernels for 14%

profile of v7, /device:TPU:0, one launch (start us, length us, event | category | flops | bytes accessed | tf_op | source)
XLA Modules:
  0.0 43.8 jit_solution(16111893340923889802)
XLA Ops:
  0.6 3.0 %collective-permute-start.1 = (bf16[256,512]{1,0:T(8,128)(2,1)}, bf16[256,512]{1,0:T(8,128)(2,1)S(1)}, u32[]{:S(2)}, u32[]{:S(2)}) collective-permute-start(bf16[256,512]{1,0:T(8,128)(2,1)} %bitcast.19), channel_id=1, source_target_pairs={{0,1},{1,0},{2,3},{3,2},{4,5},{5,4},{6,7},{7,6},{8,9},{9,8},{10,11... | collective-permute-start | bytes 786440 | tf_op jit(solution)/shard_map/ppermute | solution.py:377
  3.6 2.6 %collective-permute-start.2 = (bf16[256,512]{1,0:T(8,128)(2,1)}, bf16[256,512]{1,0:T(8,128)(2,1)S(1)}, u32[]{:S(2)}, u32[]{:S(2)}) collective-permute-start(bf16[256,512]{1,0:T(8,128)(2,1)} %bitcast.12), channel_id=1, source_target_pairs={{2,0},{3,1},{0,4},{1,5},{4,6},{5,7},{6,2},{7,3},{10,8},{11,9},{8,1... | collective-permute-start | bytes 786440 | tf_op jit(solution)/shard_map/ppermute | solution.py:371
  6.2 1.2 %copy-done = bf16[1,256,2048]{2,1,0:T(8,128)(2,1)S(1)} copy-done((bf16[1,256,2048]{2,1,0:T(8,128)(2,1)S(1)}, bf16[1,256,2048]{2,1,0:T(8,128)(2,1)}, u32[]{:S(2)}) %copy-start) | copy-done | bytes 1048600
  7.5 0.6 %collective-permute-start = (bf16[2,256,256]{2,1,0:T(8,128)(2,1)S(1)}, bf16[2,256,256]{2,1,0:T(8,128)(2,1)S(1)}, u32[]{:S(2)}, u32[]{:S(2)}) collective-permute-start(bf16[2,256,256]{2,1,0:T(8,128)(2,1)S(1)} %pack_columns.2.refs_1_), channel_id=1, source_target_pairs={{0,1},{1,0},{2,3},{3,2},{4,5},{5,4},{6,7},{7,6},{8,9},{9,8},{10,11... | collective-permute-start | bytes 786440 | tf_op jit(solution)/shard_map/ppermute | solution.py:377
  8.4 2.4 %collective-permute-done.1.refs_1_.refs_3_ = bf16[256,512]{1,0:T(8,128)(2,1)S(1)} collective-permute-done((bf16[256,512]{1,0:T(8,128)(2,1)}, bf16[256,512]{1,0:T(8,128)(2,1)S(1)}, u32[]{:S(2)}, u32[]{:S(2)}) %collective-permute-start.1) | collective-permute-done | bytes 262176 | tf_op jit(solution)/shard_map/ppermute | solution.py:377
  10.9 2.3 %collective-permute-start.4 = (bf16[2,256,256]{2,1,0:T(8,128)(2,1)S(1)}, bf16[2,256,256]{2,1,0:T(8,128)(2,1)S(1)}, u32[]{:S(2)}, u32[]{:S(2)}) collective-permute-start(bf16[2,256,256]{2,1,0:T(8,128)(2,1)S(1)} %pack_columns.3), channel_id=1, source_target_pairs={{0,1},{1,0},{2,3},{3,2},{4,5},{5,4},{6,7},{7,6},{8,9},{9,8},{10,11... | collective-permute-start | bytes 786440 | tf_op jit(solution)/shard_map/ppermute | solution.py:377
  13.3 3.3 %collective-permute-start.3 = (bf16[256,512]{1,0:T(8,128)(2,1)S(1)}, bf16[256,512]{1,0:T(8,128)(2,1)S(1)}, u32[]{:S(2)}, u32[]{:S(2)}) collective-permute-start(bf16[256,512]{1,0:T(8,128)(2,1)S(1)} %collective-permute-done.2.refs_3_.refs_4_), channel_id=1, source_target_pairs={{2,0},{3,1},{0,4},{1,5},{4,6},{5,7},{6,2},{7,3},{10,8},{11,9},{8,1... | collective-permute-start | bytes 786440 | tf_op jit(solution)/shard_map/ppermute | solution.py:371
  16.6 1.6 %collective-permute-start.11 = (bf16[1,256,256]{2,1,0:T(8,128)(2,1)S(1)}, bf16[1,256,256]{2,1,0:T(8,128)(2,1)S(1)}, u32[]{:S(2)}, u32[]{:S(2)}) collective-permute-start(bf16[1,256,256]{2,1,0:T(8,128)(2,1)S(1)} %partner_columns.2), channel_id=1, source_target_pairs={{0,16},{8,24},{16,0},{24,8},{1,17},{9,25},{17,1},{25,9},{2,18},{10... | collective-permute-start | bytes 393224 | tf_op jit(solution)/shard_map/ppermute | solution.py:106
  18.7 0.6 %collective-permute-start.9 = (bf16[256,512]{1,0:T(8,128)(2,1)S(1)}, bf16[256,512]{1,0:T(8,128)(2,1)S(1)}, u32[]{:S(2)}, u32[]{:S(2)}) collective-permute-start(bf16[256,512]{1,0:T(8,128)(2,1)S(1)} %get-tuple-element.22.refs_5_.refs_2_), channel_id=1, source_target_pairs={{0,2},{1,3},{4,0},{5,1},{6,4},{7,5},{2,6},{3,7},{8,10},{9,11},{12,... | collective-permute-start | bytes 786440 | tf_op jit(solution)/shard_map/ppermute | solution.py:374
  19.3 2.4 %collective-permute-done.11.refs_1_ = bf16[1,256,256]{2,1,0:T(8,128)(2,1)S(1)} collective-permute-done((bf16[1,256,256]{2,1,0:T(8,128)(2,1)S(1)}, bf16[1,256,256]{2,1,0:T(8,128)(2,1)S(1)}, u32[]{:S(2)}, u32[]{:S(2)}) %collective-permute-start.11) | collective-permute-done | bytes 131104 | tf_op jit(solution)/shard_map/ppermute | solution.py:106
  21.8 2.5 %collective-permute-done.5.refs_4_.refs_5_ = bf16[256,512]{1,0:T(8,128)(2,1)S(1)} collective-permute-done((bf16[256,512]{1,0:T(8,128)(2,1)S(1)}, bf16[256,512]{1,0:T(8,128)(2,1)S(1)}, u32[]{:S(2)}, u32[]{:S(2)}) %collective-permute-start.5) | collective-permute-done | bytes 262176 | tf_op jit(solution)/shard_map/ppermute | solution.py:374
  24.3 0.6 %near_grads.1 = (bf16[3,256,256]{2,1,0:T(8,128)(2,1)S(1)}, bf16[3,256,256]{2,1,0:T(8,128)(2,1)S(1)}) custom-call(bf16[256,512]{1,0:T(8,128)(2,1)S(1)} %bitcast.21, bf16[256,512]{1,0:T(8,128)(2,1)S(1)} %collective-permute-done.1.refs_1_.refs_3_, bf16[256,512]{1,0:T(8,128)(2,1)S(1)} %bitcast.16, bf16[256,512]{1,0:T(8,128)(2,1)S(1)} %collective-permute-done.2.refs_3_.refs_4_, ...), custom_call_target="tpu_custom_call" | custom-call | flops 402653184 | bytes 1310720 | tf_op jit(solution)/shard_map/near_grads/pallas_call | solution.py:48
  26.2 1.9 %collective-permute-start.6 = (bf16[3,256,256]{2,1,0:T(8,128)(2,1)S(1)}, bf16[3,256,256]{2,1,0:T(8,128)(2,1)S(1)}, u32[]{:S(2)}, u32[]{:S(2)}) collective-permute-start(bf16[3,256,256]{2,1,0:T(8,128)(2,1)S(1)} %get-tuple-element.28.refs_2_), channel_id=1, source_target_pairs={{0,1},{1,0},{2,3},{3,2},{4,5},{5,4},{6,7},{7,6},{8,9},{9,8},{10,11... | collective-permute-start | bytes 1179656 | tf_op jit(solution)/shard_map/ppermute | solution.py:377
  28.1 0.8 %collective-permute-start.8 = (bf16[256,512]{1,0:T(8,128)(2,1)S(1)}, bf16[256,512]{1,0:T(8,128)(2,1)S(1)}, u32[]{:S(2)}, u32[]{:S(2)}) collective-permute-start(bf16[256,512]{1,0:T(8,128)(2,1)S(1)} %get-tuple-element.23.refs_6_.refs_3_), channel_id=1, source_target_pairs={{2,0},{3,1},{0,4},{1,5},{4,6},{5,7},{6,2},{7,3},{10,8},{11,9},{8,1... | collective-permute-start | bytes 786440 | tf_op jit(solution)/shard_map/ppermute | solution.py:371
  29.4 2.5 %collective-permute-done.9.refs_1_ = bf16[256,512]{1,0:T(8,128)(2,1)S(1)} collective-permute-done((bf16[256,512]{1,0:T(8,128)(2,1)S(1)}, bf16[256,512]{1,0:T(8,128)(2,1)S(1)}, u32[]{:S(2)}, u32[]{:S(2)}) %collective-permute-start.9) | collective-permute-done | bytes 262176 | tf_op jit(solution)/shard_map/ppermute | solution.py:374
  31.9 0.8 %collective-permute-start.10 = (bf16[256,512]{1,0:T(8,128)(2,1)S(1)}, bf16[256,512]{1,0:T(8,128)(2,1)S(1)}, u32[]{:S(2)}, u32[]{:S(2)}) collective-permute-start(bf16[256,512]{1,0:T(8,128)(2,1)S(1)} %add_terms.1.refs_5_), channel_id=1, source_target_pairs={{0,2},{1,3},{4,0},{5,1},{6,4},{7,5},{2,6},{3,7},{8,10},{9,11},{12,... | collective-permute-start | bytes 786440 | tf_op jit(solution)/shard_map/ppermute | solution.py:374
  32.9 1.1 %outer_update.1 = (bf16[256,128]{1,0:T(8,128)(2,1)S(1)}, f32[256,128]{1,0:T(8,128)}) custom-call(bf16[256,512]{1,0:T(8,128)(2,1)S(1)} %bitcast.18, bf16[1,256,256]{2,1,0:T(8,128)(2,1)S(1)} %collective-permute-done.11.refs_1_, bf16[2,256,128]{2,1,0:T(8,128)(2,1)S(1)} %collective-permute-done.12.refs_2_, bf16[256,512]{1,0:T(8,128)(2,1)S(1)} %copy-done.4, ...), custom_call_target="tpu_custom_call" | custom-call | bytes 917504 | tf_op jit(solution)/shard_map/outer_update/pallas_call | solution.py:48
  33.9 1.5 %collective-permute-start.13 = (bf16[256,128]{1,0:T(8,128)(2,1)S(1)}, bf16[256,128]{1,0:T(8,128)(2,1)S(1)}, u32[]{:S(2)}, u32[]{:S(2)}) collective-permute-start(bf16[256,128]{1,0:T(8,128)(2,1)S(1)} %get-tuple-element.36), channel_id=1, source_target_pairs={{0,16},{8,24},{16,0},{24,8},{1,17},{9,25},{17,1},{25,9},{2,18},{10... | collective-permute-start | bytes 196616 | tf_op jit(solution)/shard_map/ppermute | solution.py:106
  35.5 2.7 %collective-permute-done.13 = bf16[256,128]{1,0:T(8,128)(2,1)S(1)} collective-permute-done((bf16[256,128]{1,0:T(8,128)(2,1)S(1)}, bf16[256,128]{1,0:T(8,128)(2,1)S(1)}, u32[]{:S(2)}, u32[]{:S(2)}) %collective-permute-start.13) | collective-permute-done | bytes 65568 | tf_op jit(solution)/shard_map/ppermute | solution.py:106
  38.3 1.0 %collect.1 = (bf16[256,2048]{1,0:T(8,128)(2,1)}, f32[8,128]{1,0:T(8,128)S(1)}) custom-call(bf16[3,256,256]{2,1,0:T(8,128)(2,1)S(1)} %get-tuple-element.29.near_ref, bf16[1,256,256]{2,1,0:T(8,128)(2,1)S(1)} %get-tuple-element.30.last_ref, bf16[3,256,256]{2,1,0:T(8,128)(2,1)S(1)} %collective-permute-done.7.early_ref), custom_call_target="tpu_custom_call" | custom-call | bytes 1048576 | tf_op jit(solution)/shard_map/collect/pallas_call | solution.py:348
  39.6 0.8 %join_shares.1 = bf16[256,512]{1,0:T(8,128)(2,1)} custom-call(bf16[256,256]{1,0:T(8,128)(2,1)S(1)} %constant_dynamic-update-slice_fusion.refs_0_, bf16[256,256]{1,0:T(8,128)(2,1)S(1)} %collective-permute-done.14.refs_1_, f32[8,128]{1,0:T(8,128)S(1)} %get-tuple-element.37.refs_2_), custom_call_target="tpu_custom_call" | custom-call | bytes 262144 | tf_op jit(solution)/shard_map/join_shares/pallas_call | solution.py:48
  40.4 1.2 %collective-permute-done.10.refs_2_ = bf16[256,512]{1,0:T(8,128)(2,1)S(1)} collective-permute-done((bf16[256,512]{1,0:T(8,128)(2,1)S(1)}, bf16[256,512]{1,0:T(8,128)(2,1)S(1)}, u32[]{:S(2)}, u32[]{:S(2)}) %collective-permute-start.10) | collective-permute-done | bytes 262176 | tf_op jit(solution)/shard_map/ppermute | solution.py:374
  41.7 0.8 %end_terms.1 = bf16[256,512]{1,0:T(8,128)(2,1)} custom-call(f32[256,512]{1,0:T(8,128)S(1)} %get-tuple-element.34.refs_0_, bf16[256,512]{1,0:T(8,128)(2,1)S(1)} %collective-permute-done.8.refs_1_, bf16[256,512]{1,0:T(8,128)(2,1)S(1)} %collective-permute-done.10.refs_2_), custom_call_target="tpu_custom_call" | custom-call | bytes 1048576 | tf_op jit(solution)/shard_map/end_terms/pallas_call | solution.py:48
  42.4 1.4 %collect_last.1 = (bf16[256,512]{1,0:T(8,128)(2,1)}, bf16[256,2048]{1,0:T(8,128)(2,1)}) custom-call(f32[256,512]{1,0:T(8,128)S(1)} %get-tuple-element.27.total_ref, bf16[3,256,256]{2,1,0:T(8,128)(2,1)S(1)} %collective-permute-done.6.late_ref, bf16[256,2048]{1,0:T(8,128)(2,1)} %get-tuple-element.31._), custom_call_target="tpu_custom_call", output_to_operand_aliasing={{1}: (2, {})} | custom-call | bytes 1048576 | tf_op jit(solution)/shard_map/collect_last/pallas_call | solution.py:348
  (35 shorter events, 3.5 us)
Async XLA Ops:
  0.6 10.2 %collective-permute-start.1 = (bf16[256,512]{1,0:T(8,128)(2,1)}, bf16[256,512]{1,0:T(8,128)(2,1)S(1)}, u32[]{:S(2)}, u32[]{:S(2)}) collective-permute-start(bf16[256,512]{1,0:T(8,128)(2,1)} %bitcast.19), channel_id=1, source_target_pairs={{0,1},{1,0},{2,3},{3,2},{4,5},{5,4},{6,7},{7,6},{8,9},{9,8},{10,11... | collective-permute-start | bytes 786440 | tf_op jit(solution)/shard_map/ppermute | solution.py:377
  3.6 9.7 %collective-permute-start.2 = (bf16[256,512]{1,0:T(8,128)(2,1)}, bf16[256,512]{1,0:T(8,128)(2,1)S(1)}, u32[]{:S(2)}, u32[]{:S(2)}) collective-permute-start(bf16[256,512]{1,0:T(8,128)(2,1)} %bitcast.12), channel_id=1, source_target_pairs={{2,0},{3,1},{0,4},{1,5},{4,6},{5,7},{6,2},{7,3},{10,8},{11,9},{8,1... | collective-permute-start | bytes 786440 | tf_op jit(solution)/shard_map/ppermute | solution.py:371
  6.2 1.2 %copy-start = (bf16[1,256,2048]{2,1,0:T(8,128)(2,1)S(1)}, bf16[1,256,2048]{2,1,0:T(8,128)(2,1)}, u32[]{:S(2)}) copy-start(bf16[1,256,2048]{2,1,0:T(8,128)(2,1)} %param.8) | copy-start | bytes 3145732
  7.4 0.9 %copy-start.2 = (bf16[1,256,512]{2,1,0:T(8,128)(2,1)S(1)}, bf16[1,256,512]{2,1,0:T(8,128)(2,1)}, u32[]{:S(2)}) copy-start(bf16[1,256,512]{2,1,0:T(8,128)(2,1)} %param.5) | copy-start | bytes 786436
  7.5 10.7 %copy-start.1 = (bf16[1,256,2048]{2,1,0:T(8,128)(2,1)S(1)}, bf16[1,256,2048]{2,1,0:T(8,128)(2,1)}, u32[]{:S(2)}) copy-start(bf16[1,256,2048]{2,1,0:T(8,128)(2,1)} %param.8) | copy-start | bytes 3145732
  7.5 10.7 %collective-permute-start = (bf16[2,256,256]{2,1,0:T(8,128)(2,1)S(1)}, bf16[2,256,256]{2,1,0:T(8,128)(2,1)S(1)}, u32[]{:S(2)}, u32[]{:S(2)}) collective-permute-start(bf16[2,256,256]{2,1,0:T(8,128)(2,1)S(1)} %pack_columns.2.refs_1_), channel_id=1, source_target_pairs={{0,1},{1,0},{2,3},{3,2},{4,5},{5,4},{6,7},{7,6},{8,9},{9,8},{10,11... | collective-permute-start | bytes 786440 | tf_op jit(solution)/shard_map/ppermute | solution.py:377
  8.4 15.9 %collective-permute-start.5 = (bf16[256,512]{1,0:T(8,128)(2,1)S(1)}, bf16[256,512]{1,0:T(8,128)(2,1)S(1)}, u32[]{:S(2)}, u32[]{:S(2)}) collective-permute-start(bf16[256,512]{1,0:T(8,128)(2,1)S(1)} %bitcast.13), channel_id=1, source_target_pairs={{0,2},{1,3},{4,0},{5,1},{6,4},{7,5},{2,6},{3,7},{8,10},{9,11},{12,... | collective-permute-start | bytes 786440 | tf_op jit(solution)/shard_map/ppermute | solution.py:374
  10.8 7.4 %copy-start.3 = (bf16[1,256,512]{2,1,0:T(8,128)(2,1)S(1)}, bf16[1,256,512]{2,1,0:T(8,128)(2,1)}, u32[]{:S(2)}) copy-start(bf16[1,256,512]{2,1,0:T(8,128)(2,1)} %param.9) | copy-start | bytes 786436
  10.9 14.3 %collective-permute-start.4 = (bf16[2,256,256]{2,1,0:T(8,128)(2,1)S(1)}, bf16[2,256,256]{2,1,0:T(8,128)(2,1)S(1)}, u32[]{:S(2)}, u32[]{:S(2)}) collective-permute-start(bf16[2,256,256]{2,1,0:T(8,128)(2,1)S(1)} %pack_columns.3), channel_id=1, source_target_pairs={{0,1},{1,0},{2,3},{3,2},{4,5},{5,4},{6,7},{7,6},{8,9},{9,8},{10,11... | collective-permute-start | bytes 786440 | tf_op jit(solution)/shard_map/ppermute | solution.py:377
  13.3 12.4 %collective-permute-start.3 = (bf16[256,512]{1,0:T(8,128)(2,1)S(1)}, bf16[256,512]{1,0:T(8,128)(2,1)S(1)}, u32[]{:S(2)}, u32[]{:S(2)}) collective-permute-start(bf16[256,512]{1,0:T(8,128)(2,1)S(1)} %collective-permute-done.2.refs_3_.refs_4_), channel_id=1, source_target_pairs={{2,0},{3,1},{0,4},{1,5},{4,6},{5,7},{6,2},{7,3},{10,8},{11,9},{8,1... | collective-permute-start | bytes 786440 | tf_op jit(solution)/shard_map/ppermute | solution.py:371
  16.6 5.0 %collective-permute-start.11 = (bf16[1,256,256]{2,1,0:T(8,128)(2,1)S(1)}, bf16[1,256,256]{2,1,0:T(8,128)(2,1)S(1)}, u32[]{:S(2)}, u32[]{:S(2)}) collective-permute-start(bf16[1,256,256]{2,1,0:T(8,128)(2,1)S(1)} %partner_columns.2), channel_id=1, source_target_pairs={{0,16},{8,24},{16,0},{24,8},{1,17},{9,25},{17,1},{25,9},{2,18},{10... | collective-permute-start | bytes 393224 | tf_op jit(solution)/shard_map/ppermute | solution.py:106
  18.7 13.2 %collective-permute-start.9 = (bf16[256,512]{1,0:T(8,128)(2,1)S(1)}, bf16[256,512]{1,0:T(8,128)(2,1)S(1)}, u32[]{:S(2)}, u32[]{:S(2)}) collective-permute-start(bf16[256,512]{1,0:T(8,128)(2,1)S(1)} %get-tuple-element.22.refs_5_.refs_2_), channel_id=1, source_target_pairs={{0,2},{1,3},{4,0},{5,1},{6,4},{7,5},{2,6},{3,7},{8,10},{9,11},{12,... | collective-permute-start | bytes 786440 | tf_op jit(solution)/shard_map/ppermute | solution.py:374
  21.7 11.0 %collective-permute-start.12 = (bf16[2,256,128]{2,1,0:T(8,128)(2,1)S(1)}, bf16[2,256,128]{2,1,0:T(8,128)(2,1)S(1)}, u32[]{:S(2)}, u32[]{:S(2)}) collective-permute-start(bf16[2,256,128]{2,1,0:T(8,128)(2,1)S(1)} %partner_columns.3), channel_id=1, source_target_pairs={{0,8},{8,0},{16,24},{24,16},{1,9},{9,1},{17,25},{25,17},{2,10},{10... | collective-permute-start | bytes 393224 | tf_op jit(solution)/shard_map/ppermute | solution.py:106
  24.9 13.4 %collective-permute-start.7 = (bf16[3,256,256]{2,1,0:T(8,128)(2,1)S(1)}, bf16[3,256,256]{2,1,0:T(8,128)(2,1)S(1)}, u32[]{:S(2)}, u32[]{:S(2)}) collective-permute-start(bf16[3,256,256]{2,1,0:T(8,128)(2,1)S(1)} %get-tuple-element.24.refs_6_.refs_4_), channel_id=1, source_target_pairs={{0,1},{1,0},{2,3},{3,2},{4,5},{5,4},{6,7},{7,6},{8,9},{9,8},{10,11... | collective-permute-start | bytes 1179656 | tf_op jit(solution)/shard_map/ppermute | solution.py:377
  26.2 16.3 %collective-permute-start.6 = (bf16[3,256,256]{2,1,0:T(8,128)(2,1)S(1)}, bf16[3,256,256]{2,1,0:T(8,128)(2,1)S(1)}, u32[]{:S(2)}, u32[]{:S(2)}) collective-permute-start(bf16[3,256,256]{2,1,0:T(8,128)(2,1)S(1)} %get-tuple-element.28.refs_2_), channel_id=1, source_target_pairs={{0,1},{1,0},{2,3},{3,2},{4,5},{5,4},{6,7},{7,6},{8,9},{9,8},{10,11... | collective-permute-start | bytes 1179656 | tf_op jit(solution)/shard_map/ppermute | solution.py:377
  28.1 12.3 %collective-permute-start.8 = (bf16[256,512]{1,0:T(8,128)(2,1)S(1)}, bf16[256,512]{1,0:T(8,128)(2,1)S(1)}, u32[]{:S(2)}, u32[]{:S(2)}) collective-permute-start(bf16[256,512]{1,0:T(8,128)(2,1)S(1)} %get-tuple-element.23.refs_6_.refs_3_), channel_id=1, source_target_pairs={{2,0},{3,1},{0,4},{1,5},{4,6},{5,7},{6,2},{7,3},{10,8},{11,9},{8,1... | collective-permute-start | bytes 786440 | tf_op jit(solution)/shard_map/ppermute | solution.py:371
  31.9 1.0 %copy-start.4 = (bf16[256,512]{1,0:T(8,128)(2,1)S(1)}, bf16[256,512]{1,0:T(8,128)(2,1)}, u32[]{:S(2)}) copy-start(bf16[256,512]{1,0:T(8,128)(2,1)} %refs_3_.1) | copy-start | bytes 786436
  31.9 1.0 %copy-start.5 = (f32[256,128]{1,0:T(8,128)S(1)}, f32[256,128]{1,0:T(8,128)}, u32[]{:S(2)}) copy-start(f32[256,128]{1,0:T(8,128)} %refs_4_.1) | copy-start | bytes 393220
  31.9 9.7 %collective-permute-start.10 = (bf16[256,512]{1,0:T(8,128)(2,1)S(1)}, bf16[256,512]{1,0:T(8,128)(2,1)S(1)}, u32[]{:S(2)}, u32[]{:S(2)}) collective-permute-start(bf16[256,512]{1,0:T(8,128)(2,1)S(1)} %add_terms.1.refs_5_), channel_id=1, source_target_pairs={{0,2},{1,3},{4,0},{5,1},{6,4},{7,5},{2,6},{3,7},{8,10},{9,11},{12,... | collective-permute-start | bytes 786440 | tf_op jit(solution)/shard_map/ppermute | solution.py:374
  33.9 4.3 %collective-permute-start.13 = (bf16[256,128]{1,0:T(8,128)(2,1)S(1)}, bf16[256,128]{1,0:T(8,128)(2,1)S(1)}, u32[]{:S(2)}, u32[]{:S(2)}) collective-permute-start(bf16[256,128]{1,0:T(8,128)(2,1)S(1)} %get-tuple-element.36), channel_id=1, source_target_pairs={{0,16},{8,24},{16,0},{24,8},{1,17},{9,25},{17,1},{25,9},{2,18},{10... | collective-permute-start | bytes 196616 | tf_op jit(solution)/shard_map/ppermute | solution.py:106
  38.2 1.4 %collective-permute-start.14 = (bf16[256,256]{1,0:T(8,128)(2,1)S(1)}, bf16[256,256]{1,0:T(8,128)(2,1)S(1)}, u32[]{:S(2)}, u32[]{:S(2)}) collective-permute-start(bf16[256,256]{1,0:T(8,128)(2,1)S(1)} %constant_dynamic-update-slice_fusion.refs_0_), channel_id=1, source_target_pairs={{0,8},{8,0},{16,24},{24,16},{1,9},{9,1},{17,25},{25,17},{2,10},{10... | collective-permute-start | bytes 393224 | tf_op jit(solution)/shard_map/ppermute | solution.py:106

commit v8 on v7

--- a/solution.py
+++ b/solution.py
@@ -231,10 +231,6 @@
     out_ref[...] = (terms_ref[...] + sum_ref[...].astype(F32)).astype(BF16)
 
 
-def end_kernel(terms_ref, up_ref, down_ref, out_ref):
-    out_ref[...] = (terms_ref[...] + up_ref[...].astype(F32) + down_ref[...].astype(F32)).astype(BF16)
-
-
 def back_product(cotangent, block):
     return lax.dot_general(cotangent, block, (((1,), (1,)), ((), ())), preferred_element_type=F32).astype(BF16)
 
@@ -279,33 +275,34 @@
     )
 
 
-def last_kernel(
-    size, offset, inputs_ref, cotangent_ref, partner_ref, partner_cotangent_ref, block_ref, here_ref, there_ref, *outs
-):
-    rows_ref, grad_ref, leaving_ref = outs
-    depth = block_ref.shape[0]
-    leaving_ref[0] = back_product(partner_cotangent_ref[...], block_ref[...])
-    there = there_ref[...] + jnp.dot(
-        partner_ref[PARTNER[offset][1]], block_ref[...], preferred_element_type=F32
-    )
+def last_kernel(size, offsets, inputs_ref, cotangent_ref, partner_ref, partner_cotangent_ref, *refs):
+    block_refs, (here_ref, there_ref, rows_ref, grad_ref, leaving_ref) = refs[: len(offsets)], refs[len(offsets) :]
+    depth = block_refs[0].shape[0]
+    for number, block_ref in enumerate(block_refs):
+        leaving_ref[number] = back_product(partner_cotangent_ref[...], block_ref[...])
+    last = block_refs[-1][...]
+    there = there_ref[...] + jnp.dot(partner_ref[PARTNER[offsets[-1]][1]], last, preferred_element_type=F32)
     for part in range(there.shape[1] // depth):
-        leaving_ref[1 + part] = there[:, part * depth : (part + 1) * depth].astype(BF16)
-    grad_ref[0] = back_product(cotangent_ref[...], block_ref[...])
-    columns = inputs_ref[:, pl.ds(block_start(offset, size, depth), depth)]
-    rows_ref[...] = here_ref[...] + jnp.dot(columns, block_ref[...], preferred_element_type=F32)
-
-
-def last_products(inputs_here, cotangent, partner_inputs, partner_cotangent, block, totals, size, offset):
+        leaving_ref[len(offsets) + part] = there[:, part * depth : (part + 1) * depth].astype(BF16)
+    for number, block_ref in enumerate(block_refs):
+        grad_ref[number] = back_product(cotangent_ref[...], block_ref[...])
+    columns = inputs_ref[:, pl.ds(block_start(offsets[-1], size, depth), depth)]
+    rows_ref[...] = here_ref[...] + jnp.dot(columns, last, preferred_element_type=F32)
+
+
+def last_products(inputs_here, cotangent, partner_inputs, partner_cotangent, blocks, totals, size):
     tokens = inputs_here.shape[0]
-    depth, kv_width = block.shape
+    offsets = list(blocks)
+    depth, kv_width = blocks[offsets[-1]].shape
+    partner = partner_inputs[PARTNER[offsets[-1]][0]]
     return vmem_call(
-        functools.partial(last_kernel, size, offset),
+        functools.partial(last_kernel, size, offsets),
         [
             shape_of(tokens, kv_width, F32),
-            jax.ShapeDtypeStruct((1, tokens, depth), BF16),
-            jax.ShapeDtypeStruct((1 + kv_width // depth, tokens, depth), BF16),
+            jax.ShapeDtypeStruct((len(blocks), tokens, depth), BF16),
+            jax.ShapeDtypeStruct((len(blocks) + kv_width // depth, tokens, depth), BF16),
         ],
-        [inputs_here, cotangent, partner_inputs[PARTNER[offset][0]], partner_cotangent, block, *totals],
+        [inputs_here, cotangent, partner, partner_cotangent, *blocks.values(), *totals],
         8 * tokens * depth * kv_width,
         "last_products",
     )
@@ -321,41 +318,66 @@
     return copies
 
 
-def collect_kernel(size, offsets, near_ref, last_ref, early_ref, *refs):
-    grad_ref, mark_ref, sems = refs[-3:]
-    sources = [(near_ref, number, offset, 0) for number, offset in enumerate(offsets[:-1])]
-    sources += [(last_ref, 0, offsets[-1], 0)]
-    sources += [(early_ref, number, offset, 1) for number, offset in enumerate(offsets[:-1])]
+def collect_kernel(size, early, late, near_ref, last_ref, early_ref, grad_ref, mark_ref, sems):
+    sources = [(near_ref, number, offset, 0) for number, offset in enumerate(early)]
+    sources += [(last_ref, number, offset, 0) for number, offset in enumerate(late)]
+    sources += [(early_ref, number, offset, 1) for number, offset in enumerate(early)]
     copies = write_columns(size, sources, grad_ref, sems)
     mark_ref[...] = jnp.zeros_like(mark_ref)
     for copy in copies:
         copy.wait()
 
 
-def collect_last_kernel(size, offset, total_ref, late_ref, _, rows_ref, grad_ref, sems):
-    copies = write_columns(size, [(late_ref, 0, offset, 1)], grad_ref, sems)
+def collect(grads, width, size, early, late):
+    whole, anywhere = pl.BlockSpec(memory_space=pltpu.VMEM), pl.BlockSpec(memory_space=pl.ANY)
+    return pl.pallas_call(
+        functools.partial(collect_kernel, size, early, late),
+        out_shape=(shape_of(grads[0].shape[1], width, BF16), shape_of(8, LANES, F32)),
+        in_specs=[whole] * len(grads),
+        out_specs=(anywhere, whole),
+        scratch_shapes=[pltpu.SemaphoreType.DMA((2 * len(early) + len(late),))],
+        compiler_params=pltpu.CompilerParams(vmem_limit_bytes=VMEM_BYTES),
+        cost_estimate=pl.CostEstimate(flops=0, bytes_accessed=2**20, transcendentals=0),
+        name="collect",
+    )(*grads)
+
+
+def finish_kernel(size, late, total_ref, late_ref, terms_ref, up_ref, down_ref, _, *refs):
+    rows_ref, grad_ref, sum_ref, rows_held, sum_held, sems, sem_rows, sem_sum = refs
+    copies = write_columns(size, [(late_ref, number, offset, 1) for number, offset in enumerate(late)], grad_ref, sems)
     depth = late_ref.shape[-1]
     for part in range(total_ref.shape[1] // depth):
         columns = slice(part * depth, (part + 1) * depth)
-        rows_ref[:, columns] = (total_ref[:, columns] + late_ref[1 + part].astype(F32)).astype(BF16)
+        rows_held[:, columns] = (total_ref[:, columns] + late_ref[len(late) + part].astype(F32)).astype(BF16)
+    copies.append(pltpu.make_async_copy(rows_held, rows_ref, sem_rows))
+    copies[-1].start()
+    sum_held[...] = (terms_ref[...] + up_ref[...].astype(F32) + down_ref[...].astype(F32)).astype(BF16)
+    copies.append(pltpu.make_async_copy(sum_held, sum_ref, sem_sum))
+    copies[-1].start()
     for copy in copies:
         copy.wait()
 
 
-def collect(kernel, out_shape, operands, grad, count, name, after=()):
+def finish(total, late, sums, grad, size, offsets):
     whole, anywhere = pl.BlockSpec(memory_space=pltpu.VMEM), pl.BlockSpec(memory_space=pl.ANY)
-    given = [] if grad is None else [grad]
+    rows, summed = shape_of(*total.shape, BF16), shape_of(*sums[0].shape, BF16)
     return pl.pallas_call(
-        kernel,
-        out_shape=out_shape,
-        in_specs=[whole] * len(operands) + [anywhere] * (len(given) + len(after)),
-        out_specs=(anywhere, whole) if grad is None else (whole, anywhere),
-        scratch_shapes=[pltpu.SemaphoreType.DMA((count,))],
-        input_output_aliases={} if grad is None else {len(operands): 1},
+        functools.partial(finish_kernel, size, offsets),
+        out_shape=(rows, shape_of(*grad.shape, BF16), summed),
+        in_specs=[whole] * 5 + [anywhere],
+        out_specs=(anywhere,) * 3,
+        scratch_shapes=[
+            pltpu.VMEM(rows.shape, BF16),
+            pltpu.VMEM(summed.shape, BF16),
+            pltpu.SemaphoreType.DMA((len(offsets),)),
+            pltpu.SemaphoreType.DMA,
+            pltpu.SemaphoreType.DMA,
+        ],
+        input_output_aliases={5: 1},
         compiler_params=pltpu.CompilerParams(vmem_limit_bytes=VMEM_BYTES),
         cost_estimate=pl.CostEstimate(flops=0, bytes_accessed=2**20, transcendentals=0),
-        name=name,
-    )(*operands, *given, *after)
+        name="finish",
+    )(total, late, *sums, grad)
 
 
 def inner_and_outer(local_shard, global_weights, momentum, inputs_here, cotangent):
@@ -379,33 +401,32 @@
     from_below, from_above = upward(local_shard), downward(local_shard)
     partner_cotangent = across(cotangent)
     packed = pack(inputs_here, size, 0)
-    partner_inputs = [across(packed), across(pack(inputs_here, size, 1, (partner_cotangent,)))]
 
     bits = lax.axis_size("replica") // 2
     held = send_windows([local_shard], bits, kv_width, (packed,))
-
-    blocks = {0: local_shard, 3: from_below, 1: from_above}
-    farthest = upward(from_below)
+    partner_inputs = [across(packed), across(pack(inputs_here, size, 1, (partner_cotangent, from_below)))]
+
+    early_blocks, late_blocks = {0: local_shard, 3: from_below}, {1: from_above, 2: upward(from_below)}
     operands = [inputs_here, cotangent, partner_inputs[0], partner_cotangent]
     first = token_terms(operands, size, [2, 1], BF16, token_weight)
     sum_down, sum_up = downward(first[0]), upward(first[1])
     while bits > 1:
         bits //= 2
         held = send_windows(held, bits, kv_width, first)
-    grads, leaving = near_grads(cotangent, partner_cotangent, blocks, first)
+    near, leaving = near_grads(cotangent, partner_cotangent, early_blocks, (first[0], held[1]))
     early = across(leaving)
     operands[2] = partner_inputs[1]
     terms = token_terms(operands, size, [3, 0], F32, token_weight, (leaving,))
-    totals = near_rows(inputs_here, partner_inputs, blocks, size, (leaving,))
-    rows, last_grads, leaving = last_products(
-        inputs_here, cotangent, partner_inputs, partner_cotangent, farthest, totals, size, 2
+    totals = near_rows(inputs_here, partner_inputs, {**early_blocks, 1: from_above}, size, (leaving,))
+    rows, last, leaving = last_products(
+        inputs_here, cotangent, partner_inputs, partner_cotangent, late_blocks, totals, size
     )
     late = across(leaving)
     total_down = vmem_call(
         add_kernel, shape_of(depth, kv_width, BF16), [terms[0], sum_down], 0, "add_terms", (leaving,)
     )
     sum_down = downward(total_down)
-    new_share, new_momentum = update_share(held, global_weights, momentum, (total_down,))
+    new_share, new_momentum = update_share(held, global_weights, momentum, (total_down, early))
     bits = lax.axis_size("replica")
     shares, joined = [new_share], [0]
     while bits > 1:
@@ -413,26 +434,10 @@
         shares = [shares[0] if len(shares) == 1 else jnp.concatenate(shares, axis=1)]
         shares.append(swap(shares[0], bits))
         joined += [place ^ bits for place in joined]
-    offsets = [*blocks, 2]
-    grad, mark = collect(
-        functools.partial(collect_kernel, size, offsets),
-        (shape_of(tokens, width, BF16), shape_of(8, LANES, F32)),
-        [grads, last_grads, early],
-        None,
-        2 * len(offsets) - 1,
-        "collect",
-    )
+    grad, mark = collect([near, last, early], width, size, list(early_blocks), list(late_blocks))
     new_global = join_shares(shares, joined, kv_width, (mark,))
-    grad_rows = vmem_call(
-        end_kernel, shape_of(depth, kv_width, BF16), [terms[1], sum_up, sum_down], 0, "end_terms", ()
-    )
-    kv_rows, grad_in = collect(
-        functools.partial(collect_last_kernel, size, offsets[-1]),
-        (shape_of(tokens, kv_width, BF16), shape_of(tokens, width, BF16)),
-        [rows, late],
-        grad,
-        1,
-        "collect_last",
+    kv_rows, grad_in, grad_rows = finish(
+        rows, late, [terms[1], sum_up, sum_down], grad, size, list(late_blocks)
     )
     return kv_rows, grad_in, grad_rows, new_global, new_momentum
 

time: 44 us -> 44.5 us (1.011)
  waiting for transfers between devices: 14.3 us -> 15.8 us
  Pallas kernels: 7.67 us -> 6.41 us
    ppermute x3, waiting for transfers between devices: 0.18 us -> 2.76 us  [upward(): return lax.ppermute(array, 'fsdp', pairs)]
    ppermute x3, waiting for transfers between devices: 6.27 us -> 4.57 us  [downward(): lax.ppermute(array, 'fsdp', [(target, source) for source, target in pairs])]
    ppermute x3, starting transfers between devices: 6.7 us -> 7.71 us  [upward(): return lax.ppermute(array, 'fsdp', pairs)]
    pallas_call x13 -> x12, Pallas kernels: 5.29 us -> 4.54 us  [vmem_call(): pl.pallas_call(body, out_shape=out_shape, in_specs=[whole] * len(operands...]
    ppermute x4, waiting for transfers between devices: 5.45 us -> 6.02 us  [swap(): lax.ppermute(array, 'replica', [(at, at ^ bits) for at in range(lax.axis_...]
    ppermute x3, starting transfers between devices: 1.35 us -> 0.83 us  [downward(): lax.ppermute(array, 'fsdp', [(target, source) for source, target in pairs])]
    pallas_call x2, Pallas kernels: 2.38 us -> 1.87 us  [the longest x1 0.94 us: collect(): pl.pallas_call(functools.partial(collect_kernel, size, early, late), out_...]
  transfers between devices with their start and end apart: 15 -> 15, of which waited for: 8 -> 8; matrix products, arithmetic and copies ran while one was open for 0% -> 0% of each run, Pallas kernels for 14% -> 12%
where the time goes in v8:
time: 44.5 us; the launch traced here: 44.3 us
  starting transfers between devices  19.6 us (44%)
  waiting for transfers between devices  15.8 us (36%)
  Pallas kernels  6.41 us (14%)
  local copies, waits for them, and re-layouts  1.72 us (4%)
  between operations  0.76 us (2%)
    ppermute x5, starting transfers between devices, across(): return lax.ppermute(array, 'fsdp', [(at, at ^ 1) for at in range(size)])  7.84 us
    ppermute x3, starting transfers between devices, upward(): return lax.ppermute(array, 'fsdp', pairs)  7.71 us
    ppermute x4, waiting for transfers between devices, swap(): lax.ppermute(array, 'replica', [(at, at ^ bits) for at in range(lax.axis_...  6.02 us
    ppermute x3, waiting for transfers between devices, downward(): lax.ppermute(array, 'fsdp', [(target, source) for source, target in pairs])  4.57 us
    pallas_call x12, Pallas kernels, vmem_call(): pl.pallas_call(body, out_shape=out_shape, in_specs=[whole] * len(operands...  4.54 us
    ppermute x4, starting transfers between devices, swap(): lax.ppermute(array, 'replica', [(at, at ^ bits) for at in range(lax.axis_...  3.25 us
    ppermute x3, waiting for transfers between devices, upward(): return lax.ppermute(array, 'fsdp', pairs)  2.76 us
    ppermute x5, waiting for transfers between devices, across(): return lax.ppermute(array, 'fsdp', [(at, at ^ 1) for at in range(size)])  2.41 us
  transfers between devices with their start and end apart: 15, of which 8 were waited for; matrix products, arithmetic and copies ran while one was open for 0% of the time, Pallas kernels for 12%

profile of v8, /device:TPU:0, one launch (start us, length us, event | category | flops | bytes accessed | tf_op | source)
XLA Modules:
  0.0 44.3 jit_solution(10823801355890791751)
XLA Ops:
  0.6 3.0 %collective-permute-start.1 = (bf16[256,512]{1,0:T(8,128)(2,1)}, bf16[256,512]{1,0:T(8,128)(2,1)S(1)}, u32[]{:S(2)}, u32[]{:S(2)}) collective-permute-start(bf16[256,512]{1,0:T(8,128)(2,1)} %bitcast.19), channel_id=1, source_target_pairs={{0,1},{1,0},{2,3},{3,2},{4,5},{5,4},{6,7},{7,6},{8,9},{9,8},{10,11... | collective-permute-start | bytes 786440 | tf_op jit(solution)/shard_map/ppermute | solution.py:399
  3.6 2.6 %collective-permute-start.3 = (bf16[256,512]{1,0:T(8,128)(2,1)}, bf16[256,512]{1,0:T(8,128)(2,1)S(1)}, u32[]{:S(2)}, u32[]{:S(2)}) collective-permute-start(bf16[256,512]{1,0:T(8,128)(2,1)} %bitcast.12), channel_id=1, source_target_pairs={{2,0},{3,1},{0,4},{1,5},{4,6},{5,7},{6,2},{7,3},{10,8},{11,9},{8,1... | collective-permute-start | bytes 786440 | tf_op jit(solution)/shard_map/ppermute | solution.py:393
  6.2 1.2 %copy-done = bf16[1,256,2048]{2,1,0:T(8,128)(2,1)S(1)} copy-done((bf16[1,256,2048]{2,1,0:T(8,128)(2,1)S(1)}, bf16[1,256,2048]{2,1,0:T(8,128)(2,1)}, u32[]{:S(2)}) %copy-start) | copy-done | bytes 1048600
  7.5 0.6 %collective-permute-start = (bf16[2,256,256]{2,1,0:T(8,128)(2,1)S(1)}, bf16[2,256,256]{2,1,0:T(8,128)(2,1)S(1)}, u32[]{:S(2)}, u32[]{:S(2)}) collective-permute-start(bf16[2,256,256]{2,1,0:T(8,128)(2,1)S(1)} %pack_columns.2.refs_1_), channel_id=1, source_target_pairs={{0,1},{1,0},{2,3},{3,2},{4,5},{5,4},{6,7},{7,6},{8,9},{9,8},{10,11... | collective-permute-start | bytes 786440 | tf_op jit(solution)/shard_map/ppermute | solution.py:399
  8.4 2.4 %collective-permute-done.1.refs_1_.refs_3_ = bf16[256,512]{1,0:T(8,128)(2,1)S(1)} collective-permute-done((bf16[256,512]{1,0:T(8,128)(2,1)}, bf16[256,512]{1,0:T(8,128)(2,1)S(1)}, u32[]{:S(2)}, u32[]{:S(2)}) %collective-permute-start.1) | collective-permute-done | bytes 262176 | tf_op jit(solution)/shard_map/ppermute | solution.py:399
  10.8 2.5 %collective-permute-done.3.refs_2_.refs_3_.refs_4_ = bf16[256,512]{1,0:T(8,128)(2,1)S(1)} collective-permute-done((bf16[256,512]{1,0:T(8,128)(2,1)}, bf16[256,512]{1,0:T(8,128)(2,1)S(1)}, u32[]{:S(2)}, u32[]{:S(2)}) %collective-permute-start.3) | collective-permute-done | bytes 262176 | tf_op jit(solution)/shard_map/ppermute | solution.py:393
  13.4 0.6 %collective-permute-start.5 = (bf16[2,256,256]{2,1,0:T(8,128)(2,1)S(1)}, bf16[2,256,256]{2,1,0:T(8,128)(2,1)S(1)}, u32[]{:S(2)}, u32[]{:S(2)}) collective-permute-start(bf16[2,256,256]{2,1,0:T(8,128)(2,1)S(1)} %pack_columns.3), channel_id=1, source_target_pairs={{0,1},{1,0},{2,3},{3,2},{4,5},{5,4},{6,7},{7,6},{8,9},{9,8},{10,11... | collective-permute-start | bytes 786440 | tf_op jit(solution)/shard_map/ppermute | solution.py:399
  14.0 3.3 %collective-permute-start.4 = (bf16[256,512]{1,0:T(8,128)(2,1)S(1)}, bf16[256,512]{1,0:T(8,128)(2,1)S(1)}, u32[]{:S(2)}, u32[]{:S(2)}) collective-permute-start(bf16[256,512]{1,0:T(8,128)(2,1)S(1)} %collective-permute-done.3.refs_2_.refs_3_.refs_4_), channel_id=1, source_target_pairs={{2,0},{3,1},{0,4},{1,5},{4,6},{5,7},{6,2},{7,3},{10,8},{11,9},{8,1... | collective-permute-start | bytes 786440 | tf_op jit(solution)/shard_map/ppermute | solution.py:393
  17.2 1.6 %collective-permute-start.6 = (bf16[1,256,256]{2,1,0:T(8,128)(2,1)S(1)}, bf16[1,256,256]{2,1,0:T(8,128)(2,1)S(1)}, u32[]{:S(2)}, u32[]{:S(2)}) collective-permute-start(bf16[1,256,256]{2,1,0:T(8,128)(2,1)S(1)} %partner_columns.2), channel_id=1, source_target_pairs={{0,16},{8,24},{16,0},{24,8},{1,17},{9,25},{17,1},{25,9},{2,18},{10... | collective-permute-start | bytes 393224 | tf_op jit(solution)/shard_map/ppermute | solution.py:106
  19.4 2.9 %collective-permute-done.6.refs_5_.refs_1_ = bf16[1,256,256]{2,1,0:T(8,128)(2,1)S(1)} collective-permute-done((bf16[1,256,256]{2,1,0:T(8,128)(2,1)S(1)}, bf16[1,256,256]{2,1,0:T(8,128)(2,1)S(1)}, u32[]{:S(2)}, u32[]{:S(2)}) %collective-permute-start.6) | collective-permute-done | bytes 131104 | tf_op jit(solution)/shard_map/ppermute | solution.py:106
  22.3 0.5 %near_grads.1 = (bf16[2,256,256]{2,1,0:T(8,128)(2,1)S(1)}, bf16[2,256,256]{2,1,0:T(8,128)(2,1)S(1)}) custom-call(bf16[256,512]{1,0:T(8,128)(2,1)S(1)} %bitcast.21, bf16[256,512]{1,0:T(8,128)(2,1)S(1)} %collective-permute-done.1.refs_1_.refs_3_, bf16[256,512]{1,0:T(8,128)(2,1)S(1)} %bitcast.15, ...), custom_call_target="tpu_custom_call" | custom-call | flops 268435456 | bytes 1048576 | tf_op jit(solution)/shard_map/near_grads/pallas_call | solution.py:48
  22.8 1.6 %collective-permute-start.11 = (bf16[2,256,256]{2,1,0:T(8,128)(2,1)S(1)}, bf16[2,256,256]{2,1,0:T(8,128)(2,1)S(1)}, u32[]{:S(2)}, u32[]{:S(2)}) collective-permute-start(bf16[2,256,256]{2,1,0:T(8,128)(2,1)S(1)} %get-tuple-element.24.refs_6_.refs_4_), channel_id=1, source_target_pairs={{0,1},{1,0},{2,3},{3,2},{4,5},{5,4},{6,7},{7,6},{8,9},{9,8},{10,11... | collective-permute-start | bytes 786440 | tf_op jit(solution)/shard_map/ppermute | solution.py:399
  24.3 0.6 %near_rows.1 = (f32[256,512]{1,0:T(8,128)S(1)}, f32[256,512]{1,0:T(8,128)S(1)}) custom-call(bf16[256,2048]{1,0:T(8,128)(2,1)S(1)} %bitcast.9, bf16[2,256,256]{2,1,0:T(8,128)(2,1)S(1)} %collective-permute-done.refs_2_.refs_1_, bf16[2,256,256]{2,1,0:T(8,128)(2,1)S(1)} %collective-permute-done.5.refs_2_, bf16[256,512]{1,0:T(8,128)(2,1)S(1)} %bitcast.16, ...), custom_call_target="tpu_custom_call" | custom-call | flops 402653184 | bytes 2359296 | tf_op jit(solution)/shard_map/near_rows/pallas_call | solution.py:48
  25.1 0.6 %last_products.1 = (f32[256,512]{1,0:T(8,128)S(1)}, bf16[2,256,256]{2,1,0:T(8,128)(2,1)S(1)}, bf16[4,256,256]{2,1,0:T(8,128)(2,1)S(1)}) custom-call(bf16[256,2048]{1,0:T(8,128)(2,1)S(1)} %bitcast.10, bf16[256,512]{1,0:T(8,128)(2,1)S(1)} %bitcast.22, bf16[2,256,256]{2,1,0:T(8,128)(2,1)S(1)} %collective-permute-done.refs_2_.refs_1_, ...), custom_call_target="tpu_custom_call" | custom-call | flops 268435456 | bytes 3407872 | tf_op jit(solution)/shard_map/last_products/pallas_call | solution.py:48
  25.8 2.1 %collective-permute-start.7 = (bf16[4,256,256]{2,1,0:T(8,128)(2,1)S(1)}, bf16[4,256,256]{2,1,0:T(8,128)(2,1)S(1)}, u32[]{:S(2)}, u32[]{:S(2)}) collective-permute-start(bf16[4,256,256]{2,1,0:T(8,128)(2,1)S(1)} %get-tuple-element.28.refs_2_), channel_id=1, source_target_pairs={{0,1},{1,0},{2,3},{3,2},{4,5},{5,4},{6,7},{7,6},{8,9},{9,8},{10,11... | collective-permute-start | bytes 1572872 | tf_op jit(solution)/shard_map/ppermute | solution.py:399
  27.9 1.8 %collective-permute-start.8 = (bf16[256,512]{1,0:T(8,128)(2,1)S(1)}, bf16[256,512]{1,0:T(8,128)(2,1)S(1)}, u32[]{:S(2)}, u32[]{:S(2)}) collective-permute-start(bf16[256,512]{1,0:T(8,128)(2,1)S(1)} %get-tuple-element.30.refs_3_), channel_id=1, source_target_pairs={{2,0},{3,1},{0,4},{1,5},{4,6},{5,7},{6,2},{7,3},{10,8},{11,9},{8,1... | collective-permute-start | bytes 786440 | tf_op jit(solution)/shard_map/ppermute | solution.py:393
  30.5 0.8 %collective-permute-start.10 = (bf16[256,512]{1,0:T(8,128)(2,1)S(1)}, bf16[256,512]{1,0:T(8,128)(2,1)S(1)}, u32[]{:S(2)}, u32[]{:S(2)}) collective-permute-start(bf16[256,512]{1,0:T(8,128)(2,1)S(1)} %add_terms.1.refs_5_), channel_id=1, source_target_pairs={{0,2},{1,3},{4,0},{5,1},{6,4},{7,5},{2,6},{3,7},{8,10},{9,11},{12,... | collective-permute-start | bytes 786440 | tf_op jit(solution)/shard_map/ppermute | solution.py:396
  31.4 1.1 %outer_update.1 = (bf16[256,128]{1,0:T(8,128)(2,1)S(1)}, f32[256,128]{1,0:T(8,128)}) custom-call(bf16[256,512]{1,0:T(8,128)(2,1)S(1)} %bitcast.18, bf16[1,256,256]{2,1,0:T(8,128)(2,1)S(1)} %collective-permute-done.6.refs_5_.refs_1_, bf16[2,256,128]{2,1,0:T(8,128)(2,1)S(1)} %collective-permute-done.12.refs_2_, bf16[256,512]{1,0:T(8,128)(2,1)S(1)} %copy-done.4, ...), custom_call_target="tpu_custom_call" | custom-call | bytes 917504 | tf_op jit(solution)/shard_map/outer_update/pallas_call | solution.py:48
  32.5 1.5 %collective-permute-start.13 = (bf16[256,128]{1,0:T(8,128)(2,1)S(1)}, bf16[256,128]{1,0:T(8,128)(2,1)S(1)}, u32[]{:S(2)}, u32[]{:S(2)}) collective-permute-start(bf16[256,128]{1,0:T(8,128)(2,1)S(1)} %get-tuple-element.38), channel_id=1, source_target_pairs={{0,16},{8,24},{16,0},{24,8},{1,17},{9,25},{17,1},{25,9},{2,18},{10... | collective-permute-start | bytes 196616 | tf_op jit(solution)/shard_map/ppermute | solution.py:106
  34.0 2.7 %collective-permute-done.13 = bf16[256,128]{1,0:T(8,128)(2,1)S(1)} collective-permute-done((bf16[256,128]{1,0:T(8,128)(2,1)S(1)}, bf16[256,128]{1,0:T(8,128)(2,1)S(1)}, u32[]{:S(2)}, u32[]{:S(2)}) %collective-permute-start.13) | collective-permute-done | bytes 65568 | tf_op jit(solution)/shard_map/ppermute | solution.py:106
  36.8 0.9 %collect.1 = (bf16[256,2048]{1,0:T(8,128)(2,1)}, f32[8,128]{1,0:T(8,128)S(1)}) custom-call(bf16[2,256,256]{2,1,0:T(8,128)(2,1)S(1)} %get-tuple-element.32.near_ref, bf16[2,256,256]{2,1,0:T(8,128)(2,1)S(1)} %get-tuple-element.33.last_ref, bf16[2,256,256]{2,1,0:T(8,128)(2,1)S(1)} %collective-permute-done.11.early_ref.refs_6_), custom_call_target="tpu_custom_call" | custom-call | bytes 1048576 | tf_op jit(solution)/shard_map/collect/pallas_call | solution.py:333
  38.2 0.8 %join_shares.1 = bf16[256,512]{1,0:T(8,128)(2,1)} custom-call(bf16[256,256]{1,0:T(8,128)(2,1)S(1)} %constant_dynamic-update-slice_fusion.refs_0_, bf16[256,256]{1,0:T(8,128)(2,1)S(1)} %collective-permute-done.14.refs_1_, f32[8,128]{1,0:T(8,128)S(1)} %get-tuple-element.39.refs_2_), custom_call_target="tpu_custom_call" | custom-call | bytes 262144 | tf_op jit(solution)/shard_map/join_shares/pallas_call | solution.py:48
  38.9 4.4 %collective-permute-done.10.down_ref = bf16[256,512]{1,0:T(8,128)(2,1)S(1)} collective-permute-done((bf16[256,512]{1,0:T(8,128)(2,1)S(1)}, bf16[256,512]{1,0:T(8,128)(2,1)S(1)}, u32[]{:S(2)}, u32[]{:S(2)}) %collective-permute-start.10) | collective-permute-done | bytes 262176 | tf_op jit(solution)/shard_map/ppermute | solution.py:396
  43.3 0.9 %finish.1 = (bf16[256,512]{1,0:T(8,128)(2,1)}, bf16[256,2048]{1,0:T(8,128)(2,1)}, bf16[256,512]{1,0:T(8,128)(2,1)}) custom-call(f32[256,512]{1,0:T(8,128)S(1)} %get-tuple-element.27.total_ref, bf16[4,256,256]{2,1,0:T(8,128)(2,1)S(1)} %collective-permute-done.7.late_ref, f32[256,512]{1,0:T(8,128)S(1)} %get-tuple-element.29.terms_ref, ...), custom_call_target="tpu_custom_call", output_to_operand_aliasing={{1}: (5, {})} | custom-call | bytes 1048576 | tf_op jit(solution)/shard_map/finish/pallas_call | solution.py:364
  (34 shorter events, 2.6 us)
Async XLA Ops:
  0.6 10.2 %collective-permute-start.1 = (bf16[256,512]{1,0:T(8,128)(2,1)}, bf16[256,512]{1,0:T(8,128)(2,1)S(1)}, u32[]{:S(2)}, u32[]{:S(2)}) collective-permute-start(bf16[256,512]{1,0:T(8,128)(2,1)} %bitcast.19), channel_id=1, source_target_pairs={{0,1},{1,0},{2,3},{3,2},{4,5},{5,4},{6,7},{7,6},{8,9},{9,8},{10,11... | collective-permute-start | bytes 786440 | tf_op jit(solution)/shard_map/ppermute | solution.py:399
  3.6 9.7 %collective-permute-start.3 = (bf16[256,512]{1,0:T(8,128)(2,1)}, bf16[256,512]{1,0:T(8,128)(2,1)S(1)}, u32[]{:S(2)}, u32[]{:S(2)}) collective-permute-start(bf16[256,512]{1,0:T(8,128)(2,1)} %bitcast.12), channel_id=1, source_target_pairs={{2,0},{3,1},{0,4},{1,5},{4,6},{5,7},{6,2},{7,3},{10,8},{11,9},{8,1... | collective-permute-start | bytes 786440 | tf_op jit(solution)/shard_map/ppermute | solution.py:393
  6.2 1.2 %copy-start = (bf16[1,256,2048]{2,1,0:T(8,128)(2,1)S(1)}, bf16[1,256,2048]{2,1,0:T(8,128)(2,1)}, u32[]{:S(2)}) copy-start(bf16[1,256,2048]{2,1,0:T(8,128)(2,1)} %param.8) | copy-start | bytes 3145732
  7.4 0.9 %copy-start.2 = (bf16[1,256,512]{2,1,0:T(8,128)(2,1)S(1)}, bf16[1,256,512]{2,1,0:T(8,128)(2,1)}, u32[]{:S(2)}) copy-start(bf16[1,256,512]{2,1,0:T(8,128)(2,1)} %param.5) | copy-start | bytes 786436
  7.5 11.3 %copy-start.1 = (bf16[1,256,2048]{2,1,0:T(8,128)(2,1)S(1)}, bf16[1,256,2048]{2,1,0:T(8,128)(2,1)}, u32[]{:S(2)}) copy-start(bf16[1,256,2048]{2,1,0:T(8,128)(2,1)} %param.8) | copy-start | bytes 3145732
  7.5 11.3 %collective-permute-start = (bf16[2,256,256]{2,1,0:T(8,128)(2,1)S(1)}, bf16[2,256,256]{2,1,0:T(8,128)(2,1)S(1)}, u32[]{:S(2)}, u32[]{:S(2)}) collective-permute-start(bf16[2,256,256]{2,1,0:T(8,128)(2,1)S(1)} %pack_columns.2.refs_1_), channel_id=1, source_target_pairs={{0,1},{1,0},{2,3},{3,2},{4,5},{5,4},{6,7},{7,6},{8,9},{9,8},{10,11... | collective-permute-start | bytes 786440 | tf_op jit(solution)/shard_map/ppermute | solution.py:399
  8.4 15.9 %collective-permute-start.2 = (bf16[256,512]{1,0:T(8,128)(2,1)S(1)}, bf16[256,512]{1,0:T(8,128)(2,1)S(1)}, u32[]{:S(2)}, u32[]{:S(2)}) collective-permute-start(bf16[256,512]{1,0:T(8,128)(2,1)S(1)} %bitcast.13), channel_id=1, source_target_pairs={{0,2},{1,3},{4,0},{5,1},{6,4},{7,5},{2,6},{3,7},{8,10},{9,11},{12,... | collective-permute-start | bytes 786440 | tf_op jit(solution)/shard_map/ppermute | solution.py:396
  13.4 5.5 %copy-start.3 = (bf16[1,256,512]{2,1,0:T(8,128)(2,1)S(1)}, bf16[1,256,512]{2,1,0:T(8,128)(2,1)}, u32[]{:S(2)}) copy-start(bf16[1,256,512]{2,1,0:T(8,128)(2,1)} %param.9) | copy-start | bytes 786436
  13.4 11.0 %collective-permute-start.5 = (bf16[2,256,256]{2,1,0:T(8,128)(2,1)S(1)}, bf16[2,256,256]{2,1,0:T(8,128)(2,1)S(1)}, u32[]{:S(2)}, u32[]{:S(2)}) collective-permute-start(bf16[2,256,256]{2,1,0:T(8,128)(2,1)S(1)} %pack_columns.3), channel_id=1, source_target_pairs={{0,1},{1,0},{2,3},{3,2},{4,5},{5,4},{6,7},{7,6},{8,9},{9,8},{10,11... | collective-permute-start | bytes 786440 | tf_op jit(solution)/shard_map/ppermute | solution.py:399
  14.0 11.2 %collective-permute-start.4 = (bf16[256,512]{1,0:T(8,128)(2,1)S(1)}, bf16[256,512]{1,0:T(8,128)(2,1)S(1)}, u32[]{:S(2)}, u32[]{:S(2)}) collective-permute-start(bf16[256,512]{1,0:T(8,128)(2,1)S(1)} %collective-permute-done.3.refs_2_.refs_3_.refs_4_), channel_id=1, source_target_pairs={{2,0},{3,1},{0,4},{1,5},{4,6},{5,7},{6,2},{7,3},{10,8},{11,9},{8,1... | collective-permute-start | bytes 786440 | tf_op jit(solution)/shard_map/ppermute | solution.py:393
  17.2 5.0 %collective-permute-start.6 = (bf16[1,256,256]{2,1,0:T(8,128)(2,1)S(1)}, bf16[1,256,256]{2,1,0:T(8,128)(2,1)S(1)}, u32[]{:S(2)}, u32[]{:S(2)}) collective-permute-start(bf16[1,256,256]{2,1,0:T(8,128)(2,1)S(1)} %partner_columns.2), channel_id=1, source_target_pairs={{0,16},{8,24},{16,0},{24,8},{1,17},{9,25},{17,1},{25,9},{2,18},{10... | collective-permute-start | bytes 393224 | tf_op jit(solution)/shard_map/ppermute | solution.py:106
  19.3 11.1 %collective-permute-start.9 = (bf16[256,512]{1,0:T(8,128)(2,1)S(1)}, bf16[256,512]{1,0:T(8,128)(2,1)S(1)}, u32[]{:S(2)}, u32[]{:S(2)}) collective-permute-start(bf16[256,512]{1,0:T(8,128)(2,1)S(1)} %get-tuple-element.23.refs_4_.refs_2_), channel_id=1, source_target_pairs={{0,2},{1,3},{4,0},{5,1},{6,4},{7,5},{2,6},{3,7},{8,10},{9,11},{12,... | collective-permute-start | bytes 786440 | tf_op jit(solution)/shard_map/ppermute | solution.py:396
  22.8 8.5 %collective-permute-start.11 = (bf16[2,256,256]{2,1,0:T(8,128)(2,1)S(1)}, bf16[2,256,256]{2,1,0:T(8,128)(2,1)S(1)}, u32[]{:S(2)}, u32[]{:S(2)}) collective-permute-start(bf16[2,256,256]{2,1,0:T(8,128)(2,1)S(1)} %get-tuple-element.24.refs_6_.refs_4_), channel_id=1, source_target_pairs={{0,1},{1,0},{2,3},{3,2},{4,5},{5,4},{6,7},{7,6},{8,9},{9,8},{10,11... | collective-permute-start | bytes 786440 | tf_op jit(solution)/shard_map/ppermute | solution.py:399
  25.8 17.6 %collective-permute-start.7 = (bf16[4,256,256]{2,1,0:T(8,128)(2,1)S(1)}, bf16[4,256,256]{2,1,0:T(8,128)(2,1)S(1)}, u32[]{:S(2)}, u32[]{:S(2)}) collective-permute-start(bf16[4,256,256]{2,1,0:T(8,128)(2,1)S(1)} %get-tuple-element.28.refs_2_), channel_id=1, source_target_pairs={{0,1},{1,0},{2,3},{3,2},{4,5},{5,4},{6,7},{7,6},{8,9},{9,8},{10,11... | collective-permute-start | bytes 1572872 | tf_op jit(solution)/shard_map/ppermute | solution.py:399
  27.9 3.4 %collective-permute-start.12 = (bf16[2,256,128]{2,1,0:T(8,128)(2,1)S(1)}, bf16[2,256,128]{2,1,0:T(8,128)(2,1)S(1)}, u32[]{:S(2)}, u32[]{:S(2)}) collective-permute-start(bf16[2,256,128]{2,1,0:T(8,128)(2,1)S(1)} %partner_columns.3), channel_id=1, source_target_pairs={{0,8},{8,0},{16,24},{24,16},{1,9},{9,1},{17,25},{25,17},{2,10},{10... | collective-permute-start | bytes 393224 | tf_op jit(solution)/shard_map/ppermute | solution.py:106
  27.9 11.0 %collective-permute-start.8 = (bf16[256,512]{1,0:T(8,128)(2,1)S(1)}, bf16[256,512]{1,0:T(8,128)(2,1)S(1)}, u32[]{:S(2)}, u32[]{:S(2)}) collective-permute-start(bf16[256,512]{1,0:T(8,128)(2,1)S(1)} %get-tuple-element.30.refs_3_), channel_id=1, source_target_pairs={{2,0},{3,1},{0,4},{1,5},{4,6},{5,7},{6,2},{7,3},{10,8},{11,9},{8,1... | collective-permute-start | bytes 786440 | tf_op jit(solution)/shard_map/ppermute | solution.py:393
  30.4 1.0 %copy-start.4 = (bf16[256,512]{1,0:T(8,128)(2,1)S(1)}, bf16[256,512]{1,0:T(8,128)(2,1)}, u32[]{:S(2)}) copy-start(bf16[256,512]{1,0:T(8,128)(2,1)} %refs_3_.1) | copy-start | bytes 786436
  30.4 1.0 %copy-start.5 = (f32[256,128]{1,0:T(8,128)S(1)}, f32[256,128]{1,0:T(8,128)}, u32[]{:S(2)}) copy-start(f32[256,128]{1,0:T(8,128)} %refs_4_.1) | copy-start | bytes 393220
  30.5 12.9 %collective-permute-start.10 = (bf16[256,512]{1,0:T(8,128)(2,1)S(1)}, bf16[256,512]{1,0:T(8,128)(2,1)S(1)}, u32[]{:S(2)}, u32[]{:S(2)}) collective-permute-start(bf16[256,512]{1,0:T(8,128)(2,1)S(1)} %add_terms.1.refs_5_), channel_id=1, source_target_pairs={{0,2},{1,3},{4,0},{5,1},{6,4},{7,5},{2,6},{3,7},{8,10},{9,11},{12,... | collective-permute-start | bytes 786440 | tf_op jit(solution)/shard_map/ppermute | solution.py:396
  32.5 4.3 %collective-permute-start.13 = (bf16[256,128]{1,0:T(8,128)(2,1)S(1)}, bf16[256,128]{1,0:T(8,128)(2,1)S(1)}, u32[]{:S(2)}, u32[]{:S(2)}) collective-permute-start(bf16[256,128]{1,0:T(8,128)(2,1)S(1)} %get-tuple-element.38), channel_id=1, source_target_pairs={{0,16},{8,24},{16,0},{24,8},{1,17},{9,25},{17,1},{25,9},{2,18},{10... | collective-permute-start | bytes 196616 | tf_op jit(solution)/shard_map/ppermute | solution.py:106
  36.8 1.4 %collective-permute-start.14 = (bf16[256,256]{1,0:T(8,128)(2,1)S(1)}, bf16[256,256]{1,0:T(8,128)(2,1)S(1)}, u32[]{:S(2)}, u32[]{:S(2)}) collective-permute-start(bf16[256,256]{1,0:T(8,128)(2,1)S(1)} %constant_dynamic-update-slice_fusion.refs_0_), channel_id=1, source_target_pairs={{0,8},{8,0},{16,24},{24,16},{1,9},{9,1},{17,25},{25,17},{2,10},{10... | collective-permute-start | bytes 393224 | tf_op jit(solution)/shard_map/ppermute | solution.py:106

commit v9 on v8

--- a/solution.py
+++ b/solution.py
@@ -19,23 +19,9 @@
 VMEM_BYTES = 8 * 2**20
 
 
-def ring_order(size):
-    return list(range(0, size, 2)) + list(range(1, size, 2))[::-1]
-
-
-def ring_place(index, size):
-    return jnp.where((index & 1) == 0, index >> 1, size - 1 - (index >> 1))
-
-
-def ring_index(place, size):
-    place = lax.rem(place + size, size)
-    evens = (size + 1) // 2
-    return jnp.where(place < evens, 2 * place, 2 * (size - 1 - place) + 1)
-
-
 def block_start(offset, size, depth, other=0):
     me = lax.axis_index("fsdp")
-    row = ring_index(ring_place(me >> 1, size // 2) + offset, size // 2)
+    row = lax.rem((me >> 1) + offset + size, size // 2)
     return pl.multiple_of((2 * row + ((me & 1) ^ other)) * depth, depth)
 
 
@@ -386,8 +372,7 @@
     size = lax.axis_size("fsdp")
     ring = size // 2
     token_weight = 1.0 / (tokens * size)
-    order = ring_order(ring)
-    pairs = [(2 * order[at - 1] + side, 2 * order[at] + side) for at in range(ring) for side in (0, 1)]
+    pairs = [(2 * at + side, 2 * ((at + 1) % ring) + side) for at in range(ring) for side in (0, 1)]
 
     def upward(array):
         return lax.ppermute(array, "fsdp", pairs)

time: 44.5 us -> 47.9 us (1.076)
  starting transfers between devices: 19.6 us -> 23.9 us
  waiting for transfers between devices: 15.8 us -> 15.1 us
    ppermute x3, starting transfers between devices: 0.83 us -> 10.4 us  [downward(): lax.ppermute(array, 'fsdp', [(target, source) for source, target in pairs])]
    ppermute x3, waiting for transfers between devices: 2.76 us -> 6.53 us  [upward(): return lax.ppermute(array, 'fsdp', pairs)]
    ppermute x3, starting transfers between devices: 7.71 us -> 3.97 us  [upward(): return lax.ppermute(array, 'fsdp', pairs)]
    ppermute x4, waiting for transfers between devices: 6.02 us -> 3.13 us  [swap(): lax.ppermute(array, 'replica', [(at, at ^ bits) for at in range(lax.axis_...]
    ppermute x5, starting transfers between devices: 7.84 us -> 6 us  [across(): return lax.ppermute(array, 'fsdp', [(at, at ^ 1) for at in range(size)])]
    ppermute x5, waiting for transfers between devices: 2.41 us -> 1.36 us  [across(): return lax.ppermute(array, 'fsdp', [(at, at ^ 1) for at in range(size)])]
    ppermute x3, waiting for transfers between devices: 4.57 us -> 4.04 us  [downward(): lax.ppermute(array, 'fsdp', [(target, source) for source, target in pairs])]
  transfers between devices with their start and end apart: 15 -> 15, of which waited for: 8 -> 6; matrix products, arithmetic and copies ran while one was open for 0% -> 0% of each run, Pallas kernels for 12% -> 12%
where the time goes in v9:
time: 47.9 us; the launch traced here: 47.7 us
  starting transfers between devices  23.9 us (50%)
  waiting for transfers between devices  15.1 us (32%)
  Pallas kernels  6.42 us (13%)
  local copies, waits for them, and re-layouts  1.58 us (3%)
  between operations  0.79 us (2%)
    ppermute x3, starting transfers between devices, downward(): lax.ppermute(array, 'fsdp', [(target, source) for source, target in pairs])  10.4 us
    ppermute x3, waiting for transfers between devices, upward(): return lax.ppermute(array, 'fsdp', pairs)  6.53 us
    ppermute x5, starting transfers between devices, across(): return lax.ppermute(array, 'fsdp', [(at, at ^ 1) for at in range(size)])  6 us
    pallas_call x12, Pallas kernels, vmem_call(): pl.pallas_call(body, out_shape=out_shape, in_specs=[whole] * len(operands...  4.56 us
    ppermute x3, waiting for transfers between devices, downward(): lax.ppermute(array, 'fsdp', [(target, source) for source, target in pairs])  4.04 us
    ppermute x3, starting transfers between devices, upward(): return lax.ppermute(array, 'fsdp', pairs)  3.97 us
    ppermute x4, starting transfers between devices, swap(): lax.ppermute(array, 'replica', [(at, at ^ bits) for at in range(lax.axis_...  3.47 us
    ppermute x4, waiting for transfers between devices, swap(): lax.ppermute(array, 'replica', [(at, at ^ bits) for at in range(lax.axis_...  3.13 us
  transfers between devices with their start and end apart: 15, of which 6 were waited for; matrix products, arithmetic and copies ran while one was open for 0% of the time, Pallas kernels for 12%

profile of v9, /device:TPU:0, one launch (start us, length us, event | category | flops | bytes accessed | tf_op | source)
XLA Modules:
  0.0 47.7 jit_solution(16498818002564406002)
XLA Ops:
  0.6 3.0 %collective-permute-start.1 = (bf16[256,512]{1,0:T(8,128)(2,1)}, bf16[256,512]{1,0:T(8,128)(2,1)S(1)}, u32[]{:S(2)}, u32[]{:S(2)}) collective-permute-start(bf16[256,512]{1,0:T(8,128)(2,1)} %bitcast.19), channel_id=1, source_target_pairs={{0,1},{1,0},{2,3},{3,2},{4,5},{5,4},{6,7},{7,6},{8,9},{9,8},{10,11... | collective-permute-start | bytes 786440 | tf_op jit(solution)/shard_map/ppermute | solution.py:384
  3.6 1.6 %collective-permute-start.3 = (bf16[256,512]{1,0:T(8,128)(2,1)}, bf16[256,512]{1,0:T(8,128)(2,1)S(1)}, u32[]{:S(2)}, u32[]{:S(2)}) collective-permute-start(bf16[256,512]{1,0:T(8,128)(2,1)} %bitcast.12), channel_id=1, source_target_pairs={{0,2},{1,3},{2,4},{3,5},{4,6},{5,7},{6,0},{7,1},{8,10},{9,11},{10,... | collective-permute-start | bytes 786440 | tf_op jit(solution)/shard_map/ppermute | solution.py:378
  5.2 1.2 %copy-done = bf16[1,256,2048]{2,1,0:T(8,128)(2,1)S(1)} copy-done((bf16[1,256,2048]{2,1,0:T(8,128)(2,1)S(1)}, bf16[1,256,2048]{2,1,0:T(8,128)(2,1)}, u32[]{:S(2)}) %copy-start) | copy-done | bytes 1048600
  6.5 0.6 %collective-permute-start = (bf16[2,256,256]{2,1,0:T(8,128)(2,1)S(1)}, bf16[2,256,256]{2,1,0:T(8,128)(2,1)S(1)}, u32[]{:S(2)}, u32[]{:S(2)}) collective-permute-start(bf16[2,256,256]{2,1,0:T(8,128)(2,1)S(1)} %pack_columns.2.refs_1_), channel_id=1, source_target_pairs={{0,1},{1,0},{2,3},{3,2},{4,5},{5,4},{6,7},{7,6},{8,9},{9,8},{10,11... | collective-permute-start | bytes 786440 | tf_op jit(solution)/shard_map/ppermute | solution.py:384
  7.4 2.2 %collective-permute-start.2 = (bf16[256,512]{1,0:T(8,128)(2,1)S(1)}, bf16[256,512]{1,0:T(8,128)(2,1)S(1)}, u32[]{:S(2)}, u32[]{:S(2)}) collective-permute-start(bf16[256,512]{1,0:T(8,128)(2,1)S(1)} %bitcast.13), channel_id=1, source_target_pairs={{2,0},{3,1},{4,2},{5,3},{6,4},{7,5},{0,6},{1,7},{10,8},{11,9},{12,... | collective-permute-start | bytes 786440 | tf_op jit(solution)/shard_map/ppermute | solution.py:381
  9.6 1.3 %collective-permute-done.1.refs_1_.refs_3_ = bf16[256,512]{1,0:T(8,128)(2,1)S(1)} collective-permute-done((bf16[256,512]{1,0:T(8,128)(2,1)}, bf16[256,512]{1,0:T(8,128)(2,1)S(1)}, u32[]{:S(2)}, u32[]{:S(2)}) %collective-permute-start.1) | collective-permute-done | bytes 262176 | tf_op jit(solution)/shard_map/ppermute | solution.py:384
  11.0 3.9 %collective-permute-done.3.refs_2_.refs_3_.refs_4_ = bf16[256,512]{1,0:T(8,128)(2,1)S(1)} collective-permute-done((bf16[256,512]{1,0:T(8,128)(2,1)}, bf16[256,512]{1,0:T(8,128)(2,1)S(1)}, u32[]{:S(2)}, u32[]{:S(2)}) %collective-permute-start.3) | collective-permute-done | bytes 262176 | tf_op jit(solution)/shard_map/ppermute | solution.py:378
  15.3 1.8 %collective-permute-start.6 = (bf16[1,256,256]{2,1,0:T(8,128)(2,1)S(1)}, bf16[1,256,256]{2,1,0:T(8,128)(2,1)S(1)}, u32[]{:S(2)}, u32[]{:S(2)}) collective-permute-start(bf16[1,256,256]{2,1,0:T(8,128)(2,1)S(1)} %partner_columns.2), channel_id=1, source_target_pairs={{0,16},{8,24},{16,0},{24,8},{1,17},{9,25},{17,1},{25,9},{2,18},{10... | collective-permute-start | bytes 393224 | tf_op jit(solution)/shard_map/ppermute | solution.py:92
  17.6 5.0 %collective-permute-start.9 = (bf16[256,512]{1,0:T(8,128)(2,1)S(1)}, bf16[256,512]{1,0:T(8,128)(2,1)S(1)}, u32[]{:S(2)}, u32[]{:S(2)}) collective-permute-start(bf16[256,512]{1,0:T(8,128)(2,1)S(1)} %get-tuple-element.23.refs_4_.refs_2_), channel_id=1, source_target_pairs={{2,0},{3,1},{4,2},{5,3},{6,4},{7,5},{0,6},{1,7},{10,8},{11,9},{12,... | collective-permute-start | bytes 786440 | tf_op jit(solution)/shard_map/ppermute | solution.py:381
  23.1 1.3 %collective-permute-start.11 = (bf16[2,256,256]{2,1,0:T(8,128)(2,1)S(1)}, bf16[2,256,256]{2,1,0:T(8,128)(2,1)S(1)}, u32[]{:S(2)}, u32[]{:S(2)}) collective-permute-start(bf16[2,256,256]{2,1,0:T(8,128)(2,1)S(1)} %get-tuple-element.24.refs_6_.refs_4_), channel_id=1, source_target_pairs={{0,1},{1,0},{2,3},{3,2},{4,5},{5,4},{6,7},{7,6},{8,9},{9,8},{10,11... | collective-permute-start | bytes 786440 | tf_op jit(solution)/shard_map/ppermute | solution.py:384
  24.4 0.6 %near_rows.1 = (f32[256,512]{1,0:T(8,128)S(1)}, f32[256,512]{1,0:T(8,128)S(1)}) custom-call(bf16[256,2048]{1,0:T(8,128)(2,1)S(1)} %bitcast.9, bf16[2,256,256]{2,1,0:T(8,128)(2,1)S(1)} %collective-permute-done.refs_2_.refs_1_, bf16[2,256,256]{2,1,0:T(8,128)(2,1)S(1)} %collective-permute-done.5.refs_2_, bf16[256,512]{1,0:T(8,128)(2,1)S(1)} %bitcast.16, ...), custom_call_target="tpu_custom_call" | custom-call | flops 402653184 | bytes 2359296 | tf_op jit(solution)/shard_map/near_rows/pallas_call | solution.py:34
  25.0 2.6 %collective-permute-done.4.refs_5_ = bf16[256,512]{1,0:T(8,128)(2,1)S(1)} collective-permute-done((bf16[256,512]{1,0:T(8,128)(2,1)S(1)}, bf16[256,512]{1,0:T(8,128)(2,1)S(1)}, u32[]{:S(2)}, u32[]{:S(2)}) %collective-permute-start.4) | collective-permute-done | bytes 262176 | tf_op jit(solution)/shard_map/ppermute | solution.py:378
  27.6 0.6 %last_products.1 = (f32[256,512]{1,0:T(8,128)S(1)}, bf16[2,256,256]{2,1,0:T(8,128)(2,1)S(1)}, bf16[4,256,256]{2,1,0:T(8,128)(2,1)S(1)}) custom-call(bf16[256,2048]{1,0:T(8,128)(2,1)S(1)} %bitcast.10, bf16[256,512]{1,0:T(8,128)(2,1)S(1)} %bitcast.22, bf16[2,256,256]{2,1,0:T(8,128)(2,1)S(1)} %collective-permute-done.refs_2_.refs_1_, ...), custom_call_target="tpu_custom_call" | custom-call | flops 268435456 | bytes 3407872 | tf_op jit(solution)/shard_map/last_products/pallas_call | solution.py:34
  28.2 0.7 %collective-permute-start.7 = (bf16[4,256,256]{2,1,0:T(8,128)(2,1)S(1)}, bf16[4,256,256]{2,1,0:T(8,128)(2,1)S(1)}, u32[]{:S(2)}, u32[]{:S(2)}) collective-permute-start(bf16[4,256,256]{2,1,0:T(8,128)(2,1)S(1)} %get-tuple-element.28.refs_2_), channel_id=1, source_target_pairs={{0,1},{1,0},{2,3},{3,2},{4,5},{5,4},{6,7},{7,6},{8,9},{9,8},{10,11... | collective-permute-start | bytes 1572872 | tf_op jit(solution)/shard_map/ppermute | solution.py:384
  29.1 2.4 %collective-permute-start.8 = (bf16[256,512]{1,0:T(8,128)(2,1)S(1)}, bf16[256,512]{1,0:T(8,128)(2,1)S(1)}, u32[]{:S(2)}, u32[]{:S(2)}) collective-permute-start(bf16[256,512]{1,0:T(8,128)(2,1)S(1)} %get-tuple-element.30.refs_3_), channel_id=1, source_target_pairs={{0,2},{1,3},{2,4},{3,5},{4,6},{5,7},{6,0},{7,1},{8,10},{9,11},{10,... | collective-permute-start | bytes 786440 | tf_op jit(solution)/shard_map/ppermute | solution.py:378
  31.5 0.5 token_terms.3
  32.0 3.2 %collective-permute-start.10 = (bf16[256,512]{1,0:T(8,128)(2,1)S(1)}, bf16[256,512]{1,0:T(8,128)(2,1)S(1)}, u32[]{:S(2)}, u32[]{:S(2)}) collective-permute-start(bf16[256,512]{1,0:T(8,128)(2,1)S(1)} %add_terms.1.refs_5_), channel_id=1, source_target_pairs={{2,0},{3,1},{4,2},{5,3},{6,4},{7,5},{0,6},{1,7},{10,8},{11,9},{12,... | collective-permute-start | bytes 786440 | tf_op jit(solution)/shard_map/ppermute | solution.py:381
  35.2 1.1 %outer_update.1 = (bf16[256,128]{1,0:T(8,128)(2,1)S(1)}, f32[256,128]{1,0:T(8,128)}) custom-call(bf16[256,512]{1,0:T(8,128)(2,1)S(1)} %bitcast.18, bf16[1,256,256]{2,1,0:T(8,128)(2,1)S(1)} %collective-permute-done.6.refs_5_.refs_1_, bf16[2,256,128]{2,1,0:T(8,128)(2,1)S(1)} %collective-permute-done.12.refs_2_, bf16[256,512]{1,0:T(8,128)(2,1)S(1)} %copy-done.4, ...), custom_call_target="tpu_custom_call" | custom-call | bytes 917504 | tf_op jit(solution)/shard_map/outer_update/pallas_call | solution.py:34
  36.3 1.5 %collective-permute-start.13 = (bf16[256,128]{1,0:T(8,128)(2,1)S(1)}, bf16[256,128]{1,0:T(8,128)(2,1)S(1)}, u32[]{:S(2)}, u32[]{:S(2)}) collective-permute-start(bf16[256,128]{1,0:T(8,128)(2,1)S(1)} %get-tuple-element.38), channel_id=1, source_target_pairs={{0,16},{8,24},{16,0},{24,8},{1,17},{9,25},{17,1},{25,9},{2,18},{10... | collective-permute-start | bytes 196616 | tf_op jit(solution)/shard_map/ppermute | solution.py:92
  37.8 2.7 %collective-permute-done.13 = bf16[256,128]{1,0:T(8,128)(2,1)S(1)} collective-permute-done((bf16[256,128]{1,0:T(8,128)(2,1)S(1)}, bf16[256,128]{1,0:T(8,128)(2,1)S(1)}, u32[]{:S(2)}, u32[]{:S(2)}) %collective-permute-start.13) | collective-permute-done | bytes 65568 | tf_op jit(solution)/shard_map/ppermute | solution.py:92
  40.7 0.9 %collect.1 = (bf16[256,2048]{1,0:T(8,128)(2,1)}, f32[8,128]{1,0:T(8,128)S(1)}) custom-call(bf16[2,256,256]{2,1,0:T(8,128)(2,1)S(1)} %get-tuple-element.32.near_ref, bf16[2,256,256]{2,1,0:T(8,128)(2,1)S(1)} %get-tuple-element.33.last_ref, bf16[2,256,256]{2,1,0:T(8,128)(2,1)S(1)} %collective-permute-done.11.early_ref.refs_6_), custom_call_target="tpu_custom_call" | custom-call | bytes 1048576 | tf_op jit(solution)/shard_map/collect/pallas_call | solution.py:319
  42.0 0.8 %join_shares.1 = bf16[256,512]{1,0:T(8,128)(2,1)} custom-call(bf16[256,256]{1,0:T(8,128)(2,1)S(1)} %constant_dynamic-update-slice_fusion.refs_0_, bf16[256,256]{1,0:T(8,128)(2,1)S(1)} %collective-permute-done.14.refs_1_, f32[8,128]{1,0:T(8,128)S(1)} %get-tuple-element.39.refs_2_), custom_call_target="tpu_custom_call" | custom-call | bytes 262144 | tf_op jit(solution)/shard_map/join_shares/pallas_call | solution.py:34
  42.8 4.0 %collective-permute-done.10.down_ref = bf16[256,512]{1,0:T(8,128)(2,1)S(1)} collective-permute-done((bf16[256,512]{1,0:T(8,128)(2,1)S(1)}, bf16[256,512]{1,0:T(8,128)(2,1)S(1)}, u32[]{:S(2)}, u32[]{:S(2)}) %collective-permute-start.10) | collective-permute-done | bytes 262176 | tf_op jit(solution)/shard_map/ppermute | solution.py:381
  46.8 0.9 %finish.1 = (bf16[256,512]{1,0:T(8,128)(2,1)}, bf16[256,2048]{1,0:T(8,128)(2,1)}, bf16[256,512]{1,0:T(8,128)(2,1)}) custom-call(f32[256,512]{1,0:T(8,128)S(1)} %get-tuple-element.27.total_ref, bf16[4,256,256]{2,1,0:T(8,128)(2,1)S(1)} %collective-permute-done.7.late_ref, f32[256,512]{1,0:T(8,128)S(1)} %get-tuple-element.29.terms_ref, ...), custom_call_target="tpu_custom_call", output_to_operand_aliasing={{1}: (5, {})} | custom-call | bytes 1048576 | tf_op jit(solution)/shard_map/finish/pallas_call | solution.py:350
  (34 shorter events, 2.3 us)
Async XLA Ops:
  0.6 10.4 %collective-permute-start.1 = (bf16[256,512]{1,0:T(8,128)(2,1)}, bf16[256,512]{1,0:T(8,128)(2,1)S(1)}, u32[]{:S(2)}, u32[]{:S(2)}) collective-permute-start(bf16[256,512]{1,0:T(8,128)(2,1)} %bitcast.19), channel_id=1, source_target_pairs={{0,1},{1,0},{2,3},{3,2},{4,5},{5,4},{6,7},{7,6},{8,9},{9,8},{10,11... | collective-permute-start | bytes 786440 | tf_op jit(solution)/shard_map/ppermute | solution.py:384
  3.6 11.3 %collective-permute-start.3 = (bf16[256,512]{1,0:T(8,128)(2,1)}, bf16[256,512]{1,0:T(8,128)(2,1)S(1)}, u32[]{:S(2)}, u32[]{:S(2)}) collective-permute-start(bf16[256,512]{1,0:T(8,128)(2,1)} %bitcast.12), channel_id=1, source_target_pairs={{0,2},{1,3},{2,4},{3,5},{4,6},{5,7},{6,0},{7,1},{8,10},{9,11},{10,... | collective-permute-start | bytes 786440 | tf_op jit(solution)/shard_map/ppermute | solution.py:378
  5.2 1.2 %copy-start = (bf16[1,256,2048]{2,1,0:T(8,128)(2,1)S(1)}, bf16[1,256,2048]{2,1,0:T(8,128)(2,1)}, u32[]{:S(2)}) copy-start(bf16[1,256,2048]{2,1,0:T(8,128)(2,1)} %param.8) | copy-start | bytes 3145732
  6.4 0.9 %copy-start.2 = (bf16[1,256,512]{2,1,0:T(8,128)(2,1)S(1)}, bf16[1,256,512]{2,1,0:T(8,128)(2,1)}, u32[]{:S(2)}) copy-start(bf16[1,256,512]{2,1,0:T(8,128)(2,1)} %param.5) | copy-start | bytes 786436
  6.5 10.7 %copy-start.1 = (bf16[1,256,2048]{2,1,0:T(8,128)(2,1)S(1)}, bf16[1,256,2048]{2,1,0:T(8,128)(2,1)}, u32[]{:S(2)}) copy-start(bf16[1,256,2048]{2,1,0:T(8,128)(2,1)} %param.8) | copy-start | bytes 3145732
  6.5 10.6 %collective-permute-start = (bf16[2,256,256]{2,1,0:T(8,128)(2,1)S(1)}, bf16[2,256,256]{2,1,0:T(8,128)(2,1)S(1)}, u32[]{:S(2)}, u32[]{:S(2)}) collective-permute-start(bf16[2,256,256]{2,1,0:T(8,128)(2,1)S(1)} %pack_columns.2.refs_1_), channel_id=1, source_target_pairs={{0,1},{1,0},{2,3},{3,2},{4,5},{5,4},{6,7},{7,6},{8,9},{9,8},{10,11... | collective-permute-start | bytes 786440 | tf_op jit(solution)/shard_map/ppermute | solution.py:384
  7.4 17.0 %collective-permute-start.2 = (bf16[256,512]{1,0:T(8,128)(2,1)S(1)}, bf16[256,512]{1,0:T(8,128)(2,1)S(1)}, u32[]{:S(2)}, u32[]{:S(2)}) collective-permute-start(bf16[256,512]{1,0:T(8,128)(2,1)S(1)} %bitcast.13), channel_id=1, source_target_pairs={{2,0},{3,1},{4,2},{5,3},{6,4},{7,5},{0,6},{1,7},{10,8},{11,9},{12,... | collective-permute-start | bytes 786440 | tf_op jit(solution)/shard_map/ppermute | solution.py:381
  14.9 2.2 %copy-start.3 = (bf16[1,256,512]{2,1,0:T(8,128)(2,1)S(1)}, bf16[1,256,512]{2,1,0:T(8,128)(2,1)}, u32[]{:S(2)}) copy-start(bf16[1,256,512]{2,1,0:T(8,128)(2,1)} %param.9) | copy-start | bytes 786436
  15.0 9.5 %collective-permute-start.5 = (bf16[2,256,256]{2,1,0:T(8,128)(2,1)S(1)}, bf16[2,256,256]{2,1,0:T(8,128)(2,1)S(1)}, u32[]{:S(2)}, u32[]{:S(2)}) collective-permute-start(bf16[2,256,256]{2,1,0:T(8,128)(2,1)S(1)} %pack_columns.3), channel_id=1, source_target_pairs={{0,1},{1,0},{2,3},{3,2},{4,5},{5,4},{6,7},{7,6},{8,9},{9,8},{10,11... | collective-permute-start | bytes 786440 | tf_op jit(solution)/shard_map/ppermute | solution.py:384
  15.3 12.3 %collective-permute-start.4 = (bf16[256,512]{1,0:T(8,128)(2,1)S(1)}, bf16[256,512]{1,0:T(8,128)(2,1)S(1)}, u32[]{:S(2)}, u32[]{:S(2)}) collective-permute-start(bf16[256,512]{1,0:T(8,128)(2,1)S(1)} %collective-permute-done.3.refs_2_.refs_3_.refs_4_), channel_id=1, source_target_pairs={{0,2},{1,3},{2,4},{3,5},{4,6},{5,7},{6,0},{7,1},{8,10},{9,11},{10,... | collective-permute-start | bytes 786440 | tf_op jit(solution)/shard_map/ppermute | solution.py:378
  15.3 7.3 %collective-permute-start.6 = (bf16[1,256,256]{2,1,0:T(8,128)(2,1)S(1)}, bf16[1,256,256]{2,1,0:T(8,128)(2,1)S(1)}, u32[]{:S(2)}, u32[]{:S(2)}) collective-permute-start(bf16[1,256,256]{2,1,0:T(8,128)(2,1)S(1)} %partner_columns.2), channel_id=1, source_target_pairs={{0,16},{8,24},{16,0},{24,8},{1,17},{9,25},{17,1},{25,9},{2,18},{10... | collective-permute-start | bytes 393224 | tf_op jit(solution)/shard_map/ppermute | solution.py:92
  17.6 14.3 %collective-permute-start.9 = (bf16[256,512]{1,0:T(8,128)(2,1)S(1)}, bf16[256,512]{1,0:T(8,128)(2,1)S(1)}, u32[]{:S(2)}, u32[]{:S(2)}) collective-permute-start(bf16[256,512]{1,0:T(8,128)(2,1)S(1)} %get-tuple-element.23.refs_4_.refs_2_), channel_id=1, source_target_pairs={{2,0},{3,1},{4,2},{5,3},{6,4},{7,5},{0,6},{1,7},{10,8},{11,9},{12,... | collective-permute-start | bytes 786440 | tf_op jit(solution)/shard_map/ppermute | solution.py:381
  23.1 12.1 %collective-permute-start.11 = (bf16[2,256,256]{2,1,0:T(8,128)(2,1)S(1)}, bf16[2,256,256]{2,1,0:T(8,128)(2,1)S(1)}, u32[]{:S(2)}, u32[]{:S(2)}) collective-permute-start(bf16[2,256,256]{2,1,0:T(8,128)(2,1)S(1)} %get-tuple-element.24.refs_6_.refs_4_), channel_id=1, source_target_pairs={{0,1},{1,0},{2,3},{3,2},{4,5},{5,4},{6,7},{7,6},{8,9},{9,8},{10,11... | collective-permute-start | bytes 786440 | tf_op jit(solution)/shard_map/ppermute | solution.py:384
  28.2 18.6 %collective-permute-start.7 = (bf16[4,256,256]{2,1,0:T(8,128)(2,1)S(1)}, bf16[4,256,256]{2,1,0:T(8,128)(2,1)S(1)}, u32[]{:S(2)}, u32[]{:S(2)}) collective-permute-start(bf16[4,256,256]{2,1,0:T(8,128)(2,1)S(1)} %get-tuple-element.28.refs_2_), channel_id=1, source_target_pairs={{0,1},{1,0},{2,3},{3,2},{4,5},{5,4},{6,7},{7,6},{8,9},{9,8},{10,11... | collective-permute-start | bytes 1572872 | tf_op jit(solution)/shard_map/ppermute | solution.py:384
  29.0 6.2 %collective-permute-start.12 = (bf16[2,256,128]{2,1,0:T(8,128)(2,1)S(1)}, bf16[2,256,128]{2,1,0:T(8,128)(2,1)S(1)}, u32[]{:S(2)}, u32[]{:S(2)}) collective-permute-start(bf16[2,256,128]{2,1,0:T(8,128)(2,1)S(1)} %partner_columns.3), channel_id=1, source_target_pairs={{0,8},{8,0},{16,24},{24,16},{1,9},{9,1},{17,25},{25,17},{2,10},{10... | collective-permute-start | bytes 393224 | tf_op jit(solution)/shard_map/ppermute | solution.py:92
  29.1 13.7 %collective-permute-start.8 = (bf16[256,512]{1,0:T(8,128)(2,1)S(1)}, bf16[256,512]{1,0:T(8,128)(2,1)S(1)}, u32[]{:S(2)}, u32[]{:S(2)}) collective-permute-start(bf16[256,512]{1,0:T(8,128)(2,1)S(1)} %get-tuple-element.30.refs_3_), channel_id=1, source_target_pairs={{0,2},{1,3},{2,4},{3,5},{4,6},{5,7},{6,0},{7,1},{8,10},{9,11},{10,... | collective-permute-start | bytes 786440 | tf_op jit(solution)/shard_map/ppermute | solution.py:378
  31.9 3.3 %copy-start.4 = (bf16[256,512]{1,0:T(8,128)(2,1)S(1)}, bf16[256,512]{1,0:T(8,128)(2,1)}, u32[]{:S(2)}) copy-start(bf16[256,512]{1,0:T(8,128)(2,1)} %refs_3_.1) | copy-start | bytes 786436
  31.9 3.2 %copy-start.5 = (f32[256,128]{1,0:T(8,128)S(1)}, f32[256,128]{1,0:T(8,128)}, u32[]{:S(2)}) copy-start(f32[256,128]{1,0:T(8,128)} %refs_4_.1) | copy-start | bytes 393220
  32.0 14.8 %collective-permute-start.10 = (bf16[256,512]{1,0:T(8,128)(2,1)S(1)}, bf16[256,512]{1,0:T(8,128)(2,1)S(1)}, u32[]{:S(2)}, u32[]{:S(2)}) collective-permute-start(bf16[256,512]{1,0:T(8,128)(2,1)S(1)} %add_terms.1.refs_5_), channel_id=1, source_target_pairs={{2,0},{3,1},{4,2},{5,3},{6,4},{7,5},{0,6},{1,7},{10,8},{11,9},{12,... | collective-permute-start | bytes 786440 | tf_op jit(solution)/shard_map/ppermute | solution.py:381
  36.3 4.3 %collective-permute-start.13 = (bf16[256,128]{1,0:T(8,128)(2,1)S(1)}, bf16[256,128]{1,0:T(8,128)(2,1)S(1)}, u32[]{:S(2)}, u32[]{:S(2)}) collective-permute-start(bf16[256,128]{1,0:T(8,128)(2,1)S(1)} %get-tuple-element.38), channel_id=1, source_target_pairs={{0,16},{8,24},{16,0},{24,8},{1,17},{9,25},{17,1},{25,9},{2,18},{10... | collective-permute-start | bytes 196616 | tf_op jit(solution)/shard_map/ppermute | solution.py:92
  40.6 1.4 %collective-permute-start.14 = (bf16[256,256]{1,0:T(8,128)(2,1)S(1)}, bf16[256,256]{1,0:T(8,128)(2,1)S(1)}, u32[]{:S(2)}, u32[]{:S(2)}) collective-permute-start(bf16[256,256]{1,0:T(8,128)(2,1)S(1)} %constant_dynamic-update-slice_fusion.refs_0_), channel_id=1, source_target_pairs={{0,8},{8,0},{16,24},{24,16},{1,9},{9,1},{17,25},{25,17},{2,10},{10... | collective-permute-start | bytes 393224 | tf_op jit(solution)/shard_map/ppermute | solution.py:92

commit v10 on v8

--- a/solution.py
+++ b/solution.py
@@ -426,7 +426,7 @@
         add_kernel, shape_of(depth, kv_width, BF16), [terms[0], sum_down], 0, "add_terms", (leaving,)
     )
     sum_down = downward(total_down)
-    new_share, new_momentum = update_share(held, global_weights, momentum, (total_down, early))
+    new_share, new_momentum = update_share(held, global_weights, momentum, (total_down, early, sum_up))
     bits = lax.axis_size("replica")
     shares, joined = [new_share], [0]
     while bits > 1:

time: 44.5 us -> 44.4 us (level)
  waiting for transfers between devices: 15.8 us -> 18.8 us
  starting transfers between devices: 19.6 us -> 16.7 us
    ppermute x3, waiting for transfers between devices: 2.76 us -> 9.73 us  [upward(): return lax.ppermute(array, 'fsdp', pairs)]
    ppermute x3, waiting for transfers between devices: 4.57 us -> 0.66 us  [downward(): lax.ppermute(array, 'fsdp', [(target, source) for source, target in pairs])]
    ppermute x3, starting transfers between devices: 7.71 us -> 5.88 us  [upward(): return lax.ppermute(array, 'fsdp', pairs)]
    ppermute x5, starting transfers between devices: 7.84 us -> 6.75 us  [across(): return lax.ppermute(array, 'fsdp', [(at, at ^ 1) for at in range(size)])]
where the time goes in v10:
time: 44.4 us; the launch traced here: 44.2 us
  waiting for transfers between devices  18.8 us (42%)
  starting transfers between devices  16.7 us (38%)
  Pallas kernels  6.43 us (14%)
  local copies, waits for them, and re-layouts  1.57 us (4%)
  between operations  0.76 us (2%)
    ppermute x3, waiting for transfers between devices, upward(): return lax.ppermute(array, 'fsdp', pairs)  9.73 us
    ppermute x5, starting transfers between devices, across(): return lax.ppermute(array, 'fsdp', [(at, at ^ 1) for at in range(size)])  6.75 us
    ppermute x4, waiting for transfers between devices, swap(): lax.ppermute(array, 'replica', [(at, at ^ bits) for at in range(lax.axis_...  6.02 us
    ppermute x3, starting transfers between devices, upward(): return lax.ppermute(array, 'fsdp', pairs)  5.88 us
    pallas_call x12, Pallas kernels, vmem_call(): pl.pallas_call(body, out_shape=out_shape, in_specs=[whole] * len(operands...  4.56 us
    ppermute x4, starting transfers between devices, swap(): lax.ppermute(array, 'replica', [(at, at ^ bits) for at in range(lax.axis_...  3.25 us
    ppermute x5, waiting for transfers between devices, across(): return lax.ppermute(array, 'fsdp', [(at, at ^ 1) for at in range(size)])  2.41 us
    unnamed x13, local copies, waits for them, and re-layouts  1.56 us
  transfers between devices with their start and end apart: 15, of which 8 were waited for; matrix products, arithmetic and copies ran while one was open for 0% of the time, Pallas kernels for 12%

profile of v10, /device:TPU:0, one launch (start us, length us, event | category | flops | bytes accessed | tf_op | source)
XLA Modules:
  0.0 44.2 jit_solution(1972288803023862549)
XLA Ops:
  0.6 3.0 %collective-permute-start.1 = (bf16[256,512]{1,0:T(8,128)(2,1)}, bf16[256,512]{1,0:T(8,128)(2,1)S(1)}, u32[]{:S(2)}, u32[]{:S(2)}) collective-permute-start(bf16[256,512]{1,0:T(8,128)(2,1)} %bitcast.19), channel_id=1, source_target_pairs={{0,1},{1,0},{2,3},{3,2},{4,5},{5,4},{6,7},{7,6},{8,9},{9,8},{10,11... | collective-permute-start | bytes 786440 | tf_op jit(solution)/shard_map/ppermute | solution.py:399
  3.6 2.6 %collective-permute-start.3 = (bf16[256,512]{1,0:T(8,128)(2,1)}, bf16[256,512]{1,0:T(8,128)(2,1)S(1)}, u32[]{:S(2)}, u32[]{:S(2)}) collective-permute-start(bf16[256,512]{1,0:T(8,128)(2,1)} %bitcast.12), channel_id=1, source_target_pairs={{2,0},{3,1},{0,4},{1,5},{4,6},{5,7},{6,2},{7,3},{10,8},{11,9},{8,1... | collective-permute-start | bytes 786440 | tf_op jit(solution)/shard_map/ppermute | solution.py:393
  6.2 1.2 %copy-done = bf16[1,256,2048]{2,1,0:T(8,128)(2,1)S(1)} copy-done((bf16[1,256,2048]{2,1,0:T(8,128)(2,1)S(1)}, bf16[1,256,2048]{2,1,0:T(8,128)(2,1)}, u32[]{:S(2)}) %copy-start) | copy-done | bytes 1048600
  7.5 0.6 %collective-permute-start = (bf16[2,256,256]{2,1,0:T(8,128)(2,1)S(1)}, bf16[2,256,256]{2,1,0:T(8,128)(2,1)S(1)}, u32[]{:S(2)}, u32[]{:S(2)}) collective-permute-start(bf16[2,256,256]{2,1,0:T(8,128)(2,1)S(1)} %pack_columns.2.refs_1_), channel_id=1, source_target_pairs={{0,1},{1,0},{2,3},{3,2},{4,5},{5,4},{6,7},{7,6},{8,9},{9,8},{10,11... | collective-permute-start | bytes 786440 | tf_op jit(solution)/shard_map/ppermute | solution.py:399
  8.4 2.4 %collective-permute-done.1.refs_1_.refs_3_ = bf16[256,512]{1,0:T(8,128)(2,1)S(1)} collective-permute-done((bf16[256,512]{1,0:T(8,128)(2,1)}, bf16[256,512]{1,0:T(8,128)(2,1)S(1)}, u32[]{:S(2)}, u32[]{:S(2)}) %collective-permute-start.1) | collective-permute-done | bytes 262176 | tf_op jit(solution)/shard_map/ppermute | solution.py:399
  10.8 2.5 %collective-permute-done.3.refs_2_.refs_3_.refs_4_ = bf16[256,512]{1,0:T(8,128)(2,1)S(1)} collective-permute-done((bf16[256,512]{1,0:T(8,128)(2,1)}, bf16[256,512]{1,0:T(8,128)(2,1)S(1)}, u32[]{:S(2)}, u32[]{:S(2)}) %collective-permute-start.3) | collective-permute-done | bytes 262176 | tf_op jit(solution)/shard_map/ppermute | solution.py:393
  13.4 0.6 %collective-permute-start.5 = (bf16[2,256,256]{2,1,0:T(8,128)(2,1)S(1)}, bf16[2,256,256]{2,1,0:T(8,128)(2,1)S(1)}, u32[]{:S(2)}, u32[]{:S(2)}) collective-permute-start(bf16[2,256,256]{2,1,0:T(8,128)(2,1)S(1)} %pack_columns.3), channel_id=1, source_target_pairs={{0,1},{1,0},{2,3},{3,2},{4,5},{5,4},{6,7},{7,6},{8,9},{9,8},{10,11... | collective-permute-start | bytes 786440 | tf_op jit(solution)/shard_map/ppermute | solution.py:399
  14.0 3.3 %collective-permute-start.4 = (bf16[256,512]{1,0:T(8,128)(2,1)S(1)}, bf16[256,512]{1,0:T(8,128)(2,1)S(1)}, u32[]{:S(2)}, u32[]{:S(2)}) collective-permute-start(bf16[256,512]{1,0:T(8,128)(2,1)S(1)} %collective-permute-done.3.refs_2_.refs_3_.refs_4_), channel_id=1, source_target_pairs={{2,0},{3,1},{0,4},{1,5},{4,6},{5,7},{6,2},{7,3},{10,8},{11,9},{8,1... | collective-permute-start | bytes 786440 | tf_op jit(solution)/shard_map/ppermute | solution.py:393
  17.2 1.6 %collective-permute-start.6 = (bf16[1,256,256]{2,1,0:T(8,128)(2,1)S(1)}, bf16[1,256,256]{2,1,0:T(8,128)(2,1)S(1)}, u32[]{:S(2)}, u32[]{:S(2)}) collective-permute-start(bf16[1,256,256]{2,1,0:T(8,128)(2,1)S(1)} %partner_columns.2), channel_id=1, source_target_pairs={{0,16},{8,24},{16,0},{24,8},{1,17},{9,25},{17,1},{25,9},{2,18},{10... | collective-permute-start | bytes 393224 | tf_op jit(solution)/shard_map/ppermute | solution.py:106
  19.4 2.9 %collective-permute-done.6.refs_5_.refs_1_ = bf16[1,256,256]{2,1,0:T(8,128)(2,1)S(1)} collective-permute-done((bf16[1,256,256]{2,1,0:T(8,128)(2,1)S(1)}, bf16[1,256,256]{2,1,0:T(8,128)(2,1)S(1)}, u32[]{:S(2)}, u32[]{:S(2)}) %collective-permute-start.6) | collective-permute-done | bytes 131104 | tf_op jit(solution)/shard_map/ppermute | solution.py:106
  22.8 1.6 %collective-permute-start.11 = (bf16[2,256,256]{2,1,0:T(8,128)(2,1)S(1)}, bf16[2,256,256]{2,1,0:T(8,128)(2,1)S(1)}, u32[]{:S(2)}, u32[]{:S(2)}) collective-permute-start(bf16[2,256,256]{2,1,0:T(8,128)(2,1)S(1)} %get-tuple-element.24.refs_6_.refs_4_), channel_id=1, source_target_pairs={{0,1},{1,0},{2,3},{3,2},{4,5},{5,4},{6,7},{7,6},{8,9},{9,8},{10,11... | collective-permute-start | bytes 786440 | tf_op jit(solution)/shard_map/ppermute | solution.py:399
  24.4 0.6 %near_rows.1 = (f32[256,512]{1,0:T(8,128)S(1)}, f32[256,512]{1,0:T(8,128)S(1)}) custom-call(bf16[256,2048]{1,0:T(8,128)(2,1)S(1)} %bitcast.9, bf16[2,256,256]{2,1,0:T(8,128)(2,1)S(1)} %collective-permute-done.refs_2_.refs_1_, bf16[2,256,256]{2,1,0:T(8,128)(2,1)S(1)} %collective-permute-done.5.refs_2_, bf16[256,512]{1,0:T(8,128)(2,1)S(1)} %bitcast.16, ...), custom_call_target="tpu_custom_call" | custom-call | flops 402653184 | bytes 2359296 | tf_op jit(solution)/shard_map/near_rows/pallas_call | solution.py:48
  24.9 4.2 %collective-permute-done.4.refs_5_ = bf16[256,512]{1,0:T(8,128)(2,1)S(1)} collective-permute-done((bf16[256,512]{1,0:T(8,128)(2,1)S(1)}, bf16[256,512]{1,0:T(8,128)(2,1)S(1)}, u32[]{:S(2)}, u32[]{:S(2)}) %collective-permute-start.4) | collective-permute-done | bytes 262176 | tf_op jit(solution)/shard_map/ppermute | solution.py:393
  29.1 0.6 %last_products.1 = (f32[256,512]{1,0:T(8,128)S(1)}, bf16[2,256,256]{2,1,0:T(8,128)(2,1)S(1)}, bf16[4,256,256]{2,1,0:T(8,128)(2,1)S(1)}) custom-call(bf16[256,2048]{1,0:T(8,128)(2,1)S(1)} %bitcast.10, bf16[256,512]{1,0:T(8,128)(2,1)S(1)} %bitcast.22, bf16[2,256,256]{2,1,0:T(8,128)(2,1)S(1)} %collective-permute-done.refs_2_.refs_1_, ...), custom_call_target="tpu_custom_call" | custom-call | flops 268435456 | bytes 3407872 | tf_op jit(solution)/shard_map/last_products/pallas_call | solution.py:48
  29.7 1.0 %collective-permute-start.7 = (bf16[4,256,256]{2,1,0:T(8,128)(2,1)S(1)}, bf16[4,256,256]{2,1,0:T(8,128)(2,1)S(1)}, u32[]{:S(2)}, u32[]{:S(2)}) collective-permute-start(bf16[4,256,256]{2,1,0:T(8,128)(2,1)S(1)} %get-tuple-element.28.refs_2_), channel_id=1, source_target_pairs={{0,1},{1,0},{2,3},{3,2},{4,5},{5,4},{6,7},{7,6},{8,9},{9,8},{10,11... | collective-permute-start | bytes 1572872 | tf_op jit(solution)/shard_map/ppermute | solution.py:399
  31.3 0.7 %collective-permute-done.9.refs_1_ = bf16[256,512]{1,0:T(8,128)(2,1)S(1)} collective-permute-done((bf16[256,512]{1,0:T(8,128)(2,1)S(1)}, bf16[256,512]{1,0:T(8,128)(2,1)S(1)}, u32[]{:S(2)}, u32[]{:S(2)}) %collective-permute-start.9) | collective-permute-done | bytes 262176 | tf_op jit(solution)/shard_map/ppermute | solution.py:396
  32.0 0.7 %collective-permute-start.10 = (bf16[256,512]{1,0:T(8,128)(2,1)S(1)}, bf16[256,512]{1,0:T(8,128)(2,1)S(1)}, u32[]{:S(2)}, u32[]{:S(2)}) collective-permute-start(bf16[256,512]{1,0:T(8,128)(2,1)S(1)} %add_terms.1.refs_5_), channel_id=1, source_target_pairs={{0,2},{1,3},{4,0},{5,1},{6,4},{7,5},{2,6},{3,7},{8,10},{9,11},{12,... | collective-permute-start | bytes 786440 | tf_op jit(solution)/shard_map/ppermute | solution.py:396
  32.7 3.0 %collective-permute-done.8.up_ref.refs_7_ = bf16[256,512]{1,0:T(8,128)(2,1)S(1)} collective-permute-done((bf16[256,512]{1,0:T(8,128)(2,1)S(1)}, bf16[256,512]{1,0:T(8,128)(2,1)S(1)}, u32[]{:S(2)}, u32[]{:S(2)}) %collective-permute-start.8) | collective-permute-done | bytes 262176 | tf_op jit(solution)/shard_map/ppermute | solution.py:393
  35.7 1.1 %outer_update.1 = (bf16[256,128]{1,0:T(8,128)(2,1)S(1)}, f32[256,128]{1,0:T(8,128)}) custom-call(bf16[256,512]{1,0:T(8,128)(2,1)S(1)} %bitcast.18, bf16[1,256,256]{2,1,0:T(8,128)(2,1)S(1)} %collective-permute-done.6.refs_5_.refs_1_, bf16[2,256,128]{2,1,0:T(8,128)(2,1)S(1)} %collective-permute-done.12.refs_2_, bf16[256,512]{1,0:T(8,128)(2,1)S(1)} %copy-done.4, ...), custom_call_target="tpu_custom_call" | custom-call | bytes 917504 | tf_op jit(solution)/shard_map/outer_update/pallas_call | solution.py:48
  36.8 1.5 %collective-permute-start.13 = (bf16[256,128]{1,0:T(8,128)(2,1)S(1)}, bf16[256,128]{1,0:T(8,128)(2,1)S(1)}, u32[]{:S(2)}, u32[]{:S(2)}) collective-permute-start(bf16[256,128]{1,0:T(8,128)(2,1)S(1)} %get-tuple-element.38), channel_id=1, source_target_pairs={{0,16},{8,24},{16,0},{24,8},{1,17},{9,25},{17,1},{25,9},{2,18},{10... | collective-permute-start | bytes 196616 | tf_op jit(solution)/shard_map/ppermute | solution.py:106
  38.4 2.7 %collective-permute-done.13 = bf16[256,128]{1,0:T(8,128)(2,1)S(1)} collective-permute-done((bf16[256,128]{1,0:T(8,128)(2,1)S(1)}, bf16[256,128]{1,0:T(8,128)(2,1)S(1)}, u32[]{:S(2)}, u32[]{:S(2)}) %collective-permute-start.13) | collective-permute-done | bytes 65568 | tf_op jit(solution)/shard_map/ppermute | solution.py:106
  41.2 0.9 %collect.1 = (bf16[256,2048]{1,0:T(8,128)(2,1)}, f32[8,128]{1,0:T(8,128)S(1)}) custom-call(bf16[2,256,256]{2,1,0:T(8,128)(2,1)S(1)} %get-tuple-element.32.near_ref, bf16[2,256,256]{2,1,0:T(8,128)(2,1)S(1)} %get-tuple-element.33.last_ref, bf16[2,256,256]{2,1,0:T(8,128)(2,1)S(1)} %collective-permute-done.11.early_ref.refs_6_), custom_call_target="tpu_custom_call" | custom-call | bytes 1048576 | tf_op jit(solution)/shard_map/collect/pallas_call | solution.py:333
  42.5 0.8 %join_shares.1 = bf16[256,512]{1,0:T(8,128)(2,1)} custom-call(bf16[256,256]{1,0:T(8,128)(2,1)S(1)} %constant_dynamic-update-slice_fusion.refs_0_, bf16[256,256]{1,0:T(8,128)(2,1)S(1)} %collective-permute-done.14.refs_1_, f32[8,128]{1,0:T(8,128)S(1)} %get-tuple-element.39.refs_2_), custom_call_target="tpu_custom_call" | custom-call | bytes 262144 | tf_op jit(solution)/shard_map/join_shares/pallas_call | solution.py:48
  43.3 0.9 %finish.1 = (bf16[256,512]{1,0:T(8,128)(2,1)}, bf16[256,2048]{1,0:T(8,128)(2,1)}, bf16[256,512]{1,0:T(8,128)(2,1)}) custom-call(f32[256,512]{1,0:T(8,128)S(1)} %get-tuple-element.27.total_ref, bf16[4,256,256]{2,1,0:T(8,128)(2,1)S(1)} %collective-permute-done.7.late_ref, f32[256,512]{1,0:T(8,128)S(1)} %get-tuple-element.29.terms_ref, ...), custom_call_target="tpu_custom_call", output_to_operand_aliasing={{1}: (5, {})} | custom-call | bytes 1048576 | tf_op jit(solution)/shard_map/finish/pallas_call | solution.py:364
  (34 shorter events, 2.5 us)
Async XLA Ops:
  0.6 10.2 %collective-permute-start.1 = (bf16[256,512]{1,0:T(8,128)(2,1)}, bf16[256,512]{1,0:T(8,128)(2,1)S(1)}, u32[]{:S(2)}, u32[]{:S(2)}) collective-permute-start(bf16[256,512]{1,0:T(8,128)(2,1)} %bitcast.19), channel_id=1, source_target_pairs={{0,1},{1,0},{2,3},{3,2},{4,5},{5,4},{6,7},{7,6},{8,9},{9,8},{10,11... | collective-permute-start | bytes 786440 | tf_op jit(solution)/shard_map/ppermute | solution.py:399
  3.6 9.7 %collective-permute-start.3 = (bf16[256,512]{1,0:T(8,128)(2,1)}, bf16[256,512]{1,0:T(8,128)(2,1)S(1)}, u32[]{:S(2)}, u32[]{:S(2)}) collective-permute-start(bf16[256,512]{1,0:T(8,128)(2,1)} %bitcast.12), channel_id=1, source_target_pairs={{2,0},{3,1},{0,4},{1,5},{4,6},{5,7},{6,2},{7,3},{10,8},{11,9},{8,1... | collective-permute-start | bytes 786440 | tf_op jit(solution)/shard_map/ppermute | solution.py:393
  6.2 1.2 %copy-start = (bf16[1,256,2048]{2,1,0:T(8,128)(2,1)S(1)}, bf16[1,256,2048]{2,1,0:T(8,128)(2,1)}, u32[]{:S(2)}) copy-start(bf16[1,256,2048]{2,1,0:T(8,128)(2,1)} %param.8) | copy-start | bytes 3145732
  7.4 0.9 %copy-start.2 = (bf16[1,256,512]{2,1,0:T(8,128)(2,1)S(1)}, bf16[1,256,512]{2,1,0:T(8,128)(2,1)}, u32[]{:S(2)}) copy-start(bf16[1,256,512]{2,1,0:T(8,128)(2,1)} %param.5) | copy-start | bytes 786436
  7.5 11.3 %copy-start.1 = (bf16[1,256,2048]{2,1,0:T(8,128)(2,1)S(1)}, bf16[1,256,2048]{2,1,0:T(8,128)(2,1)}, u32[]{:S(2)}) copy-start(bf16[1,256,2048]{2,1,0:T(8,128)(2,1)} %param.8) | copy-start | bytes 3145732
  7.5 11.3 %collective-permute-start = (bf16[2,256,256]{2,1,0:T(8,128)(2,1)S(1)}, bf16[2,256,256]{2,1,0:T(8,128)(2,1)S(1)}, u32[]{:S(2)}, u32[]{:S(2)}) collective-permute-start(bf16[2,256,256]{2,1,0:T(8,128)(2,1)S(1)} %pack_columns.2.refs_1_), channel_id=1, source_target_pairs={{0,1},{1,0},{2,3},{3,2},{4,5},{5,4},{6,7},{7,6},{8,9},{9,8},{10,11... | collective-permute-start | bytes 786440 | tf_op jit(solution)/shard_map/ppermute | solution.py:399
  8.4 15.9 %collective-permute-start.2 = (bf16[256,512]{1,0:T(8,128)(2,1)S(1)}, bf16[256,512]{1,0:T(8,128)(2,1)S(1)}, u32[]{:S(2)}, u32[]{:S(2)}) collective-permute-start(bf16[256,512]{1,0:T(8,128)(2,1)S(1)} %bitcast.13), channel_id=1, source_target_pairs={{0,2},{1,3},{4,0},{5,1},{6,4},{7,5},{2,6},{3,7},{8,10},{9,11},{12,... | collective-permute-start | bytes 786440 | tf_op jit(solution)/shard_map/ppermute | solution.py:396
  13.4 5.5 %copy-start.3 = (bf16[1,256,512]{2,1,0:T(8,128)(2,1)S(1)}, bf16[1,256,512]{2,1,0:T(8,128)(2,1)}, u32[]{:S(2)}) copy-start(bf16[1,256,512]{2,1,0:T(8,128)(2,1)} %param.9) | copy-start | bytes 786436
  13.4 11.0 %collective-permute-start.5 = (bf16[2,256,256]{2,1,0:T(8,128)(2,1)S(1)}, bf16[2,256,256]{2,1,0:T(8,128)(2,1)S(1)}, u32[]{:S(2)}, u32[]{:S(2)}) collective-permute-start(bf16[2,256,256]{2,1,0:T(8,128)(2,1)S(1)} %pack_columns.3), channel_id=1, source_target_pairs={{0,1},{1,0},{2,3},{3,2},{4,5},{5,4},{6,7},{7,6},{8,9},{9,8},{10,11... | collective-permute-start | bytes 786440 | tf_op jit(solution)/shard_map/ppermute | solution.py:399
  14.0 15.2 %collective-permute-start.4 = (bf16[256,512]{1,0:T(8,128)(2,1)S(1)}, bf16[256,512]{1,0:T(8,128)(2,1)S(1)}, u32[]{:S(2)}, u32[]{:S(2)}) collective-permute-start(bf16[256,512]{1,0:T(8,128)(2,1)S(1)} %collective-permute-done.3.refs_2_.refs_3_.refs_4_), channel_id=1, source_target_pairs={{2,0},{3,1},{0,4},{1,5},{4,6},{5,7},{6,2},{7,3},{10,8},{11,9},{8,1... | collective-permute-start | bytes 786440 | tf_op jit(solution)/shard_map/ppermute | solution.py:393
  17.2 5.0 %collective-permute-start.6 = (bf16[1,256,256]{2,1,0:T(8,128)(2,1)S(1)}, bf16[1,256,256]{2,1,0:T(8,128)(2,1)S(1)}, u32[]{:S(2)}, u32[]{:S(2)}) collective-permute-start(bf16[1,256,256]{2,1,0:T(8,128)(2,1)S(1)} %partner_columns.2), channel_id=1, source_target_pairs={{0,16},{8,24},{16,0},{24,8},{1,17},{9,25},{17,1},{25,9},{2,18},{10... | collective-permute-start | bytes 393224 | tf_op jit(solution)/shard_map/ppermute | solution.py:106
  19.3 12.6 %collective-permute-start.9 = (bf16[256,512]{1,0:T(8,128)(2,1)S(1)}, bf16[256,512]{1,0:T(8,128)(2,1)S(1)}, u32[]{:S(2)}, u32[]{:S(2)}) collective-permute-start(bf16[256,512]{1,0:T(8,128)(2,1)S(1)} %get-tuple-element.23.refs_4_.refs_2_), channel_id=1, source_target_pairs={{0,2},{1,3},{4,0},{5,1},{6,4},{7,5},{2,6},{3,7},{8,10},{9,11},{12,... | collective-permute-start | bytes 786440 | tf_op jit(solution)/shard_map/ppermute | solution.py:396
  22.8 10.0 %collective-permute-start.11 = (bf16[2,256,256]{2,1,0:T(8,128)(2,1)S(1)}, bf16[2,256,256]{2,1,0:T(8,128)(2,1)S(1)}, u32[]{:S(2)}, u32[]{:S(2)}) collective-permute-start(bf16[2,256,256]{2,1,0:T(8,128)(2,1)S(1)} %get-tuple-element.24.refs_6_.refs_4_), channel_id=1, source_target_pairs={{0,1},{1,0},{2,3},{3,2},{4,5},{5,4},{6,7},{7,6},{8,9},{9,8},{10,11... | collective-permute-start | bytes 786440 | tf_op jit(solution)/shard_map/ppermute | solution.py:399
  24.3 11.4 %collective-permute-start.8 = (bf16[256,512]{1,0:T(8,128)(2,1)S(1)}, bf16[256,512]{1,0:T(8,128)(2,1)S(1)}, u32[]{:S(2)}, u32[]{:S(2)}) collective-permute-start(bf16[256,512]{1,0:T(8,128)(2,1)S(1)} %get-tuple-element.30.refs_3_), channel_id=1, source_target_pairs={{2,0},{3,1},{0,4},{1,5},{4,6},{5,7},{6,2},{7,3},{10,8},{11,9},{8,1... | collective-permute-start | bytes 786440 | tf_op jit(solution)/shard_map/ppermute | solution.py:393
  29.7 13.6 %collective-permute-start.7 = (bf16[4,256,256]{2,1,0:T(8,128)(2,1)S(1)}, bf16[4,256,256]{2,1,0:T(8,128)(2,1)S(1)}, u32[]{:S(2)}, u32[]{:S(2)}) collective-permute-start(bf16[4,256,256]{2,1,0:T(8,128)(2,1)S(1)} %get-tuple-element.28.refs_2_), channel_id=1, source_target_pairs={{0,1},{1,0},{2,3},{3,2},{4,5},{5,4},{6,7},{7,6},{8,9},{9,8},{10,11... | collective-permute-start | bytes 1572872 | tf_op jit(solution)/shard_map/ppermute | solution.py:399
  30.7 2.0 %collective-permute-start.12 = (bf16[2,256,128]{2,1,0:T(8,128)(2,1)S(1)}, bf16[2,256,128]{2,1,0:T(8,128)(2,1)S(1)}, u32[]{:S(2)}, u32[]{:S(2)}) collective-permute-start(bf16[2,256,128]{2,1,0:T(8,128)(2,1)S(1)} %partner_columns.3), channel_id=1, source_target_pairs={{0,8},{8,0},{16,24},{24,16},{1,9},{9,1},{17,25},{25,17},{2,10},{10... | collective-permute-start | bytes 393224 | tf_op jit(solution)/shard_map/ppermute | solution.py:106
  31.9 3.8 %copy-start.4 = (bf16[256,512]{1,0:T(8,128)(2,1)S(1)}, bf16[256,512]{1,0:T(8,128)(2,1)}, u32[]{:S(2)}) copy-start(bf16[256,512]{1,0:T(8,128)(2,1)} %refs_3_.1) | copy-start | bytes 786436
  31.9 3.8 %copy-start.5 = (f32[256,128]{1,0:T(8,128)S(1)}, f32[256,128]{1,0:T(8,128)}, u32[]{:S(2)}) copy-start(f32[256,128]{1,0:T(8,128)} %refs_4_.1) | copy-start | bytes 393220
  32.0 11.3 %collective-permute-start.10 = (bf16[256,512]{1,0:T(8,128)(2,1)S(1)}, bf16[256,512]{1,0:T(8,128)(2,1)S(1)}, u32[]{:S(2)}, u32[]{:S(2)}) collective-permute-start(bf16[256,512]{1,0:T(8,128)(2,1)S(1)} %add_terms.1.refs_5_), channel_id=1, source_target_pairs={{0,2},{1,3},{4,0},{5,1},{6,4},{7,5},{2,6},{3,7},{8,10},{9,11},{12,... | collective-permute-start | bytes 786440 | tf_op jit(solution)/shard_map/ppermute | solution.py:396
  36.8 4.3 %collective-permute-start.13 = (bf16[256,128]{1,0:T(8,128)(2,1)S(1)}, bf16[256,128]{1,0:T(8,128)(2,1)S(1)}, u32[]{:S(2)}, u32[]{:S(2)}) collective-permute-start(bf16[256,128]{1,0:T(8,128)(2,1)S(1)} %get-tuple-element.38), channel_id=1, source_target_pairs={{0,16},{8,24},{16,0},{24,8},{1,17},{9,25},{17,1},{25,9},{2,18},{10... | collective-permute-start | bytes 196616 | tf_op jit(solution)/shard_map/ppermute | solution.py:106
  41.1 1.4 %collective-permute-start.14 = (bf16[256,256]{1,0:T(8,128)(2,1)S(1)}, bf16[256,256]{1,0:T(8,128)(2,1)S(1)}, u32[]{:S(2)}, u32[]{:S(2)}) collective-permute-start(bf16[256,256]{1,0:T(8,128)(2,1)S(1)} %constant_dynamic-update-slice_fusion.refs_0_), channel_id=1, source_target_pairs={{0,8},{8,0},{16,24},{24,16},{1,9},{9,1},{17,25},{25,17},{2,10},{10... | collective-permute-start | bytes 393224 | tf_op jit(solution)/shard_map/ppermute | solution.py:106

commit v11 on v10

--- a/solution.py
+++ b/solution.py
@@ -169,6 +169,19 @@
             at += 1
 
 
+def beside_kernel(left_ref, right_ref, out_ref):
+    width = left_ref.shape[1]
+    out_ref[:, :width] = left_ref[...]
+    out_ref[:, width:] = right_ref[...]
+
+
+def beside(left, right, after):
+    rows, width = left.shape
+    if width % LANES:
+        return jnp.concatenate([left, right], axis=1)
+    return vmem_call(beside_kernel, shape_of(rows, 2 * width, BF16), [left, right], 0, "beside", after)
+
+
 def join_shares(held, places, kv_width, after):
     rows = held[0].shape[0]
     width = kv_width // len(places)
@@ -187,6 +200,14 @@
 PARTNER = {2: (0, 0), 1: (0, 1), 3: (1, 0), 0: (1, 1)}
 
 
+def mark_kernel(out_ref):
+    out_ref[...] = jnp.zeros_like(out_ref)
+
+
+def arrived(after):
+    return vmem_call(mark_kernel, shape_of(8, LANES, F32), [], 0, "mark", after)
+
+
 def pack_kernel(size, part, inputs_ref, out_ref):
     depth = inputs_ref.shape[1] // size
     for offset, (at, slot) in PARTNER.items():
@@ -290,7 +311,7 @@
     rows_ref[...] = here_ref[...] + jnp.dot(columns, last, preferred_element_type=F32)
 
 
-def last_products(inputs_here, cotangent, partner_inputs, partner_cotangent, blocks, totals, size):
+def last_products(inputs_here, cotangent, partner_inputs, partner_cotangent, blocks, totals, size, after):
     tokens = inputs_here.shape[0]
     offsets = list(blocks)
     depth, kv_width = blocks[offsets[-1]].shape
@@ -305,6 +326,7 @@
         [inputs_here, cotangent, partner, partner_cotangent, *blocks.values(), *totals],
         8 * tokens * depth * kv_width,
         "last_products",
+        after,
     )
 
 
@@ -404,7 +426,7 @@
 
     bits = lax.axis_size("replica") // 2
     held = send_windows([local_shard], bits, kv_width, (packed,))
-    partner_inputs = [across(packed), across(pack(inputs_here, size, 1, (partner_cotangent, from_below)))]
+    partner_inputs = [across(packed), across(pack(inputs_here, size, 1, (partner_cotangent, arrived((from_below,)))))]
 
     early_blocks, late_blocks = {0: local_shard, 3: from_below}, {1: from_above, 2: upward(from_below)}
     operands = [inputs_here, cotangent, partner_inputs[0], partner_cotangent]
@@ -419,19 +441,19 @@
     terms = token_terms(operands, size, [3, 0], F32, token_weight, (leaving,))
     totals = near_rows(inputs_here, partner_inputs, {**early_blocks, 1: from_above}, size, (leaving,))
     rows, last, leaving = last_products(
-        inputs_here, cotangent, partner_inputs, partner_cotangent, late_blocks, totals, size
+        inputs_here, cotangent, partner_inputs, partner_cotangent, late_blocks, totals, size, ()
     )
     late = across(leaving)
     total_down = vmem_call(
-        add_kernel, shape_of(depth, kv_width, BF16), [terms[0], sum_down], 0, "add_terms", (leaving,)
+        add_kernel, shape_of(depth, kv_width, BF16), [terms[0], sum_down], 0, "add_terms", (leaving, early)
     )
     sum_down = downward(total_down)
-    new_share, new_momentum = update_share(held, global_weights, momentum, (total_down, early, sum_up))
+    new_share, new_momentum = update_share(held, global_weights, momentum, (total_down,))
     bits = lax.axis_size("replica")
     shares, joined = [new_share], [0]
     while bits > 1:
         bits //= 2
-        shares = [shares[0] if len(shares) == 1 else jnp.concatenate(shares, axis=1)]
+        shares = [shares[0] if len(shares) == 1 else beside(*shares, (sum_up,))]
         shares.append(swap(shares[0], bits))
         joined += [place ^ bits for place in joined]
     grad, mark = collect([near, last, early], width, size, list(early_blocks), list(late_blocks))

time: 44.4 us -> 42.5 us (0.957)
  waiting for transfers between devices: 18.8 us -> 16.3 us
  local copies, waits for them, and re-layouts: 1.57 us -> 2.06 us
    ppermute x3, waiting for transfers between devices: 9.73 us -> 3.38 us  [upward(): return lax.ppermute(array, 'fsdp', pairs)]
    ppermute x5, waiting for transfers between devices: 2.41 us -> 7.03 us  [across(): return lax.ppermute(array, 'fsdp', [(at, at ^ 1) for at in range(size)])]
    ppermute x3, starting transfers between devices: 5.88 us -> 7.24 us  [upward(): return lax.ppermute(array, 'fsdp', pairs)]
    ppermute x5, starting transfers between devices: 6.75 us -> 5.82 us  [across(): return lax.ppermute(array, 'fsdp', [(at, at ^ 1) for at in range(size)])]
    ppermute x4, waiting for transfers between devices: 6.02 us -> 5.2 us  [swap(): lax.ppermute(array, 'replica', [(at, at ^ bits) for at in range(lax.axis_...]
    unnamed x13 -> x12, local copies, waits for them, and re-layouts: 1.56 us -> 2.06 us
    pallas_call x12 -> x14, Pallas kernels: 4.56 us -> 4.57 us  [vmem_call(): pl.pallas_call(body, out_shape=out_shape, in_specs=[whole] * len(operands...]
  transfers between devices with their start and end apart: 15 -> 15, of which waited for: 8 -> 9; matrix products, arithmetic and copies ran while one was open for 0% -> 0% of each run, Pallas kernels for 12% -> 13%
where the time goes in v11:
time: 42.5 us; the launch traced here: 42.3 us
  starting transfers between devices  16.8 us (40%)
  waiting for transfers between devices  16.3 us (38%)
  Pallas kernels  6.44 us (15%)
  local copies, waits for them, and re-layouts  2.06 us (5%)
  between operations  0.76 us (2%)
    ppermute x3, starting transfers between devices, upward(): return lax.ppermute(array, 'fsdp', pairs)  7.24 us
    ppermute x5, waiting for transfers between devices, across(): return lax.ppermute(array, 'fsdp', [(at, at ^ 1) for at in range(size)])  7.03 us
    ppermute x5, starting transfers between devices, across(): return lax.ppermute(array, 'fsdp', [(at, at ^ 1) for at in range(size)])  5.82 us
    ppermute x4, waiting for transfers between devices, swap(): lax.ppermute(array, 'replica', [(at, at ^ bits) for at in range(lax.axis_...  5.2 us
    pallas_call x14, Pallas kernels, vmem_call(): pl.pallas_call(body, out_shape=out_shape, in_specs=[whole] * len(operands...  4.57 us
    ppermute x3, waiting for transfers between devices, upward(): return lax.ppermute(array, 'fsdp', pairs)  3.38 us
    ppermute x4, starting transfers between devices, swap(): lax.ppermute(array, 'replica', [(at, at ^ bits) for at in range(lax.axis_...  3.25 us
    unnamed x12, local copies, waits for them, and re-layouts  2.06 us
  transfers between devices with their start and end apart: 15, of which 9 were waited for; matrix products, arithmetic and copies ran while one was open for 0% of the time, Pallas kernels for 13%

profile of v11, /device:TPU:0, one launch (start us, length us, event | category | flops | bytes accessed | tf_op | source)
XLA Modules:
  0.0 42.3 jit_solution(5631443745330025506)
XLA Ops:
  0.6 4.1 %collective-permute-start.3 = (bf16[256,512]{1,0:T(8,128)(2,1)}, bf16[256,512]{1,0:T(8,128)(2,1)S(1)}, u32[]{:S(2)}, u32[]{:S(2)}) collective-permute-start(bf16[256,512]{1,0:T(8,128)(2,1)} %bitcast.12), channel_id=1, source_target_pairs={{2,0},{3,1},{0,4},{1,5},{4,6},{5,7},{6,2},{7,3},{10,8},{11,9},{8,1... | collective-permute-start | bytes 786440 | tf_op jit(solution)/shard_map/ppermute | solution.py:415
  4.7 1.5 %collective-permute-start.1 = (bf16[256,512]{1,0:T(8,128)(2,1)}, bf16[256,512]{1,0:T(8,128)(2,1)S(1)}, u32[]{:S(2)}, u32[]{:S(2)}) collective-permute-start(bf16[256,512]{1,0:T(8,128)(2,1)} %bitcast.19), channel_id=1, source_target_pairs={{0,1},{1,0},{2,3},{3,2},{4,5},{5,4},{6,7},{7,6},{8,9},{9,8},{10,11... | collective-permute-start | bytes 786440 | tf_op jit(solution)/shard_map/ppermute | solution.py:421
  6.2 1.2 %copy-done = bf16[1,256,2048]{2,1,0:T(8,128)(2,1)S(1)} copy-done((bf16[1,256,2048]{2,1,0:T(8,128)(2,1)S(1)}, bf16[1,256,2048]{2,1,0:T(8,128)(2,1)}, u32[]{:S(2)}) %copy-start) | copy-done | bytes 1048600
  7.5 0.6 %collective-permute-start = (bf16[2,256,256]{2,1,0:T(8,128)(2,1)S(1)}, bf16[2,256,256]{2,1,0:T(8,128)(2,1)S(1)}, u32[]{:S(2)}, u32[]{:S(2)}) collective-permute-start(bf16[2,256,256]{2,1,0:T(8,128)(2,1)S(1)} %pack_columns.2.refs_1_), channel_id=1, source_target_pairs={{0,1},{1,0},{2,3},{3,2},{4,5},{5,4},{6,7},{7,6},{8,9},{9,8},{10,11... | collective-permute-start | bytes 786440 | tf_op jit(solution)/shard_map/ppermute | solution.py:421
  8.4 3.4 %collective-permute-done.3.refs_0_.refs_3_.refs_4_ = bf16[256,512]{1,0:T(8,128)(2,1)S(1)} collective-permute-done((bf16[256,512]{1,0:T(8,128)(2,1)}, bf16[256,512]{1,0:T(8,128)(2,1)S(1)}, u32[]{:S(2)}, u32[]{:S(2)}) %collective-permute-start.3) | collective-permute-done | bytes 262176 | tf_op jit(solution)/shard_map/ppermute | solution.py:415
  11.7 2.4 %collective-permute-done.1.refs_1_.refs_3_ = bf16[256,512]{1,0:T(8,128)(2,1)S(1)} collective-permute-done((bf16[256,512]{1,0:T(8,128)(2,1)}, bf16[256,512]{1,0:T(8,128)(2,1)S(1)}, u32[]{:S(2)}, u32[]{:S(2)}) %collective-permute-start.1) | collective-permute-done | bytes 262176 | tf_op jit(solution)/shard_map/ppermute | solution.py:421
  14.2 1.6 %collective-permute-start.5 = (bf16[2,256,256]{2,1,0:T(8,128)(2,1)S(1)}, bf16[2,256,256]{2,1,0:T(8,128)(2,1)S(1)}, u32[]{:S(2)}, u32[]{:S(2)}) collective-permute-start(bf16[2,256,256]{2,1,0:T(8,128)(2,1)S(1)} %pack_columns.3), channel_id=1, source_target_pairs={{0,1},{1,0},{2,3},{3,2},{4,5},{5,4},{6,7},{7,6},{8,9},{9,8},{10,11... | collective-permute-start | bytes 786440 | tf_op jit(solution)/shard_map/ppermute | solution.py:421
  15.8 1.6 %collective-permute-start.4 = (bf16[256,512]{1,0:T(8,128)(2,1)S(1)}, bf16[256,512]{1,0:T(8,128)(2,1)S(1)}, u32[]{:S(2)}, u32[]{:S(2)}) collective-permute-start(bf16[256,512]{1,0:T(8,128)(2,1)S(1)} %collective-permute-done.3.refs_0_.refs_3_.refs_4_), channel_id=1, source_target_pairs={{2,0},{3,1},{0,4},{1,5},{4,6},{5,7},{6,2},{7,3},{10,8},{11,9},{8,1... | collective-permute-start | bytes 786440 | tf_op jit(solution)/shard_map/ppermute | solution.py:415
  17.4 1.6 %collective-permute-start.6 = (bf16[1,256,256]{2,1,0:T(8,128)(2,1)S(1)}, bf16[1,256,256]{2,1,0:T(8,128)(2,1)S(1)}, u32[]{:S(2)}, u32[]{:S(2)}) collective-permute-start(bf16[1,256,256]{2,1,0:T(8,128)(2,1)S(1)} %partner_columns.2), channel_id=1, source_target_pairs={{0,16},{8,24},{16,0},{24,8},{1,17},{9,25},{17,1},{25,9},{2,18},{10... | collective-permute-start | bytes 393224 | tf_op jit(solution)/shard_map/ppermute | solution.py:106
  18.9 0.8 %collective-permute-done.refs_2_.refs_1_ = bf16[2,256,256]{2,1,0:T(8,128)(2,1)S(1)} collective-permute-done((bf16[2,256,256]{2,1,0:T(8,128)(2,1)S(1)}, bf16[2,256,256]{2,1,0:T(8,128)(2,1)S(1)}, u32[]{:S(2)}, u32[]{:S(2)}) %collective-permute-start) | collective-permute-done | bytes 262176 | tf_op jit(solution)/shard_map/ppermute | solution.py:421
  20.3 2.1 %collective-permute-done.6.refs_5_.refs_1_ = bf16[1,256,256]{2,1,0:T(8,128)(2,1)S(1)} collective-permute-done((bf16[1,256,256]{2,1,0:T(8,128)(2,1)S(1)}, bf16[1,256,256]{2,1,0:T(8,128)(2,1)S(1)}, u32[]{:S(2)}, u32[]{:S(2)}) %collective-permute-start.6) | collective-permute-done | bytes 131104 | tf_op jit(solution)/shard_map/ppermute | solution.py:106
  22.9 0.6 %collective-permute-start.10 = (bf16[2,256,256]{2,1,0:T(8,128)(2,1)S(1)}, bf16[2,256,256]{2,1,0:T(8,128)(2,1)S(1)}, u32[]{:S(2)}, u32[]{:S(2)}) collective-permute-start(bf16[2,256,256]{2,1,0:T(8,128)(2,1)S(1)} %get-tuple-element.24.refs_6_.refs_4_), channel_id=1, source_target_pairs={{0,1},{1,0},{2,3},{3,2},{4,5},{5,4},{6,7},{7,6},{8,9},{9,8},{10,11... | collective-permute-start | bytes 786440 | tf_op jit(solution)/shard_map/ppermute | solution.py:421
  23.5 1.9 %collective-permute-done.5.refs_2_ = bf16[2,256,256]{2,1,0:T(8,128)(2,1)S(1)} collective-permute-done((bf16[2,256,256]{2,1,0:T(8,128)(2,1)S(1)}, bf16[2,256,256]{2,1,0:T(8,128)(2,1)S(1)}, u32[]{:S(2)}, u32[]{:S(2)}) %collective-permute-start.5) | collective-permute-done | bytes 262176 | tf_op jit(solution)/shard_map/ppermute | solution.py:421
  26.0 0.6 %last_products.1 = (f32[256,512]{1,0:T(8,128)S(1)}, bf16[2,256,256]{2,1,0:T(8,128)(2,1)S(1)}, bf16[4,256,256]{2,1,0:T(8,128)(2,1)S(1)}) custom-call(bf16[256,2048]{1,0:T(8,128)(2,1)S(1)} %bitcast.10, bf16[256,512]{1,0:T(8,128)(2,1)S(1)} %bitcast.22, bf16[2,256,256]{2,1,0:T(8,128)(2,1)S(1)} %collective-permute-done.refs_2_.refs_1_, ...), custom_call_target="tpu_custom_call" | custom-call | flops 268435456 | bytes 3407872 | tf_op jit(solution)/shard_map/last_products/pallas_call | solution.py:48
  26.6 1.6 %collective-permute-start.7 = (bf16[4,256,256]{2,1,0:T(8,128)(2,1)S(1)}, bf16[4,256,256]{2,1,0:T(8,128)(2,1)S(1)}, u32[]{:S(2)}, u32[]{:S(2)}) collective-permute-start(bf16[4,256,256]{2,1,0:T(8,128)(2,1)S(1)} %get-tuple-element.28.refs_2_), channel_id=1, source_target_pairs={{0,1},{1,0},{2,3},{3,2},{4,5},{5,4},{6,7},{7,6},{8,9},{9,8},{10,11... | collective-permute-start | bytes 1572872 | tf_op jit(solution)/shard_map/ppermute | solution.py:421
  28.2 1.6 %collective-permute-start.8 = (bf16[256,512]{1,0:T(8,128)(2,1)S(1)}, bf16[256,512]{1,0:T(8,128)(2,1)S(1)}, u32[]{:S(2)}, u32[]{:S(2)}) collective-permute-start(bf16[256,512]{1,0:T(8,128)(2,1)S(1)} %get-tuple-element.30.refs_3_), channel_id=1, source_target_pairs={{2,0},{3,1},{0,4},{1,5},{4,6},{5,7},{6,2},{7,3},{10,8},{11,9},{8,1... | collective-permute-start | bytes 786440 | tf_op jit(solution)/shard_map/ppermute | solution.py:415
  30.3 1.9 %collective-permute-done.10.refs_3_.early_ref = bf16[2,256,256]{2,1,0:T(8,128)(2,1)S(1)} collective-permute-done((bf16[2,256,256]{2,1,0:T(8,128)(2,1)S(1)}, bf16[2,256,256]{2,1,0:T(8,128)(2,1)S(1)}, u32[]{:S(2)}, u32[]{:S(2)}) %collective-permute-start.10) | collective-permute-done | bytes 262176 | tf_op jit(solution)/shard_map/ppermute | solution.py:421
  33.2 1.1 %outer_update.1 = (bf16[256,128]{1,0:T(8,128)(2,1)S(1)}, f32[256,128]{1,0:T(8,128)}) custom-call(bf16[256,512]{1,0:T(8,128)(2,1)S(1)} %bitcast.18, bf16[1,256,256]{2,1,0:T(8,128)(2,1)S(1)} %collective-permute-done.6.refs_5_.refs_1_, bf16[2,256,128]{2,1,0:T(8,128)(2,1)S(1)} %collective-permute-done.12.refs_2_, bf16[256,512]{1,0:T(8,128)(2,1)S(1)} %copy-done.4, ...), custom_call_target="tpu_custom_call" | custom-call | bytes 917504 | tf_op jit(solution)/shard_map/outer_update/pallas_call | solution.py:48
  34.2 1.5 %collective-permute-start.13 = (bf16[256,128]{1,0:T(8,128)(2,1)S(1)}, bf16[256,128]{1,0:T(8,128)(2,1)S(1)}, u32[]{:S(2)}, u32[]{:S(2)}) collective-permute-start(bf16[256,128]{1,0:T(8,128)(2,1)S(1)} %get-tuple-element.38.refs_0_), channel_id=1, source_target_pairs={{0,16},{8,24},{16,0},{24,8},{1,17},{9,25},{17,1},{25,9},{2,18},{10... | collective-permute-start | bytes 196616 | tf_op jit(solution)/shard_map/ppermute | solution.py:106
  35.8 2.7 %collective-permute-done.13.refs_1_ = bf16[256,128]{1,0:T(8,128)(2,1)S(1)} collective-permute-done((bf16[256,128]{1,0:T(8,128)(2,1)S(1)}, bf16[256,128]{1,0:T(8,128)(2,1)S(1)}, u32[]{:S(2)}, u32[]{:S(2)}) %collective-permute-start.13) | collective-permute-done | bytes 65568 | tf_op jit(solution)/shard_map/ppermute | solution.py:106
  38.6 0.9 %collect.1 = (bf16[256,2048]{1,0:T(8,128)(2,1)}, f32[8,128]{1,0:T(8,128)S(1)}) custom-call(bf16[2,256,256]{2,1,0:T(8,128)(2,1)S(1)} %get-tuple-element.32.near_ref, bf16[2,256,256]{2,1,0:T(8,128)(2,1)S(1)} %get-tuple-element.33.last_ref, bf16[2,256,256]{2,1,0:T(8,128)(2,1)S(1)} %collective-permute-done.10.refs_3_.early_ref), custom_call_target="tpu_custom_call" | custom-call | bytes 1048576 | tf_op jit(solution)/shard_map/collect/pallas_call | solution.py:355
  39.9 0.8 %join_shares.1 = bf16[256,512]{1,0:T(8,128)(2,1)} custom-call(bf16[256,256]{1,0:T(8,128)(2,1)S(1)} %beside.1.refs_0_, bf16[256,256]{1,0:T(8,128)(2,1)S(1)} %collective-permute-done.14.refs_1_, f32[8,128]{1,0:T(8,128)S(1)} %get-tuple-element.39.refs_2_), custom_call_target="tpu_custom_call" | custom-call | bytes 262144 | tf_op jit(solution)/shard_map/join_shares/pallas_call | solution.py:48
  40.7 0.7 %collective-permute-done.11.down_ref = bf16[256,512]{1,0:T(8,128)(2,1)S(1)} collective-permute-done((bf16[256,512]{1,0:T(8,128)(2,1)S(1)}, bf16[256,512]{1,0:T(8,128)(2,1)S(1)}, u32[]{:S(2)}, u32[]{:S(2)}) %collective-permute-start.11) | collective-permute-done | bytes 262176 | tf_op jit(solution)/shard_map/ppermute | solution.py:418
  41.4 0.9 %finish.1 = (bf16[256,512]{1,0:T(8,128)(2,1)}, bf16[256,2048]{1,0:T(8,128)(2,1)}, bf16[256,512]{1,0:T(8,128)(2,1)}) custom-call(f32[256,512]{1,0:T(8,128)S(1)} %get-tuple-element.27.total_ref, bf16[4,256,256]{2,1,0:T(8,128)(2,1)S(1)} %collective-permute-done.7.late_ref, f32[256,512]{1,0:T(8,128)S(1)} %get-tuple-element.29.terms_ref, ...), custom_call_target="tpu_custom_call", output_to_operand_aliasing={{1}: (5, {})} | custom-call | bytes 1048576 | tf_op jit(solution)/shard_map/finish/pallas_call | solution.py:386
  (34 shorter events, 4.0 us)
Async XLA Ops:
  0.6 11.1 %collective-permute-start.3 = (bf16[256,512]{1,0:T(8,128)(2,1)}, bf16[256,512]{1,0:T(8,128)(2,1)S(1)}, u32[]{:S(2)}, u32[]{:S(2)}) collective-permute-start(bf16[256,512]{1,0:T(8,128)(2,1)} %bitcast.12), channel_id=1, source_target_pairs={{2,0},{3,1},{0,4},{1,5},{4,6},{5,7},{6,2},{7,3},{10,8},{11,9},{8,1... | collective-permute-start | bytes 786440 | tf_op jit(solution)/shard_map/ppermute | solution.py:415
  4.7 9.4 %collective-permute-start.1 = (bf16[256,512]{1,0:T(8,128)(2,1)}, bf16[256,512]{1,0:T(8,128)(2,1)S(1)}, u32[]{:S(2)}, u32[]{:S(2)}) collective-permute-start(bf16[256,512]{1,0:T(8,128)(2,1)} %bitcast.19), channel_id=1, source_target_pairs={{0,1},{1,0},{2,3},{3,2},{4,5},{5,4},{6,7},{7,6},{8,9},{9,8},{10,11... | collective-permute-start | bytes 786440 | tf_op jit(solution)/shard_map/ppermute | solution.py:421
  6.2 1.2 %copy-start = (bf16[1,256,2048]{2,1,0:T(8,128)(2,1)S(1)}, bf16[1,256,2048]{2,1,0:T(8,128)(2,1)}, u32[]{:S(2)}) copy-start(bf16[1,256,2048]{2,1,0:T(8,128)(2,1)} %param.8) | copy-start | bytes 3145732
  7.4 0.9 %copy-start.2 = (bf16[1,256,512]{2,1,0:T(8,128)(2,1)S(1)}, bf16[1,256,512]{2,1,0:T(8,128)(2,1)}, u32[]{:S(2)}) copy-start(bf16[1,256,512]{2,1,0:T(8,128)(2,1)} %param.5) | copy-start | bytes 786436
  7.4 6.7 %copy-start.1 = (bf16[1,256,2048]{2,1,0:T(8,128)(2,1)S(1)}, bf16[1,256,2048]{2,1,0:T(8,128)(2,1)}, u32[]{:S(2)}) copy-start(bf16[1,256,2048]{2,1,0:T(8,128)(2,1)} %param.8) | copy-start | bytes 3145732
  7.5 12.3 %collective-permute-start = (bf16[2,256,256]{2,1,0:T(8,128)(2,1)S(1)}, bf16[2,256,256]{2,1,0:T(8,128)(2,1)S(1)}, u32[]{:S(2)}, u32[]{:S(2)}) collective-permute-start(bf16[2,256,256]{2,1,0:T(8,128)(2,1)S(1)} %pack_columns.2.refs_1_), channel_id=1, source_target_pairs={{0,1},{1,0},{2,3},{3,2},{4,5},{5,4},{6,7},{7,6},{8,9},{9,8},{10,11... | collective-permute-start | bytes 786440 | tf_op jit(solution)/shard_map/ppermute | solution.py:421
  8.4 15.1 %collective-permute-start.2 = (bf16[256,512]{1,0:T(8,128)(2,1)S(1)}, bf16[256,512]{1,0:T(8,128)(2,1)S(1)}, u32[]{:S(2)}, u32[]{:S(2)}) collective-permute-start(bf16[256,512]{1,0:T(8,128)(2,1)S(1)} %bitcast.13), channel_id=1, source_target_pairs={{0,2},{1,3},{4,0},{5,1},{6,4},{7,5},{2,6},{3,7},{8,10},{9,11},{12,... | collective-permute-start | bytes 786440 | tf_op jit(solution)/shard_map/ppermute | solution.py:418
  14.2 5.6 %copy-start.3 = (bf16[1,256,512]{2,1,0:T(8,128)(2,1)S(1)}, bf16[1,256,512]{2,1,0:T(8,128)(2,1)}, u32[]{:S(2)}) copy-start(bf16[1,256,512]{2,1,0:T(8,128)(2,1)} %param.9) | copy-start | bytes 786436
  14.2 11.2 %collective-permute-start.5 = (bf16[2,256,256]{2,1,0:T(8,128)(2,1)S(1)}, bf16[2,256,256]{2,1,0:T(8,128)(2,1)S(1)}, u32[]{:S(2)}, u32[]{:S(2)}) collective-permute-start(bf16[2,256,256]{2,1,0:T(8,128)(2,1)S(1)} %pack_columns.3), channel_id=1, source_target_pairs={{0,1},{1,0},{2,3},{3,2},{4,5},{5,4},{6,7},{7,6},{8,9},{9,8},{10,11... | collective-permute-start | bytes 786440 | tf_op jit(solution)/shard_map/ppermute | solution.py:421
  15.8 10.2 %collective-permute-start.4 = (bf16[256,512]{1,0:T(8,128)(2,1)S(1)}, bf16[256,512]{1,0:T(8,128)(2,1)S(1)}, u32[]{:S(2)}, u32[]{:S(2)}) collective-permute-start(bf16[256,512]{1,0:T(8,128)(2,1)S(1)} %collective-permute-done.3.refs_0_.refs_3_.refs_4_), channel_id=1, source_target_pairs={{2,0},{3,1},{0,4},{1,5},{4,6},{5,7},{6,2},{7,3},{10,8},{11,9},{8,1... | collective-permute-start | bytes 786440 | tf_op jit(solution)/shard_map/ppermute | solution.py:415
  17.4 5.0 %collective-permute-start.6 = (bf16[1,256,256]{2,1,0:T(8,128)(2,1)S(1)}, bf16[1,256,256]{2,1,0:T(8,128)(2,1)S(1)}, u32[]{:S(2)}, u32[]{:S(2)}) collective-permute-start(bf16[1,256,256]{2,1,0:T(8,128)(2,1)S(1)} %partner_columns.2), channel_id=1, source_target_pairs={{0,16},{8,24},{16,0},{24,8},{1,17},{9,25},{17,1},{25,9},{2,18},{10... | collective-permute-start | bytes 393224 | tf_op jit(solution)/shard_map/ppermute | solution.py:106
  20.2 11.9 %collective-permute-start.9 = (bf16[256,512]{1,0:T(8,128)(2,1)S(1)}, bf16[256,512]{1,0:T(8,128)(2,1)S(1)}, u32[]{:S(2)}, u32[]{:S(2)}) collective-permute-start(bf16[256,512]{1,0:T(8,128)(2,1)S(1)} %get-tuple-element.23.refs_4_.refs_2_), channel_id=1, source_target_pairs={{0,2},{1,3},{4,0},{5,1},{6,4},{7,5},{2,6},{3,7},{8,10},{9,11},{12,... | collective-permute-start | bytes 786440 | tf_op jit(solution)/shard_map/ppermute | solution.py:418
  22.9 9.3 %collective-permute-start.10 = (bf16[2,256,256]{2,1,0:T(8,128)(2,1)S(1)}, bf16[2,256,256]{2,1,0:T(8,128)(2,1)S(1)}, u32[]{:S(2)}, u32[]{:S(2)}) collective-permute-start(bf16[2,256,256]{2,1,0:T(8,128)(2,1)S(1)} %get-tuple-element.24.refs_6_.refs_4_), channel_id=1, source_target_pairs={{0,1},{1,0},{2,3},{3,2},{4,5},{5,4},{6,7},{7,6},{8,9},{9,8},{10,11... | collective-permute-start | bytes 786440 | tf_op jit(solution)/shard_map/ppermute | solution.py:421
  26.6 14.8 %collective-permute-start.7 = (bf16[4,256,256]{2,1,0:T(8,128)(2,1)S(1)}, bf16[4,256,256]{2,1,0:T(8,128)(2,1)S(1)}, u32[]{:S(2)}, u32[]{:S(2)}) collective-permute-start(bf16[4,256,256]{2,1,0:T(8,128)(2,1)S(1)} %get-tuple-element.28.refs_2_), channel_id=1, source_target_pairs={{0,1},{1,0},{2,3},{3,2},{4,5},{5,4},{6,7},{7,6},{8,9},{9,8},{10,11... | collective-permute-start | bytes 1572872 | tf_op jit(solution)/shard_map/ppermute | solution.py:421
  28.2 7.6 %collective-permute-start.8 = (bf16[256,512]{1,0:T(8,128)(2,1)S(1)}, bf16[256,512]{1,0:T(8,128)(2,1)S(1)}, u32[]{:S(2)}, u32[]{:S(2)}) collective-permute-start(bf16[256,512]{1,0:T(8,128)(2,1)S(1)} %get-tuple-element.30.refs_3_), channel_id=1, source_target_pairs={{2,0},{3,1},{0,4},{1,5},{4,6},{5,7},{6,2},{7,3},{10,8},{11,9},{8,1... | collective-permute-start | bytes 786440 | tf_op jit(solution)/shard_map/ppermute | solution.py:415
  29.8 2.9 %collective-permute-start.12 = (bf16[2,256,128]{2,1,0:T(8,128)(2,1)S(1)}, bf16[2,256,128]{2,1,0:T(8,128)(2,1)S(1)}, u32[]{:S(2)}, u32[]{:S(2)}) collective-permute-start(bf16[2,256,128]{2,1,0:T(8,128)(2,1)S(1)} %partner_columns.3), channel_id=1, source_target_pairs={{0,8},{8,0},{16,24},{24,16},{1,9},{9,1},{17,25},{25,17},{2,10},{10... | collective-permute-start | bytes 393224 | tf_op jit(solution)/shard_map/ppermute | solution.py:106
  32.2 1.0 %copy-start.4 = (bf16[256,512]{1,0:T(8,128)(2,1)S(1)}, bf16[256,512]{1,0:T(8,128)(2,1)}, u32[]{:S(2)}) copy-start(bf16[256,512]{1,0:T(8,128)(2,1)} %refs_3_.1) | copy-start | bytes 786436
  32.2 1.0 %copy-start.5 = (f32[256,128]{1,0:T(8,128)S(1)}, f32[256,128]{1,0:T(8,128)}, u32[]{:S(2)}) copy-start(f32[256,128]{1,0:T(8,128)} %refs_4_.1) | copy-start | bytes 393220
  32.2 9.1 %collective-permute-start.11 = (bf16[256,512]{1,0:T(8,128)(2,1)S(1)}, bf16[256,512]{1,0:T(8,128)(2,1)S(1)}, u32[]{:S(2)}, u32[]{:S(2)}) collective-permute-start(bf16[256,512]{1,0:T(8,128)(2,1)S(1)} %add_terms.1.refs_5_), channel_id=1, source_target_pairs={{0,2},{1,3},{4,0},{5,1},{6,4},{7,5},{2,6},{3,7},{8,10},{9,11},{12,... | collective-permute-start | bytes 786440 | tf_op jit(solution)/shard_map/ppermute | solution.py:418
  34.2 4.3 %collective-permute-start.13 = (bf16[256,128]{1,0:T(8,128)(2,1)S(1)}, bf16[256,128]{1,0:T(8,128)(2,1)S(1)}, u32[]{:S(2)}, u32[]{:S(2)}) collective-permute-start(bf16[256,128]{1,0:T(8,128)(2,1)S(1)} %get-tuple-element.38.refs_0_), channel_id=1, source_target_pairs={{0,16},{8,24},{16,0},{24,8},{1,17},{9,25},{17,1},{25,9},{2,18},{10... | collective-permute-start | bytes 196616 | tf_op jit(solution)/shard_map/ppermute | solution.py:106
  38.5 1.4 %collective-permute-start.14 = (bf16[256,256]{1,0:T(8,128)(2,1)S(1)}, bf16[256,256]{1,0:T(8,128)(2,1)S(1)}, u32[]{:S(2)}, u32[]{:S(2)}) collective-permute-start(bf16[256,256]{1,0:T(8,128)(2,1)S(1)} %beside.1.refs_0_), channel_id=1, source_target_pairs={{0,8},{8,0},{16,24},{24,16},{1,9},{9,1},{17,25},{25,17},{2,10},{10... | collective-permute-start | bytes 393224 | tf_op jit(solution)/shard_map/ppermute | solution.py:106

commit v12 on v11

--- a/solution.py
+++ b/solution.py
@@ -340,7 +340,8 @@
     return copies
 
 
-def collect_kernel(size, early, late, near_ref, last_ref, early_ref, grad_ref, mark_ref, sems):
+def collect_kernel(size, early, late, near_ref, last_ref, early_ref, *refs):
+    grad_ref, mark_ref, sems = refs[-3:]
     sources = [(near_ref, number, offset, 0) for number, offset in enumerate(early)]
     sources += [(last_ref, number, offset, 0) for number, offset in enumerate(late)]
     sources += [(early_ref, number, offset, 1) for number, offset in enumerate(early)]
@@ -350,18 +351,18 @@
         copy.wait()
 
 
-def collect(grads, width, size, early, late):
+def collect(grads, width, size, early, late, after):
     whole, anywhere = pl.BlockSpec(memory_space=pltpu.VMEM), pl.BlockSpec(memory_space=pl.ANY)
     return pl.pallas_call(
         functools.partial(collect_kernel, size, early, late),
         out_shape=(shape_of(grads[0].shape[1], width, BF16), shape_of(8, LANES, F32)),
-        in_specs=[whole] * len(grads),
+        in_specs=[whole] * len(grads) + [anywhere] * len(after),
         out_specs=(anywhere, whole),
         scratch_shapes=[pltpu.SemaphoreType.DMA((2 * len(early) + len(late),))],
         compiler_params=pltpu.CompilerParams(vmem_limit_bytes=VMEM_BYTES),
         cost_estimate=pl.CostEstimate(flops=0, bytes_accessed=2**20, transcendentals=0),
         name="collect",
-    )(*grads)
+    )(*grads, *after)
 
 
 def finish_kernel(size, late, total_ref, late_ref, terms_ref, up_ref, down_ref, _, *refs):
@@ -439,24 +440,24 @@
     early = across(leaving)
     operands[2] = partner_inputs[1]
     terms = token_terms(operands, size, [3, 0], F32, token_weight, (leaving,))
-    totals = near_rows(inputs_here, partner_inputs, {**early_blocks, 1: from_above}, size, (leaving,))
+    totals = near_rows(inputs_here, partner_inputs, {**early_blocks, 1: from_above}, size, (leaving, held[-1]))
     rows, last, leaving = last_products(
         inputs_here, cotangent, partner_inputs, partner_cotangent, late_blocks, totals, size, ()
     )
     late = across(leaving)
     total_down = vmem_call(
-        add_kernel, shape_of(depth, kv_width, BF16), [terms[0], sum_down], 0, "add_terms", (leaving, early)
+        add_kernel, shape_of(depth, kv_width, BF16), [terms[0], sum_down], 0, "add_terms", (leaving,)
     )
     sum_down = downward(total_down)
-    new_share, new_momentum = update_share(held, global_weights, momentum, (total_down,))
+    new_share, new_momentum = update_share(held, global_weights, momentum, (total_down, early))
     bits = lax.axis_size("replica")
     shares, joined = [new_share], [0]
     while bits > 1:
         bits //= 2
-        shares = [shares[0] if len(shares) == 1 else beside(*shares, (sum_up,))]
+        shares = [shares[0] if len(shares) == 1 else jnp.concatenate(shares, axis=1)]
         shares.append(swap(shares[0], bits))
         joined += [place ^ bits for place in joined]
-    grad, mark = collect([near, last, early], width, size, list(early_blocks), list(late_blocks))
+    grad, mark = collect([near, last, early], width, size, list(early_blocks), list(late_blocks), ())
     new_global = join_shares(shares, joined, kv_width, (mark,))
     kv_rows, grad_in, grad_rows = finish(
         rows, late, [terms[1], sum_up, sum_down], grad, size, list(late_blocks)

time: 42.5 us -> 42.5 us (level)
  waiting for transfers between devices: 16.3 us -> 15.3 us
  starting transfers between devices: 16.8 us -> 17.4 us
    ppermute x3, waiting for transfers between devices: 0.66 us -> 4.09 us  [downward(): lax.ppermute(array, 'fsdp', [(target, source) for source, target in pairs])]
    ppermute x4, waiting for transfers between devices: 5.2 us -> 3.13 us  [swap(): lax.ppermute(array, 'replica', [(at, at ^ bits) for at in range(lax.axis_...]
    ppermute x3, waiting for transfers between devices: 3.38 us -> 1.76 us  [upward(): return lax.ppermute(array, 'fsdp', pairs)]
    ppermute x5, starting transfers between devices: 5.82 us -> 6.77 us  [across(): return lax.ppermute(array, 'fsdp', [(at, at ^ 1) for at in range(size)])]
    ppermute x5, waiting for transfers between devices: 7.03 us -> 6.28 us  [across(): return lax.ppermute(array, 'fsdp', [(at, at ^ 1) for at in range(size)])]
    unnamed x12 -> x13, local copies, waits for them, and re-layouts: 2.06 us -> 2.41 us
    pallas_call x14 -> x13, Pallas kernels: 4.57 us -> 4.57 us  [vmem_call(): pl.pallas_call(body, out_shape=out_shape, in_specs=[whole] * len(operands...]
  transfers between devices with their start and end apart: 15 -> 15, of which waited for: 9 -> 8; matrix products, arithmetic and copies ran while one was open for 0% -> 0% of each run, Pallas kernels for 13% -> 13%
where the time goes in v12:
time: 42.5 us; the launch traced here: 42.3 us
  starting transfers between devices  17.4 us (41%)
  waiting for transfers between devices  15.3 us (36%)
  Pallas kernels  6.44 us (15%)
  local copies, waits for them, and re-layouts  2.43 us (6%)
  between operations  0.79 us (2%)
    ppermute x3, starting transfers between devices, upward(): return lax.ppermute(array, 'fsdp', pairs)  7.24 us
    ppermute x5, starting transfers between devices, across(): return lax.ppermute(array, 'fsdp', [(at, at ^ 1) for at in range(size)])  6.77 us
    ppermute x5, waiting for transfers between devices, across(): return lax.ppermute(array, 'fsdp', [(at, at ^ 1) for at in range(size)])  6.28 us
    pallas_call x13, Pallas kernels, vmem_call(): pl.pallas_call(body, out_shape=out_shape, in_specs=[whole] * len(operands...  4.57 us
    ppermute x3, waiting for transfers between devices, downward(): lax.ppermute(array, 'fsdp', [(target, source) for source, target in pairs])  4.09 us
    ppermute x4, starting transfers between devices, swap(): lax.ppermute(array, 'replica', [(at, at ^ bits) for at in range(lax.axis_...  3.24 us
    ppermute x4, waiting for transfers between devices, swap(): lax.ppermute(array, 'replica', [(at, at ^ bits) for at in range(lax.axis_...  3.13 us
    unnamed x13, local copies, waits for them, and re-layouts  2.41 us
  transfers between devices with their start and end apart: 15, of which 8 were waited for; matrix products, arithmetic and copies ran while one was open for 0% of the time, Pallas kernels for 13%

profile of v12, /device:TPU:0, one launch (start us, length us, event | category | flops | bytes accessed | tf_op | source)
XLA Modules:
  0.0 42.3 jit_solution(10305462050448389895)
XLA Ops:
  0.6 4.1 %collective-permute-start.3 = (bf16[256,512]{1,0:T(8,128)(2,1)}, bf16[256,512]{1,0:T(8,128)(2,1)S(1)}, u32[]{:S(2)}, u32[]{:S(2)}) collective-permute-start(bf16[256,512]{1,0:T(8,128)(2,1)} %bitcast.12), channel_id=1, source_target_pairs={{2,0},{3,1},{0,4},{1,5},{4,6},{5,7},{6,2},{7,3},{10,8},{11,9},{8,1... | collective-permute-start | bytes 786440 | tf_op jit(solution)/shard_map/ppermute | solution.py:416
  4.7 1.5 %collective-permute-start.1 = (bf16[256,512]{1,0:T(8,128)(2,1)}, bf16[256,512]{1,0:T(8,128)(2,1)S(1)}, u32[]{:S(2)}, u32[]{:S(2)}) collective-permute-start(bf16[256,512]{1,0:T(8,128)(2,1)} %bitcast.19), channel_id=1, source_target_pairs={{0,1},{1,0},{2,3},{3,2},{4,5},{5,4},{6,7},{7,6},{8,9},{9,8},{10,11... | collective-permute-start | bytes 786440 | tf_op jit(solution)/shard_map/ppermute | solution.py:422
  6.2 1.2 %copy-done = bf16[1,256,2048]{2,1,0:T(8,128)(2,1)S(1)} copy-done((bf16[1,256,2048]{2,1,0:T(8,128)(2,1)S(1)}, bf16[1,256,2048]{2,1,0:T(8,128)(2,1)}, u32[]{:S(2)}) %copy-start) | copy-done | bytes 1048600
  7.5 0.6 %collective-permute-start = (bf16[2,256,256]{2,1,0:T(8,128)(2,1)S(1)}, bf16[2,256,256]{2,1,0:T(8,128)(2,1)S(1)}, u32[]{:S(2)}, u32[]{:S(2)}) collective-permute-start(bf16[2,256,256]{2,1,0:T(8,128)(2,1)S(1)} %pack_columns.2.refs_1_), channel_id=1, source_target_pairs={{0,1},{1,0},{2,3},{3,2},{4,5},{5,4},{6,7},{7,6},{8,9},{9,8},{10,11... | collective-permute-start | bytes 786440 | tf_op jit(solution)/shard_map/ppermute | solution.py:422
  8.4 1.6 %collective-permute-start.6 = (bf16[1,256,256]{2,1,0:T(8,128)(2,1)S(1)}, bf16[1,256,256]{2,1,0:T(8,128)(2,1)S(1)}, u32[]{:S(2)}, u32[]{:S(2)}) collective-permute-start(bf16[1,256,256]{2,1,0:T(8,128)(2,1)S(1)} %partner_columns.2), channel_id=1, source_target_pairs={{0,16},{8,24},{16,0},{24,8},{1,17},{9,25},{17,1},{25,9},{2,18},{10... | collective-permute-start | bytes 393224 | tf_op jit(solution)/shard_map/ppermute | solution.py:106
  10.0 1.8 %collective-permute-done.3.refs_0_.refs_3_.refs_4_ = bf16[256,512]{1,0:T(8,128)(2,1)S(1)} collective-permute-done((bf16[256,512]{1,0:T(8,128)(2,1)}, bf16[256,512]{1,0:T(8,128)(2,1)S(1)}, u32[]{:S(2)}, u32[]{:S(2)}) %collective-permute-start.3) | collective-permute-done | bytes 262176 | tf_op jit(solution)/shard_map/ppermute | solution.py:416
  11.8 2.4 %collective-permute-done.1.refs_1_.refs_3_ = bf16[256,512]{1,0:T(8,128)(2,1)S(1)} collective-permute-done((bf16[256,512]{1,0:T(8,128)(2,1)}, bf16[256,512]{1,0:T(8,128)(2,1)S(1)}, u32[]{:S(2)}, u32[]{:S(2)}) %collective-permute-start.1) | collective-permute-done | bytes 262176 | tf_op jit(solution)/shard_map/ppermute | solution.py:422
  14.2 1.6 %collective-permute-start.5 = (bf16[2,256,256]{2,1,0:T(8,128)(2,1)S(1)}, bf16[2,256,256]{2,1,0:T(8,128)(2,1)S(1)}, u32[]{:S(2)}, u32[]{:S(2)}) collective-permute-start(bf16[2,256,256]{2,1,0:T(8,128)(2,1)S(1)} %pack_columns.3), channel_id=1, source_target_pairs={{0,1},{1,0},{2,3},{3,2},{4,5},{5,4},{6,7},{7,6},{8,9},{9,8},{10,11... | collective-permute-start | bytes 786440 | tf_op jit(solution)/shard_map/ppermute | solution.py:422
  15.8 1.6 %collective-permute-start.4 = (bf16[256,512]{1,0:T(8,128)(2,1)S(1)}, bf16[256,512]{1,0:T(8,128)(2,1)S(1)}, u32[]{:S(2)}, u32[]{:S(2)}) collective-permute-start(bf16[256,512]{1,0:T(8,128)(2,1)S(1)} %collective-permute-done.3.refs_0_.refs_3_.refs_4_), channel_id=1, source_target_pairs={{2,0},{3,1},{0,4},{1,5},{4,6},{5,7},{6,2},{7,3},{10,8},{11,9},{8,1... | collective-permute-start | bytes 786440 | tf_op jit(solution)/shard_map/ppermute | solution.py:416
  17.3 2.4 %collective-permute-done.refs_2_.refs_1_ = bf16[2,256,256]{2,1,0:T(8,128)(2,1)S(1)} collective-permute-done((bf16[2,256,256]{2,1,0:T(8,128)(2,1)S(1)}, bf16[2,256,256]{2,1,0:T(8,128)(2,1)S(1)}, u32[]{:S(2)}, u32[]{:S(2)}) %collective-permute-start) | collective-permute-done | bytes 262176 | tf_op jit(solution)/shard_map/ppermute | solution.py:422
  20.9 1.6 %collective-permute-start.12 = (bf16[2,256,256]{2,1,0:T(8,128)(2,1)S(1)}, bf16[2,256,256]{2,1,0:T(8,128)(2,1)S(1)}, u32[]{:S(2)}, u32[]{:S(2)}) collective-permute-start(bf16[2,256,256]{2,1,0:T(8,128)(2,1)S(1)} %get-tuple-element.24.refs_6_.refs_4_), channel_id=1, source_target_pairs={{0,1},{1,0},{2,3},{3,2},{4,5},{5,4},{6,7},{7,6},{8,9},{9,8},{10,11... | collective-permute-start | bytes 786440 | tf_op jit(solution)/shard_map/ppermute | solution.py:422
  22.5 1.4 %collective-permute-done.5.refs_2_ = bf16[2,256,256]{2,1,0:T(8,128)(2,1)S(1)} collective-permute-done((bf16[2,256,256]{2,1,0:T(8,128)(2,1)S(1)}, bf16[2,256,256]{2,1,0:T(8,128)(2,1)S(1)}, u32[]{:S(2)}, u32[]{:S(2)}) %collective-permute-start.5) | collective-permute-done | bytes 262176 | tf_op jit(solution)/shard_map/ppermute | solution.py:422
  24.5 0.6 %last_products.1 = (f32[256,512]{1,0:T(8,128)S(1)}, bf16[2,256,256]{2,1,0:T(8,128)(2,1)S(1)}, bf16[4,256,256]{2,1,0:T(8,128)(2,1)S(1)}) custom-call(bf16[256,2048]{1,0:T(8,128)(2,1)S(1)} %bitcast.10, bf16[256,512]{1,0:T(8,128)(2,1)S(1)} %bitcast.22, bf16[2,256,256]{2,1,0:T(8,128)(2,1)S(1)} %collective-permute-done.refs_2_.refs_1_, ...), custom_call_target="tpu_custom_call" | custom-call | flops 268435456 | bytes 3407872 | tf_op jit(solution)/shard_map/last_products/pallas_call | solution.py:48
  25.1 1.6 %collective-permute-start.8 = (bf16[4,256,256]{2,1,0:T(8,128)(2,1)S(1)}, bf16[4,256,256]{2,1,0:T(8,128)(2,1)S(1)}, u32[]{:S(2)}, u32[]{:S(2)}) collective-permute-start(bf16[4,256,256]{2,1,0:T(8,128)(2,1)S(1)} %get-tuple-element.29.refs_2_), channel_id=1, source_target_pairs={{0,1},{1,0},{2,3},{3,2},{4,5},{5,4},{6,7},{7,6},{8,9},{9,8},{10,11... | collective-permute-start | bytes 1572872 | tf_op jit(solution)/shard_map/ppermute | solution.py:422
  26.7 1.6 %collective-permute-start.9 = (bf16[256,512]{1,0:T(8,128)(2,1)S(1)}, bf16[256,512]{1,0:T(8,128)(2,1)S(1)}, u32[]{:S(2)}, u32[]{:S(2)}) collective-permute-start(bf16[256,512]{1,0:T(8,128)(2,1)S(1)} %get-tuple-element.25.refs_3_), channel_id=1, source_target_pairs={{2,0},{3,1},{0,4},{1,5},{4,6},{5,7},{6,2},{7,3},{10,8},{11,9},{8,1... | collective-permute-start | bytes 786440 | tf_op jit(solution)/shard_map/ppermute | solution.py:416
  28.7 1.7 %collective-permute-done.10.refs_1_ = bf16[256,512]{1,0:T(8,128)(2,1)S(1)} collective-permute-done((bf16[256,512]{1,0:T(8,128)(2,1)S(1)}, bf16[256,512]{1,0:T(8,128)(2,1)S(1)}, u32[]{:S(2)}, u32[]{:S(2)}) %collective-permute-start.10) | collective-permute-done | bytes 262176 | tf_op jit(solution)/shard_map/ppermute | solution.py:419
  30.6 0.8 %copy-done.4 = bf16[256,512]{1,0:T(8,128)(2,1)S(1)} copy-done((bf16[256,512]{1,0:T(8,128)(2,1)S(1)}, bf16[256,512]{1,0:T(8,128)(2,1)}, u32[]{:S(2)}) %copy-start.4) | copy-done | bytes 262168
  31.4 1.1 %outer_update.1 = (bf16[256,128]{1,0:T(8,128)(2,1)S(1)}, f32[256,128]{1,0:T(8,128)}) custom-call(bf16[256,512]{1,0:T(8,128)(2,1)S(1)} %bitcast.18, bf16[1,256,256]{2,1,0:T(8,128)(2,1)S(1)} %collective-permute-done.6.refs_5_.refs_1_, bf16[2,256,128]{2,1,0:T(8,128)(2,1)S(1)} %collective-permute-done.7.refs_7_.refs_2_, bf16[256,512]{1,0:T(8,128)(2,1)S(1)} %copy-done.4, ...), custom_call_target="tpu_custom_call" | custom-call | bytes 917504 | tf_op jit(solution)/shard_map/outer_update/pallas_call | solution.py:48
  32.5 1.5 %collective-permute-start.13 = (bf16[256,128]{1,0:T(8,128)(2,1)S(1)}, bf16[256,128]{1,0:T(8,128)(2,1)S(1)}, u32[]{:S(2)}, u32[]{:S(2)}) collective-permute-start(bf16[256,128]{1,0:T(8,128)(2,1)S(1)} %get-tuple-element.38), channel_id=1, source_target_pairs={{0,16},{8,24},{16,0},{24,8},{1,17},{9,25},{17,1},{25,9},{2,18},{10... | collective-permute-start | bytes 196616 | tf_op jit(solution)/shard_map/ppermute | solution.py:106
  34.0 2.7 %collective-permute-done.13 = bf16[256,128]{1,0:T(8,128)(2,1)S(1)} collective-permute-done((bf16[256,128]{1,0:T(8,128)(2,1)S(1)}, bf16[256,128]{1,0:T(8,128)(2,1)S(1)}, u32[]{:S(2)}, u32[]{:S(2)}) %collective-permute-start.13) | collective-permute-done | bytes 65568 | tf_op jit(solution)/shard_map/ppermute | solution.py:106
  36.8 0.9 %collect.1 = (bf16[256,2048]{1,0:T(8,128)(2,1)}, f32[8,128]{1,0:T(8,128)S(1)}) custom-call(bf16[2,256,256]{2,1,0:T(8,128)(2,1)S(1)} %get-tuple-element.32.near_ref, bf16[2,256,256]{2,1,0:T(8,128)(2,1)S(1)} %get-tuple-element.33.last_ref, bf16[2,256,256]{2,1,0:T(8,128)(2,1)S(1)} %collective-permute-done.12.early_ref.refs_6_), custom_call_target="tpu_custom_call" | custom-call | bytes 1048576 | tf_op jit(solution)/shard_map/collect/pallas_call | solution.py:356
  38.2 0.8 %join_shares.1 = bf16[256,512]{1,0:T(8,128)(2,1)} custom-call(bf16[256,256]{1,0:T(8,128)(2,1)S(1)} %constant_dynamic-update-slice_fusion.refs_0_, bf16[256,256]{1,0:T(8,128)(2,1)S(1)} %collective-permute-done.14.refs_1_, f32[8,128]{1,0:T(8,128)S(1)} %get-tuple-element.39.refs_2_), custom_call_target="tpu_custom_call" | custom-call | bytes 262144 | tf_op jit(solution)/shard_map/join_shares/pallas_call | solution.py:48
  38.9 2.4 %collective-permute-done.11.down_ref = bf16[256,512]{1,0:T(8,128)(2,1)S(1)} collective-permute-done((bf16[256,512]{1,0:T(8,128)(2,1)S(1)}, bf16[256,512]{1,0:T(8,128)(2,1)S(1)}, u32[]{:S(2)}, u32[]{:S(2)}) %collective-permute-start.11) | collective-permute-done | bytes 262176 | tf_op jit(solution)/shard_map/ppermute | solution.py:419
  41.4 0.9 %finish.1 = (bf16[256,512]{1,0:T(8,128)(2,1)}, bf16[256,2048]{1,0:T(8,128)(2,1)}, bf16[256,512]{1,0:T(8,128)(2,1)}) custom-call(f32[256,512]{1,0:T(8,128)S(1)} %get-tuple-element.28.total_ref, bf16[4,256,256]{2,1,0:T(8,128)(2,1)S(1)} %collective-permute-done.8.late_ref, f32[256,512]{1,0:T(8,128)S(1)} %get-tuple-element.30.terms_ref, ...), custom_call_target="tpu_custom_call", output_to_operand_aliasing={{1}: (5, {})} | custom-call | bytes 1048576 | tf_op jit(solution)/shard_map/finish/pallas_call | solution.py:387
  (35 shorter events, 3.2 us)
Async XLA Ops:
  0.6 11.1 %collective-permute-start.3 = (bf16[256,512]{1,0:T(8,128)(2,1)}, bf16[256,512]{1,0:T(8,128)(2,1)S(1)}, u32[]{:S(2)}, u32[]{:S(2)}) collective-permute-start(bf16[256,512]{1,0:T(8,128)(2,1)} %bitcast.12), channel_id=1, source_target_pairs={{2,0},{3,1},{0,4},{1,5},{4,6},{5,7},{6,2},{7,3},{10,8},{11,9},{8,1... | collective-permute-start | bytes 786440 | tf_op jit(solution)/shard_map/ppermute | solution.py:416
  4.7 9.4 %collective-permute-start.1 = (bf16[256,512]{1,0:T(8,128)(2,1)}, bf16[256,512]{1,0:T(8,128)(2,1)S(1)}, u32[]{:S(2)}, u32[]{:S(2)}) collective-permute-start(bf16[256,512]{1,0:T(8,128)(2,1)} %bitcast.19), channel_id=1, source_target_pairs={{0,1},{1,0},{2,3},{3,2},{4,5},{5,4},{6,7},{7,6},{8,9},{9,8},{10,11... | collective-permute-start | bytes 786440 | tf_op jit(solution)/shard_map/ppermute | solution.py:422
  6.2 1.2 %copy-start = (bf16[1,256,2048]{2,1,0:T(8,128)(2,1)S(1)}, bf16[1,256,2048]{2,1,0:T(8,128)(2,1)}, u32[]{:S(2)}) copy-start(bf16[1,256,2048]{2,1,0:T(8,128)(2,1)} %param.8) | copy-start | bytes 3145732
  7.4 0.9 %copy-start.2 = (bf16[1,256,512]{2,1,0:T(8,128)(2,1)S(1)}, bf16[1,256,512]{2,1,0:T(8,128)(2,1)}, u32[]{:S(2)}) copy-start(bf16[1,256,512]{2,1,0:T(8,128)(2,1)} %param.5) | copy-start | bytes 786436
  7.4 6.7 %copy-start.1 = (bf16[1,256,2048]{2,1,0:T(8,128)(2,1)S(1)}, bf16[1,256,2048]{2,1,0:T(8,128)(2,1)}, u32[]{:S(2)}) copy-start(bf16[1,256,2048]{2,1,0:T(8,128)(2,1)} %param.8) | copy-start | bytes 3145732
  7.5 12.3 %collective-permute-start = (bf16[2,256,256]{2,1,0:T(8,128)(2,1)S(1)}, bf16[2,256,256]{2,1,0:T(8,128)(2,1)S(1)}, u32[]{:S(2)}, u32[]{:S(2)}) collective-permute-start(bf16[2,256,256]{2,1,0:T(8,128)(2,1)S(1)} %pack_columns.2.refs_1_), channel_id=1, source_target_pairs={{0,1},{1,0},{2,3},{3,2},{4,5},{5,4},{6,7},{7,6},{8,9},{9,8},{10,11... | collective-permute-start | bytes 786440 | tf_op jit(solution)/shard_map/ppermute | solution.py:422
  8.4 12.5 %collective-permute-start.2 = (bf16[256,512]{1,0:T(8,128)(2,1)S(1)}, bf16[256,512]{1,0:T(8,128)(2,1)S(1)}, u32[]{:S(2)}, u32[]{:S(2)}) collective-permute-start(bf16[256,512]{1,0:T(8,128)(2,1)S(1)} %bitcast.13), channel_id=1, source_target_pairs={{0,2},{1,3},{4,0},{5,1},{6,4},{7,5},{2,6},{3,7},{8,10},{9,11},{12,... | collective-permute-start | bytes 786440 | tf_op jit(solution)/shard_map/ppermute | solution.py:419
  8.4 11.8 %collective-permute-start.6 = (bf16[1,256,256]{2,1,0:T(8,128)(2,1)S(1)}, bf16[1,256,256]{2,1,0:T(8,128)(2,1)S(1)}, u32[]{:S(2)}, u32[]{:S(2)}) collective-permute-start(bf16[1,256,256]{2,1,0:T(8,128)(2,1)S(1)} %partner_columns.2), channel_id=1, source_target_pairs={{0,16},{8,24},{16,0},{24,8},{1,17},{9,25},{17,1},{25,9},{2,18},{10... | collective-permute-start | bytes 393224 | tf_op jit(solution)/shard_map/ppermute | solution.py:106
  11.7 8.0 %copy-start.3 = (bf16[1,256,512]{2,1,0:T(8,128)(2,1)S(1)}, bf16[1,256,512]{2,1,0:T(8,128)(2,1)}, u32[]{:S(2)}) copy-start(bf16[1,256,512]{2,1,0:T(8,128)(2,1)} %param.9) | copy-start | bytes 786436
  14.2 9.7 %collective-permute-start.5 = (bf16[2,256,256]{2,1,0:T(8,128)(2,1)S(1)}, bf16[2,256,256]{2,1,0:T(8,128)(2,1)S(1)}, u32[]{:S(2)}, u32[]{:S(2)}) collective-permute-start(bf16[2,256,256]{2,1,0:T(8,128)(2,1)S(1)} %pack_columns.3), channel_id=1, source_target_pairs={{0,1},{1,0},{2,3},{3,2},{4,5},{5,4},{6,7},{7,6},{8,9},{9,8},{10,11... | collective-permute-start | bytes 786440 | tf_op jit(solution)/shard_map/ppermute | solution.py:422
  15.8 8.7 %collective-permute-start.4 = (bf16[256,512]{1,0:T(8,128)(2,1)S(1)}, bf16[256,512]{1,0:T(8,128)(2,1)S(1)}, u32[]{:S(2)}, u32[]{:S(2)}) collective-permute-start(bf16[256,512]{1,0:T(8,128)(2,1)S(1)} %collective-permute-done.3.refs_0_.refs_3_.refs_4_), channel_id=1, source_target_pairs={{2,0},{3,1},{0,4},{1,5},{4,6},{5,7},{6,2},{7,3},{10,8},{11,9},{8,1... | collective-permute-start | bytes 786440 | tf_op jit(solution)/shard_map/ppermute | solution.py:416
  20.3 2.2 %collective-permute-start.7 = (bf16[2,256,128]{2,1,0:T(8,128)(2,1)S(1)}, bf16[2,256,128]{2,1,0:T(8,128)(2,1)S(1)}, u32[]{:S(2)}, u32[]{:S(2)}) collective-permute-start(bf16[2,256,128]{2,1,0:T(8,128)(2,1)S(1)} %partner_columns.3), channel_id=1, source_target_pairs={{0,8},{8,0},{16,24},{24,16},{1,9},{9,1},{17,25},{25,17},{2,10},{10... | collective-permute-start | bytes 393224 | tf_op jit(solution)/shard_map/ppermute | solution.py:106
  20.4 10.0 %collective-permute-start.10 = (bf16[256,512]{1,0:T(8,128)(2,1)S(1)}, bf16[256,512]{1,0:T(8,128)(2,1)S(1)}, u32[]{:S(2)}, u32[]{:S(2)}) collective-permute-start(bf16[256,512]{1,0:T(8,128)(2,1)S(1)} %get-tuple-element.23.refs_4_.refs_2_), channel_id=1, source_target_pairs={{0,2},{1,3},{4,0},{5,1},{6,4},{7,5},{2,6},{3,7},{8,10},{9,11},{12,... | collective-permute-start | bytes 786440 | tf_op jit(solution)/shard_map/ppermute | solution.py:419
  20.9 9.6 %collective-permute-start.12 = (bf16[2,256,256]{2,1,0:T(8,128)(2,1)S(1)}, bf16[2,256,256]{2,1,0:T(8,128)(2,1)S(1)}, u32[]{:S(2)}, u32[]{:S(2)}) collective-permute-start(bf16[2,256,256]{2,1,0:T(8,128)(2,1)S(1)} %get-tuple-element.24.refs_6_.refs_4_), channel_id=1, source_target_pairs={{0,1},{1,0},{2,3},{3,2},{4,5},{5,4},{6,7},{7,6},{8,9},{9,8},{10,11... | collective-permute-start | bytes 786440 | tf_op jit(solution)/shard_map/ppermute | solution.py:422
  25.1 16.2 %collective-permute-start.8 = (bf16[4,256,256]{2,1,0:T(8,128)(2,1)S(1)}, bf16[4,256,256]{2,1,0:T(8,128)(2,1)S(1)}, u32[]{:S(2)}, u32[]{:S(2)}) collective-permute-start(bf16[4,256,256]{2,1,0:T(8,128)(2,1)S(1)} %get-tuple-element.29.refs_2_), channel_id=1, source_target_pairs={{0,1},{1,0},{2,3},{3,2},{4,5},{5,4},{6,7},{7,6},{8,9},{9,8},{10,11... | collective-permute-start | bytes 1572872 | tf_op jit(solution)/shard_map/ppermute | solution.py:422
  26.7 12.3 %collective-permute-start.9 = (bf16[256,512]{1,0:T(8,128)(2,1)S(1)}, bf16[256,512]{1,0:T(8,128)(2,1)S(1)}, u32[]{:S(2)}, u32[]{:S(2)}) collective-permute-start(bf16[256,512]{1,0:T(8,128)(2,1)S(1)} %get-tuple-element.25.refs_3_), channel_id=1, source_target_pairs={{2,0},{3,1},{0,4},{1,5},{4,6},{5,7},{6,2},{7,3},{10,8},{11,9},{8,1... | collective-permute-start | bytes 786440 | tf_op jit(solution)/shard_map/ppermute | solution.py:416
  30.4 1.0 %copy-start.4 = (bf16[256,512]{1,0:T(8,128)(2,1)S(1)}, bf16[256,512]{1,0:T(8,128)(2,1)}, u32[]{:S(2)}) copy-start(bf16[256,512]{1,0:T(8,128)(2,1)} %refs_3_.1) | copy-start | bytes 786436
  30.4 1.0 %copy-start.5 = (f32[256,128]{1,0:T(8,128)S(1)}, f32[256,128]{1,0:T(8,128)}, u32[]{:S(2)}) copy-start(f32[256,128]{1,0:T(8,128)} %refs_4_.1) | copy-start | bytes 393220
  30.5 10.9 %collective-permute-start.11 = (bf16[256,512]{1,0:T(8,128)(2,1)S(1)}, bf16[256,512]{1,0:T(8,128)(2,1)S(1)}, u32[]{:S(2)}, u32[]{:S(2)}) collective-permute-start(bf16[256,512]{1,0:T(8,128)(2,1)S(1)} %add_terms.1.refs_5_), channel_id=1, source_target_pairs={{0,2},{1,3},{4,0},{5,1},{6,4},{7,5},{2,6},{3,7},{8,10},{9,11},{12,... | collective-permute-start | bytes 786440 | tf_op jit(solution)/shard_map/ppermute | solution.py:419
  32.5 4.3 %collective-permute-start.13 = (bf16[256,128]{1,0:T(8,128)(2,1)S(1)}, bf16[256,128]{1,0:T(8,128)(2,1)S(1)}, u32[]{:S(2)}, u32[]{:S(2)}) collective-permute-start(bf16[256,128]{1,0:T(8,128)(2,1)S(1)} %get-tuple-element.38), channel_id=1, source_target_pairs={{0,16},{8,24},{16,0},{24,8},{1,17},{9,25},{17,1},{25,9},{2,18},{10... | collective-permute-start | bytes 196616 | tf_op jit(solution)/shard_map/ppermute | solution.py:106
  36.8 1.4 %collective-permute-start.14 = (bf16[256,256]{1,0:T(8,128)(2,1)S(1)}, bf16[256,256]{1,0:T(8,128)(2,1)S(1)}, u32[]{:S(2)}, u32[]{:S(2)}) collective-permute-start(bf16[256,256]{1,0:T(8,128)(2,1)S(1)} %constant_dynamic-update-slice_fusion.refs_0_), channel_id=1, source_target_pairs={{0,8},{8,0},{16,24},{24,16},{1,9},{9,1},{17,25},{25,17},{2,10},{10... | collective-permute-start | bytes 393224 | tf_op jit(solution)/shard_map/ppermute | solution.py:106

commit v13 on v12

--- a/solution.py
+++ b/solution.py
@@ -440,7 +440,7 @@
     early = across(leaving)
     operands[2] = partner_inputs[1]
     terms = token_terms(operands, size, [3, 0], F32, token_weight, (leaving,))
-    totals = near_rows(inputs_here, partner_inputs, {**early_blocks, 1: from_above}, size, (leaving, held[-1]))
+    totals = near_rows(inputs_here, partner_inputs, {**early_blocks, 1: from_above}, size, (leaving, arrived((late_blocks[2],))))
     rows, last, leaving = last_products(
         inputs_here, cotangent, partner_inputs, partner_cotangent, late_blocks, totals, size, ()
     )

time: 42.5 us -> 43.9 us (1.033)
  starting transfers between devices: 17.4 us -> 18.6 us
  waiting for transfers between devices: 15.3 us -> 16.4 us
  local copies, waits for them, and re-layouts: 2.43 us -> 1.59 us
    ppermute x3, waiting for transfers between devices: 1.76 us -> 4.48 us  [upward(): return lax.ppermute(array, 'fsdp', pairs)]
    ppermute x5, waiting for transfers between devices: 6.28 us -> 3.59 us  [across(): return lax.ppermute(array, 'fsdp', [(at, at ^ 1) for at in range(size)])]
    ppermute x3, starting transfers between devices: 7.24 us -> 9 us  [upward(): return lax.ppermute(array, 'fsdp', pairs)]
    ppermute x4, waiting for transfers between devices: 3.13 us -> 4.51 us  [swap(): lax.ppermute(array, 'replica', [(at, at ^ bits) for at in range(lax.axis_...]
    ppermute x5, starting transfers between devices: 6.77 us -> 5.8 us  [across(): return lax.ppermute(array, 'fsdp', [(at, at ^ 1) for at in range(size)])]
    unnamed x13, local copies, waits for them, and re-layouts: 2.41 us -> 1.57 us
    ppermute x3, starting transfers between devices: 0.12 us -> 0.56 us  [downward(): lax.ppermute(array, 'fsdp', [(target, source) for source, target in pairs])]
    pallas_call x13 -> x14, Pallas kernels: 4.57 us -> 4.55 us  [vmem_call(): pl.pallas_call(body, out_shape=out_shape, in_specs=[whole] * len(operands...]
  transfers between devices with their start and end apart: 15 -> 15, of which waited for: 8 -> 9; matrix products, arithmetic and copies ran while one was open for 0% -> 0% of each run, Pallas kernels for 13% -> 13%
where the time goes in v13:
time: 43.9 us; the launch traced here: 43.7 us
  starting transfers between devices  18.6 us (42%)
  waiting for transfers between devices  16.4 us (37%)
  Pallas kernels  6.43 us (15%)
  local copies, waits for them, and re-layouts  1.59 us (4%)
  between operations  0.78 us (2%)
    ppermute x3, starting transfers between devices, upward(): return lax.ppermute(array, 'fsdp', pairs)  9 us
    ppermute x5, starting transfers between devices, across(): return lax.ppermute(array, 'fsdp', [(at, at ^ 1) for at in range(size)])  5.8 us
    pallas_call x14, Pallas kernels, vmem_call(): pl.pallas_call(body, out_shape=out_shape, in_specs=[whole] * len(operands...  4.55 us
    ppermute x4, waiting for transfers between devices, swap(): lax.ppermute(array, 'replica', [(at, at ^ bits) for at in range(lax.axis_...  4.51 us
    ppermute x3, waiting for transfers between devices, upward(): return lax.ppermute(array, 'fsdp', pairs)  4.48 us
    ppermute x3, waiting for transfers between devices, downward(): lax.ppermute(array, 'fsdp', [(target, source) for source, target in pairs])  3.77 us
    ppermute x5, waiting for transfers between devices, across(): return lax.ppermute(array, 'fsdp', [(at, at ^ 1) for at in range(size)])  3.59 us
    ppermute x4, starting transfers between devices, swap(): lax.ppermute(array, 'replica', [(at, at ^ bits) for at in range(lax.axis_...  3.25 us
  transfers between devices with their start and end apart: 15, of which 9 were waited for; matrix products, arithmetic and copies ran while one was open for 0% of the time, Pallas kernels for 13%

profile of v13, /device:TPU:0, one launch (start us, length us, event | category | flops | bytes accessed | tf_op | source)
XLA Modules:
  0.0 43.7 jit_solution(17481199024108929328)
XLA Ops:
  0.6 4.1 %collective-permute-start.3 = (bf16[256,512]{1,0:T(8,128)(2,1)}, bf16[256,512]{1,0:T(8,128)(2,1)S(1)}, u32[]{:S(2)}, u32[]{:S(2)}) collective-permute-start(bf16[256,512]{1,0:T(8,128)(2,1)} %bitcast.12), channel_id=1, source_target_pairs={{2,0},{3,1},{0,4},{1,5},{4,6},{5,7},{6,2},{7,3},{10,8},{11,9},{8,1... | collective-permute-start | bytes 786440 | tf_op jit(solution)/shard_map/ppermute | solution.py:416
  4.7 1.5 %collective-permute-start.1 = (bf16[256,512]{1,0:T(8,128)(2,1)}, bf16[256,512]{1,0:T(8,128)(2,1)S(1)}, u32[]{:S(2)}, u32[]{:S(2)}) collective-permute-start(bf16[256,512]{1,0:T(8,128)(2,1)} %bitcast.19), channel_id=1, source_target_pairs={{0,1},{1,0},{2,3},{3,2},{4,5},{5,4},{6,7},{7,6},{8,9},{9,8},{10,11... | collective-permute-start | bytes 786440 | tf_op jit(solution)/shard_map/ppermute | solution.py:422
  6.2 1.2 %copy-done = bf16[1,256,2048]{2,1,0:T(8,128)(2,1)S(1)} copy-done((bf16[1,256,2048]{2,1,0:T(8,128)(2,1)S(1)}, bf16[1,256,2048]{2,1,0:T(8,128)(2,1)}, u32[]{:S(2)}) %copy-start) | copy-done | bytes 1048600
  7.5 0.6 %collective-permute-start = (bf16[2,256,256]{2,1,0:T(8,128)(2,1)S(1)}, bf16[2,256,256]{2,1,0:T(8,128)(2,1)S(1)}, u32[]{:S(2)}, u32[]{:S(2)}) collective-permute-start(bf16[2,256,256]{2,1,0:T(8,128)(2,1)S(1)} %pack_columns.2.refs_1_), channel_id=1, source_target_pairs={{0,1},{1,0},{2,3},{3,2},{4,5},{5,4},{6,7},{7,6},{8,9},{9,8},{10,11... | collective-permute-start | bytes 786440 | tf_op jit(solution)/shard_map/ppermute | solution.py:422
  8.4 3.4 %collective-permute-done.3.refs_0_.refs_3_.refs_4_ = bf16[256,512]{1,0:T(8,128)(2,1)S(1)} collective-permute-done((bf16[256,512]{1,0:T(8,128)(2,1)}, bf16[256,512]{1,0:T(8,128)(2,1)S(1)}, u32[]{:S(2)}, u32[]{:S(2)}) %collective-permute-start.3) | collective-permute-done | bytes 262176 | tf_op jit(solution)/shard_map/ppermute | solution.py:416
  11.7 3.3 %collective-permute-start.4 = (bf16[256,512]{1,0:T(8,128)(2,1)S(1)}, bf16[256,512]{1,0:T(8,128)(2,1)S(1)}, u32[]{:S(2)}, u32[]{:S(2)}) collective-permute-start(bf16[256,512]{1,0:T(8,128)(2,1)S(1)} %collective-permute-done.3.refs_0_.refs_3_.refs_4_), channel_id=1, source_target_pairs={{2,0},{3,1},{0,4},{1,5},{4,6},{5,7},{6,2},{7,3},{10,8},{11,9},{8,1... | collective-permute-start | bytes 786440 | tf_op jit(solution)/shard_map/ppermute | solution.py:416
  15.1 1.6 %collective-permute-start.5 = (bf16[2,256,256]{2,1,0:T(8,128)(2,1)S(1)}, bf16[2,256,256]{2,1,0:T(8,128)(2,1)S(1)}, u32[]{:S(2)}, u32[]{:S(2)}) collective-permute-start(bf16[2,256,256]{2,1,0:T(8,128)(2,1)S(1)} %pack_columns.3), channel_id=1, source_target_pairs={{0,1},{1,0},{2,3},{3,2},{4,5},{5,4},{6,7},{7,6},{8,9},{9,8},{10,11... | collective-permute-start | bytes 786440 | tf_op jit(solution)/shard_map/ppermute | solution.py:422
  16.7 1.6 %collective-permute-start.6 = (bf16[1,256,256]{2,1,0:T(8,128)(2,1)S(1)}, bf16[1,256,256]{2,1,0:T(8,128)(2,1)S(1)}, u32[]{:S(2)}, u32[]{:S(2)}) collective-permute-start(bf16[1,256,256]{2,1,0:T(8,128)(2,1)S(1)} %partner_columns.2), channel_id=1, source_target_pairs={{0,16},{8,24},{16,0},{24,8},{1,17},{9,25},{17,1},{25,9},{2,18},{10... | collective-permute-start | bytes 393224 | tf_op jit(solution)/shard_map/ppermute | solution.py:106
  18.3 1.5 %collective-permute-done.refs_2_.refs_1_ = bf16[2,256,256]{2,1,0:T(8,128)(2,1)S(1)} collective-permute-done((bf16[2,256,256]{2,1,0:T(8,128)(2,1)S(1)}, bf16[2,256,256]{2,1,0:T(8,128)(2,1)S(1)}, u32[]{:S(2)}, u32[]{:S(2)}) %collective-permute-start) | collective-permute-done | bytes 262176 | tf_op jit(solution)/shard_map/ppermute | solution.py:422
  20.3 1.4 %collective-permute-done.6.refs_5_.refs_1_ = bf16[1,256,256]{2,1,0:T(8,128)(2,1)S(1)} collective-permute-done((bf16[1,256,256]{2,1,0:T(8,128)(2,1)S(1)}, bf16[1,256,256]{2,1,0:T(8,128)(2,1)S(1)}, u32[]{:S(2)}, u32[]{:S(2)}) %collective-permute-start.6) | collective-permute-done | bytes 131104 | tf_op jit(solution)/shard_map/ppermute | solution.py:106
  22.2 0.6 %collective-permute-start.11 = (bf16[2,256,256]{2,1,0:T(8,128)(2,1)S(1)}, bf16[2,256,256]{2,1,0:T(8,128)(2,1)S(1)}, u32[]{:S(2)}, u32[]{:S(2)}) collective-permute-start(bf16[2,256,256]{2,1,0:T(8,128)(2,1)S(1)} %get-tuple-element.24.refs_6_.refs_4_), channel_id=1, source_target_pairs={{0,1},{1,0},{2,3},{3,2},{4,5},{5,4},{6,7},{7,6},{8,9},{9,8},{10,11... | collective-permute-start | bytes 786440 | tf_op jit(solution)/shard_map/ppermute | solution.py:422
  22.8 1.1 %collective-permute-done.4.refs_0_.refs_5_ = bf16[256,512]{1,0:T(8,128)(2,1)S(1)} collective-permute-done((bf16[256,512]{1,0:T(8,128)(2,1)S(1)}, bf16[256,512]{1,0:T(8,128)(2,1)S(1)}, u32[]{:S(2)}, u32[]{:S(2)}) %collective-permute-start.4) | collective-permute-done | bytes 262176 | tf_op jit(solution)/shard_map/ppermute | solution.py:416
  23.9 1.5 %collective-permute-done.5.refs_2_ = bf16[2,256,256]{2,1,0:T(8,128)(2,1)S(1)} collective-permute-done((bf16[2,256,256]{2,1,0:T(8,128)(2,1)S(1)}, bf16[2,256,256]{2,1,0:T(8,128)(2,1)S(1)}, u32[]{:S(2)}, u32[]{:S(2)}) %collective-permute-start.5) | collective-permute-done | bytes 262176 | tf_op jit(solution)/shard_map/ppermute | solution.py:422
  25.4 0.6 %near_rows.1 = (f32[256,512]{1,0:T(8,128)S(1)}, f32[256,512]{1,0:T(8,128)S(1)}) custom-call(bf16[256,2048]{1,0:T(8,128)(2,1)S(1)} %bitcast.9, bf16[2,256,256]{2,1,0:T(8,128)(2,1)S(1)} %collective-permute-done.refs_2_.refs_1_, bf16[2,256,256]{2,1,0:T(8,128)(2,1)S(1)} %collective-permute-done.5.refs_2_, bf16[256,512]{1,0:T(8,128)(2,1)S(1)} %bitcast.16, ...), custom_call_target="tpu_custom_call" | custom-call | flops 402653184 | bytes 2359296 | tf_op jit(solution)/shard_map/near_rows/pallas_call | solution.py:48
  26.0 0.6 %last_products.1 = (f32[256,512]{1,0:T(8,128)S(1)}, bf16[2,256,256]{2,1,0:T(8,128)(2,1)S(1)}, bf16[4,256,256]{2,1,0:T(8,128)(2,1)S(1)}) custom-call(bf16[256,2048]{1,0:T(8,128)(2,1)S(1)} %bitcast.10, bf16[256,512]{1,0:T(8,128)(2,1)S(1)} %bitcast.22, bf16[2,256,256]{2,1,0:T(8,128)(2,1)S(1)} %collective-permute-done.refs_2_.refs_1_, ...), custom_call_target="tpu_custom_call" | custom-call | flops 268435456 | bytes 3407872 | tf_op jit(solution)/shard_map/last_products/pallas_call | solution.py:48
  26.6 1.6 %collective-permute-start.7 = (bf16[4,256,256]{2,1,0:T(8,128)(2,1)S(1)}, bf16[4,256,256]{2,1,0:T(8,128)(2,1)S(1)}, u32[]{:S(2)}, u32[]{:S(2)}) collective-permute-start(bf16[4,256,256]{2,1,0:T(8,128)(2,1)S(1)} %get-tuple-element.28.refs_2_), channel_id=1, source_target_pairs={{0,1},{1,0},{2,3},{3,2},{4,5},{5,4},{6,7},{7,6},{8,9},{9,8},{10,11... | collective-permute-start | bytes 1572872 | tf_op jit(solution)/shard_map/ppermute | solution.py:422
  28.3 1.6 %collective-permute-start.8 = (bf16[256,512]{1,0:T(8,128)(2,1)S(1)}, bf16[256,512]{1,0:T(8,128)(2,1)S(1)}, u32[]{:S(2)}, u32[]{:S(2)}) collective-permute-start(bf16[256,512]{1,0:T(8,128)(2,1)S(1)} %get-tuple-element.30.refs_3_), channel_id=1, source_target_pairs={{2,0},{3,1},{0,4},{1,5},{4,6},{5,7},{6,2},{7,3},{10,8},{11,9},{8,1... | collective-permute-start | bytes 786440 | tf_op jit(solution)/shard_map/ppermute | solution.py:416
  31.5 1.1 %outer_update.1 = (bf16[256,128]{1,0:T(8,128)(2,1)S(1)}, f32[256,128]{1,0:T(8,128)}) custom-call(bf16[256,512]{1,0:T(8,128)(2,1)S(1)} %bitcast.18, bf16[1,256,256]{2,1,0:T(8,128)(2,1)S(1)} %collective-permute-done.6.refs_5_.refs_1_, bf16[2,256,128]{2,1,0:T(8,128)(2,1)S(1)} %collective-permute-done.12.refs_2_, bf16[256,512]{1,0:T(8,128)(2,1)S(1)} %copy-done.4, ...), custom_call_target="tpu_custom_call" | custom-call | bytes 917504 | tf_op jit(solution)/shard_map/outer_update/pallas_call | solution.py:48
  32.6 1.5 %collective-permute-start.13 = (bf16[256,128]{1,0:T(8,128)(2,1)S(1)}, bf16[256,128]{1,0:T(8,128)(2,1)S(1)}, u32[]{:S(2)}, u32[]{:S(2)}) collective-permute-start(bf16[256,128]{1,0:T(8,128)(2,1)S(1)} %get-tuple-element.38), channel_id=1, source_target_pairs={{0,16},{8,24},{16,0},{24,8},{1,17},{9,25},{17,1},{25,9},{2,18},{10... | collective-permute-start | bytes 196616 | tf_op jit(solution)/shard_map/ppermute | solution.py:106
  34.1 2.7 %collective-permute-done.13 = bf16[256,128]{1,0:T(8,128)(2,1)S(1)} collective-permute-done((bf16[256,128]{1,0:T(8,128)(2,1)S(1)}, bf16[256,128]{1,0:T(8,128)(2,1)S(1)}, u32[]{:S(2)}, u32[]{:S(2)}) %collective-permute-start.13) | collective-permute-done | bytes 65568 | tf_op jit(solution)/shard_map/ppermute | solution.py:106
  36.9 0.9 %collect.1 = (bf16[256,2048]{1,0:T(8,128)(2,1)}, f32[8,128]{1,0:T(8,128)S(1)}) custom-call(bf16[2,256,256]{2,1,0:T(8,128)(2,1)S(1)} %get-tuple-element.32.near_ref, bf16[2,256,256]{2,1,0:T(8,128)(2,1)S(1)} %get-tuple-element.33.last_ref, bf16[2,256,256]{2,1,0:T(8,128)(2,1)S(1)} %collective-permute-done.11.early_ref.refs_6_), custom_call_target="tpu_custom_call" | custom-call | bytes 1048576 | tf_op jit(solution)/shard_map/collect/pallas_call | solution.py:356
  38.3 0.8 %join_shares.1 = bf16[256,512]{1,0:T(8,128)(2,1)} custom-call(bf16[256,256]{1,0:T(8,128)(2,1)S(1)} %constant_dynamic-update-slice_fusion.refs_0_, bf16[256,256]{1,0:T(8,128)(2,1)S(1)} %collective-permute-done.14.refs_1_, f32[8,128]{1,0:T(8,128)S(1)} %get-tuple-element.39.refs_2_), custom_call_target="tpu_custom_call" | custom-call | bytes 262144 | tf_op jit(solution)/shard_map/join_shares/pallas_call | solution.py:48
  39.0 3.8 %collective-permute-done.10.down_ref = bf16[256,512]{1,0:T(8,128)(2,1)S(1)} collective-permute-done((bf16[256,512]{1,0:T(8,128)(2,1)S(1)}, bf16[256,512]{1,0:T(8,128)(2,1)S(1)}, u32[]{:S(2)}, u32[]{:S(2)}) %collective-permute-start.10) | collective-permute-done | bytes 262176 | tf_op jit(solution)/shard_map/ppermute | solution.py:419
  42.8 0.9 %finish.1 = (bf16[256,512]{1,0:T(8,128)(2,1)}, bf16[256,2048]{1,0:T(8,128)(2,1)}, bf16[256,512]{1,0:T(8,128)(2,1)}) custom-call(f32[256,512]{1,0:T(8,128)S(1)} %get-tuple-element.27.total_ref, bf16[4,256,256]{2,1,0:T(8,128)(2,1)S(1)} %collective-permute-done.7.late_ref, f32[256,512]{1,0:T(8,128)S(1)} %get-tuple-element.29.terms_ref, ...), custom_call_target="tpu_custom_call", output_to_operand_aliasing={{1}: (5, {})} | custom-call | bytes 1048576 | tf_op jit(solution)/shard_map/finish/pallas_call | solution.py:387
  (36 shorter events, 3.5 us)
Async XLA Ops:
  0.6 11.1 %collective-permute-start.3 = (bf16[256,512]{1,0:T(8,128)(2,1)}, bf16[256,512]{1,0:T(8,128)(2,1)S(1)}, u32[]{:S(2)}, u32[]{:S(2)}) collective-permute-start(bf16[256,512]{1,0:T(8,128)(2,1)} %bitcast.12), channel_id=1, source_target_pairs={{2,0},{3,1},{0,4},{1,5},{4,6},{5,7},{6,2},{7,3},{10,8},{11,9},{8,1... | collective-permute-start | bytes 786440 | tf_op jit(solution)/shard_map/ppermute | solution.py:416
  4.7 10.3 %collective-permute-start.1 = (bf16[256,512]{1,0:T(8,128)(2,1)}, bf16[256,512]{1,0:T(8,128)(2,1)S(1)}, u32[]{:S(2)}, u32[]{:S(2)}) collective-permute-start(bf16[256,512]{1,0:T(8,128)(2,1)} %bitcast.19), channel_id=1, source_target_pairs={{0,1},{1,0},{2,3},{3,2},{4,5},{5,4},{6,7},{7,6},{8,9},{9,8},{10,11... | collective-permute-start | bytes 786440 | tf_op jit(solution)/shard_map/ppermute | solution.py:422
  6.2 1.2 %copy-start = (bf16[1,256,2048]{2,1,0:T(8,128)(2,1)S(1)}, bf16[1,256,2048]{2,1,0:T(8,128)(2,1)}, u32[]{:S(2)}) copy-start(bf16[1,256,2048]{2,1,0:T(8,128)(2,1)} %param.8) | copy-start | bytes 3145732
  7.4 0.9 %copy-start.2 = (bf16[1,256,512]{2,1,0:T(8,128)(2,1)S(1)}, bf16[1,256,512]{2,1,0:T(8,128)(2,1)}, u32[]{:S(2)}) copy-start(bf16[1,256,512]{2,1,0:T(8,128)(2,1)} %param.5) | copy-start | bytes 786436
  7.4 7.6 %copy-start.1 = (bf16[1,256,2048]{2,1,0:T(8,128)(2,1)S(1)}, bf16[1,256,2048]{2,1,0:T(8,128)(2,1)}, u32[]{:S(2)}) copy-start(bf16[1,256,2048]{2,1,0:T(8,128)(2,1)} %param.8) | copy-start | bytes 3145732
  7.5 12.3 %collective-permute-start = (bf16[2,256,256]{2,1,0:T(8,128)(2,1)S(1)}, bf16[2,256,256]{2,1,0:T(8,128)(2,1)S(1)}, u32[]{:S(2)}, u32[]{:S(2)}) collective-permute-start(bf16[2,256,256]{2,1,0:T(8,128)(2,1)S(1)} %pack_columns.2.refs_1_), channel_id=1, source_target_pairs={{0,1},{1,0},{2,3},{3,2},{4,5},{5,4},{6,7},{7,6},{8,9},{9,8},{10,11... | collective-permute-start | bytes 786440 | tf_op jit(solution)/shard_map/ppermute | solution.py:422
  8.4 15.5 %collective-permute-start.2 = (bf16[256,512]{1,0:T(8,128)(2,1)S(1)}, bf16[256,512]{1,0:T(8,128)(2,1)S(1)}, u32[]{:S(2)}, u32[]{:S(2)}) collective-permute-start(bf16[256,512]{1,0:T(8,128)(2,1)S(1)} %bitcast.13), channel_id=1, source_target_pairs={{0,2},{1,3},{4,0},{5,1},{6,4},{7,5},{2,6},{3,7},{8,10},{9,11},{12,... | collective-permute-start | bytes 786440 | tf_op jit(solution)/shard_map/ppermute | solution.py:419
  11.7 12.1 %collective-permute-start.4 = (bf16[256,512]{1,0:T(8,128)(2,1)S(1)}, bf16[256,512]{1,0:T(8,128)(2,1)S(1)}, u32[]{:S(2)}, u32[]{:S(2)}) collective-permute-start(bf16[256,512]{1,0:T(8,128)(2,1)S(1)} %collective-permute-done.3.refs_0_.refs_3_.refs_4_), channel_id=1, source_target_pairs={{2,0},{3,1},{0,4},{1,5},{4,6},{5,7},{6,2},{7,3},{10,8},{11,9},{8,1... | collective-permute-start | bytes 786440 | tf_op jit(solution)/shard_map/ppermute | solution.py:416
  15.1 4.7 %copy-start.3 = (bf16[1,256,512]{2,1,0:T(8,128)(2,1)S(1)}, bf16[1,256,512]{2,1,0:T(8,128)(2,1)}, u32[]{:S(2)}) copy-start(bf16[1,256,512]{2,1,0:T(8,128)(2,1)} %param.9) | copy-start | bytes 786436
  15.1 10.3 %collective-permute-start.5 = (bf16[2,256,256]{2,1,0:T(8,128)(2,1)S(1)}, bf16[2,256,256]{2,1,0:T(8,128)(2,1)S(1)}, u32[]{:S(2)}, u32[]{:S(2)}) collective-permute-start(bf16[2,256,256]{2,1,0:T(8,128)(2,1)S(1)} %pack_columns.3), channel_id=1, source_target_pairs={{0,1},{1,0},{2,3},{3,2},{4,5},{5,4},{6,7},{7,6},{8,9},{9,8},{10,11... | collective-permute-start | bytes 786440 | tf_op jit(solution)/shard_map/ppermute | solution.py:422
  16.7 5.0 %collective-permute-start.6 = (bf16[1,256,256]{2,1,0:T(8,128)(2,1)S(1)}, bf16[1,256,256]{2,1,0:T(8,128)(2,1)S(1)}, u32[]{:S(2)}, u32[]{:S(2)}) collective-permute-start(bf16[1,256,256]{2,1,0:T(8,128)(2,1)S(1)} %partner_columns.2), channel_id=1, source_target_pairs={{0,16},{8,24},{16,0},{24,8},{1,17},{9,25},{17,1},{25,9},{2,18},{10... | collective-permute-start | bytes 393224 | tf_op jit(solution)/shard_map/ppermute | solution.py:106
  20.2 10.1 %collective-permute-start.9 = (bf16[256,512]{1,0:T(8,128)(2,1)S(1)}, bf16[256,512]{1,0:T(8,128)(2,1)S(1)}, u32[]{:S(2)}, u32[]{:S(2)}) collective-permute-start(bf16[256,512]{1,0:T(8,128)(2,1)S(1)} %get-tuple-element.23.refs_4_.refs_2_), channel_id=1, source_target_pairs={{0,2},{1,3},{4,0},{5,1},{6,4},{7,5},{2,6},{3,7},{8,10},{9,11},{12,... | collective-permute-start | bytes 786440 | tf_op jit(solution)/shard_map/ppermute | solution.py:419
  22.2 9.3 %collective-permute-start.11 = (bf16[2,256,256]{2,1,0:T(8,128)(2,1)S(1)}, bf16[2,256,256]{2,1,0:T(8,128)(2,1)S(1)}, u32[]{:S(2)}, u32[]{:S(2)}) collective-permute-start(bf16[2,256,256]{2,1,0:T(8,128)(2,1)S(1)} %get-tuple-element.24.refs_6_.refs_4_), channel_id=1, source_target_pairs={{0,1},{1,0},{2,3},{3,2},{4,5},{5,4},{6,7},{7,6},{8,9},{9,8},{10,11... | collective-permute-start | bytes 786440 | tf_op jit(solution)/shard_map/ppermute | solution.py:422
  26.6 16.2 %collective-permute-start.7 = (bf16[4,256,256]{2,1,0:T(8,128)(2,1)S(1)}, bf16[4,256,256]{2,1,0:T(8,128)(2,1)S(1)}, u32[]{:S(2)}, u32[]{:S(2)}) collective-permute-start(bf16[4,256,256]{2,1,0:T(8,128)(2,1)S(1)} %get-tuple-element.28.refs_2_), channel_id=1, source_target_pairs={{0,1},{1,0},{2,3},{3,2},{4,5},{5,4},{6,7},{7,6},{8,9},{9,8},{10,11... | collective-permute-start | bytes 1572872 | tf_op jit(solution)/shard_map/ppermute | solution.py:422
  28.2 2.8 %collective-permute-start.12 = (bf16[2,256,128]{2,1,0:T(8,128)(2,1)S(1)}, bf16[2,256,128]{2,1,0:T(8,128)(2,1)S(1)}, u32[]{:S(2)}, u32[]{:S(2)}) collective-permute-start(bf16[2,256,128]{2,1,0:T(8,128)(2,1)S(1)} %partner_columns.3), channel_id=1, source_target_pairs={{0,8},{8,0},{16,24},{24,16},{1,9},{9,1},{17,25},{25,17},{2,10},{10... | collective-permute-start | bytes 393224 | tf_op jit(solution)/shard_map/ppermute | solution.py:106
  28.3 10.8 %collective-permute-start.8 = (bf16[256,512]{1,0:T(8,128)(2,1)S(1)}, bf16[256,512]{1,0:T(8,128)(2,1)S(1)}, u32[]{:S(2)}, u32[]{:S(2)}) collective-permute-start(bf16[256,512]{1,0:T(8,128)(2,1)S(1)} %get-tuple-element.30.refs_3_), channel_id=1, source_target_pairs={{2,0},{3,1},{0,4},{1,5},{4,6},{5,7},{6,2},{7,3},{10,8},{11,9},{8,1... | collective-permute-start | bytes 786440 | tf_op jit(solution)/shard_map/ppermute | solution.py:416
  30.4 1.1 %copy-start.4 = (bf16[256,512]{1,0:T(8,128)(2,1)S(1)}, bf16[256,512]{1,0:T(8,128)(2,1)}, u32[]{:S(2)}) copy-start(bf16[256,512]{1,0:T(8,128)(2,1)} %refs_3_.1) | copy-start | bytes 786436
  30.4 1.1 %copy-start.5 = (f32[256,128]{1,0:T(8,128)S(1)}, f32[256,128]{1,0:T(8,128)}, u32[]{:S(2)}) copy-start(f32[256,128]{1,0:T(8,128)} %refs_4_.1) | copy-start | bytes 393220
  30.4 12.4 %collective-permute-start.10 = (bf16[256,512]{1,0:T(8,128)(2,1)S(1)}, bf16[256,512]{1,0:T(8,128)(2,1)S(1)}, u32[]{:S(2)}, u32[]{:S(2)}) collective-permute-start(bf16[256,512]{1,0:T(8,128)(2,1)S(1)} %add_terms.1.refs_5_), channel_id=1, source_target_pairs={{0,2},{1,3},{4,0},{5,1},{6,4},{7,5},{2,6},{3,7},{8,10},{9,11},{12,... | collective-permute-start | bytes 786440 | tf_op jit(solution)/shard_map/ppermute | solution.py:419
  32.6 4.3 %collective-permute-start.13 = (bf16[256,128]{1,0:T(8,128)(2,1)S(1)}, bf16[256,128]{1,0:T(8,128)(2,1)S(1)}, u32[]{:S(2)}, u32[]{:S(2)}) collective-permute-start(bf16[256,128]{1,0:T(8,128)(2,1)S(1)} %get-tuple-element.38), channel_id=1, source_target_pairs={{0,16},{8,24},{16,0},{24,8},{1,17},{9,25},{17,1},{25,9},{2,18},{10... | collective-permute-start | bytes 196616 | tf_op jit(solution)/shard_map/ppermute | solution.py:106
  36.9 1.4 %collective-permute-start.14 = (bf16[256,256]{1,0:T(8,128)(2,1)S(1)}, bf16[256,256]{1,0:T(8,128)(2,1)S(1)}, u32[]{:S(2)}, u32[]{:S(2)}) collective-permute-start(bf16[256,256]{1,0:T(8,128)(2,1)S(1)} %constant_dynamic-update-slice_fusion.refs_0_), channel_id=1, source_target_pairs={{0,8},{8,0},{16,24},{24,16},{1,9},{9,1},{17,25},{25,17},{2,10},{10... | collective-permute-start | bytes 393224 | tf_op jit(solution)/shard_map/ppermute | solution.py:106

commit v14 on v13

--- a/solution.py
+++ b/solution.py
@@ -440,7 +440,7 @@
     early = across(leaving)
     operands[2] = partner_inputs[1]
     terms = token_terms(operands, size, [3, 0], F32, token_weight, (leaving,))
-    totals = near_rows(inputs_here, partner_inputs, {**early_blocks, 1: from_above}, size, (leaving, arrived((late_blocks[2],))))
+    totals = near_rows(inputs_here, partner_inputs, {**early_blocks, 1: from_above}, size, (leaving, held[-1], arrived((late_blocks[2],))))
     rows, last, leaving = last_products(
         inputs_here, cotangent, partner_inputs, partner_cotangent, late_blocks, totals, size, ()
     )
@@ -449,7 +449,7 @@
         add_kernel, shape_of(depth, kv_width, BF16), [terms[0], sum_down], 0, "add_terms", (leaving,)
     )
     sum_down = downward(total_down)
-    new_share, new_momentum = update_share(held, global_weights, momentum, (total_down, early))
+    new_share, new_momentum = update_share(held, global_weights, momentum, (total_down, early, sum_up))
     bits = lax.axis_size("replica")
     shares, joined = [new_share], [0]
     while bits > 1:

time: 43.9 us -> 44.7 us (1.018)
  starting transfers between devices: 18.6 us -> 19.8 us
  waiting for transfers between devices: 16.4 us -> 15.8 us
    ppermute x3, waiting for transfers between devices: 4.48 us -> 9.53 us  [upward(): return lax.ppermute(array, 'fsdp', pairs)]
    ppermute x3, waiting for transfers between devices: 3.77 us -> 1.66 us  [downward(): lax.ppermute(array, 'fsdp', [(target, source) for source, target in pairs])]
    ppermute x5, waiting for transfers between devices: 3.59 us -> 1.52 us  [across(): return lax.ppermute(array, 'fsdp', [(at, at ^ 1) for at in range(size)])]
    ppermute x4, waiting for transfers between devices: 4.51 us -> 3.13 us  [swap(): lax.ppermute(array, 'replica', [(at, at ^ bits) for at in range(lax.axis_...]
    ppermute x5, starting transfers between devices: 5.8 us -> 6.83 us  [across(): return lax.ppermute(array, 'fsdp', [(at, at ^ 1) for at in range(size)])]
    ppermute x3, starting transfers between devices: 9 us -> 9.61 us  [upward(): return lax.ppermute(array, 'fsdp', pairs)]
  transfers between devices with their start and end apart: 15 -> 15, of which waited for: 9 -> 7; matrix products, arithmetic and copies ran while one was open for 0% -> 0% of each run, Pallas kernels for 13% -> 12%
where the time goes in v14:
time: 44.7 us; the launch traced here: 44.5 us
  starting transfers between devices  19.8 us (44%)
  waiting for transfers between devices  15.8 us (35%)
  Pallas kernels  6.49 us (15%)
  local copies, waits for them, and re-layouts  1.58 us (4%)
  between operations  0.79 us (2%)
    ppermute x3, starting transfers between devices, upward(): return lax.ppermute(array, 'fsdp', pairs)  9.61 us
    ppermute x3, waiting for transfers between devices, upward(): return lax.ppermute(array, 'fsdp', pairs)  9.53 us
    ppermute x5, starting transfers between devices, across(): return lax.ppermute(array, 'fsdp', [(at, at ^ 1) for at in range(size)])  6.83 us
    pallas_call x14, Pallas kernels, vmem_call(): pl.pallas_call(body, out_shape=out_shape, in_specs=[whole] * len(operands...  4.62 us
    ppermute x4, starting transfers between devices, swap(): lax.ppermute(array, 'replica', [(at, at ^ bits) for at in range(lax.axis_...  3.24 us
    ppermute x4, waiting for transfers between devices, swap(): lax.ppermute(array, 'replica', [(at, at ^ bits) for at in range(lax.axis_...  3.13 us
    ppermute x3, waiting for transfers between devices, downward(): lax.ppermute(array, 'fsdp', [(target, source) for source, target in pairs])  1.66 us
    unnamed x13, local copies, waits for them, and re-layouts  1.56 us
  transfers between devices with their start and end apart: 15, of which 7 were waited for; matrix products, arithmetic and copies ran while one was open for 0% of the time, Pallas kernels for 12%

profile of v14, /device:TPU:0, one launch (start us, length us, event | category | flops | bytes accessed | tf_op | source)
XLA Modules:
  0.0 44.5 jit_solution(9624457653549683868)
XLA Ops:
  0.6 4.1 %collective-permute-start.3 = (bf16[256,512]{1,0:T(8,128)(2,1)}, bf16[256,512]{1,0:T(8,128)(2,1)S(1)}, u32[]{:S(2)}, u32[]{:S(2)}) collective-permute-start(bf16[256,512]{1,0:T(8,128)(2,1)} %bitcast.12), channel_id=1, source_target_pairs={{2,0},{3,1},{0,4},{1,5},{4,6},{5,7},{6,2},{7,3},{10,8},{11,9},{8,1... | collective-permute-start | bytes 786440 | tf_op jit(solution)/shard_map/ppermute | solution.py:416
  4.7 1.5 %collective-permute-start.1 = (bf16[256,512]{1,0:T(8,128)(2,1)}, bf16[256,512]{1,0:T(8,128)(2,1)S(1)}, u32[]{:S(2)}, u32[]{:S(2)}) collective-permute-start(bf16[256,512]{1,0:T(8,128)(2,1)} %bitcast.19), channel_id=1, source_target_pairs={{0,1},{1,0},{2,3},{3,2},{4,5},{5,4},{6,7},{7,6},{8,9},{9,8},{10,11... | collective-permute-start | bytes 786440 | tf_op jit(solution)/shard_map/ppermute | solution.py:422
  6.2 1.2 %copy-done = bf16[1,256,2048]{2,1,0:T(8,128)(2,1)S(1)} copy-done((bf16[1,256,2048]{2,1,0:T(8,128)(2,1)S(1)}, bf16[1,256,2048]{2,1,0:T(8,128)(2,1)}, u32[]{:S(2)}) %copy-start) | copy-done | bytes 1048600
  7.5 0.6 %collective-permute-start = (bf16[2,256,256]{2,1,0:T(8,128)(2,1)S(1)}, bf16[2,256,256]{2,1,0:T(8,128)(2,1)S(1)}, u32[]{:S(2)}, u32[]{:S(2)}) collective-permute-start(bf16[2,256,256]{2,1,0:T(8,128)(2,1)S(1)} %pack_columns.2.refs_1_), channel_id=1, source_target_pairs={{0,1},{1,0},{2,3},{3,2},{4,5},{5,4},{6,7},{7,6},{8,9},{9,8},{10,11... | collective-permute-start | bytes 786440 | tf_op jit(solution)/shard_map/ppermute | solution.py:422
  8.4 3.4 %collective-permute-done.3.refs_0_.refs_3_.refs_4_ = bf16[256,512]{1,0:T(8,128)(2,1)S(1)} collective-permute-done((bf16[256,512]{1,0:T(8,128)(2,1)}, bf16[256,512]{1,0:T(8,128)(2,1)S(1)}, u32[]{:S(2)}, u32[]{:S(2)}) %collective-permute-start.3) | collective-permute-done | bytes 262176 | tf_op jit(solution)/shard_map/ppermute | solution.py:416
  11.7 3.3 %collective-permute-start.4 = (bf16[256,512]{1,0:T(8,128)(2,1)S(1)}, bf16[256,512]{1,0:T(8,128)(2,1)S(1)}, u32[]{:S(2)}, u32[]{:S(2)}) collective-permute-start(bf16[256,512]{1,0:T(8,128)(2,1)S(1)} %collective-permute-done.3.refs_0_.refs_3_.refs_4_), channel_id=1, source_target_pairs={{2,0},{3,1},{0,4},{1,5},{4,6},{5,7},{6,2},{7,3},{10,8},{11,9},{8,1... | collective-permute-start | bytes 786440 | tf_op jit(solution)/shard_map/ppermute | solution.py:416
  15.0 1.6 %collective-permute-start.6 = (bf16[1,256,256]{2,1,0:T(8,128)(2,1)S(1)}, bf16[1,256,256]{2,1,0:T(8,128)(2,1)S(1)}, u32[]{:S(2)}, u32[]{:S(2)}) collective-permute-start(bf16[1,256,256]{2,1,0:T(8,128)(2,1)S(1)} %partner_columns.2), channel_id=1, source_target_pairs={{0,16},{8,24},{16,0},{24,8},{1,17},{9,25},{17,1},{25,9},{2,18},{10... | collective-permute-start | bytes 393224 | tf_op jit(solution)/shard_map/ppermute | solution.py:106
  16.7 1.6 %collective-permute-start.5 = (bf16[2,256,256]{2,1,0:T(8,128)(2,1)S(1)}, bf16[2,256,256]{2,1,0:T(8,128)(2,1)S(1)}, u32[]{:S(2)}, u32[]{:S(2)}) collective-permute-start(bf16[2,256,256]{2,1,0:T(8,128)(2,1)S(1)} %pack_columns.3), channel_id=1, source_target_pairs={{0,1},{1,0},{2,3},{3,2},{4,5},{5,4},{6,7},{7,6},{8,9},{9,8},{10,11... | collective-permute-start | bytes 786440 | tf_op jit(solution)/shard_map/ppermute | solution.py:422
  18.3 1.5 %collective-permute-done.refs_2_.refs_1_ = bf16[2,256,256]{2,1,0:T(8,128)(2,1)S(1)} collective-permute-done((bf16[2,256,256]{2,1,0:T(8,128)(2,1)S(1)}, bf16[2,256,256]{2,1,0:T(8,128)(2,1)S(1)}, u32[]{:S(2)}, u32[]{:S(2)}) %collective-permute-start) | collective-permute-done | bytes 262176 | tf_op jit(solution)/shard_map/ppermute | solution.py:422
  20.5 0.5 %near_grads.1 = (bf16[2,256,256]{2,1,0:T(8,128)(2,1)S(1)}, bf16[2,256,256]{2,1,0:T(8,128)(2,1)S(1)}) custom-call(bf16[256,512]{1,0:T(8,128)(2,1)S(1)} %bitcast.21, bf16[256,512]{1,0:T(8,128)(2,1)S(1)} %collective-permute-done.1.refs_1_.refs_3_, bf16[256,512]{1,0:T(8,128)(2,1)S(1)} %bitcast.16, ...), custom_call_target="tpu_custom_call" | custom-call | flops 268435456 | bytes 1048576 | tf_op jit(solution)/shard_map/near_grads/pallas_call | solution.py:48
  20.9 1.6 %collective-permute-start.12 = (bf16[2,256,256]{2,1,0:T(8,128)(2,1)S(1)}, bf16[2,256,256]{2,1,0:T(8,128)(2,1)S(1)}, u32[]{:S(2)}, u32[]{:S(2)}) collective-permute-start(bf16[2,256,256]{2,1,0:T(8,128)(2,1)S(1)} %get-tuple-element.24.refs_6_.refs_4_), channel_id=1, source_target_pairs={{0,1},{1,0},{2,3},{3,2},{4,5},{5,4},{6,7},{7,6},{8,9},{9,8},{10,11... | collective-permute-start | bytes 786440 | tf_op jit(solution)/shard_map/ppermute | solution.py:422
  22.5 0.7 %collective-permute-done.4.refs_0_.refs_5_ = bf16[256,512]{1,0:T(8,128)(2,1)S(1)} collective-permute-done((bf16[256,512]{1,0:T(8,128)(2,1)S(1)}, bf16[256,512]{1,0:T(8,128)(2,1)S(1)}, u32[]{:S(2)}, u32[]{:S(2)}) %collective-permute-start.4) | collective-permute-done | bytes 262176 | tf_op jit(solution)/shard_map/ppermute | solution.py:416
  23.2 2.2 %collective-permute-start.9 = (bf16[256,512]{1,0:T(8,128)(2,1)S(1)}, bf16[256,512]{1,0:T(8,128)(2,1)S(1)}, u32[]{:S(2)}, u32[]{:S(2)}) collective-permute-start(bf16[256,512]{1,0:T(8,128)(2,1)S(1)} %get-tuple-element.25.refs_3_), channel_id=1, source_target_pairs={{2,0},{3,1},{0,4},{1,5},{4,6},{5,7},{6,2},{7,3},{10,8},{11,9},{8,1... | collective-permute-start | bytes 786440 | tf_op jit(solution)/shard_map/ppermute | solution.py:416
  25.5 0.6 %near_rows.1 = (f32[256,512]{1,0:T(8,128)S(1)}, f32[256,512]{1,0:T(8,128)S(1)}) custom-call(bf16[256,2048]{1,0:T(8,128)(2,1)S(1)} %bitcast.9, bf16[2,256,256]{2,1,0:T(8,128)(2,1)S(1)} %collective-permute-done.refs_2_.refs_1_, bf16[2,256,256]{2,1,0:T(8,128)(2,1)S(1)} %collective-permute-done.5.refs_2_, bf16[256,512]{1,0:T(8,128)(2,1)S(1)} %bitcast.17, ...), custom_call_target="tpu_custom_call" | custom-call | flops 402653184 | bytes 2359296 | tf_op jit(solution)/shard_map/near_rows/pallas_call | solution.py:48
  26.1 0.6 %last_products.1 = (f32[256,512]{1,0:T(8,128)S(1)}, bf16[2,256,256]{2,1,0:T(8,128)(2,1)S(1)}, bf16[4,256,256]{2,1,0:T(8,128)(2,1)S(1)}) custom-call(bf16[256,2048]{1,0:T(8,128)(2,1)S(1)} %bitcast.10, bf16[256,512]{1,0:T(8,128)(2,1)S(1)} %bitcast.22, bf16[2,256,256]{2,1,0:T(8,128)(2,1)S(1)} %collective-permute-done.refs_2_.refs_1_, ...), custom_call_target="tpu_custom_call" | custom-call | flops 268435456 | bytes 3407872 | tf_op jit(solution)/shard_map/last_products/pallas_call | solution.py:48
  26.7 1.6 %collective-permute-start.8 = (bf16[4,256,256]{2,1,0:T(8,128)(2,1)S(1)}, bf16[4,256,256]{2,1,0:T(8,128)(2,1)S(1)}, u32[]{:S(2)}, u32[]{:S(2)}) collective-permute-start(bf16[4,256,256]{2,1,0:T(8,128)(2,1)S(1)} %get-tuple-element.29.refs_2_), channel_id=1, source_target_pairs={{0,1},{1,0},{2,3},{3,2},{4,5},{5,4},{6,7},{7,6},{8,9},{9,8},{10,11... | collective-permute-start | bytes 1572872 | tf_op jit(solution)/shard_map/ppermute | solution.py:422
  28.8 1.7 %collective-permute-done.10.refs_1_ = bf16[256,512]{1,0:T(8,128)(2,1)S(1)} collective-permute-done((bf16[256,512]{1,0:T(8,128)(2,1)S(1)}, bf16[256,512]{1,0:T(8,128)(2,1)S(1)}, u32[]{:S(2)}, u32[]{:S(2)}) %collective-permute-start.10) | collective-permute-done | bytes 262176 | tf_op jit(solution)/shard_map/ppermute | solution.py:419
  30.6 5.4 %collective-permute-done.9.up_ref.refs_7_ = bf16[256,512]{1,0:T(8,128)(2,1)S(1)} collective-permute-done((bf16[256,512]{1,0:T(8,128)(2,1)S(1)}, bf16[256,512]{1,0:T(8,128)(2,1)S(1)}, u32[]{:S(2)}, u32[]{:S(2)}) %collective-permute-start.9) | collective-permute-done | bytes 262176 | tf_op jit(solution)/shard_map/ppermute | solution.py:416
  36.0 1.1 %outer_update.1 = (bf16[256,128]{1,0:T(8,128)(2,1)S(1)}, f32[256,128]{1,0:T(8,128)}) custom-call(bf16[256,512]{1,0:T(8,128)(2,1)S(1)} %bitcast.18, bf16[1,256,256]{2,1,0:T(8,128)(2,1)S(1)} %collective-permute-done.6.refs_5_.refs_1_, bf16[2,256,128]{2,1,0:T(8,128)(2,1)S(1)} %collective-permute-done.7.refs_7_.refs_2_, bf16[256,512]{1,0:T(8,128)(2,1)S(1)} %copy-done.4, ...), custom_call_target="tpu_custom_call" | custom-call | bytes 917504 | tf_op jit(solution)/shard_map/outer_update/pallas_call | solution.py:48
  37.1 1.5 %collective-permute-start.13 = (bf16[256,128]{1,0:T(8,128)(2,1)S(1)}, bf16[256,128]{1,0:T(8,128)(2,1)S(1)}, u32[]{:S(2)}, u32[]{:S(2)}) collective-permute-start(bf16[256,128]{1,0:T(8,128)(2,1)S(1)} %get-tuple-element.38), channel_id=1, source_target_pairs={{0,16},{8,24},{16,0},{24,8},{1,17},{9,25},{17,1},{25,9},{2,18},{10... | collective-permute-start | bytes 196616 | tf_op jit(solution)/shard_map/ppermute | solution.py:106
  38.6 2.7 %collective-permute-done.13 = bf16[256,128]{1,0:T(8,128)(2,1)S(1)} collective-permute-done((bf16[256,128]{1,0:T(8,128)(2,1)S(1)}, bf16[256,128]{1,0:T(8,128)(2,1)S(1)}, u32[]{:S(2)}, u32[]{:S(2)}) %collective-permute-start.13) | collective-permute-done | bytes 65568 | tf_op jit(solution)/shard_map/ppermute | solution.py:106
  41.5 0.9 %collect.1 = (bf16[256,2048]{1,0:T(8,128)(2,1)}, f32[8,128]{1,0:T(8,128)S(1)}) custom-call(bf16[2,256,256]{2,1,0:T(8,128)(2,1)S(1)} %get-tuple-element.32.near_ref, bf16[2,256,256]{2,1,0:T(8,128)(2,1)S(1)} %get-tuple-element.33.last_ref, bf16[2,256,256]{2,1,0:T(8,128)(2,1)S(1)} %collective-permute-done.12.early_ref.refs_6_), custom_call_target="tpu_custom_call" | custom-call | bytes 1048576 | tf_op jit(solution)/shard_map/collect/pallas_call | solution.py:356
  42.8 0.8 %join_shares.1 = bf16[256,512]{1,0:T(8,128)(2,1)} custom-call(bf16[256,256]{1,0:T(8,128)(2,1)S(1)} %constant_dynamic-update-slice_fusion.refs_0_, bf16[256,256]{1,0:T(8,128)(2,1)S(1)} %collective-permute-done.14.refs_1_, f32[8,128]{1,0:T(8,128)S(1)} %get-tuple-element.39.refs_2_), custom_call_target="tpu_custom_call" | custom-call | bytes 262144 | tf_op jit(solution)/shard_map/join_shares/pallas_call | solution.py:48
  43.6 0.9 %finish.1 = (bf16[256,512]{1,0:T(8,128)(2,1)}, bf16[256,2048]{1,0:T(8,128)(2,1)}, bf16[256,512]{1,0:T(8,128)(2,1)}) custom-call(f32[256,512]{1,0:T(8,128)S(1)} %get-tuple-element.28.total_ref, bf16[4,256,256]{2,1,0:T(8,128)(2,1)S(1)} %collective-permute-done.8.late_ref, f32[256,512]{1,0:T(8,128)S(1)} %get-tuple-element.30.terms_ref, ...), custom_call_target="tpu_custom_call", output_to_operand_aliasing={{1}: (5, {})} | custom-call | bytes 1048576 | tf_op jit(solution)/shard_map/finish/pallas_call | solution.py:387
  (36 shorter events, 2.1 us)
Async XLA Ops:
  0.6 11.1 %collective-permute-start.3 = (bf16[256,512]{1,0:T(8,128)(2,1)}, bf16[256,512]{1,0:T(8,128)(2,1)S(1)}, u32[]{:S(2)}, u32[]{:S(2)}) collective-permute-start(bf16[256,512]{1,0:T(8,128)(2,1)} %bitcast.12), channel_id=1, source_target_pairs={{2,0},{3,1},{0,4},{1,5},{4,6},{5,7},{6,2},{7,3},{10,8},{11,9},{8,1... | collective-permute-start | bytes 786440 | tf_op jit(solution)/shard_map/ppermute | solution.py:416
  4.7 11.9 %collective-permute-start.1 = (bf16[256,512]{1,0:T(8,128)(2,1)}, bf16[256,512]{1,0:T(8,128)(2,1)S(1)}, u32[]{:S(2)}, u32[]{:S(2)}) collective-permute-start(bf16[256,512]{1,0:T(8,128)(2,1)} %bitcast.19), channel_id=1, source_target_pairs={{0,1},{1,0},{2,3},{3,2},{4,5},{5,4},{6,7},{7,6},{8,9},{9,8},{10,11... | collective-permute-start | bytes 786440 | tf_op jit(solution)/shard_map/ppermute | solution.py:422
  6.2 1.2 %copy-start = (bf16[1,256,2048]{2,1,0:T(8,128)(2,1)S(1)}, bf16[1,256,2048]{2,1,0:T(8,128)(2,1)}, u32[]{:S(2)}) copy-start(bf16[1,256,2048]{2,1,0:T(8,128)(2,1)} %param.8) | copy-start | bytes 3145732
  7.4 0.9 %copy-start.2 = (bf16[1,256,512]{2,1,0:T(8,128)(2,1)S(1)}, bf16[1,256,512]{2,1,0:T(8,128)(2,1)}, u32[]{:S(2)}) copy-start(bf16[1,256,512]{2,1,0:T(8,128)(2,1)} %param.5) | copy-start | bytes 786436
  7.4 9.2 %copy-start.1 = (bf16[1,256,2048]{2,1,0:T(8,128)(2,1)S(1)}, bf16[1,256,2048]{2,1,0:T(8,128)(2,1)}, u32[]{:S(2)}) copy-start(bf16[1,256,2048]{2,1,0:T(8,128)(2,1)} %param.8) | copy-start | bytes 3145732
  7.5 12.3 %collective-permute-start = (bf16[2,256,256]{2,1,0:T(8,128)(2,1)S(1)}, bf16[2,256,256]{2,1,0:T(8,128)(2,1)S(1)}, u32[]{:S(2)}, u32[]{:S(2)}) collective-permute-start(bf16[2,256,256]{2,1,0:T(8,128)(2,1)S(1)} %pack_columns.2.refs_1_), channel_id=1, source_target_pairs={{0,1},{1,0},{2,3},{3,2},{4,5},{5,4},{6,7},{7,6},{8,9},{9,8},{10,11... | collective-permute-start | bytes 786440 | tf_op jit(solution)/shard_map/ppermute | solution.py:422
  8.4 12.6 %collective-permute-start.2 = (bf16[256,512]{1,0:T(8,128)(2,1)S(1)}, bf16[256,512]{1,0:T(8,128)(2,1)S(1)}, u32[]{:S(2)}, u32[]{:S(2)}) collective-permute-start(bf16[256,512]{1,0:T(8,128)(2,1)S(1)} %bitcast.13), channel_id=1, source_target_pairs={{0,2},{1,3},{4,0},{5,1},{6,4},{7,5},{2,6},{3,7},{8,10},{9,11},{12,... | collective-permute-start | bytes 786440 | tf_op jit(solution)/shard_map/ppermute | solution.py:419
  11.7 11.5 %collective-permute-start.4 = (bf16[256,512]{1,0:T(8,128)(2,1)S(1)}, bf16[256,512]{1,0:T(8,128)(2,1)S(1)}, u32[]{:S(2)}, u32[]{:S(2)}) collective-permute-start(bf16[256,512]{1,0:T(8,128)(2,1)S(1)} %collective-permute-done.3.refs_0_.refs_3_.refs_4_), channel_id=1, source_target_pairs={{2,0},{3,1},{0,4},{1,5},{4,6},{5,7},{6,2},{7,3},{10,8},{11,9},{8,1... | collective-permute-start | bytes 786440 | tf_op jit(solution)/shard_map/ppermute | solution.py:416
  15.0 5.2 %collective-permute-start.6 = (bf16[1,256,256]{2,1,0:T(8,128)(2,1)S(1)}, bf16[1,256,256]{2,1,0:T(8,128)(2,1)S(1)}, u32[]{:S(2)}, u32[]{:S(2)}) collective-permute-start(bf16[1,256,256]{2,1,0:T(8,128)(2,1)S(1)} %partner_columns.2), channel_id=1, source_target_pairs={{0,16},{8,24},{16,0},{24,8},{1,17},{9,25},{17,1},{25,9},{2,18},{10... | collective-permute-start | bytes 393224 | tf_op jit(solution)/shard_map/ppermute | solution.py:106
  16.6 3.2 %copy-start.3 = (bf16[1,256,512]{2,1,0:T(8,128)(2,1)S(1)}, bf16[1,256,512]{2,1,0:T(8,128)(2,1)}, u32[]{:S(2)}) copy-start(bf16[1,256,512]{2,1,0:T(8,128)(2,1)} %param.9) | copy-start | bytes 786436
  16.7 8.8 %collective-permute-start.5 = (bf16[2,256,256]{2,1,0:T(8,128)(2,1)S(1)}, bf16[2,256,256]{2,1,0:T(8,128)(2,1)S(1)}, u32[]{:S(2)}, u32[]{:S(2)}) collective-permute-start(bf16[2,256,256]{2,1,0:T(8,128)(2,1)S(1)} %pack_columns.3), channel_id=1, source_target_pairs={{0,1},{1,0},{2,3},{3,2},{4,5},{5,4},{6,7},{7,6},{8,9},{9,8},{10,11... | collective-permute-start | bytes 786440 | tf_op jit(solution)/shard_map/ppermute | solution.py:422
  20.3 5.2 %collective-permute-start.7 = (bf16[2,256,128]{2,1,0:T(8,128)(2,1)S(1)}, bf16[2,256,128]{2,1,0:T(8,128)(2,1)S(1)}, u32[]{:S(2)}, u32[]{:S(2)}) collective-permute-start(bf16[2,256,128]{2,1,0:T(8,128)(2,1)S(1)} %partner_columns.3), channel_id=1, source_target_pairs={{0,8},{8,0},{16,24},{24,16},{1,9},{9,1},{17,25},{25,17},{2,10},{10... | collective-permute-start | bytes 393224 | tf_op jit(solution)/shard_map/ppermute | solution.py:106
  20.4 10.0 %collective-permute-start.10 = (bf16[256,512]{1,0:T(8,128)(2,1)S(1)}, bf16[256,512]{1,0:T(8,128)(2,1)S(1)}, u32[]{:S(2)}, u32[]{:S(2)}) collective-permute-start(bf16[256,512]{1,0:T(8,128)(2,1)S(1)} %get-tuple-element.23.refs_4_.refs_2_), channel_id=1, source_target_pairs={{0,2},{1,3},{4,0},{5,1},{6,4},{7,5},{2,6},{3,7},{8,10},{9,11},{12,... | collective-permute-start | bytes 786440 | tf_op jit(solution)/shard_map/ppermute | solution.py:419
  20.9 9.6 %collective-permute-start.12 = (bf16[2,256,256]{2,1,0:T(8,128)(2,1)S(1)}, bf16[2,256,256]{2,1,0:T(8,128)(2,1)S(1)}, u32[]{:S(2)}, u32[]{:S(2)}) collective-permute-start(bf16[2,256,256]{2,1,0:T(8,128)(2,1)S(1)} %get-tuple-element.24.refs_6_.refs_4_), channel_id=1, source_target_pairs={{0,1},{1,0},{2,3},{3,2},{4,5},{5,4},{6,7},{7,6},{8,9},{9,8},{10,11... | collective-permute-start | bytes 786440 | tf_op jit(solution)/shard_map/ppermute | solution.py:422
  23.2 12.8 %collective-permute-start.9 = (bf16[256,512]{1,0:T(8,128)(2,1)S(1)}, bf16[256,512]{1,0:T(8,128)(2,1)S(1)}, u32[]{:S(2)}, u32[]{:S(2)}) collective-permute-start(bf16[256,512]{1,0:T(8,128)(2,1)S(1)} %get-tuple-element.25.refs_3_), channel_id=1, source_target_pairs={{2,0},{3,1},{0,4},{1,5},{4,6},{5,7},{6,2},{7,3},{10,8},{11,9},{8,1... | collective-permute-start | bytes 786440 | tf_op jit(solution)/shard_map/ppermute | solution.py:416
  26.7 16.8 %collective-permute-start.8 = (bf16[4,256,256]{2,1,0:T(8,128)(2,1)S(1)}, bf16[4,256,256]{2,1,0:T(8,128)(2,1)S(1)}, u32[]{:S(2)}, u32[]{:S(2)}) collective-permute-start(bf16[4,256,256]{2,1,0:T(8,128)(2,1)S(1)} %get-tuple-element.29.refs_2_), channel_id=1, source_target_pairs={{0,1},{1,0},{2,3},{3,2},{4,5},{5,4},{6,7},{7,6},{8,9},{9,8},{10,11... | collective-permute-start | bytes 1572872 | tf_op jit(solution)/shard_map/ppermute | solution.py:422
  30.4 5.6 %copy-start.4 = (bf16[256,512]{1,0:T(8,128)(2,1)S(1)}, bf16[256,512]{1,0:T(8,128)(2,1)}, u32[]{:S(2)}) copy-start(bf16[256,512]{1,0:T(8,128)(2,1)} %refs_3_.1) | copy-start | bytes 786436
  30.4 5.6 %copy-start.5 = (f32[256,128]{1,0:T(8,128)S(1)}, f32[256,128]{1,0:T(8,128)}, u32[]{:S(2)}) copy-start(f32[256,128]{1,0:T(8,128)} %refs_4_.1) | copy-start | bytes 393220
  30.5 13.1 %collective-permute-start.11 = (bf16[256,512]{1,0:T(8,128)(2,1)S(1)}, bf16[256,512]{1,0:T(8,128)(2,1)S(1)}, u32[]{:S(2)}, u32[]{:S(2)}) collective-permute-start(bf16[256,512]{1,0:T(8,128)(2,1)S(1)} %add_terms.1.refs_5_), channel_id=1, source_target_pairs={{0,2},{1,3},{4,0},{5,1},{6,4},{7,5},{2,6},{3,7},{8,10},{9,11},{12,... | collective-permute-start | bytes 786440 | tf_op jit(solution)/shard_map/ppermute | solution.py:419
  37.1 4.3 %collective-permute-start.13 = (bf16[256,128]{1,0:T(8,128)(2,1)S(1)}, bf16[256,128]{1,0:T(8,128)(2,1)S(1)}, u32[]{:S(2)}, u32[]{:S(2)}) collective-permute-start(bf16[256,128]{1,0:T(8,128)(2,1)S(1)} %get-tuple-element.38), channel_id=1, source_target_pairs={{0,16},{8,24},{16,0},{24,8},{1,17},{9,25},{17,1},{25,9},{2,18},{10... | collective-permute-start | bytes 196616 | tf_op jit(solution)/shard_map/ppermute | solution.py:106
  41.4 1.4 %collective-permute-start.14 = (bf16[256,256]{1,0:T(8,128)(2,1)S(1)}, bf16[256,256]{1,0:T(8,128)(2,1)S(1)}, u32[]{:S(2)}, u32[]{:S(2)}) collective-permute-start(bf16[256,256]{1,0:T(8,128)(2,1)S(1)} %constant_dynamic-update-slice_fusion.refs_0_), channel_id=1, source_target_pairs={{0,8},{8,0},{16,24},{24,16},{1,9},{9,1},{17,25},{25,17},{2,10},{10... | collective-permute-start | bytes 393224 | tf_op jit(solution)/shard_map/ppermute | solution.py:106

commit v15 on v13

--- a/solution.py
+++ b/solution.py
@@ -441,15 +441,15 @@
     operands[2] = partner_inputs[1]
     terms = token_terms(operands, size, [3, 0], F32, token_weight, (leaving,))
     totals = near_rows(inputs_here, partner_inputs, {**early_blocks, 1: from_above}, size, (leaving, arrived((late_blocks[2],))))
+    new_share, new_momentum = update_share(held, global_weights, momentum, (totals[0],))
     rows, last, leaving = last_products(
-        inputs_here, cotangent, partner_inputs, partner_cotangent, late_blocks, totals, size, ()
+        inputs_here, cotangent, partner_inputs, partner_cotangent, late_blocks, totals, size, (new_share,)
     )
     late = across(leaving)
     total_down = vmem_call(
-        add_kernel, shape_of(depth, kv_width, BF16), [terms[0], sum_down], 0, "add_terms", (leaving,)
+        add_kernel, shape_of(depth, kv_width, BF16), [terms[0], sum_down], 0, "add_terms", (leaving, early)
     )
     sum_down = downward(total_down)
-    new_share, new_momentum = update_share(held, global_weights, momentum, (total_down, early))
     bits = lax.axis_size("replica")
     shares, joined = [new_share], [0]
     while bits > 1:

time: 43.9 us -> 45.2 us (1.030)
  starting transfers between devices: 18.6 us -> 20.7 us
  waiting for transfers between devices: 16.4 us -> 15.8 us
    ppermute x4, waiting for transfers between devices: 4.51 us -> 1.85 us  [swap(): lax.ppermute(array, 'replica', [(at, at ^ bits) for at in range(lax.axis_...]
    ppermute x3, starting transfers between devices: 0.56 us -> 3 us  [downward(): lax.ppermute(array, 'fsdp', [(target, source) for source, target in pairs])]
    ppermute x3, waiting for transfers between devices: 3.77 us -> 5.96 us  [downward(): lax.ppermute(array, 'fsdp', [(target, source) for source, target in pairs])]
    ppermute x5, waiting for transfers between devices: 3.59 us -> 2.69 us  [across(): return lax.ppermute(array, 'fsdp', [(at, at ^ 1) for at in range(size)])]
    ppermute x3, waiting for transfers between devices: 4.48 us -> 5.35 us  [upward(): return lax.ppermute(array, 'fsdp', pairs)]
  transfers between devices with their start and end apart: 15 -> 15, of which waited for: 9 -> 9; matrix products, arithmetic and copies ran while one was open for 0% -> 0% of each run, Pallas kernels for 13% -> 12%
where the time goes in v15:
time: 45.2 us; the launch traced here: 45.1 us
  starting transfers between devices  20.7 us (46%)
  waiting for transfers between devices  15.8 us (35%)
  Pallas kernels  6.44 us (14%)
  local copies, waits for them, and re-layouts  1.28 us (3%)
  between operations  0.79 us (2%)
    ppermute x3, starting transfers between devices, upward(): return lax.ppermute(array, 'fsdp', pairs)  8.61 us
    ppermute x3, waiting for transfers between devices, downward(): lax.ppermute(array, 'fsdp', [(target, source) for source, target in pairs])  5.96 us
    ppermute x5, starting transfers between devices, across(): return lax.ppermute(array, 'fsdp', [(at, at ^ 1) for at in range(size)])  5.87 us
    ppermute x3, waiting for transfers between devices, upward(): return lax.ppermute(array, 'fsdp', pairs)  5.35 us
    pallas_call x14, Pallas kernels, vmem_call(): pl.pallas_call(body, out_shape=out_shape, in_specs=[whole] * len(operands...  4.57 us
    ppermute x4, starting transfers between devices, swap(): lax.ppermute(array, 'replica', [(at, at ^ bits) for at in range(lax.axis_...  3.25 us
    ppermute x3, starting transfers between devices, downward(): lax.ppermute(array, 'fsdp', [(target, source) for source, target in pairs])  3 us
    ppermute x5, waiting for transfers between devices, across(): return lax.ppermute(array, 'fsdp', [(at, at ^ 1) for at in range(size)])  2.69 us
  transfers between devices with their start and end apart: 15, of which 9 were waited for; matrix products, arithmetic and copies ran while one was open for 0% of the time, Pallas kernels for 12%

profile of v15, /device:TPU:0, one launch (start us, length us, event | category | flops | bytes accessed | tf_op | source)
XLA Modules:
  0.0 45.1 jit_solution(16239188649765386656)
XLA Ops:
  0.6 4.1 %collective-permute-start.3 = (bf16[256,512]{1,0:T(8,128)(2,1)}, bf16[256,512]{1,0:T(8,128)(2,1)S(1)}, u32[]{:S(2)}, u32[]{:S(2)}) collective-permute-start(bf16[256,512]{1,0:T(8,128)(2,1)} %bitcast.12), channel_id=1, source_target_pairs={{2,0},{3,1},{0,4},{1,5},{4,6},{5,7},{6,2},{7,3},{10,8},{11,9},{8,1... | collective-permute-start | bytes 786440 | tf_op jit(solution)/shard_map/ppermute | solution.py:416
  4.7 1.5 %collective-permute-start.1 = (bf16[256,512]{1,0:T(8,128)(2,1)}, bf16[256,512]{1,0:T(8,128)(2,1)S(1)}, u32[]{:S(2)}, u32[]{:S(2)}) collective-permute-start(bf16[256,512]{1,0:T(8,128)(2,1)} %bitcast.19), channel_id=1, source_target_pairs={{0,1},{1,0},{2,3},{3,2},{4,5},{5,4},{6,7},{7,6},{8,9},{9,8},{10,11... | collective-permute-start | bytes 786440 | tf_op jit(solution)/shard_map/ppermute | solution.py:422
  6.2 1.2 %copy-done = bf16[1,256,2048]{2,1,0:T(8,128)(2,1)S(1)} copy-done((bf16[1,256,2048]{2,1,0:T(8,128)(2,1)S(1)}, bf16[1,256,2048]{2,1,0:T(8,128)(2,1)}, u32[]{:S(2)}) %copy-start) | copy-done | bytes 1048600
  7.5 0.6 %collective-permute-start = (bf16[2,256,256]{2,1,0:T(8,128)(2,1)S(1)}, bf16[2,256,256]{2,1,0:T(8,128)(2,1)S(1)}, u32[]{:S(2)}, u32[]{:S(2)}) collective-permute-start(bf16[2,256,256]{2,1,0:T(8,128)(2,1)S(1)} %pack_columns.2.refs_1_), channel_id=1, source_target_pairs={{0,1},{1,0},{2,3},{3,2},{4,5},{5,4},{6,7},{7,6},{8,9},{9,8},{10,11... | collective-permute-start | bytes 786440 | tf_op jit(solution)/shard_map/ppermute | solution.py:422
  8.1 2.5 %collective-permute-done.3.refs_0_.refs_3_.refs_4_ = bf16[256,512]{1,0:T(8,128)(2,1)S(1)} collective-permute-done((bf16[256,512]{1,0:T(8,128)(2,1)}, bf16[256,512]{1,0:T(8,128)(2,1)S(1)}, u32[]{:S(2)}, u32[]{:S(2)}) %collective-permute-start.3) | collective-permute-done | bytes 262176 | tf_op jit(solution)/shard_map/ppermute | solution.py:416
  10.6 3.3 %collective-permute-start.4 = (bf16[256,512]{1,0:T(8,128)(2,1)S(1)}, bf16[256,512]{1,0:T(8,128)(2,1)S(1)}, u32[]{:S(2)}, u32[]{:S(2)}) collective-permute-start(bf16[256,512]{1,0:T(8,128)(2,1)S(1)} %collective-permute-done.3.refs_0_.refs_3_.refs_4_), channel_id=1, source_target_pairs={{2,0},{3,1},{0,4},{1,5},{4,6},{5,7},{6,2},{7,3},{10,8},{11,9},{8,1... | collective-permute-start | bytes 786440 | tf_op jit(solution)/shard_map/ppermute | solution.py:416
  14.2 1.6 %collective-permute-start.5 = (bf16[2,256,256]{2,1,0:T(8,128)(2,1)S(1)}, bf16[2,256,256]{2,1,0:T(8,128)(2,1)S(1)}, u32[]{:S(2)}, u32[]{:S(2)}) collective-permute-start(bf16[2,256,256]{2,1,0:T(8,128)(2,1)S(1)} %pack_columns.3), channel_id=1, source_target_pairs={{0,1},{1,0},{2,3},{3,2},{4,5},{5,4},{6,7},{7,6},{8,9},{9,8},{10,11... | collective-permute-start | bytes 786440 | tf_op jit(solution)/shard_map/ppermute | solution.py:422
  15.8 1.6 %collective-permute-start.6 = (bf16[1,256,256]{2,1,0:T(8,128)(2,1)S(1)}, bf16[1,256,256]{2,1,0:T(8,128)(2,1)S(1)}, u32[]{:S(2)}, u32[]{:S(2)}) collective-permute-start(bf16[1,256,256]{2,1,0:T(8,128)(2,1)S(1)} %partner_columns.2), channel_id=1, source_target_pairs={{0,16},{8,24},{16,0},{24,8},{1,17},{9,25},{17,1},{25,9},{2,18},{10... | collective-permute-start | bytes 393224 | tf_op jit(solution)/shard_map/ppermute | solution.py:106
  17.4 2.4 %collective-permute-done.refs_2_.refs_1_ = bf16[2,256,256]{2,1,0:T(8,128)(2,1)S(1)} collective-permute-done((bf16[2,256,256]{2,1,0:T(8,128)(2,1)S(1)}, bf16[2,256,256]{2,1,0:T(8,128)(2,1)S(1)}, u32[]{:S(2)}, u32[]{:S(2)}) %collective-permute-start) | collective-permute-done | bytes 262176 | tf_op jit(solution)/shard_map/ppermute | solution.py:422
  20.9 1.7 %collective-permute-start.10 = (bf16[256,512]{1,0:T(8,128)(2,1)S(1)}, bf16[256,512]{1,0:T(8,128)(2,1)S(1)}, u32[]{:S(2)}, u32[]{:S(2)}) collective-permute-start(bf16[256,512]{1,0:T(8,128)(2,1)S(1)} %get-tuple-element.23.refs_4_.refs_2_), channel_id=1, source_target_pairs={{0,2},{1,3},{4,0},{5,1},{6,4},{7,5},{2,6},{3,7},{8,10},{9,11},{12,... | collective-permute-start | bytes 786440 | tf_op jit(solution)/shard_map/ppermute | solution.py:419
  23.1 0.6 %collective-permute-start.11 = (bf16[2,256,256]{2,1,0:T(8,128)(2,1)S(1)}, bf16[2,256,256]{2,1,0:T(8,128)(2,1)S(1)}, u32[]{:S(2)}, u32[]{:S(2)}) collective-permute-start(bf16[2,256,256]{2,1,0:T(8,128)(2,1)S(1)} %get-tuple-element.24.refs_6_.refs_4_), channel_id=1, source_target_pairs={{0,1},{1,0},{2,3},{3,2},{4,5},{5,4},{6,7},{7,6},{8,9},{9,8},{10,11... | collective-permute-start | bytes 786440 | tf_op jit(solution)/shard_map/ppermute | solution.py:422
  23.7 2.4 %collective-permute-done.2.refs_5_.refs_4_ = bf16[256,512]{1,0:T(8,128)(2,1)S(1)} collective-permute-done((bf16[256,512]{1,0:T(8,128)(2,1)S(1)}, bf16[256,512]{1,0:T(8,128)(2,1)S(1)}, u32[]{:S(2)}, u32[]{:S(2)}) %collective-permute-start.2) | collective-permute-done | bytes 262176 | tf_op jit(solution)/shard_map/ppermute | solution.py:419
  26.7 1.1 %outer_update.1 = (bf16[256,128]{1,0:T(8,128)(2,1)S(1)}, f32[256,128]{1,0:T(8,128)}) custom-call(bf16[256,512]{1,0:T(8,128)(2,1)S(1)} %bitcast.18, bf16[1,256,256]{2,1,0:T(8,128)(2,1)S(1)} %collective-permute-done.6.refs_5_.refs_1_, bf16[2,256,128]{2,1,0:T(8,128)(2,1)S(1)} %collective-permute-done.7.refs_2_, bf16[256,512]{1,0:T(8,128)(2,1)S(1)} %copy-done.4, ...), custom_call_target="tpu_custom_call" | custom-call | bytes 917504 | tf_op jit(solution)/shard_map/outer_update/pallas_call | solution.py:48
  27.8 0.6 %last_products.1 = (f32[256,512]{1,0:T(8,128)S(1)}, bf16[2,256,256]{2,1,0:T(8,128)(2,1)S(1)}, bf16[4,256,256]{2,1,0:T(8,128)(2,1)S(1)}) custom-call(bf16[256,2048]{1,0:T(8,128)(2,1)S(1)} %bitcast.10, bf16[256,512]{1,0:T(8,128)(2,1)S(1)} %bitcast.22, bf16[2,256,256]{2,1,0:T(8,128)(2,1)S(1)} %collective-permute-done.refs_2_.refs_1_, ...), custom_call_target="tpu_custom_call" | custom-call | flops 268435456 | bytes 3407872 | tf_op jit(solution)/shard_map/last_products/pallas_call | solution.py:48
  28.4 1.6 %collective-permute-start.8 = (bf16[4,256,256]{2,1,0:T(8,128)(2,1)S(1)}, bf16[4,256,256]{2,1,0:T(8,128)(2,1)S(1)}, u32[]{:S(2)}, u32[]{:S(2)}) collective-permute-start(bf16[4,256,256]{2,1,0:T(8,128)(2,1)S(1)} %get-tuple-element.30.refs_2_), channel_id=1, source_target_pairs={{0,1},{1,0},{2,3},{3,2},{4,5},{5,4},{6,7},{7,6},{8,9},{9,8},{10,11... | collective-permute-start | bytes 1572872 | tf_op jit(solution)/shard_map/ppermute | solution.py:422
  30.0 1.2 %collective-permute-start.9 = (bf16[256,512]{1,0:T(8,128)(2,1)S(1)}, bf16[256,512]{1,0:T(8,128)(2,1)S(1)}, u32[]{:S(2)}, u32[]{:S(2)}) collective-permute-start(bf16[256,512]{1,0:T(8,128)(2,1)S(1)} %get-tuple-element.27.refs_3_), channel_id=1, source_target_pairs={{2,0},{3,1},{0,4},{1,5},{4,6},{5,7},{6,2},{7,3},{10,8},{11,9},{8,1... | collective-permute-start | bytes 786440 | tf_op jit(solution)/shard_map/ppermute | solution.py:416
  31.3 1.5 %collective-permute-start.13 = (bf16[256,128]{1,0:T(8,128)(2,1)S(1)}, bf16[256,128]{1,0:T(8,128)(2,1)S(1)}, u32[]{:S(2)}, u32[]{:S(2)}) collective-permute-start(bf16[256,128]{1,0:T(8,128)(2,1)S(1)} %get-tuple-element.28.refs_8_), channel_id=1, source_target_pairs={{0,16},{8,24},{16,0},{24,8},{1,17},{9,25},{17,1},{25,9},{2,18},{10... | collective-permute-start | bytes 196616 | tf_op jit(solution)/shard_map/ppermute | solution.py:106
  33.3 1.3 %collective-permute-start.12 = (bf16[256,512]{1,0:T(8,128)(2,1)S(1)}, bf16[256,512]{1,0:T(8,128)(2,1)S(1)}, u32[]{:S(2)}, u32[]{:S(2)}) collective-permute-start(bf16[256,512]{1,0:T(8,128)(2,1)S(1)} %add_terms.1), channel_id=1, source_target_pairs={{0,2},{1,3},{4,0},{5,1},{6,4},{7,5},{2,6},{3,7},{8,10},{9,11},{12,... | collective-permute-start | bytes 786440 | tf_op jit(solution)/shard_map/ppermute | solution.py:419
  34.6 0.9 %collective-permute-done.13 = bf16[256,128]{1,0:T(8,128)(2,1)S(1)} collective-permute-done((bf16[256,128]{1,0:T(8,128)(2,1)S(1)}, bf16[256,128]{1,0:T(8,128)(2,1)S(1)}, u32[]{:S(2)}, u32[]{:S(2)}) %collective-permute-start.13) | collective-permute-done | bytes 65568 | tf_op jit(solution)/shard_map/ppermute | solution.py:106
  35.6 0.9 %collect.1 = (bf16[256,2048]{1,0:T(8,128)(2,1)}, f32[8,128]{1,0:T(8,128)S(1)}) custom-call(bf16[2,256,256]{2,1,0:T(8,128)(2,1)S(1)} %get-tuple-element.33.near_ref, bf16[2,256,256]{2,1,0:T(8,128)(2,1)S(1)} %get-tuple-element.34.last_ref, bf16[2,256,256]{2,1,0:T(8,128)(2,1)S(1)} %collective-permute-done.11.refs_3_.early_ref), custom_call_target="tpu_custom_call" | custom-call | bytes 1048576 | tf_op jit(solution)/shard_map/collect/pallas_call | solution.py:356
  37.0 0.8 %join_shares.1 = bf16[256,512]{1,0:T(8,128)(2,1)} custom-call(bf16[256,256]{1,0:T(8,128)(2,1)S(1)} %constant_dynamic-update-slice_fusion.refs_0_, bf16[256,256]{1,0:T(8,128)(2,1)S(1)} %collective-permute-done.14.refs_1_, f32[8,128]{1,0:T(8,128)S(1)} %get-tuple-element.39.refs_2_), custom_call_target="tpu_custom_call" | custom-call | bytes 262144 | tf_op jit(solution)/shard_map/join_shares/pallas_call | solution.py:48
  37.7 2.8 %collective-permute-done.9.up_ref = bf16[256,512]{1,0:T(8,128)(2,1)S(1)} collective-permute-done((bf16[256,512]{1,0:T(8,128)(2,1)S(1)}, bf16[256,512]{1,0:T(8,128)(2,1)S(1)}, u32[]{:S(2)}, u32[]{:S(2)}) %collective-permute-start.9) | collective-permute-done | bytes 262176 | tf_op jit(solution)/shard_map/ppermute | solution.py:416
  40.6 3.6 %collective-permute-done.12.down_ref = bf16[256,512]{1,0:T(8,128)(2,1)S(1)} collective-permute-done((bf16[256,512]{1,0:T(8,128)(2,1)S(1)}, bf16[256,512]{1,0:T(8,128)(2,1)S(1)}, u32[]{:S(2)}, u32[]{:S(2)}) %collective-permute-start.12) | collective-permute-done | bytes 262176 | tf_op jit(solution)/shard_map/ppermute | solution.py:419
  44.2 0.9 %finish.1 = (bf16[256,512]{1,0:T(8,128)(2,1)}, bf16[256,2048]{1,0:T(8,128)(2,1)}, bf16[256,512]{1,0:T(8,128)(2,1)}) custom-call(f32[256,512]{1,0:T(8,128)S(1)} %get-tuple-element.29.total_ref, bf16[4,256,256]{2,1,0:T(8,128)(2,1)S(1)} %collective-permute-done.8.late_ref, f32[256,512]{1,0:T(8,128)S(1)} %get-tuple-element.31.terms_ref, ...), custom_call_target="tpu_custom_call", output_to_operand_aliasing={{1}: (5, {})} | custom-call | bytes 1048576 | tf_op jit(solution)/shard_map/finish/pallas_call | solution.py:387
  (36 shorter events, 3.6 us)
Async XLA Ops:
  0.6 10.0 %collective-permute-start.3 = (bf16[256,512]{1,0:T(8,128)(2,1)}, bf16[256,512]{1,0:T(8,128)(2,1)S(1)}, u32[]{:S(2)}, u32[]{:S(2)}) collective-permute-start(bf16[256,512]{1,0:T(8,128)(2,1)} %bitcast.12), channel_id=1, source_target_pairs={{2,0},{3,1},{0,4},{1,5},{4,6},{5,7},{6,2},{7,3},{10,8},{11,9},{8,1... | collective-permute-start | bytes 786440 | tf_op jit(solution)/shard_map/ppermute | solution.py:416
  4.7 9.4 %collective-permute-start.1 = (bf16[256,512]{1,0:T(8,128)(2,1)}, bf16[256,512]{1,0:T(8,128)(2,1)S(1)}, u32[]{:S(2)}, u32[]{:S(2)}) collective-permute-start(bf16[256,512]{1,0:T(8,128)(2,1)} %bitcast.19), channel_id=1, source_target_pairs={{0,1},{1,0},{2,3},{3,2},{4,5},{5,4},{6,7},{7,6},{8,9},{9,8},{10,11... | collective-permute-start | bytes 786440 | tf_op jit(solution)/shard_map/ppermute | solution.py:422
  6.2 1.2 %copy-start = (bf16[1,256,2048]{2,1,0:T(8,128)(2,1)S(1)}, bf16[1,256,2048]{2,1,0:T(8,128)(2,1)}, u32[]{:S(2)}) copy-start(bf16[1,256,2048]{2,1,0:T(8,128)(2,1)} %param.8) | copy-start | bytes 3145732
  7.4 6.4 %copy-start.2 = (bf16[1,256,512]{2,1,0:T(8,128)(2,1)S(1)}, bf16[1,256,512]{2,1,0:T(8,128)(2,1)}, u32[]{:S(2)}) copy-start(bf16[1,256,512]{2,1,0:T(8,128)(2,1)} %param.5) | copy-start | bytes 786436
  7.4 6.7 %copy-start.1 = (bf16[1,256,2048]{2,1,0:T(8,128)(2,1)S(1)}, bf16[1,256,2048]{2,1,0:T(8,128)(2,1)}, u32[]{:S(2)}) copy-start(bf16[1,256,2048]{2,1,0:T(8,128)(2,1)} %param.8) | copy-start | bytes 3145732
  7.5 12.3 %collective-permute-start = (bf16[2,256,256]{2,1,0:T(8,128)(2,1)S(1)}, bf16[2,256,256]{2,1,0:T(8,128)(2,1)S(1)}, u32[]{:S(2)}, u32[]{:S(2)}) collective-permute-start(bf16[2,256,256]{2,1,0:T(8,128)(2,1)S(1)} %pack_columns.2.refs_1_), channel_id=1, source_target_pairs={{0,1},{1,0},{2,3},{3,2},{4,5},{5,4},{6,7},{7,6},{8,9},{9,8},{10,11... | collective-permute-start | bytes 786440 | tf_op jit(solution)/shard_map/ppermute | solution.py:422
  10.6 12.5 %collective-permute-start.4 = (bf16[256,512]{1,0:T(8,128)(2,1)S(1)}, bf16[256,512]{1,0:T(8,128)(2,1)S(1)}, u32[]{:S(2)}, u32[]{:S(2)}) collective-permute-start(bf16[256,512]{1,0:T(8,128)(2,1)S(1)} %collective-permute-done.3.refs_0_.refs_3_.refs_4_), channel_id=1, source_target_pairs={{2,0},{3,1},{0,4},{1,5},{4,6},{5,7},{6,2},{7,3},{10,8},{11,9},{8,1... | collective-permute-start | bytes 786440 | tf_op jit(solution)/shard_map/ppermute | solution.py:416
  13.9 12.2 %collective-permute-start.2 = (bf16[256,512]{1,0:T(8,128)(2,1)S(1)}, bf16[256,512]{1,0:T(8,128)(2,1)S(1)}, u32[]{:S(2)}, u32[]{:S(2)}) collective-permute-start(bf16[256,512]{1,0:T(8,128)(2,1)S(1)} %bitcast.13), channel_id=1, source_target_pairs={{0,2},{1,3},{4,0},{5,1},{6,4},{7,5},{2,6},{3,7},{8,10},{9,11},{12,... | collective-permute-start | bytes 786440 | tf_op jit(solution)/shard_map/ppermute | solution.py:419
  14.2 5.6 %copy-start.3 = (bf16[1,256,512]{2,1,0:T(8,128)(2,1)S(1)}, bf16[1,256,512]{2,1,0:T(8,128)(2,1)}, u32[]{:S(2)}) copy-start(bf16[1,256,512]{2,1,0:T(8,128)(2,1)} %param.9) | copy-start | bytes 786436
  14.2 11.9 %collective-permute-start.5 = (bf16[2,256,256]{2,1,0:T(8,128)(2,1)S(1)}, bf16[2,256,256]{2,1,0:T(8,128)(2,1)S(1)}, u32[]{:S(2)}, u32[]{:S(2)}) collective-permute-start(bf16[2,256,256]{2,1,0:T(8,128)(2,1)S(1)} %pack_columns.3), channel_id=1, source_target_pairs={{0,1},{1,0},{2,3},{3,2},{4,5},{5,4},{6,7},{7,6},{8,9},{9,8},{10,11... | collective-permute-start | bytes 786440 | tf_op jit(solution)/shard_map/ppermute | solution.py:422
  15.8 5.0 %collective-permute-start.6 = (bf16[1,256,256]{2,1,0:T(8,128)(2,1)S(1)}, bf16[1,256,256]{2,1,0:T(8,128)(2,1)S(1)}, u32[]{:S(2)}, u32[]{:S(2)}) collective-permute-start(bf16[1,256,256]{2,1,0:T(8,128)(2,1)S(1)} %partner_columns.2), channel_id=1, source_target_pairs={{0,16},{8,24},{16,0},{24,8},{1,17},{9,25},{17,1},{25,9},{2,18},{10... | collective-permute-start | bytes 393224 | tf_op jit(solution)/shard_map/ppermute | solution.py:106
  20.8 5.8 %collective-permute-start.7 = (bf16[2,256,128]{2,1,0:T(8,128)(2,1)S(1)}, bf16[2,256,128]{2,1,0:T(8,128)(2,1)S(1)}, u32[]{:S(2)}, u32[]{:S(2)}) collective-permute-start(bf16[2,256,128]{2,1,0:T(8,128)(2,1)S(1)} %partner_columns.3), channel_id=1, source_target_pairs={{0,8},{8,0},{16,24},{24,16},{1,9},{9,1},{17,25},{25,17},{2,10},{10... | collective-permute-start | bytes 393224 | tf_op jit(solution)/shard_map/ppermute | solution.py:106
  20.9 12.3 %collective-permute-start.10 = (bf16[256,512]{1,0:T(8,128)(2,1)S(1)}, bf16[256,512]{1,0:T(8,128)(2,1)S(1)}, u32[]{:S(2)}, u32[]{:S(2)}) collective-permute-start(bf16[256,512]{1,0:T(8,128)(2,1)S(1)} %get-tuple-element.23.refs_4_.refs_2_), channel_id=1, source_target_pairs={{0,2},{1,3},{4,0},{5,1},{6,4},{7,5},{2,6},{3,7},{8,10},{9,11},{12,... | collective-permute-start | bytes 786440 | tf_op jit(solution)/shard_map/ppermute | solution.py:419
  23.1 10.2 %collective-permute-start.11 = (bf16[2,256,256]{2,1,0:T(8,128)(2,1)S(1)}, bf16[2,256,256]{2,1,0:T(8,128)(2,1)S(1)}, u32[]{:S(2)}, u32[]{:S(2)}) collective-permute-start(bf16[2,256,256]{2,1,0:T(8,128)(2,1)S(1)} %get-tuple-element.24.refs_6_.refs_4_), channel_id=1, source_target_pairs={{0,1},{1,0},{2,3},{3,2},{4,5},{5,4},{6,7},{7,6},{8,9},{9,8},{10,11... | collective-permute-start | bytes 786440 | tf_op jit(solution)/shard_map/ppermute | solution.py:422
  23.7 3.0 %copy-start.4 = (bf16[256,512]{1,0:T(8,128)(2,1)S(1)}, bf16[256,512]{1,0:T(8,128)(2,1)}, u32[]{:S(2)}) copy-start(bf16[256,512]{1,0:T(8,128)(2,1)} %refs_3_.1) | copy-start | bytes 786436
  23.7 3.0 %copy-start.5 = (f32[256,128]{1,0:T(8,128)S(1)}, f32[256,128]{1,0:T(8,128)}, u32[]{:S(2)}) copy-start(f32[256,128]{1,0:T(8,128)} %refs_4_.1) | copy-start | bytes 393220
  28.4 15.8 %collective-permute-start.8 = (bf16[4,256,256]{2,1,0:T(8,128)(2,1)S(1)}, bf16[4,256,256]{2,1,0:T(8,128)(2,1)S(1)}, u32[]{:S(2)}, u32[]{:S(2)}) collective-permute-start(bf16[4,256,256]{2,1,0:T(8,128)(2,1)S(1)} %get-tuple-element.30.refs_2_), channel_id=1, source_target_pairs={{0,1},{1,0},{2,3},{3,2},{4,5},{5,4},{6,7},{7,6},{8,9},{9,8},{10,11... | collective-permute-start | bytes 1572872 | tf_op jit(solution)/shard_map/ppermute | solution.py:422
  30.0 10.5 %collective-permute-start.9 = (bf16[256,512]{1,0:T(8,128)(2,1)S(1)}, bf16[256,512]{1,0:T(8,128)(2,1)S(1)}, u32[]{:S(2)}, u32[]{:S(2)}) collective-permute-start(bf16[256,512]{1,0:T(8,128)(2,1)S(1)} %get-tuple-element.27.refs_3_), channel_id=1, source_target_pairs={{2,0},{3,1},{0,4},{1,5},{4,6},{5,7},{6,2},{7,3},{10,8},{11,9},{8,1... | collective-permute-start | bytes 786440 | tf_op jit(solution)/shard_map/ppermute | solution.py:416
  31.3 4.3 %collective-permute-start.13 = (bf16[256,128]{1,0:T(8,128)(2,1)S(1)}, bf16[256,128]{1,0:T(8,128)(2,1)S(1)}, u32[]{:S(2)}, u32[]{:S(2)}) collective-permute-start(bf16[256,128]{1,0:T(8,128)(2,1)S(1)} %get-tuple-element.28.refs_8_), channel_id=1, source_target_pairs={{0,16},{8,24},{16,0},{24,8},{1,17},{9,25},{17,1},{25,9},{2,18},{10... | collective-permute-start | bytes 196616 | tf_op jit(solution)/shard_map/ppermute | solution.py:106
  33.3 10.8 %collective-permute-start.12 = (bf16[256,512]{1,0:T(8,128)(2,1)S(1)}, bf16[256,512]{1,0:T(8,128)(2,1)S(1)}, u32[]{:S(2)}, u32[]{:S(2)}) collective-permute-start(bf16[256,512]{1,0:T(8,128)(2,1)S(1)} %add_terms.1), channel_id=1, source_target_pairs={{0,2},{1,3},{4,0},{5,1},{6,4},{7,5},{2,6},{3,7},{8,10},{9,11},{12,... | collective-permute-start | bytes 786440 | tf_op jit(solution)/shard_map/ppermute | solution.py:419
  35.6 1.4 %collective-permute-start.14 = (bf16[256,256]{1,0:T(8,128)(2,1)S(1)}, bf16[256,256]{1,0:T(8,128)(2,1)S(1)}, u32[]{:S(2)}, u32[]{:S(2)}) collective-permute-start(bf16[256,256]{1,0:T(8,128)(2,1)S(1)} %constant_dynamic-update-slice_fusion.refs_0_), channel_id=1, source_target_pairs={{0,8},{8,0},{16,24},{24,16},{1,9},{9,1},{17,25},{25,17},{2,10},{10... | collective-permute-start | bytes 393224 | tf_op jit(solution)/shard_map/ppermute | solution.py:106

commit v16 on v11

--- a/solution.py
+++ b/solution.py
@@ -439,7 +439,7 @@
     early = across(leaving)
     operands[2] = partner_inputs[1]
     terms = token_terms(operands, size, [3, 0], F32, token_weight, (leaving,))
-    totals = near_rows(inputs_here, partner_inputs, {**early_blocks, 1: from_above}, size, (leaving,))
+    totals = near_rows(inputs_here, partner_inputs, {**early_blocks, 1: from_above}, size, (leaving, arrived((late_blocks[2],))))
     rows, last, leaving = last_products(
         inputs_here, cotangent, partner_inputs, partner_cotangent, late_blocks, totals, size, ()
     )

time: 42.5 us -> 42.6 us (level)
  waiting for transfers between devices: 16.3 us -> 14.7 us
  starting transfers between devices: 16.8 us -> 18.1 us
    ppermute x5, waiting for transfers between devices: 7.03 us -> 4.23 us  [across(): return lax.ppermute(array, 'fsdp', [(at, at ^ 1) for at in range(size)])]
    ppermute x3, waiting for transfers between devices: 3.38 us -> 5.17 us  [upward(): return lax.ppermute(array, 'fsdp', pairs)]
    ppermute x3, starting transfers between devices: 7.24 us -> 8.94 us  [upward(): return lax.ppermute(array, 'fsdp', pairs)]
    ppermute x4, waiting for transfers between devices: 5.2 us -> 3.83 us  [swap(): lax.ppermute(array, 'replica', [(at, at ^ bits) for at in range(lax.axis_...]
    ppermute x3, waiting for transfers between devices: 0.66 us -> 1.48 us  [downward(): lax.ppermute(array, 'fsdp', [(target, source) for source, target in pairs])]
    pallas_call x14 -> x15, Pallas kernels: 4.57 us -> 4.57 us  [vmem_call(): pl.pallas_call(body, out_shape=out_shape, in_specs=[whole] * len(operands...]
  transfers between devices with their start and end apart: 15 -> 15, of which waited for: 9 -> 10; matrix products, arithmetic and copies ran while one was open for 0% -> 0% of each run, Pallas kernels for 13% -> 13%
where the time goes in v16:
time: 42.6 us; the launch traced here: 42.4 us
  starting transfers between devices  18.1 us (42%)
  waiting for transfers between devices  14.7 us (35%)
  Pallas kernels  6.44 us (15%)
  local copies, waits for them, and re-layouts  2.4 us (6%)
  between operations  0.77 us (2%)
    ppermute x3, starting transfers between devices, upward(): return lax.ppermute(array, 'fsdp', pairs)  8.94 us
    ppermute x5, starting transfers between devices, across(): return lax.ppermute(array, 'fsdp', [(at, at ^ 1) for at in range(size)])  5.8 us
    ppermute x3, waiting for transfers between devices, upward(): return lax.ppermute(array, 'fsdp', pairs)  5.17 us
    pallas_call x15, Pallas kernels, vmem_call(): pl.pallas_call(body, out_shape=out_shape, in_specs=[whole] * len(operands...  4.57 us
    ppermute x5, waiting for transfers between devices, across(): return lax.ppermute(array, 'fsdp', [(at, at ^ 1) for at in range(size)])  4.23 us
    ppermute x4, waiting for transfers between devices, swap(): lax.ppermute(array, 'replica', [(at, at ^ bits) for at in range(lax.axis_...  3.83 us
    ppermute x4, starting transfers between devices, swap(): lax.ppermute(array, 'replica', [(at, at ^ bits) for at in range(lax.axis_...  3.25 us
    unnamed x12, local copies, waits for them, and re-layouts  2.4 us
  transfers between devices with their start and end apart: 15, of which 10 were waited for; matrix products, arithmetic and copies ran while one was open for 0% of the time, Pallas kernels for 13%

profile of v16, /device:TPU:0, one launch (start us, length us, event | category | flops | bytes accessed | tf_op | source)
XLA Modules:
  0.0 42.4 jit_solution(6656537136597028268)
XLA Ops:
  0.6 4.1 %collective-permute-start.3 = (bf16[256,512]{1,0:T(8,128)(2,1)}, bf16[256,512]{1,0:T(8,128)(2,1)S(1)}, u32[]{:S(2)}, u32[]{:S(2)}) collective-permute-start(bf16[256,512]{1,0:T(8,128)(2,1)} %bitcast.12), channel_id=1, source_target_pairs={{2,0},{3,1},{0,4},{1,5},{4,6},{5,7},{6,2},{7,3},{10,8},{11,9},{8,1... | collective-permute-start | bytes 786440 | tf_op jit(solution)/shard_map/ppermute | solution.py:415
  4.7 1.5 %collective-permute-start.1 = (bf16[256,512]{1,0:T(8,128)(2,1)}, bf16[256,512]{1,0:T(8,128)(2,1)S(1)}, u32[]{:S(2)}, u32[]{:S(2)}) collective-permute-start(bf16[256,512]{1,0:T(8,128)(2,1)} %bitcast.19), channel_id=1, source_target_pairs={{0,1},{1,0},{2,3},{3,2},{4,5},{5,4},{6,7},{7,6},{8,9},{9,8},{10,11... | collective-permute-start | bytes 786440 | tf_op jit(solution)/shard_map/ppermute | solution.py:421
  6.2 1.2 %copy-done = bf16[1,256,2048]{2,1,0:T(8,128)(2,1)S(1)} copy-done((bf16[1,256,2048]{2,1,0:T(8,128)(2,1)S(1)}, bf16[1,256,2048]{2,1,0:T(8,128)(2,1)}, u32[]{:S(2)}) %copy-start) | copy-done | bytes 1048600
  8.4 3.4 %collective-permute-done.3.refs_0_.refs_3_.refs_4_ = bf16[256,512]{1,0:T(8,128)(2,1)S(1)} collective-permute-done((bf16[256,512]{1,0:T(8,128)(2,1)}, bf16[256,512]{1,0:T(8,128)(2,1)S(1)}, u32[]{:S(2)}, u32[]{:S(2)}) %collective-permute-start.3) | collective-permute-done | bytes 262176 | tf_op jit(solution)/shard_map/ppermute | solution.py:415
  11.7 3.3 %collective-permute-start.4 = (bf16[256,512]{1,0:T(8,128)(2,1)S(1)}, bf16[256,512]{1,0:T(8,128)(2,1)S(1)}, u32[]{:S(2)}, u32[]{:S(2)}) collective-permute-start(bf16[256,512]{1,0:T(8,128)(2,1)S(1)} %collective-permute-done.3.refs_0_.refs_3_.refs_4_), channel_id=1, source_target_pairs={{2,0},{3,1},{0,4},{1,5},{4,6},{5,7},{6,2},{7,3},{10,8},{11,9},{8,1... | collective-permute-start | bytes 786440 | tf_op jit(solution)/shard_map/ppermute | solution.py:415
  15.1 1.6 %collective-permute-start.5 = (bf16[2,256,256]{2,1,0:T(8,128)(2,1)S(1)}, bf16[2,256,256]{2,1,0:T(8,128)(2,1)S(1)}, u32[]{:S(2)}, u32[]{:S(2)}) collective-permute-start(bf16[2,256,256]{2,1,0:T(8,128)(2,1)S(1)} %pack_columns.3), channel_id=1, source_target_pairs={{0,1},{1,0},{2,3},{3,2},{4,5},{5,4},{6,7},{7,6},{8,9},{9,8},{10,11... | collective-permute-start | bytes 786440 | tf_op jit(solution)/shard_map/ppermute | solution.py:421
  16.7 1.6 %collective-permute-start.6 = (bf16[1,256,256]{2,1,0:T(8,128)(2,1)S(1)}, bf16[1,256,256]{2,1,0:T(8,128)(2,1)S(1)}, u32[]{:S(2)}, u32[]{:S(2)}) collective-permute-start(bf16[1,256,256]{2,1,0:T(8,128)(2,1)S(1)} %partner_columns.2), channel_id=1, source_target_pairs={{0,16},{8,24},{16,0},{24,8},{1,17},{9,25},{17,1},{25,9},{2,18},{10... | collective-permute-start | bytes 393224 | tf_op jit(solution)/shard_map/ppermute | solution.py:106
  18.3 1.5 %collective-permute-done.refs_2_.refs_1_ = bf16[2,256,256]{2,1,0:T(8,128)(2,1)S(1)} collective-permute-done((bf16[2,256,256]{2,1,0:T(8,128)(2,1)S(1)}, bf16[2,256,256]{2,1,0:T(8,128)(2,1)S(1)}, u32[]{:S(2)}, u32[]{:S(2)}) %collective-permute-start) | collective-permute-done | bytes 262176 | tf_op jit(solution)/shard_map/ppermute | solution.py:421
  20.3 1.4 %collective-permute-done.6.refs_5_.refs_1_ = bf16[1,256,256]{2,1,0:T(8,128)(2,1)S(1)} collective-permute-done((bf16[1,256,256]{2,1,0:T(8,128)(2,1)S(1)}, bf16[1,256,256]{2,1,0:T(8,128)(2,1)S(1)}, u32[]{:S(2)}, u32[]{:S(2)}) %collective-permute-start.6) | collective-permute-done | bytes 131104 | tf_op jit(solution)/shard_map/ppermute | solution.py:106
  22.8 1.1 %collective-permute-done.4.refs_0_.refs_5_ = bf16[256,512]{1,0:T(8,128)(2,1)S(1)} collective-permute-done((bf16[256,512]{1,0:T(8,128)(2,1)S(1)}, bf16[256,512]{1,0:T(8,128)(2,1)S(1)}, u32[]{:S(2)}, u32[]{:S(2)}) %collective-permute-start.4) | collective-permute-done | bytes 262176 | tf_op jit(solution)/shard_map/ppermute | solution.py:415
  23.9 1.5 %collective-permute-done.5.refs_2_ = bf16[2,256,256]{2,1,0:T(8,128)(2,1)S(1)} collective-permute-done((bf16[2,256,256]{2,1,0:T(8,128)(2,1)S(1)}, bf16[2,256,256]{2,1,0:T(8,128)(2,1)S(1)}, u32[]{:S(2)}, u32[]{:S(2)}) %collective-permute-start.5) | collective-permute-done | bytes 262176 | tf_op jit(solution)/shard_map/ppermute | solution.py:421
  26.0 0.6 %last_products.1 = (f32[256,512]{1,0:T(8,128)S(1)}, bf16[2,256,256]{2,1,0:T(8,128)(2,1)S(1)}, bf16[4,256,256]{2,1,0:T(8,128)(2,1)S(1)}) custom-call(bf16[256,2048]{1,0:T(8,128)(2,1)S(1)} %bitcast.10, bf16[256,512]{1,0:T(8,128)(2,1)S(1)} %bitcast.22, bf16[2,256,256]{2,1,0:T(8,128)(2,1)S(1)} %collective-permute-done.refs_2_.refs_1_, ...), custom_call_target="tpu_custom_call" | custom-call | flops 268435456 | bytes 3407872 | tf_op jit(solution)/shard_map/last_products/pallas_call | solution.py:48
  26.6 1.6 %collective-permute-start.7 = (bf16[4,256,256]{2,1,0:T(8,128)(2,1)S(1)}, bf16[4,256,256]{2,1,0:T(8,128)(2,1)S(1)}, u32[]{:S(2)}, u32[]{:S(2)}) collective-permute-start(bf16[4,256,256]{2,1,0:T(8,128)(2,1)S(1)} %get-tuple-element.28.refs_2_), channel_id=1, source_target_pairs={{0,1},{1,0},{2,3},{3,2},{4,5},{5,4},{6,7},{7,6},{8,9},{9,8},{10,11... | collective-permute-start | bytes 1572872 | tf_op jit(solution)/shard_map/ppermute | solution.py:421
  28.1 1.6 %collective-permute-start.8 = (bf16[256,512]{1,0:T(8,128)(2,1)S(1)}, bf16[256,512]{1,0:T(8,128)(2,1)S(1)}, u32[]{:S(2)}, u32[]{:S(2)}) collective-permute-start(bf16[256,512]{1,0:T(8,128)(2,1)S(1)} %get-tuple-element.30.refs_3_), channel_id=1, source_target_pairs={{2,0},{3,1},{0,4},{1,5},{4,6},{5,7},{6,2},{7,3},{10,8},{11,9},{8,1... | collective-permute-start | bytes 786440 | tf_op jit(solution)/shard_map/ppermute | solution.py:415
  30.3 1.2 %collective-permute-done.10.refs_3_.early_ref = bf16[2,256,256]{2,1,0:T(8,128)(2,1)S(1)} collective-permute-done((bf16[2,256,256]{2,1,0:T(8,128)(2,1)S(1)}, bf16[2,256,256]{2,1,0:T(8,128)(2,1)S(1)}, u32[]{:S(2)}, u32[]{:S(2)}) %collective-permute-start.10) | collective-permute-done | bytes 262176 | tf_op jit(solution)/shard_map/ppermute | solution.py:421
  31.6 0.8 %copy-done.4 = bf16[256,512]{1,0:T(8,128)(2,1)S(1)} copy-done((bf16[256,512]{1,0:T(8,128)(2,1)S(1)}, bf16[256,512]{1,0:T(8,128)(2,1)}, u32[]{:S(2)}) %copy-start.4) | copy-done | bytes 262168
  32.5 1.1 %outer_update.1 = (bf16[256,128]{1,0:T(8,128)(2,1)S(1)}, f32[256,128]{1,0:T(8,128)}) custom-call(bf16[256,512]{1,0:T(8,128)(2,1)S(1)} %bitcast.18, bf16[1,256,256]{2,1,0:T(8,128)(2,1)S(1)} %collective-permute-done.6.refs_5_.refs_1_, bf16[2,256,128]{2,1,0:T(8,128)(2,1)S(1)} %collective-permute-done.12.refs_2_, bf16[256,512]{1,0:T(8,128)(2,1)S(1)} %copy-done.4, ...), custom_call_target="tpu_custom_call" | custom-call | bytes 917504 | tf_op jit(solution)/shard_map/outer_update/pallas_call | solution.py:48
  33.5 1.5 %collective-permute-start.13 = (bf16[256,128]{1,0:T(8,128)(2,1)S(1)}, bf16[256,128]{1,0:T(8,128)(2,1)S(1)}, u32[]{:S(2)}, u32[]{:S(2)}) collective-permute-start(bf16[256,128]{1,0:T(8,128)(2,1)S(1)} %get-tuple-element.38.refs_0_), channel_id=1, source_target_pairs={{0,16},{8,24},{16,0},{24,8},{1,17},{9,25},{17,1},{25,9},{2,18},{10... | collective-permute-start | bytes 196616 | tf_op jit(solution)/shard_map/ppermute | solution.py:106
  35.1 0.7 %collective-permute-done.8.up_ref.refs_2_ = bf16[256,512]{1,0:T(8,128)(2,1)S(1)} collective-permute-done((bf16[256,512]{1,0:T(8,128)(2,1)S(1)}, bf16[256,512]{1,0:T(8,128)(2,1)S(1)}, u32[]{:S(2)}, u32[]{:S(2)}) %collective-permute-start.8) | collective-permute-done | bytes 262176 | tf_op jit(solution)/shard_map/ppermute | solution.py:415
  35.8 2.0 %collective-permute-done.13.refs_1_ = bf16[256,128]{1,0:T(8,128)(2,1)S(1)} collective-permute-done((bf16[256,128]{1,0:T(8,128)(2,1)S(1)}, bf16[256,128]{1,0:T(8,128)(2,1)S(1)}, u32[]{:S(2)}, u32[]{:S(2)}) %collective-permute-start.13) | collective-permute-done | bytes 65568 | tf_op jit(solution)/shard_map/ppermute | solution.py:106
  37.9 0.9 %collect.1 = (bf16[256,2048]{1,0:T(8,128)(2,1)}, f32[8,128]{1,0:T(8,128)S(1)}) custom-call(bf16[2,256,256]{2,1,0:T(8,128)(2,1)S(1)} %get-tuple-element.32.near_ref, bf16[2,256,256]{2,1,0:T(8,128)(2,1)S(1)} %get-tuple-element.33.last_ref, bf16[2,256,256]{2,1,0:T(8,128)(2,1)S(1)} %collective-permute-done.10.refs_3_.early_ref), custom_call_target="tpu_custom_call" | custom-call | bytes 1048576 | tf_op jit(solution)/shard_map/collect/pallas_call | solution.py:355
  39.3 0.8 %join_shares.1 = bf16[256,512]{1,0:T(8,128)(2,1)} custom-call(bf16[256,256]{1,0:T(8,128)(2,1)S(1)} %beside.1.refs_0_, bf16[256,256]{1,0:T(8,128)(2,1)S(1)} %collective-permute-done.14.refs_1_, f32[8,128]{1,0:T(8,128)S(1)} %get-tuple-element.39.refs_2_), custom_call_target="tpu_custom_call" | custom-call | bytes 262144 | tf_op jit(solution)/shard_map/join_shares/pallas_call | solution.py:48
  40.0 1.5 %collective-permute-done.11.down_ref = bf16[256,512]{1,0:T(8,128)(2,1)S(1)} collective-permute-done((bf16[256,512]{1,0:T(8,128)(2,1)S(1)}, bf16[256,512]{1,0:T(8,128)(2,1)S(1)}, u32[]{:S(2)}, u32[]{:S(2)}) %collective-permute-start.11) | collective-permute-done | bytes 262176 | tf_op jit(solution)/shard_map/ppermute | solution.py:418
  41.5 0.9 %finish.1 = (bf16[256,512]{1,0:T(8,128)(2,1)}, bf16[256,2048]{1,0:T(8,128)(2,1)}, bf16[256,512]{1,0:T(8,128)(2,1)}) custom-call(f32[256,512]{1,0:T(8,128)S(1)} %get-tuple-element.27.total_ref, bf16[4,256,256]{2,1,0:T(8,128)(2,1)S(1)} %collective-permute-done.7.late_ref, f32[256,512]{1,0:T(8,128)S(1)} %get-tuple-element.29.terms_ref, ...), custom_call_target="tpu_custom_call", output_to_operand_aliasing={{1}: (5, {})} | custom-call | bytes 1048576 | tf_op jit(solution)/shard_map/finish/pallas_call | solution.py:386
  (35 shorter events, 4.3 us)
Async XLA Ops:
  0.6 11.1 %collective-permute-start.3 = (bf16[256,512]{1,0:T(8,128)(2,1)}, bf16[256,512]{1,0:T(8,128)(2,1)S(1)}, u32[]{:S(2)}, u32[]{:S(2)}) collective-permute-start(bf16[256,512]{1,0:T(8,128)(2,1)} %bitcast.12), channel_id=1, source_target_pairs={{2,0},{3,1},{0,4},{1,5},{4,6},{5,7},{6,2},{7,3},{10,8},{11,9},{8,1... | collective-permute-start | bytes 786440 | tf_op jit(solution)/shard_map/ppermute | solution.py:415
  4.7 10.3 %collective-permute-start.1 = (bf16[256,512]{1,0:T(8,128)(2,1)}, bf16[256,512]{1,0:T(8,128)(2,1)S(1)}, u32[]{:S(2)}, u32[]{:S(2)}) collective-permute-start(bf16[256,512]{1,0:T(8,128)(2,1)} %bitcast.19), channel_id=1, source_target_pairs={{0,1},{1,0},{2,3},{3,2},{4,5},{5,4},{6,7},{7,6},{8,9},{9,8},{10,11... | collective-permute-start | bytes 786440 | tf_op jit(solution)/shard_map/ppermute | solution.py:421
  6.2 1.2 %copy-start = (bf16[1,256,2048]{2,1,0:T(8,128)(2,1)S(1)}, bf16[1,256,2048]{2,1,0:T(8,128)(2,1)}, u32[]{:S(2)}) copy-start(bf16[1,256,2048]{2,1,0:T(8,128)(2,1)} %param.8) | copy-start | bytes 3145732
  7.4 0.9 %copy-start.2 = (bf16[1,256,512]{2,1,0:T(8,128)(2,1)S(1)}, bf16[1,256,512]{2,1,0:T(8,128)(2,1)}, u32[]{:S(2)}) copy-start(bf16[1,256,512]{2,1,0:T(8,128)(2,1)} %param.5) | copy-start | bytes 786436
  7.4 7.6 %copy-start.1 = (bf16[1,256,2048]{2,1,0:T(8,128)(2,1)S(1)}, bf16[1,256,2048]{2,1,0:T(8,128)(2,1)}, u32[]{:S(2)}) copy-start(bf16[1,256,2048]{2,1,0:T(8,128)(2,1)} %param.8) | copy-start | bytes 3145732
  7.5 12.3 %collective-permute-start = (bf16[2,256,256]{2,1,0:T(8,128)(2,1)S(1)}, bf16[2,256,256]{2,1,0:T(8,128)(2,1)S(1)}, u32[]{:S(2)}, u32[]{:S(2)}) collective-permute-start(bf16[2,256,256]{2,1,0:T(8,128)(2,1)S(1)} %pack_columns.2.refs_1_), channel_id=1, source_target_pairs={{0,1},{1,0},{2,3},{3,2},{4,5},{5,4},{6,7},{7,6},{8,9},{9,8},{10,11... | collective-permute-start | bytes 786440 | tf_op jit(solution)/shard_map/ppermute | solution.py:421
  8.4 15.5 %collective-permute-start.2 = (bf16[256,512]{1,0:T(8,128)(2,1)S(1)}, bf16[256,512]{1,0:T(8,128)(2,1)S(1)}, u32[]{:S(2)}, u32[]{:S(2)}) collective-permute-start(bf16[256,512]{1,0:T(8,128)(2,1)S(1)} %bitcast.13), channel_id=1, source_target_pairs={{0,2},{1,3},{4,0},{5,1},{6,4},{7,5},{2,6},{3,7},{8,10},{9,11},{12,... | collective-permute-start | bytes 786440 | tf_op jit(solution)/shard_map/ppermute | solution.py:418
  11.7 12.1 %collective-permute-start.4 = (bf16[256,512]{1,0:T(8,128)(2,1)S(1)}, bf16[256,512]{1,0:T(8,128)(2,1)S(1)}, u32[]{:S(2)}, u32[]{:S(2)}) collective-permute-start(bf16[256,512]{1,0:T(8,128)(2,1)S(1)} %collective-permute-done.3.refs_0_.refs_3_.refs_4_), channel_id=1, source_target_pairs={{2,0},{3,1},{0,4},{1,5},{4,6},{5,7},{6,2},{7,3},{10,8},{11,9},{8,1... | collective-permute-start | bytes 786440 | tf_op jit(solution)/shard_map/ppermute | solution.py:415
  15.1 4.7 %copy-start.3 = (bf16[1,256,512]{2,1,0:T(8,128)(2,1)S(1)}, bf16[1,256,512]{2,1,0:T(8,128)(2,1)}, u32[]{:S(2)}) copy-start(bf16[1,256,512]{2,1,0:T(8,128)(2,1)} %param.9) | copy-start | bytes 786436
  15.1 10.3 %collective-permute-start.5 = (bf16[2,256,256]{2,1,0:T(8,128)(2,1)S(1)}, bf16[2,256,256]{2,1,0:T(8,128)(2,1)S(1)}, u32[]{:S(2)}, u32[]{:S(2)}) collective-permute-start(bf16[2,256,256]{2,1,0:T(8,128)(2,1)S(1)} %pack_columns.3), channel_id=1, source_target_pairs={{0,1},{1,0},{2,3},{3,2},{4,5},{5,4},{6,7},{7,6},{8,9},{9,8},{10,11... | collective-permute-start | bytes 786440 | tf_op jit(solution)/shard_map/ppermute | solution.py:421
  16.7 5.0 %collective-permute-start.6 = (bf16[1,256,256]{2,1,0:T(8,128)(2,1)S(1)}, bf16[1,256,256]{2,1,0:T(8,128)(2,1)S(1)}, u32[]{:S(2)}, u32[]{:S(2)}) collective-permute-start(bf16[1,256,256]{2,1,0:T(8,128)(2,1)S(1)} %partner_columns.2), channel_id=1, source_target_pairs={{0,16},{8,24},{16,0},{24,8},{1,17},{9,25},{17,1},{25,9},{2,18},{10... | collective-permute-start | bytes 393224 | tf_op jit(solution)/shard_map/ppermute | solution.py:106
  20.2 11.2 %collective-permute-start.9 = (bf16[256,512]{1,0:T(8,128)(2,1)S(1)}, bf16[256,512]{1,0:T(8,128)(2,1)S(1)}, u32[]{:S(2)}, u32[]{:S(2)}) collective-permute-start(bf16[256,512]{1,0:T(8,128)(2,1)S(1)} %get-tuple-element.23.refs_4_.refs_2_), channel_id=1, source_target_pairs={{0,2},{1,3},{4,0},{5,1},{6,4},{7,5},{2,6},{3,7},{8,10},{9,11},{12,... | collective-permute-start | bytes 786440 | tf_op jit(solution)/shard_map/ppermute | solution.py:418
  22.2 9.3 %collective-permute-start.10 = (bf16[2,256,256]{2,1,0:T(8,128)(2,1)S(1)}, bf16[2,256,256]{2,1,0:T(8,128)(2,1)S(1)}, u32[]{:S(2)}, u32[]{:S(2)}) collective-permute-start(bf16[2,256,256]{2,1,0:T(8,128)(2,1)S(1)} %get-tuple-element.24.refs_6_.refs_4_), channel_id=1, source_target_pairs={{0,1},{1,0},{2,3},{3,2},{4,5},{5,4},{6,7},{7,6},{8,9},{9,8},{10,11... | collective-permute-start | bytes 786440 | tf_op jit(solution)/shard_map/ppermute | solution.py:421
  26.6 14.9 %collective-permute-start.7 = (bf16[4,256,256]{2,1,0:T(8,128)(2,1)S(1)}, bf16[4,256,256]{2,1,0:T(8,128)(2,1)S(1)}, u32[]{:S(2)}, u32[]{:S(2)}) collective-permute-start(bf16[4,256,256]{2,1,0:T(8,128)(2,1)S(1)} %get-tuple-element.28.refs_2_), channel_id=1, source_target_pairs={{0,1},{1,0},{2,3},{3,2},{4,5},{5,4},{6,7},{7,6},{8,9},{9,8},{10,11... | collective-permute-start | bytes 1572872 | tf_op jit(solution)/shard_map/ppermute | solution.py:421
  28.1 7.6 %collective-permute-start.8 = (bf16[256,512]{1,0:T(8,128)(2,1)S(1)}, bf16[256,512]{1,0:T(8,128)(2,1)S(1)}, u32[]{:S(2)}, u32[]{:S(2)}) collective-permute-start(bf16[256,512]{1,0:T(8,128)(2,1)S(1)} %get-tuple-element.30.refs_3_), channel_id=1, source_target_pairs={{2,0},{3,1},{0,4},{1,5},{4,6},{5,7},{6,2},{7,3},{10,8},{11,9},{8,1... | collective-permute-start | bytes 786440 | tf_op jit(solution)/shard_map/ppermute | solution.py:415
  29.8 1.9 %collective-permute-start.12 = (bf16[2,256,128]{2,1,0:T(8,128)(2,1)S(1)}, bf16[2,256,128]{2,1,0:T(8,128)(2,1)S(1)}, u32[]{:S(2)}, u32[]{:S(2)}) collective-permute-start(bf16[2,256,128]{2,1,0:T(8,128)(2,1)S(1)} %partner_columns.3), channel_id=1, source_target_pairs={{0,8},{8,0},{16,24},{24,16},{1,9},{9,1},{17,25},{25,17},{2,10},{10... | collective-permute-start | bytes 393224 | tf_op jit(solution)/shard_map/ppermute | solution.py:106
  31.5 1.0 %copy-start.4 = (bf16[256,512]{1,0:T(8,128)(2,1)S(1)}, bf16[256,512]{1,0:T(8,128)(2,1)}, u32[]{:S(2)}) copy-start(bf16[256,512]{1,0:T(8,128)(2,1)} %refs_3_.1) | copy-start | bytes 786436
  31.5 1.0 %copy-start.5 = (f32[256,128]{1,0:T(8,128)S(1)}, f32[256,128]{1,0:T(8,128)}, u32[]{:S(2)}) copy-start(f32[256,128]{1,0:T(8,128)} %refs_4_.1) | copy-start | bytes 393220
  31.5 9.9 %collective-permute-start.11 = (bf16[256,512]{1,0:T(8,128)(2,1)S(1)}, bf16[256,512]{1,0:T(8,128)(2,1)S(1)}, u32[]{:S(2)}, u32[]{:S(2)}) collective-permute-start(bf16[256,512]{1,0:T(8,128)(2,1)S(1)} %add_terms.1.refs_5_), channel_id=1, source_target_pairs={{0,2},{1,3},{4,0},{5,1},{6,4},{7,5},{2,6},{3,7},{8,10},{9,11},{12,... | collective-permute-start | bytes 786440 | tf_op jit(solution)/shard_map/ppermute | solution.py:418
  33.5 4.3 %collective-permute-start.13 = (bf16[256,128]{1,0:T(8,128)(2,1)S(1)}, bf16[256,128]{1,0:T(8,128)(2,1)S(1)}, u32[]{:S(2)}, u32[]{:S(2)}) collective-permute-start(bf16[256,128]{1,0:T(8,128)(2,1)S(1)} %get-tuple-element.38.refs_0_), channel_id=1, source_target_pairs={{0,16},{8,24},{16,0},{24,8},{1,17},{9,25},{17,1},{25,9},{2,18},{10... | collective-permute-start | bytes 196616 | tf_op jit(solution)/shard_map/ppermute | solution.py:106
  37.8 1.4 %collective-permute-start.14 = (bf16[256,256]{1,0:T(8,128)(2,1)S(1)}, bf16[256,256]{1,0:T(8,128)(2,1)S(1)}, u32[]{:S(2)}, u32[]{:S(2)}) collective-permute-start(bf16[256,256]{1,0:T(8,128)(2,1)S(1)} %beside.1.refs_0_), channel_id=1, source_target_pairs={{0,8},{8,0},{16,24},{24,16},{1,9},{9,1},{17,25},{25,17},{2,10},{10... | collective-permute-start | bytes 393224 | tf_op jit(solution)/shard_map/ppermute | solution.py:106

commit v17 on v16

--- a/solution.py
+++ b/solution.py
@@ -444,16 +444,16 @@
         inputs_here, cotangent, partner_inputs, partner_cotangent, late_blocks, totals, size, ()
     )
     late = across(leaving)
+    new_share, new_momentum = update_share(held, global_weights, momentum, (leaving,))
     total_down = vmem_call(
-        add_kernel, shape_of(depth, kv_width, BF16), [terms[0], sum_down], 0, "add_terms", (leaving, early)
+        add_kernel, shape_of(depth, kv_width, BF16), [terms[0], sum_down], 0, "add_terms", (new_share, early, sum_up)
     )
     sum_down = downward(total_down)
-    new_share, new_momentum = update_share(held, global_weights, momentum, (total_down,))
     bits = lax.axis_size("replica")
     shares, joined = [new_share], [0]
     while bits > 1:
         bits //= 2
-        shares = [shares[0] if len(shares) == 1 else beside(*shares, (sum_up,))]
+        shares = [shares[0] if len(shares) == 1 else beside(*shares, ())]
         shares.append(swap(shares[0], bits))
         joined += [place ^ bits for place in joined]
     grad, mark = collect([near, last, early], width, size, list(early_blocks), list(late_blocks))

time: 42.6 us -> 47.6 us (1.12)
  waiting for transfers between devices: 14.7 us -> 18.7 us
  starting transfers between devices: 18.1 us -> 20.2 us
  local copies, waits for them, and re-layouts: 2.4 us -> 1.25 us
    ppermute x3, waiting for transfers between devices: 1.48 us -> 9.05 us  [downward(): lax.ppermute(array, 'fsdp', [(target, source) for source, target in pairs])]
    ppermute x3, waiting for transfers between devices: 5.17 us -> 2.53 us  [upward(): return lax.ppermute(array, 'fsdp', pairs)]
    ppermute x5, waiting for transfers between devices: 4.23 us -> 2.69 us  [across(): return lax.ppermute(array, 'fsdp', [(at, at ^ 1) for at in range(size)])]
    ppermute x3, starting transfers between devices: 0.12 us -> 1.36 us  [downward(): lax.ppermute(array, 'fsdp', [(target, source) for source, target in pairs])]
    unnamed x12, local copies, waits for them, and re-layouts: 2.4 us -> 1.25 us
    ppermute x5, starting transfers between devices: 5.8 us -> 6.63 us  [across(): return lax.ppermute(array, 'fsdp', [(at, at ^ 1) for at in range(size)])]
    ppermute x4, waiting for transfers between devices: 3.83 us -> 4.47 us  [swap(): lax.ppermute(array, 'replica', [(at, at ^ bits) for at in range(lax.axis_...]
  transfers between devices with their start and end apart: 15 -> 15, of which waited for: 10 -> 9; matrix products, arithmetic and copies ran while one was open for 0% -> 0% of each run, Pallas kernels for 13% -> 12%
where the time goes in v17:
time: 47.6 us; the launch traced here: 47.4 us
  starting transfers between devices  20.2 us (42%)
  waiting for transfers between devices  18.7 us (39%)
  Pallas kernels  6.44 us (14%)
  local copies, waits for them, and re-layouts  1.25 us (3%)
  between operations  0.77 us (2%)
    ppermute x3, waiting for transfers between devices, downward(): lax.ppermute(array, 'fsdp', [(target, source) for source, target in pairs])  9.05 us
    ppermute x3, starting transfers between devices, upward(): return lax.ppermute(array, 'fsdp', pairs)  8.99 us
    ppermute x5, starting transfers between devices, across(): return lax.ppermute(array, 'fsdp', [(at, at ^ 1) for at in range(size)])  6.63 us
    pallas_call x15, Pallas kernels, vmem_call(): pl.pallas_call(body, out_shape=out_shape, in_specs=[whole] * len(operands...  4.57 us
    ppermute x4, waiting for transfers between devices, swap(): lax.ppermute(array, 'replica', [(at, at ^ bits) for at in range(lax.axis_...  4.47 us
    ppermute x4, starting transfers between devices, swap(): lax.ppermute(array, 'replica', [(at, at ^ bits) for at in range(lax.axis_...  3.25 us
    ppermute x5, waiting for transfers between devices, across(): return lax.ppermute(array, 'fsdp', [(at, at ^ 1) for at in range(size)])  2.69 us
    ppermute x3, waiting for transfers between devices, upward(): return lax.ppermute(array, 'fsdp', pairs)  2.53 us
  transfers between devices with their start and end apart: 15, of which 9 were waited for; matrix products, arithmetic and copies ran while one was open for 0% of the time, Pallas kernels for 12%

profile of v17, /device:TPU:0, one launch (start us, length us, event | category | flops | bytes accessed | tf_op | source)
XLA Modules:
  0.0 47.4 jit_solution(4413453303116658144)
XLA Ops:
  0.6 4.1 %collective-permute-start.3 = (bf16[256,512]{1,0:T(8,128)(2,1)}, bf16[256,512]{1,0:T(8,128)(2,1)S(1)}, u32[]{:S(2)}, u32[]{:S(2)}) collective-permute-start(bf16[256,512]{1,0:T(8,128)(2,1)} %bitcast.12), channel_id=1, source_target_pairs={{2,0},{3,1},{0,4},{1,5},{4,6},{5,7},{6,2},{7,3},{10,8},{11,9},{8,1... | collective-permute-start | bytes 786440 | tf_op jit(solution)/shard_map/ppermute | solution.py:415
  4.7 1.5 %collective-permute-start.1 = (bf16[256,512]{1,0:T(8,128)(2,1)}, bf16[256,512]{1,0:T(8,128)(2,1)S(1)}, u32[]{:S(2)}, u32[]{:S(2)}) collective-permute-start(bf16[256,512]{1,0:T(8,128)(2,1)} %bitcast.19), channel_id=1, source_target_pairs={{0,1},{1,0},{2,3},{3,2},{4,5},{5,4},{6,7},{7,6},{8,9},{9,8},{10,11... | collective-permute-start | bytes 786440 | tf_op jit(solution)/shard_map/ppermute | solution.py:421
  6.2 1.2 %copy-done = bf16[1,256,2048]{2,1,0:T(8,128)(2,1)S(1)} copy-done((bf16[1,256,2048]{2,1,0:T(8,128)(2,1)S(1)}, bf16[1,256,2048]{2,1,0:T(8,128)(2,1)}, u32[]{:S(2)}) %copy-start) | copy-done | bytes 1048600
  7.5 0.6 %collective-permute-start = (bf16[2,256,256]{2,1,0:T(8,128)(2,1)S(1)}, bf16[2,256,256]{2,1,0:T(8,128)(2,1)S(1)}, u32[]{:S(2)}, u32[]{:S(2)}) collective-permute-start(bf16[2,256,256]{2,1,0:T(8,128)(2,1)S(1)} %pack_columns.2.refs_1_), channel_id=1, source_target_pairs={{0,1},{1,0},{2,3},{3,2},{4,5},{5,4},{6,7},{7,6},{8,9},{9,8},{10,11... | collective-permute-start | bytes 786440 | tf_op jit(solution)/shard_map/ppermute | solution.py:421
  8.1 2.5 %collective-permute-done.3.refs_0_.refs_3_.refs_4_ = bf16[256,512]{1,0:T(8,128)(2,1)S(1)} collective-permute-done((bf16[256,512]{1,0:T(8,128)(2,1)}, bf16[256,512]{1,0:T(8,128)(2,1)S(1)}, u32[]{:S(2)}, u32[]{:S(2)}) %collective-permute-start.3) | collective-permute-done | bytes 262176 | tf_op jit(solution)/shard_map/ppermute | solution.py:415
  10.6 3.3 %collective-permute-start.4 = (bf16[256,512]{1,0:T(8,128)(2,1)S(1)}, bf16[256,512]{1,0:T(8,128)(2,1)S(1)}, u32[]{:S(2)}, u32[]{:S(2)}) collective-permute-start(bf16[256,512]{1,0:T(8,128)(2,1)S(1)} %collective-permute-done.3.refs_0_.refs_3_.refs_4_), channel_id=1, source_target_pairs={{2,0},{3,1},{0,4},{1,5},{4,6},{5,7},{6,2},{7,3},{10,8},{11,9},{8,1... | collective-permute-start | bytes 786440 | tf_op jit(solution)/shard_map/ppermute | solution.py:415
  14.2 1.6 %collective-permute-start.5 = (bf16[2,256,256]{2,1,0:T(8,128)(2,1)S(1)}, bf16[2,256,256]{2,1,0:T(8,128)(2,1)S(1)}, u32[]{:S(2)}, u32[]{:S(2)}) collective-permute-start(bf16[2,256,256]{2,1,0:T(8,128)(2,1)S(1)} %pack_columns.3), channel_id=1, source_target_pairs={{0,1},{1,0},{2,3},{3,2},{4,5},{5,4},{6,7},{7,6},{8,9},{9,8},{10,11... | collective-permute-start | bytes 786440 | tf_op jit(solution)/shard_map/ppermute | solution.py:421
  15.8 1.6 %collective-permute-start.6 = (bf16[1,256,256]{2,1,0:T(8,128)(2,1)S(1)}, bf16[1,256,256]{2,1,0:T(8,128)(2,1)S(1)}, u32[]{:S(2)}, u32[]{:S(2)}) collective-permute-start(bf16[1,256,256]{2,1,0:T(8,128)(2,1)S(1)} %partner_columns.2), channel_id=1, source_target_pairs={{0,16},{8,24},{16,0},{24,8},{1,17},{9,25},{17,1},{25,9},{2,18},{10... | collective-permute-start | bytes 393224 | tf_op jit(solution)/shard_map/ppermute | solution.py:106
  17.4 2.4 %collective-permute-done.refs_2_.refs_1_ = bf16[2,256,256]{2,1,0:T(8,128)(2,1)S(1)} collective-permute-done((bf16[2,256,256]{2,1,0:T(8,128)(2,1)S(1)}, bf16[2,256,256]{2,1,0:T(8,128)(2,1)S(1)}, u32[]{:S(2)}, u32[]{:S(2)}) %collective-permute-start) | collective-permute-done | bytes 262176 | tf_op jit(solution)/shard_map/ppermute | solution.py:421
  20.2 1.6 %collective-permute-start.8 = (bf16[256,512]{1,0:T(8,128)(2,1)S(1)}, bf16[256,512]{1,0:T(8,128)(2,1)S(1)}, u32[]{:S(2)}, u32[]{:S(2)}) collective-permute-start(bf16[256,512]{1,0:T(8,128)(2,1)S(1)} %get-tuple-element.30.refs_3_), channel_id=1, source_target_pairs={{2,0},{3,1},{0,4},{1,5},{4,6},{5,7},{6,2},{7,3},{10,8},{11,9},{8,1... | collective-permute-start | bytes 786440 | tf_op jit(solution)/shard_map/ppermute | solution.py:415
  23.0 1.4 %collective-permute-start.11 = (bf16[2,256,256]{2,1,0:T(8,128)(2,1)S(1)}, bf16[2,256,256]{2,1,0:T(8,128)(2,1)S(1)}, u32[]{:S(2)}, u32[]{:S(2)}) collective-permute-start(bf16[2,256,256]{2,1,0:T(8,128)(2,1)S(1)} %get-tuple-element.24.refs_6_.refs_4_), channel_id=1, source_target_pairs={{0,1},{1,0},{2,3},{3,2},{4,5},{5,4},{6,7},{7,6},{8,9},{9,8},{10,11... | collective-permute-start | bytes 786440 | tf_op jit(solution)/shard_map/ppermute | solution.py:421
  24.4 3.8 %collective-permute-done.2.refs_5_.refs_4_ = bf16[256,512]{1,0:T(8,128)(2,1)S(1)} collective-permute-done((bf16[256,512]{1,0:T(8,128)(2,1)S(1)}, bf16[256,512]{1,0:T(8,128)(2,1)S(1)}, u32[]{:S(2)}, u32[]{:S(2)}) %collective-permute-start.2) | collective-permute-done | bytes 262176 | tf_op jit(solution)/shard_map/ppermute | solution.py:418
  28.8 0.6 %last_products.1 = (f32[256,512]{1,0:T(8,128)S(1)}, bf16[2,256,256]{2,1,0:T(8,128)(2,1)S(1)}, bf16[4,256,256]{2,1,0:T(8,128)(2,1)S(1)}) custom-call(bf16[256,2048]{1,0:T(8,128)(2,1)S(1)} %bitcast.10, bf16[256,512]{1,0:T(8,128)(2,1)S(1)} %bitcast.22, bf16[2,256,256]{2,1,0:T(8,128)(2,1)S(1)} %collective-permute-done.refs_2_.refs_1_, ...), custom_call_target="tpu_custom_call" | custom-call | flops 268435456 | bytes 3407872 | tf_op jit(solution)/shard_map/last_products/pallas_call | solution.py:48
  29.4 1.6 %collective-permute-start.7 = (bf16[4,256,256]{2,1,0:T(8,128)(2,1)S(1)}, bf16[4,256,256]{2,1,0:T(8,128)(2,1)S(1)}, u32[]{:S(2)}, u32[]{:S(2)}) collective-permute-start(bf16[4,256,256]{2,1,0:T(8,128)(2,1)S(1)} %get-tuple-element.28.refs_5_), channel_id=1, source_target_pairs={{0,1},{1,0},{2,3},{3,2},{4,5},{5,4},{6,7},{7,6},{8,9},{9,8},{10,11... | collective-permute-start | bytes 1572872 | tf_op jit(solution)/shard_map/ppermute | solution.py:421
  31.1 1.3 %collective-permute-done.10.refs_2_ = bf16[2,256,128]{2,1,0:T(8,128)(2,1)S(1)} collective-permute-done((bf16[2,256,128]{2,1,0:T(8,128)(2,1)S(1)}, bf16[2,256,128]{2,1,0:T(8,128)(2,1)S(1)}, u32[]{:S(2)}, u32[]{:S(2)}) %collective-permute-start.10) | collective-permute-done | bytes 131104 | tf_op jit(solution)/shard_map/ppermute | solution.py:106
  32.4 1.1 %outer_update.1 = (bf16[256,128]{1,0:T(8,128)(2,1)S(1)}, f32[256,128]{1,0:T(8,128)}) custom-call(bf16[256,512]{1,0:T(8,128)(2,1)S(1)} %bitcast.18, bf16[1,256,256]{2,1,0:T(8,128)(2,1)S(1)} %collective-permute-done.6.refs_5_.refs_1_, bf16[2,256,128]{2,1,0:T(8,128)(2,1)S(1)} %collective-permute-done.10.refs_2_, bf16[256,512]{1,0:T(8,128)(2,1)S(1)} %copy-done.4, ...), custom_call_target="tpu_custom_call" | custom-call | bytes 917504 | tf_op jit(solution)/shard_map/outer_update/pallas_call | solution.py:48
  34.0 3.3 %collective-permute-done.9.refs_1_ = bf16[256,512]{1,0:T(8,128)(2,1)S(1)} collective-permute-done((bf16[256,512]{1,0:T(8,128)(2,1)S(1)}, bf16[256,512]{1,0:T(8,128)(2,1)S(1)}, u32[]{:S(2)}, u32[]{:S(2)}) %collective-permute-start.9) | collective-permute-done | bytes 262176 | tf_op jit(solution)/shard_map/ppermute | solution.py:418
  37.3 0.8 %collective-permute-start.12 = (bf16[256,512]{1,0:T(8,128)(2,1)S(1)}, bf16[256,512]{1,0:T(8,128)(2,1)S(1)}, u32[]{:S(2)}, u32[]{:S(2)}) collective-permute-start(bf16[256,512]{1,0:T(8,128)(2,1)S(1)} %add_terms.1), channel_id=1, source_target_pairs={{0,2},{1,3},{4,0},{5,1},{6,4},{7,5},{2,6},{3,7},{8,10},{9,11},{12,... | collective-permute-start | bytes 786440 | tf_op jit(solution)/shard_map/ppermute | solution.py:418
  38.1 1.5 %collective-permute-start.13 = (bf16[256,128]{1,0:T(8,128)(2,1)S(1)}, bf16[256,128]{1,0:T(8,128)(2,1)S(1)}, u32[]{:S(2)}, u32[]{:S(2)}) collective-permute-start(bf16[256,128]{1,0:T(8,128)(2,1)S(1)} %get-tuple-element.32.refs_2_.refs_0_), channel_id=1, source_target_pairs={{0,16},{8,24},{16,0},{24,8},{1,17},{9,25},{17,1},{25,9},{2,18},{10... | collective-permute-start | bytes 196616 | tf_op jit(solution)/shard_map/ppermute | solution.py:106
  39.6 2.7 %collective-permute-done.13.refs_1_ = bf16[256,128]{1,0:T(8,128)(2,1)S(1)} collective-permute-done((bf16[256,128]{1,0:T(8,128)(2,1)S(1)}, bf16[256,128]{1,0:T(8,128)(2,1)S(1)}, u32[]{:S(2)}, u32[]{:S(2)}) %collective-permute-start.13) | collective-permute-done | bytes 65568 | tf_op jit(solution)/shard_map/ppermute | solution.py:106
  42.5 0.9 %collect.1 = (bf16[256,2048]{1,0:T(8,128)(2,1)}, f32[8,128]{1,0:T(8,128)S(1)}) custom-call(bf16[2,256,256]{2,1,0:T(8,128)(2,1)S(1)} %get-tuple-element.33.near_ref, bf16[2,256,256]{2,1,0:T(8,128)(2,1)S(1)} %get-tuple-element.34.last_ref, bf16[2,256,256]{2,1,0:T(8,128)(2,1)S(1)} %collective-permute-done.11.refs_3_.early_ref), custom_call_target="tpu_custom_call" | custom-call | bytes 1048576 | tf_op jit(solution)/shard_map/collect/pallas_call | solution.py:355
  43.8 0.8 %join_shares.1 = bf16[256,512]{1,0:T(8,128)(2,1)} custom-call(bf16[256,256]{1,0:T(8,128)(2,1)S(1)} %beside.1.refs_0_, bf16[256,256]{1,0:T(8,128)(2,1)S(1)} %collective-permute-done.14.refs_1_, f32[8,128]{1,0:T(8,128)S(1)} %get-tuple-element.39.refs_2_), custom_call_target="tpu_custom_call" | custom-call | bytes 262144 | tf_op jit(solution)/shard_map/join_shares/pallas_call | solution.py:48
  44.6 1.9 %collective-permute-done.12.down_ref = bf16[256,512]{1,0:T(8,128)(2,1)S(1)} collective-permute-done((bf16[256,512]{1,0:T(8,128)(2,1)S(1)}, bf16[256,512]{1,0:T(8,128)(2,1)S(1)}, u32[]{:S(2)}, u32[]{:S(2)}) %collective-permute-start.12) | collective-permute-done | bytes 262176 | tf_op jit(solution)/shard_map/ppermute | solution.py:418
  46.5 0.9 %finish.1 = (bf16[256,512]{1,0:T(8,128)(2,1)}, bf16[256,2048]{1,0:T(8,128)(2,1)}, bf16[256,512]{1,0:T(8,128)(2,1)}) custom-call(f32[256,512]{1,0:T(8,128)S(1)} %get-tuple-element.27.total_ref, bf16[4,256,256]{2,1,0:T(8,128)(2,1)S(1)} %collective-permute-done.7.late_ref, f32[256,512]{1,0:T(8,128)S(1)} %get-tuple-element.29.terms_ref, ...), custom_call_target="tpu_custom_call", output_to_operand_aliasing={{1}: (5, {})} | custom-call | bytes 1048576 | tf_op jit(solution)/shard_map/finish/pallas_call | solution.py:386
  (35 shorter events, 3.6 us)
Async XLA Ops:
  0.6 10.0 %collective-permute-start.3 = (bf16[256,512]{1,0:T(8,128)(2,1)}, bf16[256,512]{1,0:T(8,128)(2,1)S(1)}, u32[]{:S(2)}, u32[]{:S(2)}) collective-permute-start(bf16[256,512]{1,0:T(8,128)(2,1)} %bitcast.12), channel_id=1, source_target_pairs={{2,0},{3,1},{0,4},{1,5},{4,6},{5,7},{6,2},{7,3},{10,8},{11,9},{8,1... | collective-permute-start | bytes 786440 | tf_op jit(solution)/shard_map/ppermute | solution.py:415
  4.7 9.4 %collective-permute-start.1 = (bf16[256,512]{1,0:T(8,128)(2,1)}, bf16[256,512]{1,0:T(8,128)(2,1)S(1)}, u32[]{:S(2)}, u32[]{:S(2)}) collective-permute-start(bf16[256,512]{1,0:T(8,128)(2,1)} %bitcast.19), channel_id=1, source_target_pairs={{0,1},{1,0},{2,3},{3,2},{4,5},{5,4},{6,7},{7,6},{8,9},{9,8},{10,11... | collective-permute-start | bytes 786440 | tf_op jit(solution)/shard_map/ppermute | solution.py:421
  6.2 1.2 %copy-start = (bf16[1,256,2048]{2,1,0:T(8,128)(2,1)S(1)}, bf16[1,256,2048]{2,1,0:T(8,128)(2,1)}, u32[]{:S(2)}) copy-start(bf16[1,256,2048]{2,1,0:T(8,128)(2,1)} %param.8) | copy-start | bytes 3145732
  7.4 6.4 %copy-start.2 = (bf16[1,256,512]{2,1,0:T(8,128)(2,1)S(1)}, bf16[1,256,512]{2,1,0:T(8,128)(2,1)}, u32[]{:S(2)}) copy-start(bf16[1,256,512]{2,1,0:T(8,128)(2,1)} %param.5) | copy-start | bytes 786436
  7.4 6.7 %copy-start.1 = (bf16[1,256,2048]{2,1,0:T(8,128)(2,1)S(1)}, bf16[1,256,2048]{2,1,0:T(8,128)(2,1)}, u32[]{:S(2)}) copy-start(bf16[1,256,2048]{2,1,0:T(8,128)(2,1)} %param.8) | copy-start | bytes 3145732
  7.5 12.3 %collective-permute-start = (bf16[2,256,256]{2,1,0:T(8,128)(2,1)S(1)}, bf16[2,256,256]{2,1,0:T(8,128)(2,1)S(1)}, u32[]{:S(2)}, u32[]{:S(2)}) collective-permute-start(bf16[2,256,256]{2,1,0:T(8,128)(2,1)S(1)} %pack_columns.2.refs_1_), channel_id=1, source_target_pairs={{0,1},{1,0},{2,3},{3,2},{4,5},{5,4},{6,7},{7,6},{8,9},{9,8},{10,11... | collective-permute-start | bytes 786440 | tf_op jit(solution)/shard_map/ppermute | solution.py:421
  10.6 12.3 %collective-permute-start.4 = (bf16[256,512]{1,0:T(8,128)(2,1)S(1)}, bf16[256,512]{1,0:T(8,128)(2,1)S(1)}, u32[]{:S(2)}, u32[]{:S(2)}) collective-permute-start(bf16[256,512]{1,0:T(8,128)(2,1)S(1)} %collective-permute-done.3.refs_0_.refs_3_.refs_4_), channel_id=1, source_target_pairs={{2,0},{3,1},{0,4},{1,5},{4,6},{5,7},{6,2},{7,3},{10,8},{11,9},{8,1... | collective-permute-start | bytes 786440 | tf_op jit(solution)/shard_map/ppermute | solution.py:415
  13.9 14.3 %collective-permute-start.2 = (bf16[256,512]{1,0:T(8,128)(2,1)S(1)}, bf16[256,512]{1,0:T(8,128)(2,1)S(1)}, u32[]{:S(2)}, u32[]{:S(2)}) collective-permute-start(bf16[256,512]{1,0:T(8,128)(2,1)S(1)} %bitcast.13), channel_id=1, source_target_pairs={{0,2},{1,3},{4,0},{5,1},{6,4},{7,5},{2,6},{3,7},{8,10},{9,11},{12,... | collective-permute-start | bytes 786440 | tf_op jit(solution)/shard_map/ppermute | solution.py:418
  14.2 5.6 %copy-start.3 = (bf16[1,256,512]{2,1,0:T(8,128)(2,1)S(1)}, bf16[1,256,512]{2,1,0:T(8,128)(2,1)}, u32[]{:S(2)}) copy-start(bf16[1,256,512]{2,1,0:T(8,128)(2,1)} %param.9) | copy-start | bytes 786436
  14.2 14.0 %collective-permute-start.5 = (bf16[2,256,256]{2,1,0:T(8,128)(2,1)S(1)}, bf16[2,256,256]{2,1,0:T(8,128)(2,1)S(1)}, u32[]{:S(2)}, u32[]{:S(2)}) collective-permute-start(bf16[2,256,256]{2,1,0:T(8,128)(2,1)S(1)} %pack_columns.3), channel_id=1, source_target_pairs={{0,1},{1,0},{2,3},{3,2},{4,5},{5,4},{6,7},{7,6},{8,9},{9,8},{10,11... | collective-permute-start | bytes 786440 | tf_op jit(solution)/shard_map/ppermute | solution.py:421
  15.8 6.1 %collective-permute-start.6 = (bf16[1,256,256]{2,1,0:T(8,128)(2,1)S(1)}, bf16[1,256,256]{2,1,0:T(8,128)(2,1)S(1)}, u32[]{:S(2)}, u32[]{:S(2)}) collective-permute-start(bf16[1,256,256]{2,1,0:T(8,128)(2,1)S(1)} %partner_columns.2), channel_id=1, source_target_pairs={{0,16},{8,24},{16,0},{24,8},{1,17},{9,25},{17,1},{25,9},{2,18},{10... | collective-permute-start | bytes 393224 | tf_op jit(solution)/shard_map/ppermute | solution.py:106
  20.2 13.7 %collective-permute-start.8 = (bf16[256,512]{1,0:T(8,128)(2,1)S(1)}, bf16[256,512]{1,0:T(8,128)(2,1)S(1)}, u32[]{:S(2)}, u32[]{:S(2)}) collective-permute-start(bf16[256,512]{1,0:T(8,128)(2,1)S(1)} %get-tuple-element.30.refs_3_), channel_id=1, source_target_pairs={{2,0},{3,1},{0,4},{1,5},{4,6},{5,7},{6,2},{7,3},{10,8},{11,9},{8,1... | collective-permute-start | bytes 786440 | tf_op jit(solution)/shard_map/ppermute | solution.py:415
  21.9 15.4 %collective-permute-start.9 = (bf16[256,512]{1,0:T(8,128)(2,1)S(1)}, bf16[256,512]{1,0:T(8,128)(2,1)S(1)}, u32[]{:S(2)}, u32[]{:S(2)}) collective-permute-start(bf16[256,512]{1,0:T(8,128)(2,1)S(1)} %get-tuple-element.23.refs_4_.refs_2_), channel_id=1, source_target_pairs={{0,2},{1,3},{4,0},{5,1},{6,4},{7,5},{2,6},{3,7},{8,10},{9,11},{12,... | collective-permute-start | bytes 786440 | tf_op jit(solution)/shard_map/ppermute | solution.py:418
  23.0 14.3 %collective-permute-start.11 = (bf16[2,256,256]{2,1,0:T(8,128)(2,1)S(1)}, bf16[2,256,256]{2,1,0:T(8,128)(2,1)S(1)}, u32[]{:S(2)}, u32[]{:S(2)}) collective-permute-start(bf16[2,256,256]{2,1,0:T(8,128)(2,1)S(1)} %get-tuple-element.24.refs_6_.refs_4_), channel_id=1, source_target_pairs={{0,1},{1,0},{2,3},{3,2},{4,5},{5,4},{6,7},{7,6},{8,9},{9,8},{10,11... | collective-permute-start | bytes 786440 | tf_op jit(solution)/shard_map/ppermute | solution.py:421
  29.4 3.0 %copy-start.4 = (bf16[256,512]{1,0:T(8,128)(2,1)S(1)}, bf16[256,512]{1,0:T(8,128)(2,1)}, u32[]{:S(2)}) copy-start(bf16[256,512]{1,0:T(8,128)(2,1)} %refs_3_.1) | copy-start | bytes 786436
  29.4 3.0 %copy-start.5 = (f32[256,128]{1,0:T(8,128)S(1)}, f32[256,128]{1,0:T(8,128)}, u32[]{:S(2)}) copy-start(f32[256,128]{1,0:T(8,128)} %refs_4_.1) | copy-start | bytes 393220
  29.4 17.1 %collective-permute-start.7 = (bf16[4,256,256]{2,1,0:T(8,128)(2,1)S(1)}, bf16[4,256,256]{2,1,0:T(8,128)(2,1)S(1)}, u32[]{:S(2)}, u32[]{:S(2)}) collective-permute-start(bf16[4,256,256]{2,1,0:T(8,128)(2,1)S(1)} %get-tuple-element.28.refs_5_), channel_id=1, source_target_pairs={{0,1},{1,0},{2,3},{3,2},{4,5},{5,4},{6,7},{7,6},{8,9},{9,8},{10,11... | collective-permute-start | bytes 1572872 | tf_op jit(solution)/shard_map/ppermute | solution.py:421
  31.0 1.4 %collective-permute-start.10 = (bf16[2,256,128]{2,1,0:T(8,128)(2,1)S(1)}, bf16[2,256,128]{2,1,0:T(8,128)(2,1)S(1)}, u32[]{:S(2)}, u32[]{:S(2)}) collective-permute-start(bf16[2,256,128]{2,1,0:T(8,128)(2,1)S(1)} %partner_columns.3), channel_id=1, source_target_pairs={{0,8},{8,0},{16,24},{24,16},{1,9},{9,1},{17,25},{25,17},{2,10},{10... | collective-permute-start | bytes 393224 | tf_op jit(solution)/shard_map/ppermute | solution.py:106
  37.3 9.2 %collective-permute-start.12 = (bf16[256,512]{1,0:T(8,128)(2,1)S(1)}, bf16[256,512]{1,0:T(8,128)(2,1)S(1)}, u32[]{:S(2)}, u32[]{:S(2)}) collective-permute-start(bf16[256,512]{1,0:T(8,128)(2,1)S(1)} %add_terms.1), channel_id=1, source_target_pairs={{0,2},{1,3},{4,0},{5,1},{6,4},{7,5},{2,6},{3,7},{8,10},{9,11},{12,... | collective-permute-start | bytes 786440 | tf_op jit(solution)/shard_map/ppermute | solution.py:418
  38.1 4.3 %collective-permute-start.13 = (bf16[256,128]{1,0:T(8,128)(2,1)S(1)}, bf16[256,128]{1,0:T(8,128)(2,1)S(1)}, u32[]{:S(2)}, u32[]{:S(2)}) collective-permute-start(bf16[256,128]{1,0:T(8,128)(2,1)S(1)} %get-tuple-element.32.refs_2_.refs_0_), channel_id=1, source_target_pairs={{0,16},{8,24},{16,0},{24,8},{1,17},{9,25},{17,1},{25,9},{2,18},{10... | collective-permute-start | bytes 196616 | tf_op jit(solution)/shard_map/ppermute | solution.py:106
  42.4 1.4 %collective-permute-start.14 = (bf16[256,256]{1,0:T(8,128)(2,1)S(1)}, bf16[256,256]{1,0:T(8,128)(2,1)S(1)}, u32[]{:S(2)}, u32[]{:S(2)}) collective-permute-start(bf16[256,256]{1,0:T(8,128)(2,1)S(1)} %beside.1.refs_0_), channel_id=1, source_target_pairs={{0,8},{8,0},{16,24},{24,16},{1,9},{9,1},{17,25},{25,17},{2,10},{10... | collective-permute-start | bytes 393224 | tf_op jit(solution)/shard_map/ppermute | solution.py:106
